TPU v7x, 32 devices: a whole 2x2x4 slice. The times are simulated.
32 devices in a mesh: groups: 2 (over y), lanes: 4 (over z), heads: 2 (over x), rep: 2 (over core).
Axes of the slice: x: 2, y: 2, z: 4, core: 2. Of those that a mesh axis runs over, the one named last changes fastest.
Arguments:
- queries: bfloat16 [4096, 2048], P(('groups', 'lanes'), ('heads', 'rep')), parts along dimension 0, may hold values from -6 to 6
- span_states: bfloat16 [4096, 896], P(('groups', 'lanes')), parts along dimension 0, may hold values from -6 to 6
- store: bfloat16 [128, 128, 896], P(('groups', 'lanes'), ('heads', 'rep')), parts along dimension 0, may hold values from -480 to 480
- entry_ids: int32 [64, 2], P(('groups', 'lanes')), parts along dimension 0, may hold values from 0 to 15
- owners: int32 [64, 2], P(('groups', 'lanes')), parts along dimension 0, may hold values from 0 to 3, as said below
- w_key: bfloat16 [896, 2048], P(None, ('heads', 'rep')), may hold values from -0.1875 to 0.1875
- w_value: bfloat16 [896, 2048], P(None, ('heads', 'rep')), may hold values from -0.1875 to 0.1875
- w_out: bfloat16 [2048, 4096], P(('heads', 'rep')), may hold values from -0.125 to 0.125
Outputs:
- attended: bfloat16 [4096, 4096], P(('groups', 'lanes', 'heads', 'rep')), parts along dimension 0
There are 2 independent parts, one for each index of `groups`. A program takes and returns all parts, laid end to end along the dimension named above; an argument that names none is the same for every part. Nothing has to cross between parts.
Inputs may be any that keep to these rules, and one draw needn't show every extreme that they name: Among the 16 neighbours of one lane's spans at most 4 have the same owner, the 2 owners of a span differ, and in every draw one owner holds 4 neighbours of every lane.
All inputs are finite; a program needn't handle non-finite values.
Results may differ from a plain program's by a relative error of at most 0.014.
The roundings to bfloat16 on the way count: a program that leaves them out, or rounds other values in their place, can miss the bound.
Values may be sent and summed in bfloat16 or wider, within the bound.
No kernel may reach another device: no remote copies, remote signals or barrier semaphores. Data moves between devices by JAX's collectives and lax.ppermute only.
A program may use at most 128 MiB of HBM per device.

v0:
```python
import jax
import jax.numpy as jnp
from jax import lax
from jax.sharding import PartitionSpec as P

HD = 128
ENCODER_HEAD_DIM = 128


def encode(tokens, states):
    enc_heads = tokens.shape[2] // ENCODER_HEAD_DIM
    token_head_rows = tokens.reshape(tokens.shape[0], tokens.shape[1], enc_heads, ENCODER_HEAD_DIM)
    head_states = states.reshape(states.shape[0], states.shape[1], enc_heads, ENCODER_HEAD_DIM)
    score_logits = jnp.einsum(
        "bmhd,bkhd->bhmk", token_head_rows, head_states, preferred_element_type=jnp.float32
    ) * ENCODER_HEAD_DIM ** (-0.5)
    attention_result = jax.nn.softmax(score_logits, axis=-1).astype(jnp.bfloat16)
    mixed_input = jnp.einsum(
        "bhmk,bkhd->bmhd", attention_result, head_states, preferred_element_type=jnp.float32
    )
    return (tokens.astype(jnp.float32) + mixed_input.reshape(tokens.shape)).astype(jnp.bfloat16)


def shards(queries, span_states, store, entry_ids, owners, w_key, w_value, w_out):
    n_lanes = lax.axis_size("lanes")
    span_count = entry_ids.shape[0]
    fanout = entry_ids.shape[1]
    requests = span_count * fanout
    capacity = max(2, (requests + n_lanes - 1) // n_lanes)
    slot_count = n_lanes * capacity
    span_len = queries.shape[0] // span_count
    width_enc = store.shape[2]
    tok_dev = store.shape[1]
    flat_owner = owners.reshape(requests)
    flat_entry = entry_ids.reshape(requests)
    order_idx = jnp.arange(requests, dtype=jnp.int32)
    same_owner = flat_owner[:, None] == flat_owner[None, :]
    earlier = order_idx[None, :] < order_idx[:, None]
    slot_rank = jnp.sum(jnp.logical_and(same_owner, earlier), axis=1)
    slot_of = flat_owner * capacity + slot_rank
    slot_hit = slot_of[:, None] == jnp.arange(slot_count, dtype=jnp.int32)[None, :]
    send_entry = jnp.sum(jnp.where(slot_hit, flat_entry[:, None], 0), axis=0)
    send_entry = send_entry.reshape(n_lanes, capacity)
    slot_mask = slot_hit.astype(jnp.bfloat16)
    states_spans = span_states.reshape(span_count, span_len, width_enc)
    fetched = jnp.take(
        store, lax.all_to_all(send_entry, "lanes", split_axis=0, concat_axis=0, tiled=True), axis=0
    )
    returned = lax.all_to_all(fetched, "lanes", split_axis=0, concat_axis=0, tiled=True)
    by_request = jnp.einsum(
        "js,ste->jte",
        slot_mask,
        returned.reshape(slot_count, tok_dev, width_enc),
        preferred_element_type=jnp.float32,
    ).astype(jnp.bfloat16)
    encoded_req = encode(by_request.reshape(span_count, fanout * tok_dev, width_enc), states_spans)
    encoded_req = encoded_req.reshape(span_count, fanout, tok_dev, width_enc)
    w_both = jnp.concatenate((w_key, w_value), axis=1)
    head_cols = w_key.shape[1]
    projected = jnp.dot(
        lax.all_gather(encoded_req, ("heads", "rep"), axis=2, tiled=True),
        w_both,
        preferred_element_type=jnp.float32,
    ).astype(jnp.bfloat16)
    heads_here = head_cols // HD
    key_heads = projected[..., :head_cols].reshape(span_count, -1, heads_here, HD)
    value_heads = projected[..., head_cols:].reshape(span_count, -1, heads_here, HD)
    query_heads = queries.reshape(span_count, span_len, heads_here, HD)
    score_logits = jnp.einsum(
        "cqhd,ckhd->chqk", query_heads, key_heads, preferred_element_type=jnp.float32
    ) * HD ** (-0.5)
    weights = jax.nn.softmax(score_logits, axis=-1).astype(jnp.bfloat16)
    mixed_heads = jnp.einsum(
        "chqk,ckhd->cqhd", weights, value_heads, preferred_element_type=jnp.float32
    ).astype(jnp.bfloat16)
    mixed_heads = mixed_heads.reshape(span_count * span_len, head_cols)
    return lax.psum_scatter(
        jnp.dot(mixed_heads, w_out, preferred_element_type=jnp.float32).astype(jnp.bfloat16),
        ("heads", "rep"),
        scatter_dimension=0,
        tiled=True,
    )


def solution(mesh):
    return jax.shard_map(
        shards,
        mesh=mesh,
        in_specs=(
            P(("groups", "lanes"), ("heads", "rep")),
            P(("groups", "lanes"), None),
            P(("groups", "lanes"), ("heads", "rep"), None),
            P(("groups", "lanes"), None),
            P(("groups", "lanes"), None),
            P(None, ("heads", "rep")),
            P(None, ("heads", "rep")),
            P(("heads", "rep"), None),
        ),
        out_specs=P(("groups", "lanes", "heads", "rep"), None),
        check_vma=False,
    )
```

profile of v0, /device:TPU:0, one launch (start us, length us, event | category | flops | bytes accessed | tf_op | source)
XLA Modules:
  0.0 188.2 jit_solution(6943457388848672781)
XLA Ops:
  6.5 0.0 copy-start
  6.5 0.8 copy.64
  7.4 0.1 reshape.80
  7.5 0.2 convert_reduce_fusion
  7.6 0.8 copy.65
  8.4 0.1 broadcast_in_dim.32
  8.5 0.1 select_reduce_fusion
  8.6 0.1 all_to_all.13
  8.7 11.7 %all_to_all.20 = s32[4,1,4]{2,1,0:T(1,128)S(1)} all-to-all(s32[4,1,4]{2,1,0:T(1,128)S(1)} %bitcast.57), channel_id=1, replica_groups=mesh['groups'=2,'lanes'=4,'heads'=2,'rep'=2] {'lanes'}, dimensions={0} | all-to-all | bytes 128 | tf_op jit(solution)/shard_map/all_to_all | solution.py:47
  20.3 0.1 reshape.90
  20.4 0.0 copy-done
  20.4 0.7 gather_fusion
  21.1 0.2 broadcast_select_fusion
  21.3 1.4 copy.67
  22.7 3.5 %all-to-all-start.1 = ((bf16[4,4,32,896]{3,1,2,0:T(4,128)(2,1)}), bf16[4,4,32,896]{3,1,2,0:T(4,128)(2,1)S(1)}, u32[]{:S(2)}, u32[]{:S(2)}) async-start(bf16[4,4,32,896]{3,1,2,0:T(4,128)(2,1)} %copy.67), calls=%async_computation.1 | async-start | bytes 1835008 | tf_op jit(solution)/shard_map/all_to_all | solution.py:49
  26.2 0.0 all-gather.2.cloned.1.call-start
  26.3 2.1 %reshape_reshape.7 = bf16[8,64,7,128]{3,2,1,0:T(8,128)(2,1)S(1)} reshape(bf16[512,896]{1,0:T(8,128)(2,1)} %param.9) | data formatting | bytes 1835008 | tf_op jit(solution)/shard_map/reshape;reshape | solution.py:13
  28.4 19.5 %all-to-all-done.1 = bf16[4,4,32,896]{3,1,2,0:T(4,128)(2,1)S(1)} async-done(((bf16[4,4,32,896]{3,1,2,0:T(4,128)(2,1)}), bf16[4,4,32,896]{3,1,2,0:T(4,128)(2,1)S(1)}, u32[]{:S(2)}, u32[]{:S(2)}) %all-to-all-start.1) | async-done | bytes 917536 | tf_op jit(solution)/shard_map/all_to_all | solution.py:49
  48.0 1.2 copy.68
  49.2 2.4 %reshape.81 = bf16[16,32,896]{2,0,1:T(8,128)(2,1)} reshape(bf16[4,4,32,896]{3,1,0,2:T(4,128)(2,1)} %copy.68) | data formatting | bytes 1835008 | tf_op jit(solution)/shard_map/reshape | solution.py:53
  51.6 1.6 convolution_convert_fusion.2
  53.2 1.1 copy.69
  54.3 2.9 %reshape_reshape.6 = bf16[8,64,7,128]{3,2,1,0:T(8,128)(2,1)} reshape(bf16[16,32,896]{2,1,0:T(8,128)(2,1)} %copy.69) | data formatting | bytes 1835008 | tf_op jit(solution)/shard_map/reshape;reshape | solution.py:12
  57.2 3.1 %fusion.22 = f32[8,7,64,64]{2,3,1,0:T(8,128)} fusion(bf16[8,64,7,128]{3,2,1,0:T(8,128)(2,1)} %reshape_reshape.6, bf16[8,64,7,128]{3,2,1,0:T(8,128)(2,1)S(1)} %reshape_reshape.7), kind=kOutput, calls=%fused_computation.29 | convolution fusion | flops 58720256 | bytes 2752512 | tf_op jit(solution)/shard_map/bmhd,bkhd->bhmk/dot_general | solution.py:14
  60.2 2.1 %fusion.61 = f32[8,7,64]{2,1,0:T(8,128)S(1)} fusion(bf16[8,64,7,128]{3,2,1,0:T(8,128)(2,1)S(1)} %reshape_reshape.7, bf16[8,64,7,128]{3,2,1,0:T(8,128)(2,1)} %reshape_reshape.6), kind=kOutput, calls=%fused_computation.59 | convolution fusion | flops 59408448 | bytes 1849344 | tf_op jit(solution)/shard_map/sub | solution.py:17
  62.3 1.5 copy.82
  63.8 3.5 %convolution_bitcast_fusion = f32[8,64,7,128]{3,1,2,0:T(8,128)} fusion(f32[8,7,64]{2,1,0:T(8,128)S(1)} %fusion.61, bf16[8,64,7,128]{3,2,1,0:T(8,128)(2,1)S(1)} %reshape_reshape.7, f32[8,7,64,64]{2,3,1,0:T(8,128)} %fusion.22), kind=kOutput, calls=%fused_computation.23 | convolution fusion | flops 59641408 | bytes 3684352 | tf_op jit(solution)/shard_map/bhmk,bkhd->bmhd/dot_general | solution.py:18
  67.4 2.6 %copy.74 = f32[8,64,7,128]{3,2,1,0:T(8,128)S(1)} copy(f32[8,64,7,128]{3,1,2,0:T(8,128)} %convolution_bitcast_fusion) | data formatting | bytes 3670016 | tf_op jit(solution)/shard_map/bhmk,bkhd->bmhd/transpose | solution.py:18
  69.9 1.6 reshape.82
  71.5 3.3 %add_convert_fusion = bf16[8,2,32,896]{3,2,1,0:T(8,128)(2,1)} fusion(f32[8,2,32,896]{3,2,1,0:T(8,128)} %bitcast.52, f32[8,2,32,896]{3,2,1,0:T(8,128)} %reshape.82), kind=kLoop, calls=%fused_computation.18 | loop fusion | flops 917504 | bytes 4587520 | tf_op jit(solution)/shard_map/convert_element_type | solution.py:21
  74.8 0.0 all-gather.2.cloned.1.call-update
  74.8 0.2 reduce-scatter.2.cloned.1.call-start
  75.1 0.1 reshape.85
  75.2 30.4 %all-gather.2.cloned.1.call-done = bf16[8,2,128,896]{3,2,1,0:T(8,128)(2,1)} async-done(((bf16[8,2,32,896]{3,2,1,0:T(8,128)(2,1)}), bf16[8,2,128,896]{3,2,1,0:T(8,128)(2,1)}) %all-gather.2.cloned.1.call-update) | async-done | bytes 3670032 | tf_op jit(solution)/shard_map/all_gather | solution.py:61
  105.6 0.0 copy-done.4
  105.6 6.8 %convolution_convert_fusion.1 = bf16[8,2,128,1024]{3,2,1,0:T(8,128)(2,1)S(1)} fusion(bf16[8,2,128,896]{3,2,1,0:T(8,128)(2,1)} %all-gather.2.cloned.1.call-done, bf16[896,512]{1,0:T(8,128)(2,1)S(1)} %copy-done.4, bf16[896,512]{1,0:T(8,128)(2,1)} %param.13), kind=kOutput, calls=%fused_computation.4 | convolution fusion | flops 3763863552 | bytes 9699328 | tf_op jit(solution)/shard_map/dot_general | solution.py:60
  112.4 2.5 %fusion.60 = (bf16[8,2,128,512]{3,2,1,0:T(8,128)(2,1)}, bf16[8,2,128,512]{3,2,1,0:T(8,128)(2,1)}) fusion(bf16[8,2,128,1024]{3,2,1,0:T(8,128)(2,1)S(1)} %convolution_convert_fusion.1), kind=kLoop, calls=%fused_computation.58 | loop fusion | bytes 8388608 | tf_op jit(solution)/shard_map/slice | solution.py:66
  114.9 2.5 %reshape.84 = bf16[8,256,4,128]{3,2,1,0:T(4,128)(2,1)S(1)} reshape(bf16[8,2,128,512]{3,2,1,0:T(8,128)(2,1)} %get-tuple-element.5) | data formatting | bytes 4194304 | tf_op jit(solution)/shard_map/reshape | solution.py:66
  117.4 0.8 fusion.6
  118.3 1.3 copy-done.2
  119.6 0.9 fusion.66
  120.4 0.7 copy-done.1
  121.2 2.1 %reshape.83 = bf16[8,256,4,128]{3,2,1,0:T(4,128)(2,1)} reshape(bf16[8,2,128,512]{3,2,1,0:T(8,128)(2,1)S(1)} %copy-done.1) | data formatting | bytes 4194304 | tf_op jit(solution)/shard_map/reshape | solution.py:67
  123.2 6.5 %fusion.17 = bf16[8,64,4,128]{3,1,2,0:T(8,128)(2,1)S(1)} fusion(bf16[8,256,4,128]{3,2,1,0:T(4,128)(2,1)} %reshape.83, f32[8,4,64]{2,1,0:T(4,128)S(1)} %fusion.66, f32[8,4,256,64]{2,3,1,0:T(8,128)} %copy-done.2), kind=kOutput, calls=%fused_computation.26 | convolution fusion | flops 137103616 | bytes 4726784 | tf_op jit(solution)/shard_map/chqk,ckhd->cqhd/dot_general | solution.py:73
  129.7 0.4 copy.79
  130.2 6.5 %convolution_convert_fusion = bf16[512,4096]{1,0:T(8,128)(2,1)} fusion(bf16[512,4096]{1,0:T(8,128)(2,1)} %param.15, bf16[64,8,4,128]{3,2,1,0:T(4,128)(2,1)S(1)} %bitcast.54), kind=kOutput, calls=%fused_computation.3 | convolution fusion | flops 2149580800 | bytes 8912896 | tf_op jit(solution)/shard_map/dot_general | solution.py:78
  136.6 0.0 reduce-scatter.2.cloned.1.call-update
  136.7 44.7 %reduce-scatter.2.cloned.1.call-done = bf16[128,4096]{1,0:T(8,128)(2,1)} async-done(((bf16[512,4096]{1,0:T(8,128)(2,1)}), bf16[128,4096]{1,0:T(8,128)(2,1)}) %reduce-scatter.2.cloned.1.call-update) | async-done | bytes 1048592 | tf_op jit(solution)/shard_map/reduce_scatter | solution.py:77
  (9 shorter events, 0.0 us)
Async XLA Ops:
  6.5 13.9 %copy-start = (bf16[16,32,896]{2,1,0:T(8,128)(2,1)S(1)}, bf16[16,32,896]{2,1,0:T(8,128)(2,1)}, u32[]{:S(2)}) copy-start(bf16[16,32,896]{2,1,0:T(8,128)(2,1)} %param.10) | copy-start | bytes 2752516
  22.7 25.2 %all-to-all-start.1 = ((bf16[4,4,32,896]{3,1,2,0:T(4,128)(2,1)}), bf16[4,4,32,896]{3,1,2,0:T(4,128)(2,1)S(1)}, u32[]{:S(2)}, u32[]{:S(2)}) async-start(bf16[4,4,32,896]{3,1,2,0:T(4,128)(2,1)} %copy.67), calls=%async_computation.1 | async-start | bytes 1835008 | tf_op jit(solution)/shard_map/all_to_all | solution.py:49
  26.2 79.4 %all-gather.2.cloned.1.call-start = ((), (), s32[]{:S(2)}) async-start(), calls=%async_computation.3 | async-start | bytes 4587520 | tf_op jit(solution)/shard_map/all_gather | solution.py:61
  71.5 3.5 %copy-start.3 = (bf16[512,512]{1,0:T(8,128)(2,1)S(1)}, bf16[512,512]{1,0:T(8,128)(2,1)}, u32[]{:S(2)}) copy-start(bf16[512,512]{1,0:T(8,128)(2,1)} %param.8) | copy-start | bytes 1572868
  71.5 34.1 %copy-start.4 = (bf16[896,512]{1,0:T(8,128)(2,1)S(1)}, bf16[896,512]{1,0:T(8,128)(2,1)}, u32[]{:S(2)}) copy-start(bf16[896,512]{1,0:T(8,128)(2,1)} %param.14) | copy-start | bytes 2752516
  74.8 106.5 %reduce-scatter.2.cloned.1.call-start = ((), (), s32[]{:S(2)}) async-start(), calls=%async_computation.4 | async-start | bytes 5242880 | tf_op jit(solution)/shard_map/reduce_scatter | solution.py:77
  118.3 1.3 copy-start.2
  119.6 1.6 copy-start.1
Sparse Core Ops, SparseCore 0:
  75.0 30.6 all-gather.1
  136.8 44.4 reduce-scatter.1
where the time goes:
time: 189 us; the launch traced here: 188 us
  waiting for transfers between devices  94.6 us (50%)
  matrix products  31 us (16%)
  local copies, waits for them, and re-layouts  29 us (15%)
  between operations  13.5 us (7%)
  blocking collectives  11.7 us (6%)
  other arithmetic  4.61 us (2%)
  starting transfers between devices  3.77 us (2%)
    reduce_scatter x1, waiting for transfers between devices, shards(): lax.psum_scatter(jnp.dot(mixed_heads, w_out, preferred_element_type=jnp.f...  44.7 us
    all_gather x1, waiting for transfers between devices, shards(): lax.all_gather(encoded_req, ('heads', 'rep'), axis=2, tiled=True)  30.4 us
    all_to_all x1, waiting for transfers between devices, shards(): lax.all_to_all(fetched, 'lanes', split_axis=0, concat_axis=0, tiled=True)  19.5 us
    all_to_all x1, blocking collectives, shards(): lax.all_to_all(send_entry, 'lanes', split_axis=0, concat_axis=0, tiled=True)  11.7 us
    dot_general x1, matrix products, shards(): jnp.dot(lax.all_gather(encoded_req, ('heads', 'rep'), axis=2, tiled=True)...  6.81 us
    dot_general x1, matrix products, shards(): jnp.einsum('chqk,ckhd->cqhd', weights, value_heads, preferred_element_typ...  6.51 us
    dot_general x1, matrix products, shards(): jnp.dot(mixed_heads, w_out, preferred_element_type=jnp.float32)  6.46 us
  transfers between devices with their start and end apart: 3, of which 3 were waited for; matrix products, arithmetic and copies ran while one was open for 1% of the time, Pallas kernels for 0%

commit v1 on v0

v1 whole, which is shorter than its diff:
```python
import functools

import jax
import jax.numpy as jnp
from jax import lax
from jax.experimental import pallas as pl
from jax.experimental.pallas import tpu as pltpu
from jax.sharding import PartitionSpec as P

HD = 128
ENCODER_HEAD_DIM = 128
F32 = jnp.float32
BF16 = jnp.bfloat16
LATER_GROUPS = 3
FIRST_COLS = 1024

VMEM = pl.BlockSpec(memory_space=pltpu.VMEM)
SMEM = pl.BlockSpec(memory_space=pltpu.SMEM)
ANY = pl.BlockSpec(memory_space=pl.ANY)


def params(mib):
    return pltpu.CompilerParams(vmem_limit_bytes=mib * 2**20)


def cost(flops, bytes_accessed):
    return pl.CostEstimate(flops=int(flops), bytes_accessed=int(bytes_accessed), transcendentals=0)


def apart(n, a, b):
    if n & (n - 1) == 0:
        return a ^ b
    return lax.rem(b - a + n, n)


def lane_pairs(n, d, reply):
    if n & (n - 1) == 0:
        return [(i, i ^ d) for i in range(n)]
    return [(i, (i - d if reply else i + d) % n) for i in range(n)]


def shift_pairs(n, s):
    return [(i, (i + s) % n) for i in range(n)]


def dot_t(a, b):
    return lax.dot_general(a, b, (((1,), (1,)), ((), ())), preferred_element_type=F32)


def dot(a, b):
    return jnp.dot(a, b, preferred_element_type=F32)


def plan_kernel(n_lanes, cap, owners_ref, entries_ref, want_ref, req_ref, slot_ref, count_ref):
    lane = lax.axis_index("lanes")
    fanout, spans = owners_ref.shape
    for i in range(n_lanes):
        count_ref[i] = 0
    for i in range(n_lanes * cap):
        want_ref[i] = 0
        req_ref[i] = 0
    for j in range(fanout * spans):
        d = apart(n_lanes, lane, owners_ref[j % fanout, j // fanout])
        rank = count_ref[d]
        count_ref[d] = rank + 1
        slot = d * cap + rank
        want_ref[slot] = entries_ref[j % fanout, j // fanout]
        req_ref[slot] = j
        slot_ref[j] = slot


def plan(owners, entry_ids, n_lanes, cap):
    requests = owners.size
    table = jax.ShapeDtypeStruct((n_lanes * cap,), jnp.int32)
    return pl.pallas_call(
        functools.partial(plan_kernel, n_lanes, cap),
        out_shape=(table, table, jax.ShapeDtypeStruct((requests,), jnp.int32)),
        in_specs=[SMEM, SMEM],
        out_specs=(SMEM, SMEM, SMEM),
        scratch_shapes=[pltpu.SMEM((n_lanes,), jnp.int32)],
        name="plan",
    )(owners.T, entry_ids.T)


def fetch_kernel(n_lanes, cap, *refs):
    others = n_lanes - 1
    asked, store_ref, outs, sem = refs[:others], refs[others], refs[others + 1 : -1], refs[-1]
    copies = []
    for d in range(1, n_lanes):
        for s in range(cap):
            entry = asked[d - 1][d * cap + s]
            copies.append(
                pltpu.make_async_copy(store_ref.at[entry], outs[d - 1].at[s], sem.at[(d - 1) * cap + s])
            )
    for copy in copies:
        copy.start()
    for copy in copies:
        copy.wait()


def fetch(asked, store, n_lanes, cap):
    block = jax.ShapeDtypeStruct((cap,) + store.shape[1:], store.dtype)
    others = n_lanes - 1
    return pl.pallas_call(
        functools.partial(fetch_kernel, n_lanes, cap),
        out_shape=[block] * others,
        in_specs=[SMEM] * others + [ANY],
        out_specs=[ANY] * others,
        scratch_shapes=[pltpu.SemaphoreType.DMA((others * cap,))],
        cost_estimate=cost(0, 2 * others * cap * store[0].size * 2),
        name="fetch",
    )(*asked, store)


def encode_slot(tokens, states):
    pieces = []
    for h in range(tokens.shape[1] // ENCODER_HEAD_DIM):
        cols = slice(h * ENCODER_HEAD_DIM, (h + 1) * ENCODER_HEAD_DIM)
        token, state = tokens[:, cols], states[:, cols]
        logits = dot_t(token, state) * ENCODER_HEAD_DIM ** (-0.5)
        weights = jnp.exp(logits - jnp.max(logits, axis=1, keepdims=True))
        weights = weights / jnp.sum(weights, axis=1, keepdims=True)
        mixed = dot(weights.astype(BF16), state)
        pieces.append((token.astype(F32) + mixed).astype(BF16))
    return jnp.concatenate(pieces, axis=1)


def encode_kernel(first, cap, fanout, span_len, req_ref, states_ref, *refs):
    blocks, out_ref = refs[:-1], refs[-1]
    for i, block in enumerate(blocks):
        for s in range(cap):
            span = lax.div(req_ref[(first + i) * cap + s], fanout)
            rows = pl.ds(pl.multiple_of(span * span_len, span_len), span_len)
            out_ref[i * cap + s] = encode_slot(block[s], states_ref[rows, :])


def encode_local_kernel(cap, fanout, span_len, req_ref, want_ref, states_ref, store_ref, out_ref, tokens_ref, sem):
    copies = [
        pltpu.make_async_copy(store_ref.at[want_ref[s]], tokens_ref.at[s], sem.at[s]) for s in range(cap)
    ]
    for copy in copies:
        copy.start()
    for s, copy in enumerate(copies):
        span = lax.div(req_ref[s], fanout)
        rows = pl.ds(pl.multiple_of(span * span_len, span_len), span_len)
        copy.wait()
        out_ref[s] = encode_slot(tokens_ref[s], states_ref[rows, :])


def encode_cost(slots, tokens, span_len, width):
    return cost(4 * slots * tokens * span_len * width, 4 * slots * tokens * width + 1024 * width)


def encode_local(plans, span_states, store, cap, fanout, span_len):
    want, req, _ = plans
    shape = (cap,) + store.shape[1:]
    return pl.pallas_call(
        functools.partial(encode_local_kernel, cap, fanout, span_len),
        out_shape=jax.ShapeDtypeStruct(shape, BF16),
        in_specs=[SMEM, SMEM, VMEM, ANY],
        out_specs=VMEM,
        scratch_shapes=[pltpu.VMEM(shape, BF16), pltpu.SemaphoreType.DMA((cap,))],
        compiler_params=params(16),
        cost_estimate=encode_cost(cap, store.shape[1], span_len, store.shape[2]),
        name="encode_local",
    )(req, want, span_states, store)


def encode(plans, span_states, blocks, first, cap, fanout, span_len):
    req = plans[1]
    _, tokens, width = blocks[0].shape
    slots = len(blocks) * cap
    return pl.pallas_call(
        functools.partial(encode_kernel, first, cap, fanout, span_len),
        out_shape=jax.ShapeDtypeStruct((slots, tokens, width), BF16),
        in_specs=[SMEM, VMEM] + [VMEM] * len(blocks),
        out_specs=VMEM,
        compiler_params=params(16),
        cost_estimate=encode_cost(slots, tokens, span_len, width),
        name="encode",
    )(req, span_states, *blocks)


def project_into(kv_ref, first, pieces, wk_ref, wv_ref):
    slots, tokens, width = pieces[0].shape
    rows = jnp.concatenate([piece[...].reshape(slots * tokens, width) for piece in pieces], axis=0)
    cols = wk_ref.shape[1]
    for side, weight in enumerate((wk_ref, wv_ref)):
        made = dot(rows, weight[...]).astype(BF16)
        for p in range(len(pieces)):
            part = made[p * slots * tokens : (p + 1) * slots * tokens]
            kv_ref[first : first + slots, p, :, side * cols : (side + 1) * cols] = part.reshape(
                slots, tokens, cols
            )


def project_kernel(n_pieces, *refs):
    pieces, (wk_ref, wv_ref, kv_ref) = refs[:n_pieces], refs[n_pieces:]
    project_into(kv_ref, 0, pieces, wk_ref, wv_ref)


def project_cost(pieces, w_key):
    rows = len(pieces) * pieces[0].shape[0] * pieces[0].shape[1]
    width, cols = w_key.shape
    return 4 * rows * width * cols, 2 * rows * (width + 2 * cols) + 4 * width * cols


def project(pieces, w_key, w_value):
    slots, tokens, _ = pieces[0].shape
    shape = (slots, len(pieces), tokens, 2 * w_key.shape[1])
    return pl.pallas_call(
        functools.partial(project_kernel, len(pieces)),
        out_shape=jax.ShapeDtypeStruct(shape, BF16),
        in_specs=[VMEM] * (len(pieces) + 2),
        out_specs=VMEM,
        compiler_params=params(32),
        cost_estimate=cost(*project_cost(pieces, w_key)),
        name="project",
    )(*pieces, w_key, w_value)


def attend_kernel(firsts, n_pieces, n_heads, n_rep, fanout, spans, slot_ref, q_ref, *refs):
    n_ready = len(firsts) - 1
    ready, refs = refs[:n_ready], refs[n_ready:]
    pieces, refs = refs[:n_pieces], refs[n_pieces:]
    wk_ref, wv_ref = refs[:2]
    outs = refs[2 : 2 + n_rep]
    kv_ref, sem = refs[2 + n_rep :]
    copies = [
        pltpu.make_async_copy(ref, kv_ref.at[pl.ds(first, ref.shape[0])], sem.at[i])
        for i, (ref, first) in enumerate(zip(ready, firsts))
    ]
    for copy in copies:
        copy.start()
    project_into(kv_ref, firsts[-1], pieces, wk_ref, wv_ref)
    for copy in copies:
        copy.wait()
    heads_at, rep_at = lax.axis_index("heads"), lax.axis_index("rep")
    cols_all = wk_ref.shape[1]
    span_len = q_ref.shape[0] // spans
    block = spans // (n_heads * n_rep)
    tokens = kv_ref.shape[1] * kv_ref.shape[2]
    for t in reversed(range(n_heads)):
        for s in range(n_rep):
            owner = lax.rem(heads_at + t, n_heads) * n_rep + lax.rem(rep_at + s, n_rep)
            for i in range(block):
                span = owner * block + i
                slots = [slot_ref[span * fanout + k] for k in range(fanout)]
                rows = pl.ds(pl.multiple_of(span * span_len, span_len), span_len)
                for h in range(cols_all // HD):
                    key_cols = slice(h * HD, (h + 1) * HD)
                    value_cols = slice(cols_all + h * HD, cols_all + (h + 1) * HD)
                    query = q_ref[rows, key_cols]
                    keys = [kv_ref[slot, :, :, key_cols].reshape(tokens, HD) for slot in slots]
                    values = [kv_ref[slot, :, :, value_cols].reshape(tokens, HD) for slot in slots]
                    logits = [dot_t(query, key) * HD ** (-0.5) for key in keys]
                    top = functools.reduce(
                        jnp.maximum, [jnp.max(part, axis=1, keepdims=True) for part in logits]
                    )
                    weights = [jnp.exp(part - top) for part in logits]
                    total = sum(jnp.sum(part, axis=1, keepdims=True) for part in weights)
                    mixed = sum(dot(part.astype(BF16), value) for part, value in zip(weights, values))
                    outs[s][t, i * span_len : (i + 1) * span_len, key_cols] = (mixed / total).astype(BF16)


def attend(plans, queries, ready, pieces, w_key, w_value, n_heads, n_rep, fanout, spans):
    firsts = [0]
    for kv in ready:
        firsts.append(firsts[-1] + kv.shape[0])
    slots, tokens, _ = pieces[0].shape
    cols = w_key.shape[1]
    rows = queries.shape[0] // (n_heads * n_rep)
    flops, moved = project_cost(pieces, w_key)
    all_slots = firsts[-1] + slots
    kv_shape = (all_slots, len(pieces), tokens, 2 * cols)
    return pl.pallas_call(
        functools.partial(attend_kernel, firsts, len(pieces), n_heads, n_rep, fanout, spans),
        out_shape=[jax.ShapeDtypeStruct((n_heads, rows, cols), BF16)] * n_rep,
        in_specs=[SMEM, VMEM] + [ANY] * len(ready) + [VMEM] * (len(pieces) + 2),
        out_specs=[VMEM] * n_rep,
        scratch_shapes=[pltpu.VMEM(kv_shape, BF16), pltpu.SemaphoreType.DMA((max(1, len(ready)),))],
        compiler_params=params(40),
        cost_estimate=cost(
            flops + 4 * queries.size * fanout * len(pieces) * tokens,
            moved + 2 * all_slots * len(pieces) * tokens * 2 * cols + 4 * queries.size,
        ),
        name="attend",
    )(plans[2], queries, *ready, *pieces, w_key, w_value)


def out_kernel(n_rep, *refs):
    mixed, weights, out_ref = refs[:n_rep], refs[n_rep:-1], refs[-1]
    out_ref[...] = sum(dot(a[0], w[...]) for a, w in zip(mixed, weights)).astype(BF16)


def out_project(mixed, weights, t, start, stop, tile):
    _, rows, depth = mixed[0].shape
    base = start // tile
    return pl.pallas_call(
        functools.partial(out_kernel, len(mixed)),
        grid=((stop - start) // tile,),
        out_shape=jax.ShapeDtypeStruct((rows, stop - start), BF16),
        in_specs=[pl.BlockSpec((1, rows, depth), lambda j: (t, 0, 0))] * len(mixed)
        + [pl.BlockSpec((depth, tile), lambda j: (0, base + j))] * len(mixed),
        out_specs=pl.BlockSpec((rows, tile), lambda j: (0, j)),
        compiler_params=params(16),
        cost_estimate=cost(
            2 * len(mixed) * rows * depth * (stop - start), 2 * len(mixed) * depth * (stop - start)
        ),
        name="out_project",
    )(*mixed, *weights)


def shards(queries, span_states, store, entry_ids, owners, w_key, w_value, w_out):
    n_lanes, n_heads, n_rep = (lax.axis_size(name) for name in ("lanes", "heads", "rep"))
    spans, fanout = entry_ids.shape
    requests = spans * fanout
    cap = max(2, (requests + n_lanes - 1) // n_lanes)
    span_len = queries.shape[0] // spans

    plans = plan(owners, entry_ids, n_lanes, cap)
    asked = [lax.ppermute(plans[0], "lanes", lane_pairs(n_lanes, d, False)) for d in range(1, n_lanes)]
    w_outs = [w_out] + [lax.ppermute(w_out, "rep", shift_pairs(n_rep, s)) for s in range(1, n_rep)]

    def gather(encoded):
        pieces = [encoded]
        pieces += [lax.ppermute(encoded, "heads", shift_pairs(n_heads, s)) for s in range(1, n_heads)]
        return pieces + [
            lax.ppermute(piece, "rep", shift_pairs(n_rep, s)) for piece in pieces for s in range(1, n_rep)
        ]

    groups = [gather(encode_local(plans, span_states, store, cap, fanout, span_len))]
    fetched = fetch(asked, store, n_lanes, cap)
    arrived = [
        lax.ppermute(fetched[d - 1], "lanes", lane_pairs(n_lanes, d, True)) for d in range(1, n_lanes)
    ]
    size = -(-(n_lanes - 1) // LATER_GROUPS)
    for first in range(1, n_lanes, size):
        blocks = arrived[first - 1 : first - 1 + size]
        groups.append(gather(encode(plans, span_states, blocks, first, cap, fanout, span_len)))
    ready = [project(pieces, w_key, w_value) for pieces in groups[:-1]]
    mixed = attend(plans, queries, ready, groups[-1], w_key, w_value, n_heads, n_rep, fanout, spans)
    mixed = [mixed[0]] + [lax.ppermute(mixed[s], "rep", shift_pairs(n_rep, s)) for s in range(1, n_rep)]

    width = w_out.shape[1]
    tile = min(FIRST_COLS, width)
    cuts = [0, tile, width] if tile < width else [0, width]
    received = []
    for t in range(1, n_heads):
        parts = []
        for start, stop in zip(cuts, cuts[1:]):
            partial = out_project(mixed, w_outs, t, start, stop, tile)
            parts.append(lax.ppermute(partial, "heads", shift_pairs(n_heads, t)))
        received.append(jnp.concatenate(parts, axis=1))
    total = out_project(mixed, w_outs, 0, 0, width, tile).astype(F32)
    for part in received:
        total = total + part.astype(F32)
    return total.astype(BF16)


def solution(mesh):
    return jax.shard_map(
        shards,
        mesh=mesh,
        in_specs=(
            P(("groups", "lanes"), ("heads", "rep")),
            P(("groups", "lanes"), None),
            P(("groups", "lanes"), ("heads", "rep"), None),
            P(("groups", "lanes"), None),
            P(("groups", "lanes"), None),
            P(None, ("heads", "rep")),
            P(None, ("heads", "rep")),
            P(("heads", "rep"), None),
        ),
        out_specs=P(("groups", "lanes", "heads", "rep"), None),
        check_vma=False,
    )
```

time: 189 us -> 145 us (0.77)
  Pallas kernels: 0 us -> 85 us
  waiting for transfers between devices: 94.6 us -> 35.3 us
  matrix products: 31 us -> 0 us
  local copies, waits for them, and re-layouts: 29 us -> 4.7 us
  starting transfers between devices: 3.77 us -> 18 us
  between operations: 13.5 us -> 0.23 us
  blocking collectives: 11.7 us -> 0 us
  other arithmetic: 4.61 us -> 1.22 us
    pallas_call x0 -> x13, Pallas kernels: none -> 85 us  [the longest x3 27.3 us: encode(): pl.pallas_call(functools.partial(encode_kernel, first, cap, fanout, span_...]
    reduce_scatter x1 -> x0, waiting for transfers between devices: 44.7 us -> none  [shards(): lax.psum_scatter(jnp.dot(mixed_heads, w_out, preferred_element_type=jnp.f...]
    ppermute x0 -> x22, waiting for transfers between devices: none -> 35.3 us  [the longest x2 17.2 us: shards(): parts.append(lax.ppermute(partial, 'heads', shift_pairs(n_heads, t)))]
    all_gather x1 -> x0, waiting for transfers between devices: 30.4 us -> none  [shards(): lax.all_gather(encoded_req, ('heads', 'rep'), axis=2, tiled=True)]
    dot_general x7 -> x0, matrix products: 28.9 us -> none  [the longest x1 6.81 us: shards(): jnp.dot(lax.all_gather(encoded_req, ('heads', 'rep'), axis=2, tiled=True)...]
    all_to_all x1 -> x0, waiting for transfers between devices: 19.5 us -> none  [shards(): lax.all_to_all(fetched, 'lanes', split_axis=0, concat_axis=0, tiled=True)]
    ppermute x0 -> x22, starting transfers between devices: none -> 18 us  [the longest x4 5.15 us: gather(): lax.ppermute(encoded, 'heads', shift_pairs(n_heads, s))]
    all_to_all x1 -> x0, blocking collectives: 11.7 us -> none  [shards(): lax.all_to_all(send_entry, 'lanes', split_axis=0, concat_axis=0, tiled=True)]
  transfers between devices with their start and end apart: 3 -> 22, of which waited for: 3 -> 6; matrix products, arithmetic and copies ran while one was open for 1% -> 0% of each run, Pallas kernels for 0% -> 56%
where the time goes in v1:
time: 145 us; the launch traced here: 144 us
  Pallas kernels  85 us (59%)
  waiting for transfers between devices  35.3 us (24%)
  starting transfers between devices  18 us (12%)
  local copies, waits for them, and re-layouts  4.7 us (3%)
    pallas_call x3, Pallas kernels, encode(): pl.pallas_call(functools.partial(encode_kernel, first, cap, fanout, span_...  27.3 us
    pallas_call x1, Pallas kernels, fetch(): pl.pallas_call(functools.partial(fetch_kernel, n_lanes, cap), out_shape=[...  22.7 us
    ppermute x2, waiting for transfers between devices, shards(): parts.append(lax.ppermute(partial, 'heads', shift_pairs(n_heads, t)))  17.2 us
    pallas_call x1, Pallas kernels, attend(): pl.pallas_call(functools.partial(attend_kernel, firsts, len(pieces), n_he...  10.6 us
    pallas_call x1, Pallas kernels, encode_local(): pl.pallas_call(functools.partial(encode_local_kernel, cap, fanout, span_l...  9.81 us
    pallas_call x3, Pallas kernels, out_project(): pl.pallas_call(functools.partial(out_kernel, len(mixed)), grid=((stop - s...  9.45 us
    ppermute x3, waiting for transfers between devices, shards(): lax.ppermute(fetched[d - 1], 'lanes', lane_pairs(n_lanes, d, True))  6.54 us
    ppermute x4, waiting for transfers between devices, gather(): lax.ppermute(encoded, 'heads', shift_pairs(n_heads, s))  6.4 us
  transfers between devices with their start and end apart: 22, of which 6 were waited for; matrix products, arithmetic and copies ran while one was open for 0% of the time, Pallas kernels for 56%

profile of v1, /device:TPU:0, one launch (start us, length us, event | category | flops | bytes accessed | tf_op | source)
XLA Modules:
  0.0 144.4 jit_solution(12047844523990204124)
XLA Ops:
  0.0 0.5 collective-permute-start.19
  0.5 1.3 plan.1
  1.8 0.0 copy-start.1
  1.8 1.2 copy-done.1
  3.0 1.2 copy-done.5
  4.2 0.6 copy-done.7
  4.8 0.7 copy-done.10
  5.4 9.8 %encode_local.1.refs_0_ = bf16[4,32,896]{2,1,0:T(8,128)(2,1)S(1)} custom-call(s32[16]{0:T(128)S(1)} %copy-done.7, s32[16]{0:T(128)S(1)} %copy-done.10, bf16[512,896]{1,0:T(8,128)(2,1)S(1)} %copy-done.1, bf16[16,32,896]{2,1,0:T(8,128)(2,1)S(1)} %copy-done.5), custom_call_target="tpu_custom_call" | custom-call | flops 29360128 | bytes 1376256 | tf_op jit(solution)/shard_map/encode_local/pallas_call | solution.py:157
  15.3 2.6 %collective-permute-start = (bf16[4,32,896]{2,1,0:T(8,128)(2,1)S(1)}, bf16[4,32,896]{2,1,0:T(8,128)(2,1)S(1)}, u32[]{:S(2)}, u32[]{:S(2)}) collective-permute-start(bf16[4,32,896]{2,1,0:T(8,128)(2,1)S(1)} %encode_local.1.refs_0_), channel_id=1, source_target_pairs={{0,2},{2,0},{1,3},{3,1},{4,6},{6,4},{5,7},{7,5},{8,10},{10,8},{9,1... | collective-permute-start | bytes 688136 | tf_op jit(solution)/shard_map/ppermute | solution.py:327
  17.8 3.6 %collective-permute-start.5 = (s32[16]{0:T(128)S(1)}, s32[16]{0:T(128)S(1)}, u32[]{:S(2)}, u32[]{:S(2)}) collective-permute-start(s32[16]{0:T(128)S(1)} %copy-done.10), channel_id=1, source_target_pairs={{0,12},{4,8},{8,4},{12,0},{1,13},{5,9},{9,5},{13,1},{2,14},{6,10},... | collective-permute-start | bytes 200 | tf_op jit(solution)/shard_map/ppermute | solution.py:322
  21.4 0.8 collective-permute-start.3
  22.2 0.9 collective-permute-done.5.refs_2_
  23.2 2.7 %collective-permute-done.4.refs_1_ = s32[16]{0:T(128)S(1)} collective-permute-done((s32[16]{0:T(128)S(1)}, s32[16]{0:T(128)S(1)}, u32[]{:S(2)}, u32[]{:S(2)}) %collective-permute-start.4) | collective-permute-done | bytes 96 | tf_op jit(solution)/shard_map/ppermute | solution.py:322
  25.9 0.5 copy-done.12
  26.4 0.5 copy-done.13
  26.9 22.7 %fetch.1 = (bf16[4,32,896]{2,1,0:T(8,128)(2,1)}, bf16[4,32,896]{2,1,0:T(8,128)(2,1)}, bf16[4,32,896]{2,1,0:T(8,128)(2,1)}) custom-call(s32[16]{0:T(128)} %copy-done.13, s32[16]{0:T(128)} %copy-done.12, s32[16]{0:T(128)} %copy-done.11, bf16[16,32,896]{2,1,0:T(8,128)(2,1)} %refs_3_.1), custom_call_target="tpu_custom_call" | custom-call | bytes 1376256 | tf_op jit(solution)/shard_map/fetch/pallas_call | solution.py:104
  49.6 0.0 copy-start.3
  49.7 0.0 copy-start.4
  49.7 0.1 collective-permute-start.6
  49.7 1.6 %collective-permute-start.10 = (bf16[4,32,896]{2,1,0:T(8,128)(2,1)}, bf16[4,32,896]{2,1,0:T(8,128)(2,1)S(1)}, u32[]{:S(2)}, u32[]{:S(2)}) collective-permute-start(bf16[4,32,896]{2,1,0:T(8,128)(2,1)} %get-tuple-element.17), channel_id=1, source_target_pairs={{0,8},{4,12},{8,0},{12,4},{1,9},{5,13},{9,1},{13,5},{2,10},{6,14},... | collective-permute-start | bytes 688136 | tf_op jit(solution)/shard_map/ppermute | solution.py:335
  51.3 2.8 %collective-permute-start.14 = (bf16[4,32,896]{2,1,0:T(8,128)(2,1)}, bf16[4,32,896]{2,1,0:T(8,128)(2,1)S(1)}, u32[]{:S(2)}, u32[]{:S(2)}) collective-permute-start(bf16[4,32,896]{2,1,0:T(8,128)(2,1)} %get-tuple-element.18), channel_id=1, source_target_pairs={{0,12},{4,8},{8,4},{12,0},{1,13},{5,9},{9,5},{13,1},{2,14},{6,10},... | collective-permute-start | bytes 688136 | tf_op jit(solution)/shard_map/ppermute | solution.py:335
  54.1 6.5 %collective-permute-done.6.refs_0_ = bf16[4,32,896]{2,1,0:T(8,128)(2,1)S(1)} collective-permute-done((bf16[4,32,896]{2,1,0:T(8,128)(2,1)}, bf16[4,32,896]{2,1,0:T(8,128)(2,1)S(1)}, u32[]{:S(2)}, u32[]{:S(2)}) %collective-permute-start.6) | collective-permute-done | bytes 229408 | tf_op jit(solution)/shard_map/ppermute | solution.py:335
  60.7 9.1 %encode.3.refs_0_ = bf16[4,32,896]{2,1,0:T(8,128)(2,1)S(1)} custom-call(s32[16]{0:T(128)S(1)} %copy-done.8, bf16[512,896]{1,0:T(8,128)(2,1)S(1)} %copy-done.2, bf16[4,32,896]{2,1,0:T(8,128)(2,1)S(1)} %collective-permute-done.6.refs_0_), custom_call_target="tpu_custom_call" | custom-call | flops 29360128 | bytes 1376256 | tf_op jit(solution)/shard_map/encode/pallas_call | solution.py:173
  69.8 0.6 collective-permute-start.7
  70.3 9.1 %encode.4.refs_0_ = bf16[4,32,896]{2,1,0:T(8,128)(2,1)S(1)} custom-call(s32[16]{0:T(128)S(1)} %copy-done.8, bf16[512,896]{1,0:T(8,128)(2,1)S(1)} %copy-done.2, bf16[4,32,896]{2,1,0:T(8,128)(2,1)S(1)} %collective-permute-done.10.refs_0_), custom_call_target="tpu_custom_call" | custom-call | flops 29360128 | bytes 1376256 | tf_op jit(solution)/shard_map/encode/pallas_call | solution.py:173
  79.4 0.2 collective-permute-start.8
  79.7 1.5 %collective-permute-start.11 = (bf16[4,32,896]{2,1,0:T(8,128)(2,1)S(1)}, bf16[4,32,896]{2,1,0:T(8,128)(2,1)S(1)}, u32[]{:S(2)}, u32[]{:S(2)}) collective-permute-start(bf16[4,32,896]{2,1,0:T(8,128)(2,1)S(1)} %encode.4.refs_0_), channel_id=1, source_target_pairs={{0,2},{2,0},{1,3},{3,1},{4,6},{6,4},{5,7},{7,5},{8,10},{10,8},{9,1... | collective-permute-start | bytes 688136 | tf_op jit(solution)/shard_map/ppermute | solution.py:327
  81.1 9.1 %encode.5.refs_3_ = bf16[4,32,896]{2,1,0:T(8,128)(2,1)S(1)} custom-call(s32[16]{0:T(128)S(1)} %copy-done.8, bf16[512,896]{1,0:T(8,128)(2,1)S(1)} %copy-done.2, bf16[4,32,896]{2,1,0:T(8,128)(2,1)S(1)} %collective-permute-done.14.refs_0_), custom_call_target="tpu_custom_call" | custom-call | flops 29360128 | bytes 1376256 | tf_op jit(solution)/shard_map/encode/pallas_call | solution.py:173
  90.2 0.6 collective-permute-start.15
  90.8 0.5 collective-permute-start.12
  91.3 0.1 collective-permute-start.13
  91.4 6.4 %collective-permute-done.15.refs_4_ = bf16[4,32,896]{2,1,0:T(8,128)(2,1)S(1)} collective-permute-done((bf16[4,32,896]{2,1,0:T(8,128)(2,1)S(1)}, bf16[4,32,896]{2,1,0:T(8,128)(2,1)S(1)}, u32[]{:S(2)}, u32[]{:S(2)}) %collective-permute-start.15) | collective-permute-done | bytes 229408 | tf_op jit(solution)/shard_map/ppermute | solution.py:327
  97.8 0.5 collective-permute-start.17
  98.3 1.3 project.3.refs_0_
  99.6 1.3 project.4.refs_1_
  100.8 0.0 copy-start.6
  100.9 1.3 project.5.refs_2_
  102.2 0.0 copy-start
  102.2 10.6 %attend.1 = (bf16[2,128,512]{2,1,0:T(8,128)(2,1)S(1)}, bf16[2,128,512]{2,1,0:T(8,128)(2,1)S(1)}) custom-call(s32[16]{0:T(128)S(1)} %copy-done.9, bf16[512,512]{1,0:T(8,128)(2,1)S(1)} %copy-done.6, bf16[4,4,32,1024]{3,2,1,0:T(8,128)(2,1)S(1)} %project.3.refs_0_, bf16[4,4,32,1024]{3,2,1,0:T(8,128)(2,1)S(1)} %project.4.refs_1_, ...), custom_call_target="tpu_custom_call" | custom-call | flops 1207959552 | bytes 9043968 | tf_op jit(solution)/shard_map/attend/pallas_call | solution.py:276
  112.8 0.1 collective-permute-start.18
  112.9 1.5 %collective-permute-done.18.refs_1_ = bf16[2,128,512]{2,1,0:T(8,128)(2,1)S(1)} collective-permute-done((bf16[2,128,512]{2,1,0:T(8,128)(2,1)S(1)}, bf16[2,128,512]{2,1,0:T(8,128)(2,1)S(1)}, u32[]{:S(2)}, u32[]{:S(2)}) %collective-permute-start.18) | collective-permute-done | bytes 262176 | tf_op jit(solution)/shard_map/ppermute | solution.py:343
  114.4 3.5 %out_project.5 = bf16[128,3072]{1,0:T(8,128)(2,1)S(1)} custom-call(bf16[2,128,512]{2,1,0:T(8,128)(2,1)S(1)} %get-tuple-element.19.refs_0_, bf16[2,128,512]{2,1,0:T(8,128)(2,1)S(1)} %collective-permute-done.18.refs_1_, bf16[512,4096]{1,0:T(8,128)(2,1)S(1)} %copy-done, bf16[512,4096]{1,0:T(8,128)(2,1)} %collective-permute-done.19.refs_3_), custom_call_target="tpu_custom_call" | custom-call | flops 805306368 | bytes 6291456 | tf_op jit(solution)/shard_map/out_project/pallas_call | solution.py:299
  117.9 0.6 collective-permute-start.21
  118.5 1.7 %out_project.4 = bf16[128,1024]{1,0:T(8,128)(2,1)S(1)} custom-call(bf16[2,128,512]{2,1,0:T(8,128)(2,1)S(1)} %get-tuple-element.19.refs_0_, bf16[2,128,512]{2,1,0:T(8,128)(2,1)S(1)} %collective-permute-done.18.refs_1_, bf16[512,4096]{1,0:T(8,128)(2,1)S(1)} %copy-done, bf16[512,4096]{1,0:T(8,128)(2,1)} %collective-permute-done.19.refs_3_), custom_call_target="tpu_custom_call" | custom-call | flops 268435456 | bytes 2097152 | tf_op jit(solution)/shard_map/out_project/pallas_call | solution.py:299
  120.3 1.6 %collective-permute-start.20 = (bf16[128,1024]{1,0:T(8,128)(2,1)S(1)}, bf16[128,1024]{1,0:T(8,128)(2,1)S(1)}, u32[]{:S(2)}, u32[]{:S(2)}) collective-permute-start(bf16[128,1024]{1,0:T(8,128)(2,1)S(1)} %out_project.4), channel_id=1, source_target_pairs={{0,2},{2,0},{1,3},{3,1},{4,6},{6,4},{5,7},{7,5},{8,10},{10,8},{9,1... | collective-permute-start | bytes 786440 | tf_op jit(solution)/shard_map/ppermute | solution.py:353
  121.8 4.2 %out_project.3 = bf16[128,4096]{1,0:T(8,128)(2,1)S(1)} custom-call(bf16[2,128,512]{2,1,0:T(8,128)(2,1)S(1)} %get-tuple-element.19.refs_0_, bf16[2,128,512]{2,1,0:T(8,128)(2,1)S(1)} %collective-permute-done.18.refs_1_, bf16[512,4096]{1,0:T(8,128)(2,1)S(1)} %copy-done, bf16[512,4096]{1,0:T(8,128)(2,1)} %collective-permute-done.19.refs_3_), custom_call_target="tpu_custom_call" | custom-call | flops 1073741824 | bytes 8388608 | tf_op jit(solution)/shard_map/out_project/pallas_call | solution.py:299
  126.0 17.2 %collective-permute-done.20 = bf16[128,1024]{1,0:T(8,128)(2,1)S(1)} collective-permute-done((bf16[128,1024]{1,0:T(8,128)(2,1)S(1)}, bf16[128,1024]{1,0:T(8,128)(2,1)S(1)}, u32[]{:S(2)}, u32[]{:S(2)}) %collective-permute-start.20) | collective-permute-done | bytes 262176 | tf_op jit(solution)/shard_map/ppermute | solution.py:353
  143.2 1.2 add_convert_fusion
  (38 shorter events, 0.1 us)
Async XLA Ops:
  0.0 114.4 %collective-permute-start.19 = (bf16[512,4096]{1,0:T(8,128)(2,1)}, bf16[512,4096]{1,0:T(8,128)(2,1)}, u32[]{:S(2)}, u32[]{:S(2)}) collective-permute-start(bf16[512,4096]{1,0:T(8,128)(2,1)} %refs_2_.5), channel_id=1, source_target_pairs={{0,1},{1,0},{2,3},{3,2},{4,5},{5,4},{6,7},{7,6},{8,9},{9,8},{10,11... | collective-permute-start | bytes 12582920 | tf_op jit(solution)/shard_map/ppermute | solution.py:323
  1.8 58.9 %copy-start.8 = (s32[16]{0:T(128)S(1)}, s32[16]{0:T(128)}, u32[]{:S(2)}) copy-start(s32[16]{0:T(128)} %get-tuple-element.14.req_ref) | copy-start | bytes 196
  1.8 1.2 copy-start.1
  3.0 1.2 copy-start.5
  4.2 0.6 copy-start.7
  4.8 0.7 copy-start.10
  5.4 55.2 %copy-start.2 = (bf16[512,896]{1,0:T(8,128)(2,1)S(1)}, bf16[512,896]{1,0:T(8,128)(2,1)}, u32[]{:S(2)}) copy-start(bf16[512,896]{1,0:T(8,128)(2,1)} %states_ref.7) | copy-start | bytes 2752516
  15.3 36.1 %collective-permute-start = (bf16[4,32,896]{2,1,0:T(8,128)(2,1)S(1)}, bf16[4,32,896]{2,1,0:T(8,128)(2,1)S(1)}, u32[]{:S(2)}, u32[]{:S(2)}) collective-permute-start(bf16[4,32,896]{2,1,0:T(8,128)(2,1)S(1)} %encode_local.1.refs_0_), channel_id=1, source_target_pairs={{0,2},{2,0},{1,3},{3,1},{4,6},{6,4},{5,7},{7,5},{8,10},{10,8},{9,1... | collective-permute-start | bytes 688136 | tf_op jit(solution)/shard_map/ppermute | solution.py:327
  17.8 5.3 %collective-permute-start.5 = (s32[16]{0:T(128)S(1)}, s32[16]{0:T(128)S(1)}, u32[]{:S(2)}, u32[]{:S(2)}) collective-permute-start(s32[16]{0:T(128)S(1)} %copy-done.10), channel_id=1, source_target_pairs={{0,12},{4,8},{8,4},{12,0},{1,13},{5,9},{9,5},{13,1},{2,14},{6,10},... | collective-permute-start | bytes 200 | tf_op jit(solution)/shard_map/ppermute | solution.py:322
  21.4 4.4 %collective-permute-start.4 = (s32[16]{0:T(128)S(1)}, s32[16]{0:T(128)S(1)}, u32[]{:S(2)}, u32[]{:S(2)}) collective-permute-start(s32[16]{0:T(128)S(1)} %copy-done.10), channel_id=1, source_target_pairs={{0,8},{4,12},{8,0},{12,4},{1,9},{5,13},{9,1},{13,5},{2,10},{6,14},... | collective-permute-start | bytes 200 | tf_op jit(solution)/shard_map/ppermute | solution.py:322
  21.4 4.4 %collective-permute-start.3 = (s32[16]{0:T(128)S(1)}, s32[16]{0:T(128)S(1)}, u32[]{:S(2)}, u32[]{:S(2)}) collective-permute-start(s32[16]{0:T(128)S(1)} %copy-done.10), channel_id=1, source_target_pairs={{0,4},{4,0},{8,12},{12,8},{1,5},{5,1},{9,13},{13,9},{2,6},{6,2},{1... | collective-permute-start | bytes 200 | tf_op jit(solution)/shard_map/ppermute | solution.py:322
  23.2 2.7 %copy-start.11 = (s32[16]{0:T(128)}, s32[16]{0:T(128)S(1)}, u32[]{:S(2)}) copy-start(s32[16]{0:T(128)S(1)} %collective-permute-done.5.refs_2_) | copy-start | bytes 196
  25.9 0.5 copy-start.12
  26.4 0.5 copy-start.13
  49.6 48.6 %copy-start.3 = (bf16[896,512]{1,0:T(8,128)(2,1)S(1)}, bf16[896,512]{1,0:T(8,128)(2,1)}, u32[]{:S(2)}) copy-start(bf16[896,512]{1,0:T(8,128)(2,1)} %refs_7_.1) | copy-start | bytes 2752516
  49.7 48.6 %copy-start.4 = (bf16[896,512]{1,0:T(8,128)(2,1)S(1)}, bf16[896,512]{1,0:T(8,128)(2,1)}, u32[]{:S(2)}) copy-start(bf16[896,512]{1,0:T(8,128)(2,1)} %refs_8_.1) | copy-start | bytes 2752516
  49.7 11.0 %collective-permute-start.6 = (bf16[4,32,896]{2,1,0:T(8,128)(2,1)}, bf16[4,32,896]{2,1,0:T(8,128)(2,1)S(1)}, u32[]{:S(2)}, u32[]{:S(2)}) collective-permute-start(bf16[4,32,896]{2,1,0:T(8,128)(2,1)} %get-tuple-element.16), channel_id=1, source_target_pairs={{0,4},{4,0},{8,12},{12,8},{1,5},{5,1},{9,13},{13,9},{2,6},{6,2},{1... | collective-permute-start | bytes 688136 | tf_op jit(solution)/shard_map/ppermute | solution.py:335
  49.7 20.0 %collective-permute-start.10 = (bf16[4,32,896]{2,1,0:T(8,128)(2,1)}, bf16[4,32,896]{2,1,0:T(8,128)(2,1)S(1)}, u32[]{:S(2)}, u32[]{:S(2)}) collective-permute-start(bf16[4,32,896]{2,1,0:T(8,128)(2,1)} %get-tuple-element.17), channel_id=1, source_target_pairs={{0,8},{4,12},{8,0},{12,4},{1,9},{5,13},{9,1},{13,5},{2,10},{6,14},... | collective-permute-start | bytes 688136 | tf_op jit(solution)/shard_map/ppermute | solution.py:335
  51.3 28.1 %collective-permute-start.1 = (bf16[4,32,896]{2,1,0:T(8,128)(2,1)S(1)}, bf16[4,32,896]{2,1,0:T(8,128)(2,1)S(1)}, u32[]{:S(2)}, u32[]{:S(2)}) collective-permute-start(bf16[4,32,896]{2,1,0:T(8,128)(2,1)S(1)} %encode_local.1.refs_0_), channel_id=1, source_target_pairs={{0,1},{1,0},{2,3},{3,2},{4,5},{5,4},{6,7},{7,6},{8,9},{9,8},{10,11... | collective-permute-start | bytes 688136 | tf_op jit(solution)/shard_map/ppermute | solution.py:329
  51.3 28.3 %collective-permute-start.14 = (bf16[4,32,896]{2,1,0:T(8,128)(2,1)}, bf16[4,32,896]{2,1,0:T(8,128)(2,1)S(1)}, u32[]{:S(2)}, u32[]{:S(2)}) collective-permute-start(bf16[4,32,896]{2,1,0:T(8,128)(2,1)} %get-tuple-element.18), channel_id=1, source_target_pairs={{0,12},{4,8},{8,4},{12,0},{1,13},{5,9},{9,5},{13,1},{2,14},{6,10},... | collective-permute-start | bytes 688136 | tf_op jit(solution)/shard_map/ppermute | solution.py:335
  60.7 29.6 %collective-permute-start.2 = (bf16[4,32,896]{2,1,0:T(8,128)(2,1)S(1)}, bf16[4,32,896]{2,1,0:T(8,128)(2,1)S(1)}, u32[]{:S(2)}, u32[]{:S(2)}) collective-permute-start(bf16[4,32,896]{2,1,0:T(8,128)(2,1)S(1)} %collective-permute-done.refs_1_), channel_id=1, source_target_pairs={{0,1},{1,0},{2,3},{3,2},{4,5},{5,4},{6,7},{7,6},{8,9},{9,8},{10,11... | collective-permute-start | bytes 688136 | tf_op jit(solution)/shard_map/ppermute | solution.py:329
  69.8 21.0 %collective-permute-start.7 = (bf16[4,32,896]{2,1,0:T(8,128)(2,1)S(1)}, bf16[4,32,896]{2,1,0:T(8,128)(2,1)S(1)}, u32[]{:S(2)}, u32[]{:S(2)}) collective-permute-start(bf16[4,32,896]{2,1,0:T(8,128)(2,1)S(1)} %encode.3.refs_0_), channel_id=1, source_target_pairs={{0,2},{2,0},{1,3},{3,1},{4,6},{6,4},{5,7},{7,5},{8,10},{10,8},{9,1... | collective-permute-start | bytes 688136 | tf_op jit(solution)/shard_map/ppermute | solution.py:327
  79.4 11.4 %collective-permute-start.8 = (bf16[4,32,896]{2,1,0:T(8,128)(2,1)S(1)}, bf16[4,32,896]{2,1,0:T(8,128)(2,1)S(1)}, u32[]{:S(2)}, u32[]{:S(2)}) collective-permute-start(bf16[4,32,896]{2,1,0:T(8,128)(2,1)S(1)} %encode.3.refs_0_), channel_id=1, source_target_pairs={{0,1},{1,0},{2,3},{3,2},{4,5},{5,4},{6,7},{7,6},{8,9},{9,8},{10,11... | collective-permute-start | bytes 688136 | tf_op jit(solution)/shard_map/ppermute | solution.py:329
  79.7 11.7 %collective-permute-start.11 = (bf16[4,32,896]{2,1,0:T(8,128)(2,1)S(1)}, bf16[4,32,896]{2,1,0:T(8,128)(2,1)S(1)}, u32[]{:S(2)}, u32[]{:S(2)}) collective-permute-start(bf16[4,32,896]{2,1,0:T(8,128)(2,1)S(1)} %encode.4.refs_0_), channel_id=1, source_target_pairs={{0,2},{2,0},{1,3},{3,1},{4,6},{6,4},{5,7},{7,5},{8,10},{10,8},{9,1... | collective-permute-start | bytes 688136 | tf_op jit(solution)/shard_map/ppermute | solution.py:327
  90.2 7.5 %collective-permute-start.15 = (bf16[4,32,896]{2,1,0:T(8,128)(2,1)S(1)}, bf16[4,32,896]{2,1,0:T(8,128)(2,1)S(1)}, u32[]{:S(2)}, u32[]{:S(2)}) collective-permute-start(bf16[4,32,896]{2,1,0:T(8,128)(2,1)S(1)} %encode.5.refs_3_), channel_id=1, source_target_pairs={{0,2},{2,0},{1,3},{3,1},{4,6},{6,4},{5,7},{7,5},{8,10},{10,8},{9,1... | collective-permute-start | bytes 688136 | tf_op jit(solution)/shard_map/ppermute | solution.py:327
  90.8 7.0 %collective-permute-start.9 = (bf16[4,32,896]{2,1,0:T(8,128)(2,1)S(1)}, bf16[4,32,896]{2,1,0:T(8,128)(2,1)S(1)}, u32[]{:S(2)}, u32[]{:S(2)}) collective-permute-start(bf16[4,32,896]{2,1,0:T(8,128)(2,1)S(1)} %collective-permute-done.7.refs_1_), channel_id=1, source_target_pairs={{0,1},{1,0},{2,3},{3,2},{4,5},{5,4},{6,7},{7,6},{8,9},{9,8},{10,11... | collective-permute-start | bytes 688136 | tf_op jit(solution)/shard_map/ppermute | solution.py:329
  90.8 10.1 %collective-permute-start.12 = (bf16[4,32,896]{2,1,0:T(8,128)(2,1)S(1)}, bf16[4,32,896]{2,1,0:T(8,128)(2,1)S(1)}, u32[]{:S(2)}, u32[]{:S(2)}) collective-permute-start(bf16[4,32,896]{2,1,0:T(8,128)(2,1)S(1)} %encode.4.refs_0_), channel_id=1, source_target_pairs={{0,1},{1,0},{2,3},{3,2},{4,5},{5,4},{6,7},{7,6},{8,9},{9,8},{10,11... | collective-permute-start | bytes 688136 | tf_op jit(solution)/shard_map/ppermute | solution.py:329
  91.3 9.6 %collective-permute-start.13 = (bf16[4,32,896]{2,1,0:T(8,128)(2,1)S(1)}, bf16[4,32,896]{2,1,0:T(8,128)(2,1)S(1)}, u32[]{:S(2)}, u32[]{:S(2)}) collective-permute-start(bf16[4,32,896]{2,1,0:T(8,128)(2,1)S(1)} %collective-permute-done.11.refs_1_), channel_id=1, source_target_pairs={{0,1},{1,0},{2,3},{3,2},{4,5},{5,4},{6,7},{7,6},{8,9},{9,8},{10,11... | collective-permute-start | bytes 688136 | tf_op jit(solution)/shard_map/ppermute | solution.py:329
  97.8 4.4 %collective-permute-start.16 = (bf16[4,32,896]{2,1,0:T(8,128)(2,1)S(1)}, bf16[4,32,896]{2,1,0:T(8,128)(2,1)S(1)}, u32[]{:S(2)}, u32[]{:S(2)}) collective-permute-start(bf16[4,32,896]{2,1,0:T(8,128)(2,1)S(1)} %encode.5.refs_3_), channel_id=1, source_target_pairs={{0,1},{1,0},{2,3},{3,2},{4,5},{5,4},{6,7},{7,6},{8,9},{9,8},{10,11... | collective-permute-start | bytes 688136 | tf_op jit(solution)/shard_map/ppermute | solution.py:329
  97.8 4.4 %collective-permute-start.17 = (bf16[4,32,896]{2,1,0:T(8,128)(2,1)S(1)}, bf16[4,32,896]{2,1,0:T(8,128)(2,1)S(1)}, u32[]{:S(2)}, u32[]{:S(2)}) collective-permute-start(bf16[4,32,896]{2,1,0:T(8,128)(2,1)S(1)} %collective-permute-done.15.refs_4_), channel_id=1, source_target_pairs={{0,1},{1,0},{2,3},{3,2},{4,5},{5,4},{6,7},{7,6},{8,9},{9,8},{10,11... | collective-permute-start | bytes 688136 | tf_op jit(solution)/shard_map/ppermute | solution.py:329
  100.8 1.3 copy-start.6
  100.8 1.3 copy-start.9
  102.2 12.2 %copy-start = (bf16[512,4096]{1,0:T(8,128)(2,1)S(1)}, bf16[512,4096]{1,0:T(8,128)(2,1)}, u32[]{:S(2)}) copy-start(bf16[512,4096]{1,0:T(8,128)(2,1)} %refs_2_.5) | copy-start | bytes 12582916
  112.8 1.6 %collective-permute-start.18 = (bf16[2,128,512]{2,1,0:T(8,128)(2,1)S(1)}, bf16[2,128,512]{2,1,0:T(8,128)(2,1)S(1)}, u32[]{:S(2)}, u32[]{:S(2)}) collective-permute-start(bf16[2,128,512]{2,1,0:T(8,128)(2,1)S(1)} %get-tuple-element.20), channel_id=1, source_target_pairs={{0,1},{1,0},{2,3},{3,2},{4,5},{5,4},{6,7},{7,6},{8,9},{9,8},{10,11... | collective-permute-start | bytes 786440 | tf_op jit(solution)/shard_map/ppermute | solution.py:343
  117.9 25.3 %collective-permute-start.21 = (bf16[128,3072]{1,0:T(8,128)(2,1)S(1)}, bf16[128,3072]{1,0:T(8,128)(2,1)S(1)}, u32[]{:S(2)}, u32[]{:S(2)}) collective-permute-start(bf16[128,3072]{1,0:T(8,128)(2,1)S(1)} %out_project.5), channel_id=1, source_target_pairs={{0,2},{2,0},{1,3},{3,1},{4,6},{6,4},{5,7},{7,5},{8,10},{10,8},{9,1... | collective-permute-start | bytes 2359304 | tf_op jit(solution)/shard_map/ppermute | solution.py:353
  120.3 22.9 %collective-permute-start.20 = (bf16[128,1024]{1,0:T(8,128)(2,1)S(1)}, bf16[128,1024]{1,0:T(8,128)(2,1)S(1)}, u32[]{:S(2)}, u32[]{:S(2)}) collective-permute-start(bf16[128,1024]{1,0:T(8,128)(2,1)S(1)} %out_project.4), channel_id=1, source_target_pairs={{0,2},{2,0},{1,3},{3,1},{4,6},{6,4},{5,7},{7,5},{8,10},{10,8},{9,1... | collective-permute-start | bytes 786440 | tf_op jit(solution)/shard_map/ppermute | solution.py:353

commit v2 on v1

v2 whole, which is shorter than its diff:
```python
import functools

import jax
import jax.numpy as jnp
from jax import lax
from jax.experimental import pallas as pl
from jax.experimental.pallas import tpu as pltpu
from jax.sharding import PartitionSpec as P

HD = 128
ENCODER_HEAD_DIM = 128
F32 = jnp.float32
BF16 = jnp.bfloat16
GROUPS = 4
FIRST_COLS = 1024

VMEM = pl.BlockSpec(memory_space=pltpu.VMEM)
SMEM = pl.BlockSpec(memory_space=pltpu.SMEM)
ANY = pl.BlockSpec(memory_space=pl.ANY)


def params(mib):
    return pltpu.CompilerParams(vmem_limit_bytes=mib * 2**20)


def cost(flops, bytes_accessed):
    return pl.CostEstimate(flops=int(flops), bytes_accessed=int(bytes_accessed), transcendentals=0)


def apart(n, a, b):
    if n & (n - 1) == 0:
        return a ^ b
    return lax.rem(b - a + n, n)


def lane_pairs(n, d, reply):
    if n & (n - 1) == 0:
        return [(i, i ^ d) for i in range(n)]
    return [(i, (i - d if reply else i + d) % n) for i in range(n)]


def shift_pairs(n, s):
    return [(i, (i + s) % n) for i in range(n)]


def dot_t(a, b):
    return lax.dot_general(a, b, (((1,), (1,)), ((), ())), preferred_element_type=F32)


def dot(a, b):
    return jnp.dot(a, b, preferred_element_type=F32)


def fetch_kernel(n_lanes, cap, own_ref, *refs):
    asked, store_ref, refs = refs[: n_lanes - 1], refs[n_lanes - 1], refs[n_lanes:]
    blocks, (req_ref, slot_ref, pick_ref, count_ref) = refs[:n_lanes], refs[n_lanes:]
    lane = lax.axis_index("lanes")
    fanout, spans = own_ref.shape[0] // 2, own_ref.shape[1]
    requests = [(j // fanout, j % fanout) for j in range(fanout * spans)]
    for i in range(n_lanes):
        count_ref[i] = 0
    for i in range(n_lanes * cap):
        pick_ref[i] = 0
        req_ref[i] = 0
    for j, (span, k) in enumerate(requests):
        d = apart(n_lanes, lane, own_ref[k, span])
        rank = count_ref[d]
        count_ref[d] = rank + 1
        slot = d * cap + rank
        pick_ref[slot] = own_ref[fanout + k, span]
        req_ref[slot] = j
        slot_ref[j] = slot
    for d in range(1, n_lanes):
        place = d * cap
        for span, k in requests:
            pick_ref[place] = asked[d - 1][fanout + k, span]
            place = place + (asked[d - 1][k, span] == lane).astype(jnp.int32)
    for d in list(range(1, n_lanes)) + [0]:
        for s in range(cap):
            blocks[d][s] = store_ref[pick_ref[d * cap + s]]


def fetch(own, asked, store, n_lanes, cap):
    block = jax.ShapeDtypeStruct((cap,) + store.shape[1:], store.dtype)
    requests = own.size // 2
    tables = (
        jax.ShapeDtypeStruct((n_lanes * cap,), jnp.int32),
        jax.ShapeDtypeStruct((requests,), jnp.int32),
    )
    return pl.pallas_call(
        functools.partial(fetch_kernel, n_lanes, cap),
        out_shape=[block] * n_lanes + list(tables),
        in_specs=[SMEM] * n_lanes + [VMEM],
        out_specs=[VMEM] * n_lanes + [SMEM, SMEM],
        scratch_shapes=[pltpu.SMEM((n_lanes * cap + 1,), jnp.int32), pltpu.SMEM((n_lanes,), jnp.int32)],
        compiler_params=params(16),
        cost_estimate=cost(0, 2 * store.size + 2 * n_lanes * cap * store[0].size),
        name="fetch",
    )(own, *asked, store)


def encode_pairs(width):
    step = 2 * ENCODER_HEAD_DIM
    return [(start, min(start + step, width)) for start in range(0, width, step)]


def spread(states, start, stop):
    part = states[:, start:stop]
    heads = (stop - start) // ENCODER_HEAD_DIM
    if heads == 1:
        return part
    rows = jnp.concatenate([part] * heads, axis=0)
    return jnp.where(own_cells(rows.shape, part.shape[0]), rows, jnp.zeros_like(rows))


def own_cells(shape, keys):
    row = lax.broadcasted_iota(jnp.int32, shape, 0)
    col = lax.broadcasted_iota(jnp.int32, shape, 1)
    return (row >= keys) == (col >= ENCODER_HEAD_DIM)


def softmax_top(logits, keys):
    if logits.shape[1] == keys:
        return jnp.max(logits, axis=1, keepdims=True)
    first = lax.broadcasted_iota(jnp.int32, logits.shape, 1) < keys
    low = jnp.max(jnp.where(first, logits, -jnp.inf), axis=1, keepdims=True)
    high = jnp.max(jnp.where(first, -jnp.inf, logits), axis=1, keepdims=True)
    return jnp.where(first, low, high)


def encode_kernel(first, cap, fanout, span_len, req_ref, states_ref, *refs):
    blocks, out_ref = refs[:-1], refs[-1]
    scale = ENCODER_HEAD_DIM ** (-0.5)
    runs = encode_pairs(states_ref.shape[1])
    for i, block in enumerate(blocks):
        units = []
        for s in range(cap):
            span = lax.div(req_ref[(first + i) * cap + s], fanout)
            states = states_ref[pl.ds(pl.multiple_of(span * span_len, span_len), span_len), :]
            units += [(s, start, stop, spread(states, start, stop)) for start, stop in runs]
        logits = [dot_t(block[s, :, start:stop], keys) for s, start, stop, keys in units]
        tops = [softmax_top(part, span_len) for part in logits]
        weights = [jnp.exp((part - top) * scale).astype(BF16) for part, top in zip(logits, tops)]
        mixed = [dot(part, keys) for part, (_, _, _, keys) in zip(weights, units)]
        sums = []
        for part, (_, start, stop, keys) in zip(weights, units):
            ones = jnp.ones(keys.shape, BF16)
            if stop - start > ENCODER_HEAD_DIM:
                ones = jnp.where(own_cells(keys.shape, span_len), ones, jnp.zeros_like(ones))
            sums.append(dot(part, ones))
        for (s, start, stop, _), top, bottom in zip(units, mixed, sums):
            token = block[s, :, start:stop].astype(F32)
            out_ref[i * cap + s, :, start:stop] = (token + top / bottom).astype(BF16)


def encode(req, span_states, blocks, first, cap, fanout, span_len):
    _, tokens, width = blocks[0].shape
    slots = len(blocks) * cap
    return pl.pallas_call(
        functools.partial(encode_kernel, first, cap, fanout, span_len),
        out_shape=jax.ShapeDtypeStruct((slots, tokens, width), BF16),
        in_specs=[SMEM, VMEM] + [VMEM] * len(blocks),
        out_specs=VMEM,
        compiler_params=params(16),
        cost_estimate=cost(16 * slots * tokens * span_len * width, 4 * slots * tokens * width),
        name="encode",
    )(req, span_states, *blocks)


def project_into(kv_ref, first, pieces, wk_ref, wv_ref):
    slots, tokens, width = pieces[0].shape
    rows = jnp.concatenate([piece[...].reshape(slots * tokens, width) for piece in pieces], axis=0)
    cols = wk_ref.shape[1]
    for side, weight in enumerate((wk_ref, wv_ref)):
        made = dot(rows, weight[...]).astype(BF16)
        for p in range(len(pieces)):
            part = made[p * slots * tokens : (p + 1) * slots * tokens]
            kv_ref[first : first + slots, p, :, side * cols : (side + 1) * cols] = part.reshape(
                slots, tokens, cols
            )


def project_kernel(n_pieces, *refs):
    pieces, (wk_ref, wv_ref, kv_ref) = refs[:n_pieces], refs[n_pieces:]
    project_into(kv_ref, 0, pieces, wk_ref, wv_ref)


def project_cost(pieces, w_key):
    rows = len(pieces) * pieces[0].shape[0] * pieces[0].shape[1]
    width, cols = w_key.shape
    return 4 * rows * width * cols, 2 * rows * (width + 2 * cols) + 4 * width * cols


def project(pieces, w_key, w_value):
    slots, tokens, _ = pieces[0].shape
    shape = (slots, len(pieces), tokens, 2 * w_key.shape[1])
    return pl.pallas_call(
        functools.partial(project_kernel, len(pieces)),
        out_shape=jax.ShapeDtypeStruct(shape, BF16),
        in_specs=[VMEM] * (len(pieces) + 2),
        out_specs=VMEM,
        compiler_params=params(32),
        cost_estimate=cost(*project_cost(pieces, w_key)),
        name="project",
    )(*pieces, w_key, w_value)


def attend_kernel(firsts, n_pieces, n_heads, n_rep, turns, fanout, spans, slot_ref, q_ref, *refs):
    n_ready = len(firsts) - 1
    ready, refs = refs[:n_ready], refs[n_ready:]
    pieces, refs = refs[:n_pieces], refs[n_pieces:]
    wk_ref, wv_ref = refs[:2]
    outs = refs[2 : 2 + n_rep]
    kv_ref, sem = refs[2 + n_rep :]
    copies = [
        pltpu.make_async_copy(ref, kv_ref.at[pl.ds(first, ref.shape[0])], sem.at[i])
        for i, (ref, first) in enumerate(zip(ready, firsts))
    ]
    for copy in copies:
        copy.start()
    project_into(kv_ref, firsts[-1], pieces, wk_ref, wv_ref)
    for copy in copies:
        copy.wait()
    heads_at, rep_at = lax.axis_index("heads"), lax.axis_index("rep")
    cols = wk_ref.shape[1]
    span_len = q_ref.shape[0] // spans
    block = spans // (n_heads * n_rep)
    tokens = kv_ref.shape[1] * kv_ref.shape[2]
    heads = [slice(h * HD, (h + 1) * HD) for h in range(cols // HD)]
    for at, t in enumerate(turns):
        for s in range(n_rep):
            owner = lax.rem(heads_at + t, n_heads) * n_rep + lax.rem(rep_at + s, n_rep)
            for i in range(block):
                span = owner * block + i
                slots = [slot_ref[span * fanout + k] for k in range(fanout)]
                rows = pl.ds(pl.multiple_of(span * span_len, span_len), span_len)

                def side(lanes):
                    return jnp.concatenate(
                        [kv_ref[slot, :, :, lanes].reshape(tokens, HD) for slot in slots], axis=0
                    )

                logits = [dot_t(q_ref[rows, lanes], side(lanes)) for lanes in heads]
                tops = [jnp.max(part, axis=1, keepdims=True) for part in logits]
                weights = [jnp.exp((part - top) * HD ** (-0.5)) for part, top in zip(logits, tops)]
                scales = [1.0 / jnp.sum(part, axis=1, keepdims=True) for part in weights]
                mixed = [
                    dot(part.astype(BF16), side(slice(cols + lanes.start, cols + lanes.stop)))
                    for part, lanes in zip(weights, heads)
                ]
                for part, scale, lanes in zip(mixed, scales, heads):
                    outs[s][at, i * span_len : (i + 1) * span_len, lanes] = (part * scale).astype(BF16)


def attend(slot, queries, ready, pieces, w_key, w_value, n_heads, n_rep, turns, fanout, spans):
    firsts = [0]
    for kv in ready:
        firsts.append(firsts[-1] + kv.shape[0])
    slots, tokens, _ = pieces[0].shape
    cols = w_key.shape[1]
    rows = queries.shape[0] // (n_heads * n_rep)
    flops, moved = project_cost(pieces, w_key)
    all_slots = firsts[-1] + slots
    kv_shape = (all_slots, len(pieces), tokens, 2 * cols)
    return pl.pallas_call(
        functools.partial(attend_kernel, firsts, len(pieces), n_heads, n_rep, turns, fanout, spans),
        out_shape=[jax.ShapeDtypeStruct((len(turns), rows, cols), BF16)] * n_rep,
        in_specs=[SMEM, VMEM] + [ANY] * len(ready) + [VMEM] * (len(pieces) + 2),
        out_specs=[VMEM] * n_rep,
        scratch_shapes=[pltpu.VMEM(kv_shape, BF16), pltpu.SemaphoreType.DMA((max(1, len(ready)),))],
        compiler_params=params(40),
        cost_estimate=cost(
            flops + 4 * queries.size * fanout * len(pieces) * tokens,
            moved + 2 * all_slots * len(pieces) * tokens * 2 * cols + 4 * queries.size,
        ),
        name="attend",
    )(slot, queries, *ready, *pieces, w_key, w_value)


def out_kernel(n_rep, *refs):
    mixed, weights, out_ref = refs[:n_rep], refs[n_rep:-1], refs[-1]
    out_ref[...] = sum(dot(a[0], w[...]) for a, w in zip(mixed, weights)).astype(BF16)


def out_project(mixed, weights, t, start, stop, tile):
    _, rows, depth = mixed[0].shape
    base = start // tile
    return pl.pallas_call(
        functools.partial(out_kernel, len(mixed)),
        grid=((stop - start) // tile,),
        out_shape=jax.ShapeDtypeStruct((rows, stop - start), BF16),
        in_specs=[pl.BlockSpec((1, rows, depth), lambda j: (t, 0, 0))] * len(mixed)
        + [pl.BlockSpec((depth, tile), lambda j: (0, base + j))] * len(mixed),
        out_specs=pl.BlockSpec((rows, tile), lambda j: (0, j)),
        compiler_params=params(16),
        cost_estimate=cost(
            2 * len(mixed) * rows * depth * (stop - start), 2 * len(mixed) * depth * (stop - start)
        ),
        name="out_project",
    )(*mixed, *weights)


def shards(queries, span_states, store, entry_ids, owners, w_key, w_value, w_out):
    n_lanes, n_heads, n_rep = (lax.axis_size(name) for name in ("lanes", "heads", "rep"))
    spans, fanout = entry_ids.shape
    requests = spans * fanout
    cap = max(2, (requests + n_lanes - 1) // n_lanes)
    span_len = queries.shape[0] // spans

    def over_rep(array):
        return [array] + [lax.ppermute(array, "rep", shift_pairs(n_rep, s)) for s in range(1, n_rep)]

    own = jnp.concatenate([owners.T, entry_ids.T], axis=0)
    asked = [lax.ppermute(own, "lanes", lane_pairs(n_lanes, d, False)) for d in range(1, n_lanes)]
    *blocks, req, slot = fetch(own, asked, store, n_lanes, cap)
    arrived = [blocks[0]]
    for d in range(1, n_lanes):
        arrived.append(lax.ppermute(blocks[d], "lanes", lane_pairs(n_lanes, d, True)))

    def gather(encoded):
        pieces = [encoded]
        pieces += [lax.ppermute(encoded, "heads", shift_pairs(n_heads, s)) for s in range(1, n_heads)]
        return [part for piece in pieces for part in over_rep(piece)]

    size = -(-n_lanes // GROUPS)
    groups = []
    for first in range(0, n_lanes, size):
        encoded = encode(req, span_states, arrived[first : first + size], first, cap, fanout, span_len)
        groups.append(gather(encoded))
    ready = [project(pieces, w_key, w_value) for pieces in groups[:-1]]

    def mix(turns, q):
        outs = attend(slot, q, ready, groups[-1], w_key, w_value, n_heads, n_rep, turns, fanout, spans)
        return [outs[0]] + [
            lax.ppermute(outs[s], "rep", shift_pairs(n_rep, s)) for s in range(1, n_rep)
        ]

    w_out_here, req = lax.optimization_barrier((w_out, req))
    w_outs = over_rep(w_out_here)
    width = w_out.shape[1]
    tile = min(FIRST_COLS, width)
    cuts = [0, tile, width] if tile < width else [0, width]
    mixed = mix(list(range(1, n_heads)), queries)
    received = []
    for t in range(1, n_heads):
        parts = []
        for start, stop in zip(cuts, cuts[1:]):
            partial = out_project(mixed, w_outs, t - 1, start, stop, tile)
            partial, mixed = lax.optimization_barrier((partial, mixed))
            parts.append(lax.ppermute(partial, "heads", shift_pairs(n_heads, t)))
        received.append(jnp.concatenate(parts, axis=1))
    queries, mixed = lax.optimization_barrier((queries, mixed))
    total = out_project(mix([0], queries), w_outs, 0, 0, width, tile).astype(F32)
    for part in received:
        total = total + part.astype(F32)
    return total.astype(BF16)


def solution(mesh):
    return jax.shard_map(
        shards,
        mesh=mesh,
        in_specs=(
            P(("groups", "lanes"), ("heads", "rep")),
            P(("groups", "lanes"), None),
            P(("groups", "lanes"), ("heads", "rep"), None),
            P(("groups", "lanes"), None),
            P(("groups", "lanes"), None),
            P(None, ("heads", "rep")),
            P(None, ("heads", "rep")),
            P(("heads", "rep"), None),
        ),
        out_specs=P(("groups", "lanes", "heads", "rep"), None),
        check_vma=False,
    )
```

time: 145 us -> 89 us (0.61)
  the two profiles are of different devices: /device:TPU:0 before, /device:TPU:28 now
where the time goes in v2:
time: 89 us; the launch traced here: 88.8 us
  waiting for transfers between devices  44.8 us (50%)
  Pallas kernels  22 us (25%)
  starting transfers between devices  17.3 us (19%)
  local copies, waits for them, and re-layouts  2.38 us (3%)
  other arithmetic  2.01 us (2%)
    ppermute x2, waiting for transfers between devices, shards(): parts.append(lax.ppermute(partial, 'heads', shift_pairs(n_heads, t)))  15.9 us
    ppermute x4, waiting for transfers between devices, gather(): lax.ppermute(encoded, 'heads', shift_pairs(n_heads, s))  13.6 us
    ppermute x3, waiting for transfers between devices, shards(): lax.ppermute(blocks[d], 'lanes', lane_pairs(n_lanes, d, True))  11.1 us
    pallas_call x2, Pallas kernels, attend(): pl.pallas_call(functools.partial(attend_kernel, firsts, len(pieces), n_he...  6.83 us
    ppermute x3, starting transfers between devices, shards(): lax.ppermute(blocks[d], 'lanes', lane_pairs(n_lanes, d, True))  5.29 us
    pallas_call x4, Pallas kernels, encode(): pl.pallas_call(functools.partial(encode_kernel, first, cap, fanout, span_...  5.01 us
    pallas_call x3, Pallas kernels, out_project(): pl.pallas_call(functools.partial(out_kernel, len(mixed)), grid=((stop - s...  4.87 us
    ppermute x3, starting transfers between devices, shards(): lax.ppermute(own, 'lanes', lane_pairs(n_lanes, d, False))  4.39 us
  transfers between devices with their start and end apart: 23, of which 11 were waited for; matrix products, arithmetic and copies ran while one was open for 0% of the time, Pallas kernels for 20%

profile of v2, /device:TPU:28, one launch (start us, length us, event | category | flops | bytes accessed | tf_op | source)
XLA Modules:
  0.0 88.8 jit_solution(4491703142449609659)
XLA Ops:
  0.0 0.8 pad_add_fusion.own_ref
  0.8 0.2 collective-permute-start.2
  1.0 1.7 %collective-permute-start.1 = (s32[4,8]{1,0:T(4,128)S(1)}, s32[4,8]{1,0:T(4,128)S(1)}, u32[]{:S(2)}, u32[]{:S(2)}) collective-permute-start(s32[4,8]{1,0:T(4,128)S(1)} %pad_add_fusion.own_ref), channel_id=1, source_target_pairs={{0,8},{4,12},{8,0},{12,4},{1,9},{5,13},{9,1},{13,5},{2,10},{6,14},... | collective-permute-start | bytes 392 | tf_op jit(solution)/shard_map/ppermute | solution.py:314
  2.7 2.5 %collective-permute-start = (s32[4,8]{1,0:T(4,128)S(1)}, s32[4,8]{1,0:T(4,128)S(1)}, u32[]{:S(2)}, u32[]{:S(2)}) collective-permute-start(s32[4,8]{1,0:T(4,128)S(1)} %pad_add_fusion.own_ref), channel_id=1, source_target_pairs={{0,4},{4,0},{8,12},{12,8},{1,5},{5,1},{9,13},{13,9},{2,6},{6,2},{1... | collective-permute-start | bytes 392 | tf_op jit(solution)/shard_map/ppermute | solution.py:314
  5.2 1.0 %collective-permute-done.2.refs_2_ = s32[4,8]{1,0:T(4,128)S(1)} collective-permute-done((s32[4,8]{1,0:T(4,128)S(1)}, s32[4,8]{1,0:T(4,128)S(1)}, u32[]{:S(2)}, u32[]{:S(2)}) %collective-permute-start.2) | collective-permute-done | bytes 160 | tf_op jit(solution)/shard_map/ppermute | solution.py:314
  6.2 0.6 collective-permute-done.refs_0_
  6.7 1.2 %copy-done.6 = bf16[16,32,896]{2,1,0:T(8,128)(2,1)S(1)} copy-done((bf16[16,32,896]{2,1,0:T(8,128)(2,1)S(1)}, bf16[16,32,896]{2,1,0:T(8,128)(2,1)}, u32[]{:S(2)}) %copy-start.6) | copy-done | bytes 917528
  7.9 1.5 %fetch.1 = (bf16[4,32,896]{2,1,0:T(8,128)(2,1)S(1)}, bf16[4,32,896]{2,1,0:T(8,128)(2,1)S(1)}, bf16[4,32,896]{2,1,0:T(8,128)(2,1)S(1)}, bf16[4,32,896]{2,1,0:T(8,...) custom-call(s32[4,8]{1,0:T(4,128)S(1)} %pad_add_fusion.own_ref, s32[4,8]{1,0:T(4,128)S(1)} %collective-permute-done.refs_0_, ...), custom_call_target="tpu_custom_call" | custom-call | bytes 1835008 | tf_op jit(solution)/shard_map/fetch/pallas_call | solution.py:90
  9.4 0.1 collective-permute-start.19
  9.5 0.0 copy-start.3
  9.5 1.2 %copy-done.3 = bf16[512,896]{1,0:T(8,128)(2,1)S(1)} copy-done((bf16[512,896]{1,0:T(8,128)(2,1)S(1)}, bf16[512,896]{1,0:T(8,128)(2,1)}, u32[]{:S(2)}) %copy-start.3) | copy-done | bytes 917528
  10.7 1.3 %encode.4.refs_0_ = bf16[4,32,896]{2,1,0:T(8,128)(2,1)S(1)} custom-call(s32[16]{0:T(128)S(1)} %get-tuple-element.21.req_ref, bf16[512,896]{1,0:T(8,128)(2,1)S(1)} %copy-done.3, bf16[4,32,896]{2,1,0:T(8,128)(2,1)S(1)} %get-tuple-element.22.refs_0_), custom_call_target="tpu_custom_call" | custom-call | flops 117440512 | bytes 458752 | tf_op jit(solution)/shard_map/encode/pallas_call | solution.py:159
  12.0 0.0 copy-start.1
  12.0 1.6 %collective-permute-start.4 = (bf16[4,32,896]{2,1,0:T(8,128)(2,1)S(1)}, bf16[4,32,896]{2,1,0:T(8,128)(2,1)S(1)}, u32[]{:S(2)}, u32[]{:S(2)}) collective-permute-start(bf16[4,32,896]{2,1,0:T(8,128)(2,1)S(1)} %encode.4.refs_0_), channel_id=1, source_target_pairs={{0,2},{2,0},{1,3},{3,1},{4,6},{6,4},{5,7},{7,5},{8,10},{10,8},{9,1... | collective-permute-start | bytes 688136 | tf_op jit(solution)/shard_map/ppermute | solution.py:322
  13.5 2.0 %collective-permute-start.6 = (bf16[4,32,896]{2,1,0:T(8,128)(2,1)S(1)}, bf16[4,32,896]{2,1,0:T(8,128)(2,1)S(1)}, u32[]{:S(2)}, u32[]{:S(2)}) collective-permute-start(bf16[4,32,896]{2,1,0:T(8,128)(2,1)S(1)} %get-tuple-element.23), channel_id=1, source_target_pairs={{0,4},{4,0},{8,12},{12,8},{1,5},{5,1},{9,13},{13,9},{2,6},{6,2},{1... | collective-permute-start | bytes 688136 | tf_op jit(solution)/shard_map/ppermute | solution.py:318
  15.6 0.9 %collective-permute-start.10 = (bf16[4,32,896]{2,1,0:T(8,128)(2,1)S(1)}, bf16[4,32,896]{2,1,0:T(8,128)(2,1)S(1)}, u32[]{:S(2)}, u32[]{:S(2)}) collective-permute-start(bf16[4,32,896]{2,1,0:T(8,128)(2,1)S(1)} %get-tuple-element.24), channel_id=1, source_target_pairs={{0,8},{4,12},{8,0},{12,4},{1,9},{5,13},{9,1},{13,5},{2,10},{6,14},... | collective-permute-start | bytes 688136 | tf_op jit(solution)/shard_map/ppermute | solution.py:318
  16.5 3.6 %collective-permute-done.4.refs_2_ = bf16[4,32,896]{2,1,0:T(8,128)(2,1)S(1)} collective-permute-done((bf16[4,32,896]{2,1,0:T(8,128)(2,1)S(1)}, bf16[4,32,896]{2,1,0:T(8,128)(2,1)S(1)}, u32[]{:S(2)}, u32[]{:S(2)}) %collective-permute-start.4) | collective-permute-done | bytes 229408 | tf_op jit(solution)/shard_map/ppermute | solution.py:322
  20.0 2.4 %collective-permute-start.14 = (bf16[4,32,896]{2,1,0:T(8,128)(2,1)S(1)}, bf16[4,32,896]{2,1,0:T(8,128)(2,1)S(1)}, u32[]{:S(2)}, u32[]{:S(2)}) collective-permute-start(bf16[4,32,896]{2,1,0:T(8,128)(2,1)S(1)} %get-tuple-element.25), channel_id=1, source_target_pairs={{0,12},{4,8},{8,4},{12,0},{1,13},{5,9},{9,5},{13,1},{2,14},{6,10},... | collective-permute-start | bytes 688136 | tf_op jit(solution)/shard_map/ppermute | solution.py:318
  22.4 2.1 %collective-permute-done.6.refs_0_ = bf16[4,32,896]{2,1,0:T(8,128)(2,1)S(1)} collective-permute-done((bf16[4,32,896]{2,1,0:T(8,128)(2,1)S(1)}, bf16[4,32,896]{2,1,0:T(8,128)(2,1)S(1)}, u32[]{:S(2)}, u32[]{:S(2)}) %collective-permute-start.6) | collective-permute-done | bytes 229408 | tf_op jit(solution)/shard_map/ppermute | solution.py:318
  24.5 1.3 %encode.5.refs_0_ = bf16[4,32,896]{2,1,0:T(8,128)(2,1)S(1)} custom-call(s32[16]{0:T(128)S(1)} %get-tuple-element.21.req_ref, bf16[512,896]{1,0:T(8,128)(2,1)S(1)} %copy-done.4, bf16[4,32,896]{2,1,0:T(8,128)(2,1)S(1)} %collective-permute-done.6.refs_0_), custom_call_target="tpu_custom_call" | custom-call | flops 117440512 | bytes 458752 | tf_op jit(solution)/shard_map/encode/pallas_call | solution.py:159
  25.8 9.0 %collective-permute-done.10.refs_0_ = bf16[4,32,896]{2,1,0:T(8,128)(2,1)S(1)} collective-permute-done((bf16[4,32,896]{2,1,0:T(8,128)(2,1)S(1)}, bf16[4,32,896]{2,1,0:T(8,128)(2,1)S(1)}, u32[]{:S(2)}, u32[]{:S(2)}) %collective-permute-start.10) | collective-permute-done | bytes 229408 | tf_op jit(solution)/shard_map/ppermute | solution.py:318
  34.8 0.5 collective-permute-start.8
  35.3 1.3 %encode.6.refs_0_ = bf16[4,32,896]{2,1,0:T(8,128)(2,1)S(1)} custom-call(s32[16]{0:T(128)S(1)} %get-tuple-element.21.req_ref, bf16[512,896]{1,0:T(8,128)(2,1)S(1)} %copy-done.4, bf16[4,32,896]{2,1,0:T(8,128)(2,1)S(1)} %collective-permute-done.10.refs_0_), custom_call_target="tpu_custom_call" | custom-call | flops 117440512 | bytes 458752 | tf_op jit(solution)/shard_map/encode/pallas_call | solution.py:159
  36.6 0.1 collective-permute-start.7
  36.7 1.6 %collective-permute-start.12 = (bf16[4,32,896]{2,1,0:T(8,128)(2,1)S(1)}, bf16[4,32,896]{2,1,0:T(8,128)(2,1)S(1)}, u32[]{:S(2)}, u32[]{:S(2)}) collective-permute-start(bf16[4,32,896]{2,1,0:T(8,128)(2,1)S(1)} %encode.6.refs_0_), channel_id=1, source_target_pairs={{0,2},{2,0},{1,3},{3,1},{4,6},{6,4},{5,7},{7,5},{8,10},{10,8},{9,1... | collective-permute-start | bytes 688136 | tf_op jit(solution)/shard_map/ppermute | solution.py:322
  38.2 1.3 %encode.7.refs_3_ = bf16[4,32,896]{2,1,0:T(8,128)(2,1)S(1)} custom-call(s32[16]{0:T(128)S(1)} %get-tuple-element.21.req_ref, bf16[512,896]{1,0:T(8,128)(2,1)S(1)} %copy-done.4, bf16[4,32,896]{2,1,0:T(8,128)(2,1)S(1)} %collective-permute-done.14.refs_0_), custom_call_target="tpu_custom_call" | custom-call | flops 117440512 | bytes 458752 | tf_op jit(solution)/shard_map/encode/pallas_call | solution.py:159
  39.5 0.6 collective-permute-start.16
  40.1 1.7 %collective-permute-done.8.refs_2_ = bf16[4,32,896]{2,1,0:T(8,128)(2,1)S(1)} collective-permute-done((bf16[4,32,896]{2,1,0:T(8,128)(2,1)S(1)}, bf16[4,32,896]{2,1,0:T(8,128)(2,1)S(1)}, u32[]{:S(2)}, u32[]{:S(2)}) %collective-permute-start.8) | collective-permute-done | bytes 229408 | tf_op jit(solution)/shard_map/ppermute | solution.py:322
  41.8 0.5 collective-permute-start.11
  42.3 4.4 %collective-permute-done.12.refs_2_ = bf16[4,32,896]{2,1,0:T(8,128)(2,1)S(1)} collective-permute-done((bf16[4,32,896]{2,1,0:T(8,128)(2,1)S(1)}, bf16[4,32,896]{2,1,0:T(8,128)(2,1)S(1)}, u32[]{:S(2)}, u32[]{:S(2)}) %collective-permute-start.12) | collective-permute-done | bytes 229408 | tf_op jit(solution)/shard_map/ppermute | solution.py:322
  46.7 4.0 %collective-permute-done.16.refs_5_ = bf16[4,32,896]{2,1,0:T(8,128)(2,1)S(1)} collective-permute-done((bf16[4,32,896]{2,1,0:T(8,128)(2,1)S(1)}, bf16[4,32,896]{2,1,0:T(8,128)(2,1)S(1)}, u32[]{:S(2)}, u32[]{:S(2)}) %collective-permute-start.16) | collective-permute-done | bytes 229408 | tf_op jit(solution)/shard_map/ppermute | solution.py:322
  50.6 0.5 collective-permute-start.17
  51.1 1.2 %project.3.refs_0_ = bf16[4,4,32,1024]{3,2,1,0:T(8,128)(2,1)S(1)} custom-call(bf16[4,32,896]{2,1,0:T(8,128)(2,1)S(1)} %encode.4.refs_0_, bf16[4,32,896]{2,1,0:T(8,128)(2,1)S(1)} %collective-permute-done.3.refs_1_, bf16[4,32,896]{2,1,0:T(8,128)(2,1)S(1)} %collective-permute-done.4.refs_2_, bf16[4,32,896]{2,1,0:T(8,128)(2,1)S(1)} %collective-permute-done.5.refs_3_, ...), custom_call_target="tpu_custom_call" | custom-call | flops 939524096 | bytes 3801088 | tf_op jit(solution)/shard_map/project/pallas_call | solution.py:197
  52.4 1.3 %project.4.refs_1_ = bf16[4,4,32,1024]{3,2,1,0:T(8,128)(2,1)S(1)} custom-call(bf16[4,32,896]{2,1,0:T(8,128)(2,1)S(1)} %encode.5.refs_0_, bf16[4,32,896]{2,1,0:T(8,128)(2,1)S(1)} %collective-permute-done.7.refs_1_, bf16[4,32,896]{2,1,0:T(8,128)(2,1)S(1)} %collective-permute-done.8.refs_2_, bf16[4,32,896]{2,1,0:T(8,128)(2,1)S(1)} %collective-permute-done.9.refs_3_, ...), custom_call_target="tpu_custom_call" | custom-call | flops 939524096 | bytes 3801088 | tf_op jit(solution)/shard_map/project/pallas_call | solution.py:197
  53.7 1.3 %project.5.refs_2_ = bf16[4,4,32,1024]{3,2,1,0:T(8,128)(2,1)S(1)} custom-call(bf16[4,32,896]{2,1,0:T(8,128)(2,1)S(1)} %encode.6.refs_0_, bf16[4,32,896]{2,1,0:T(8,128)(2,1)S(1)} %collective-permute-done.11.refs_1_, bf16[4,32,896]{2,1,0:T(8,128)(2,1)S(1)} %collective-permute-done.12.refs_2_, bf16[4,32,896]{2,1,0:T(8,128)(2,1)S(1)} %collective-permute-done.13.refs_3_, ...), custom_call_target="tpu_custom_call" | custom-call | flops 939524096 | bytes 3801088 | tf_op jit(solution)/shard_map/project/pallas_call | solution.py:197
  55.0 3.4 %attend.3 = (bf16[1,128,512]{2,1,0:T(8,128)(2,1)S(1)}, bf16[1,128,512]{2,1,0:T(8,128)(2,1)S(1)}) custom-call(s32[16]{0:T(128)S(1)} %get-tuple-element.20.slot_ref, bf16[512,512]{1,0:T(8,128)(2,1)S(1)} %copy-done.5, bf16[4,4,32,1024]{3,2,1,0:T(8,128)(2,1)S(1)} %project.3.refs_0_, bf16[4,4,32,1024]{3,2,1,0:T(8,128)(2,1)S(1)} %project.4.refs_1_, ...), custom_call_target="tpu_custom_call" | custom-call | flops 1207959552 | bytes 9043968 | tf_op jit(solution)/shard_map/attend/pallas_call | solution.py:265
  58.4 0.1 collective-permute-start.20
  58.5 1.3 %collective-permute-done.20.refs_1_ = bf16[1,128,512]{2,1,0:T(8,128)(2,1)S(1)} collective-permute-done((bf16[1,128,512]{2,1,0:T(8,128)(2,1)S(1)}, bf16[1,128,512]{2,1,0:T(8,128)(2,1)S(1)}, u32[]{:S(2)}, u32[]{:S(2)}) %collective-permute-start.20) | collective-permute-done | bytes 131104 | tf_op jit(solution)/shard_map/ppermute | solution.py:335
  59.9 0.4 out_project.4
  60.3 1.9 %out_project.5 = bf16[128,3072]{1,0:T(8,128)(2,1)S(1)} custom-call(bf16[1,128,512]{2,1,0:T(8,128)(2,1)S(1)} %get-tuple-element.32.refs_0_, bf16[1,128,512]{2,1,0:T(8,128)(2,1)S(1)} %collective-permute-done.20.refs_1_, bf16[512,4096]{1,0:T(8,128)(2,1)S(1)} %copy-done, bf16[512,4096]{1,0:T(8,128)(2,1)S(1)} %collective-permute-done.19.refs_3_), custom_call_target="tpu_custom_call" | custom-call | flops 805306368 | bytes 6291456 | tf_op jit(solution)/shard_map/out_project/pallas_call | solution.py:288
  62.3 0.6 collective-permute-start.22
  62.9 1.5 %collective-permute-start.21 = (bf16[128,1024]{1,0:T(8,128)(2,1)S(1)}, bf16[128,1024]{1,0:T(8,128)(2,1)S(1)}, u32[]{:S(2)}, u32[]{:S(2)}) collective-permute-start(bf16[128,1024]{1,0:T(8,128)(2,1)S(1)} %out_project.4), channel_id=1, source_target_pairs={{0,2},{2,0},{1,3},{3,1},{4,6},{6,4},{5,7},{7,5},{8,10},{10,8},{9,1... | collective-permute-start | bytes 786440 | tf_op jit(solution)/shard_map/ppermute | solution.py:350
  64.4 3.4 %attend.2 = (bf16[1,128,512]{2,1,0:T(8,128)(2,1)S(1)}, bf16[1,128,512]{2,1,0:T(8,128)(2,1)S(1)}) custom-call(s32[16]{0:T(128)S(1)} %get-tuple-element.20.slot_ref, bf16[512,512]{1,0:T(8,128)(2,1)S(1)} %copy-done.5, bf16[4,4,32,1024]{3,2,1,0:T(8,128)(2,1)S(1)} %project.3.refs_0_, bf16[4,4,32,1024]{3,2,1,0:T(8,128)(2,1)S(1)} %project.4.refs_1_, ...), custom_call_target="tpu_custom_call" | custom-call | flops 1207959552 | bytes 9043968 | tf_op jit(solution)/shard_map/attend/pallas_call | solution.py:265
  67.8 0.1 collective-permute-start.18
  67.8 1.3 %collective-permute-done.18.refs_1_ = bf16[1,128,512]{2,1,0:T(8,128)(2,1)S(1)} collective-permute-done((bf16[1,128,512]{2,1,0:T(8,128)(2,1)S(1)}, bf16[1,128,512]{2,1,0:T(8,128)(2,1)S(1)}, u32[]{:S(2)}, u32[]{:S(2)}) %collective-permute-start.18) | collective-permute-done | bytes 131104 | tf_op jit(solution)/shard_map/ppermute | solution.py:335
  69.2 2.5 %out_project.3 = bf16[128,4096]{1,0:T(8,128)(2,1)S(1)} custom-call(bf16[1,128,512]{2,1,0:T(8,128)(2,1)S(1)} %get-tuple-element.26.refs_0_, bf16[1,128,512]{2,1,0:T(8,128)(2,1)S(1)} %collective-permute-done.18.refs_1_, bf16[512,4096]{1,0:T(8,128)(2,1)S(1)} %copy-done, bf16[512,4096]{1,0:T(8,128)(2,1)S(1)} %collective-permute-done.19.refs_3_), custom_call_target="tpu_custom_call" | custom-call | flops 1073741824 | bytes 8388608 | tf_op jit(solution)/shard_map/out_project/pallas_call | solution.py:288
  71.7 15.9 %collective-permute-done.21 = bf16[128,1024]{1,0:T(8,128)(2,1)S(1)} collective-permute-done((bf16[128,1024]{1,0:T(8,128)(2,1)S(1)}, bf16[128,1024]{1,0:T(8,128)(2,1)S(1)}, u32[]{:S(2)}, u32[]{:S(2)}) %collective-permute-start.21) | collective-permute-done | bytes 262176 | tf_op jit(solution)/shard_map/ppermute | solution.py:350
  87.5 1.2 %add_convert_fusion = bf16[128,4096]{1,0:T(8,128)(2,1)} fusion(bf16[128,4096]{1,0:T(8,128)(2,1)S(1)} %out_project.3, bf16[128,3072]{1,0:T(8,128)(2,1)S(1)} %collective-permute-done.22, bf16[128,1024]{1,0:T(8,128)(2,1)S(1)} %collective-permute-done.21), kind=kLoop, calls=%fused_computation | loop fusion | flops 3670016 | bytes 3145728 | tf_op jit(solution)/shard_map/convert_element_type | solution.py:356
  (27 shorter events, 0.1 us)
Async XLA Ops:
  0.0 24.5 %copy-start.4 = (bf16[512,896]{1,0:T(8,128)(2,1)S(1)}, bf16[512,896]{1,0:T(8,128)(2,1)}, u32[]{:S(2)}) copy-start(bf16[512,896]{1,0:T(8,128)(2,1)} %states_ref.7) | copy-start | bytes 2752516
  0.8 5.4 %collective-permute-start.2 = (s32[4,8]{1,0:T(4,128)S(1)}, s32[4,8]{1,0:T(4,128)S(1)}, u32[]{:S(2)}, u32[]{:S(2)}) collective-permute-start(s32[4,8]{1,0:T(4,128)S(1)} %pad_add_fusion.own_ref), channel_id=1, source_target_pairs={{0,12},{4,8},{8,4},{12,0},{1,13},{5,9},{9,5},{13,1},{2,14},{6,10},... | collective-permute-start | bytes 392 | tf_op jit(solution)/shard_map/ppermute | solution.py:314
  1.0 5.2 %collective-permute-start.1 = (s32[4,8]{1,0:T(4,128)S(1)}, s32[4,8]{1,0:T(4,128)S(1)}, u32[]{:S(2)}, u32[]{:S(2)}) collective-permute-start(s32[4,8]{1,0:T(4,128)S(1)} %pad_add_fusion.own_ref), channel_id=1, source_target_pairs={{0,8},{4,12},{8,0},{12,4},{1,9},{5,13},{9,1},{13,5},{2,10},{6,14},... | collective-permute-start | bytes 392 | tf_op jit(solution)/shard_map/ppermute | solution.py:314
  2.7 4.0 %collective-permute-start = (s32[4,8]{1,0:T(4,128)S(1)}, s32[4,8]{1,0:T(4,128)S(1)}, u32[]{:S(2)}, u32[]{:S(2)}) collective-permute-start(s32[4,8]{1,0:T(4,128)S(1)} %pad_add_fusion.own_ref), channel_id=1, source_target_pairs={{0,4},{4,0},{8,12},{12,8},{1,5},{5,1},{9,13},{13,9},{2,6},{6,2},{1... | collective-permute-start | bytes 392 | tf_op jit(solution)/shard_map/ppermute | solution.py:314
  6.7 1.2 %copy-start.6 = (bf16[16,32,896]{2,1,0:T(8,128)(2,1)S(1)}, bf16[16,32,896]{2,1,0:T(8,128)(2,1)}, u32[]{:S(2)}) copy-start(bf16[16,32,896]{2,1,0:T(8,128)(2,1)} %refs_3_.1) | copy-start | bytes 2752516
  9.4 50.4 %collective-permute-start.19 = (bf16[512,4096]{1,0:T(8,128)(2,1)}, bf16[512,4096]{1,0:T(8,128)(2,1)S(1)}, u32[]{:S(2)}, u32[]{:S(2)}) collective-permute-start(bf16[512,4096]{1,0:T(8,128)(2,1)} %refs_2_.2), channel_id=1, source_target_pairs={{0,1},{1,0},{2,3},{3,2},{4,5},{5,4},{6,7},{7,6},{8,9},{9,8},{10,11... | collective-permute-start | bytes 12582920 | tf_op jit(solution)/shard_map/ppermute | solution.py:311
  9.5 1.2 %copy-start.3 = (bf16[512,896]{1,0:T(8,128)(2,1)S(1)}, bf16[512,896]{1,0:T(8,128)(2,1)}, u32[]{:S(2)}) copy-start(bf16[512,896]{1,0:T(8,128)(2,1)} %states_ref.7) | copy-start | bytes 2752516
  12.0 39.2 %copy-start.1 = (bf16[896,512]{1,0:T(8,128)(2,1)S(1)}, bf16[896,512]{1,0:T(8,128)(2,1)}, u32[]{:S(2)}) copy-start(bf16[896,512]{1,0:T(8,128)(2,1)} %refs_7_.3) | copy-start | bytes 2752516
  12.0 39.2 %copy-start.2 = (bf16[896,512]{1,0:T(8,128)(2,1)S(1)}, bf16[896,512]{1,0:T(8,128)(2,1)}, u32[]{:S(2)}) copy-start(bf16[896,512]{1,0:T(8,128)(2,1)} %refs_8_.3) | copy-start | bytes 2752516
  12.0 8.1 %collective-permute-start.4 = (bf16[4,32,896]{2,1,0:T(8,128)(2,1)S(1)}, bf16[4,32,896]{2,1,0:T(8,128)(2,1)S(1)}, u32[]{:S(2)}, u32[]{:S(2)}) collective-permute-start(bf16[4,32,896]{2,1,0:T(8,128)(2,1)S(1)} %encode.4.refs_0_), channel_id=1, source_target_pairs={{0,2},{2,0},{1,3},{3,1},{4,6},{6,4},{5,7},{7,5},{8,10},{10,8},{9,1... | collective-permute-start | bytes 688136 | tf_op jit(solution)/shard_map/ppermute | solution.py:322
  13.5 11.0 %collective-permute-start.6 = (bf16[4,32,896]{2,1,0:T(8,128)(2,1)S(1)}, bf16[4,32,896]{2,1,0:T(8,128)(2,1)S(1)}, u32[]{:S(2)}, u32[]{:S(2)}) collective-permute-start(bf16[4,32,896]{2,1,0:T(8,128)(2,1)S(1)} %get-tuple-element.23), channel_id=1, source_target_pairs={{0,4},{4,0},{8,12},{12,8},{1,5},{5,1},{9,13},{13,9},{2,6},{6,2},{1... | collective-permute-start | bytes 688136 | tf_op jit(solution)/shard_map/ppermute | solution.py:318
  15.6 19.2 %collective-permute-start.10 = (bf16[4,32,896]{2,1,0:T(8,128)(2,1)S(1)}, bf16[4,32,896]{2,1,0:T(8,128)(2,1)S(1)}, u32[]{:S(2)}, u32[]{:S(2)}) collective-permute-start(bf16[4,32,896]{2,1,0:T(8,128)(2,1)S(1)} %get-tuple-element.24), channel_id=1, source_target_pairs={{0,8},{4,12},{8,0},{12,4},{1,9},{5,13},{9,1},{13,5},{2,10},{6,14},... | collective-permute-start | bytes 688136 | tf_op jit(solution)/shard_map/ppermute | solution.py:318
  16.5 20.1 %collective-permute-start.3 = (bf16[4,32,896]{2,1,0:T(8,128)(2,1)S(1)}, bf16[4,32,896]{2,1,0:T(8,128)(2,1)S(1)}, u32[]{:S(2)}, u32[]{:S(2)}) collective-permute-start(bf16[4,32,896]{2,1,0:T(8,128)(2,1)S(1)} %encode.4.refs_0_), channel_id=1, source_target_pairs={{0,1},{1,0},{2,3},{3,2},{4,5},{5,4},{6,7},{7,6},{8,9},{9,8},{10,11... | collective-permute-start | bytes 688136 | tf_op jit(solution)/shard_map/ppermute | solution.py:311
  20.0 16.6 %collective-permute-start.14 = (bf16[4,32,896]{2,1,0:T(8,128)(2,1)S(1)}, bf16[4,32,896]{2,1,0:T(8,128)(2,1)S(1)}, u32[]{:S(2)}, u32[]{:S(2)}) collective-permute-start(bf16[4,32,896]{2,1,0:T(8,128)(2,1)S(1)} %get-tuple-element.25), channel_id=1, source_target_pairs={{0,12},{4,8},{8,4},{12,0},{1,13},{5,9},{9,5},{13,1},{2,14},{6,10},... | collective-permute-start | bytes 688136 | tf_op jit(solution)/shard_map/ppermute | solution.py:318
  24.5 15.0 %collective-permute-start.5 = (bf16[4,32,896]{2,1,0:T(8,128)(2,1)S(1)}, bf16[4,32,896]{2,1,0:T(8,128)(2,1)S(1)}, u32[]{:S(2)}, u32[]{:S(2)}) collective-permute-start(bf16[4,32,896]{2,1,0:T(8,128)(2,1)S(1)} %collective-permute-done.4.refs_2_), channel_id=1, source_target_pairs={{0,1},{1,0},{2,3},{3,2},{4,5},{5,4},{6,7},{7,6},{8,9},{9,8},{10,11... | collective-permute-start | bytes 688136 | tf_op jit(solution)/shard_map/ppermute | solution.py:311
  34.8 7.0 %collective-permute-start.8 = (bf16[4,32,896]{2,1,0:T(8,128)(2,1)S(1)}, bf16[4,32,896]{2,1,0:T(8,128)(2,1)S(1)}, u32[]{:S(2)}, u32[]{:S(2)}) collective-permute-start(bf16[4,32,896]{2,1,0:T(8,128)(2,1)S(1)} %encode.5.refs_0_), channel_id=1, source_target_pairs={{0,2},{2,0},{1,3},{3,1},{4,6},{6,4},{5,7},{7,5},{8,10},{10,8},{9,1... | collective-permute-start | bytes 688136 | tf_op jit(solution)/shard_map/ppermute | solution.py:322
  36.6 5.2 %collective-permute-start.7 = (bf16[4,32,896]{2,1,0:T(8,128)(2,1)S(1)}, bf16[4,32,896]{2,1,0:T(8,128)(2,1)S(1)}, u32[]{:S(2)}, u32[]{:S(2)}) collective-permute-start(bf16[4,32,896]{2,1,0:T(8,128)(2,1)S(1)} %encode.5.refs_0_), channel_id=1, source_target_pairs={{0,1},{1,0},{2,3},{3,2},{4,5},{5,4},{6,7},{7,6},{8,9},{9,8},{10,11... | collective-permute-start | bytes 688136 | tf_op jit(solution)/shard_map/ppermute | solution.py:311
  36.7 10.0 %collective-permute-start.12 = (bf16[4,32,896]{2,1,0:T(8,128)(2,1)S(1)}, bf16[4,32,896]{2,1,0:T(8,128)(2,1)S(1)}, u32[]{:S(2)}, u32[]{:S(2)}) collective-permute-start(bf16[4,32,896]{2,1,0:T(8,128)(2,1)S(1)} %encode.6.refs_0_), channel_id=1, source_target_pairs={{0,2},{2,0},{1,3},{3,1},{4,6},{6,4},{5,7},{7,5},{8,10},{10,8},{9,1... | collective-permute-start | bytes 688136 | tf_op jit(solution)/shard_map/ppermute | solution.py:322
  39.5 11.1 %collective-permute-start.16 = (bf16[4,32,896]{2,1,0:T(8,128)(2,1)S(1)}, bf16[4,32,896]{2,1,0:T(8,128)(2,1)S(1)}, u32[]{:S(2)}, u32[]{:S(2)}) collective-permute-start(bf16[4,32,896]{2,1,0:T(8,128)(2,1)S(1)} %encode.7.refs_3_), channel_id=1, source_target_pairs={{0,2},{2,0},{1,3},{3,1},{4,6},{6,4},{5,7},{7,5},{8,10},{10,8},{9,1... | collective-permute-start | bytes 688136 | tf_op jit(solution)/shard_map/ppermute | solution.py:322
  41.7 8.9 %collective-permute-start.9 = (bf16[4,32,896]{2,1,0:T(8,128)(2,1)S(1)}, bf16[4,32,896]{2,1,0:T(8,128)(2,1)S(1)}, u32[]{:S(2)}, u32[]{:S(2)}) collective-permute-start(bf16[4,32,896]{2,1,0:T(8,128)(2,1)S(1)} %collective-permute-done.8.refs_2_), channel_id=1, source_target_pairs={{0,1},{1,0},{2,3},{3,2},{4,5},{5,4},{6,7},{7,6},{8,9},{9,8},{10,11... | collective-permute-start | bytes 688136 | tf_op jit(solution)/shard_map/ppermute | solution.py:311
  41.8 11.9 %collective-permute-start.11 = (bf16[4,32,896]{2,1,0:T(8,128)(2,1)S(1)}, bf16[4,32,896]{2,1,0:T(8,128)(2,1)S(1)}, u32[]{:S(2)}, u32[]{:S(2)}) collective-permute-start(bf16[4,32,896]{2,1,0:T(8,128)(2,1)S(1)} %encode.6.refs_0_), channel_id=1, source_target_pairs={{0,1},{1,0},{2,3},{3,2},{4,5},{5,4},{6,7},{7,6},{8,9},{9,8},{10,11... | collective-permute-start | bytes 688136 | tf_op jit(solution)/shard_map/ppermute | solution.py:311
  46.7 7.0 %collective-permute-start.13 = (bf16[4,32,896]{2,1,0:T(8,128)(2,1)S(1)}, bf16[4,32,896]{2,1,0:T(8,128)(2,1)S(1)}, u32[]{:S(2)}, u32[]{:S(2)}) collective-permute-start(bf16[4,32,896]{2,1,0:T(8,128)(2,1)S(1)} %collective-permute-done.12.refs_2_), channel_id=1, source_target_pairs={{0,1},{1,0},{2,3},{3,2},{4,5},{5,4},{6,7},{7,6},{8,9},{9,8},{10,11... | collective-permute-start | bytes 688136 | tf_op jit(solution)/shard_map/ppermute | solution.py:311
  50.6 4.4 %collective-permute-start.15 = (bf16[4,32,896]{2,1,0:T(8,128)(2,1)S(1)}, bf16[4,32,896]{2,1,0:T(8,128)(2,1)S(1)}, u32[]{:S(2)}, u32[]{:S(2)}) collective-permute-start(bf16[4,32,896]{2,1,0:T(8,128)(2,1)S(1)} %encode.7.refs_3_), channel_id=1, source_target_pairs={{0,1},{1,0},{2,3},{3,2},{4,5},{5,4},{6,7},{7,6},{8,9},{9,8},{10,11... | collective-permute-start | bytes 688136 | tf_op jit(solution)/shard_map/ppermute | solution.py:311
  50.6 4.4 %collective-permute-start.17 = (bf16[4,32,896]{2,1,0:T(8,128)(2,1)S(1)}, bf16[4,32,896]{2,1,0:T(8,128)(2,1)S(1)}, u32[]{:S(2)}, u32[]{:S(2)}) collective-permute-start(bf16[4,32,896]{2,1,0:T(8,128)(2,1)S(1)} %collective-permute-done.16.refs_5_), channel_id=1, source_target_pairs={{0,1},{1,0},{2,3},{3,2},{4,5},{5,4},{6,7},{7,6},{8,9},{9,8},{10,11... | collective-permute-start | bytes 688136 | tf_op jit(solution)/shard_map/ppermute | solution.py:311
  53.7 1.3 %copy-start.5 = (bf16[512,512]{1,0:T(8,128)(2,1)S(1)}, bf16[512,512]{1,0:T(8,128)(2,1)}, u32[]{:S(2)}) copy-start(bf16[512,512]{1,0:T(8,128)(2,1)} %q_ref.2) | copy-start | bytes 1572868
  55.0 4.9 %copy-start = (bf16[512,4096]{1,0:T(8,128)(2,1)S(1)}, bf16[512,4096]{1,0:T(8,128)(2,1)}, u32[]{:S(2)}) copy-start(bf16[512,4096]{1,0:T(8,128)(2,1)} %refs_2_.2) | copy-start | bytes 12582916
  58.4 1.4 %collective-permute-start.20 = (bf16[1,128,512]{2,1,0:T(8,128)(2,1)S(1)}, bf16[1,128,512]{2,1,0:T(8,128)(2,1)S(1)}, u32[]{:S(2)}, u32[]{:S(2)}) collective-permute-start(bf16[1,128,512]{2,1,0:T(8,128)(2,1)S(1)} %get-tuple-element.30), channel_id=1, source_target_pairs={{0,1},{1,0},{2,3},{3,2},{4,5},{5,4},{6,7},{7,6},{8,9},{9,8},{10,11... | collective-permute-start | bytes 393224 | tf_op jit(solution)/shard_map/ppermute | solution.py:335
  62.3 25.3 %collective-permute-start.22 = (bf16[128,3072]{1,0:T(8,128)(2,1)S(1)}, bf16[128,3072]{1,0:T(8,128)(2,1)S(1)}, u32[]{:S(2)}, u32[]{:S(2)}) collective-permute-start(bf16[128,3072]{1,0:T(8,128)(2,1)S(1)} %out_project.5), channel_id=1, source_target_pairs={{0,2},{2,0},{1,3},{3,1},{4,6},{6,4},{5,7},{7,5},{8,10},{10,8},{9,1... | collective-permute-start | bytes 2359304 | tf_op jit(solution)/shard_map/ppermute | solution.py:350
  62.9 24.7 %collective-permute-start.21 = (bf16[128,1024]{1,0:T(8,128)(2,1)S(1)}, bf16[128,1024]{1,0:T(8,128)(2,1)S(1)}, u32[]{:S(2)}, u32[]{:S(2)}) collective-permute-start(bf16[128,1024]{1,0:T(8,128)(2,1)S(1)} %out_project.4), channel_id=1, source_target_pairs={{0,2},{2,0},{1,3},{3,1},{4,6},{6,4},{5,7},{7,5},{8,10},{10,8},{9,1... | collective-permute-start | bytes 786440 | tf_op jit(solution)/shard_map/ppermute | solution.py:350
  67.8 1.4 %collective-permute-start.18 = (bf16[1,128,512]{2,1,0:T(8,128)(2,1)S(1)}, bf16[1,128,512]{2,1,0:T(8,128)(2,1)S(1)}, u32[]{:S(2)}, u32[]{:S(2)}) collective-permute-start(bf16[1,128,512]{2,1,0:T(8,128)(2,1)S(1)} %get-tuple-element.27), channel_id=1, source_target_pairs={{0,1},{1,0},{2,3},{3,2},{4,5},{5,4},{6,7},{7,6},{8,9},{9,8},{10,11... | collective-permute-start | bytes 393224 | tf_op jit(solution)/shard_map/ppermute | solution.py:335

commit v3 on v2

v3 whole, which is shorter than its diff:
```python
import functools

import jax
import jax.numpy as jnp
from jax import lax
from jax.experimental import pallas as pl
from jax.experimental.pallas import tpu as pltpu
from jax.sharding import PartitionSpec as P

HD = 128
ENCODER_HEAD_DIM = 128
F32 = jnp.float32
BF16 = jnp.bfloat16
COL_TILE = 512

VMEM = pl.BlockSpec(memory_space=pltpu.VMEM)
SMEM = pl.BlockSpec(memory_space=pltpu.SMEM)
ANY = pl.BlockSpec(memory_space=pl.ANY)


def params(mib):
    return pltpu.CompilerParams(vmem_limit_bytes=mib * 2**20)


SMALL = pl.CostEstimate(flops=1024, bytes_accessed=1024, transcendentals=0)


def apart(n, a, b):
    if n & (n - 1) == 0:
        return a ^ b
    return lax.rem(b - a + n, n)


def lane_pairs(n, d, reply):
    if n & (n - 1) == 0:
        return [(i, i ^ d) for i in range(n)]
    return [(i, (i - d if reply else i + d) % n) for i in range(n)]


def shift_pairs(n, s):
    return [(i, (i + s) % n) for i in range(n)]


def dot_t(a, b):
    return lax.dot_general(a, b, (((1,), (1,)), ((), ())), preferred_element_type=F32)


def dot(a, b):
    return jnp.dot(a, b, preferred_element_type=F32)


def fetch_kernel(n_lanes, cap, *refs):
    others = n_lanes - 1
    asked, store_ref, refs = refs[:others], refs[others], refs[others + 1 :]
    blocks, (pick_ref, sem) = refs[:others], refs[others:]
    lane = lax.axis_index("lanes")
    fanout, spans = asked[0].shape[0] // 2, asked[0].shape[1]
    for i in range(others * cap):
        pick_ref[i] = 0
    copies = []
    for d in range(others):
        place = d * cap
        for span in range(spans):
            for k in range(fanout):
                pick_ref[place] = asked[d][fanout + k, span]
                place = place + (asked[d][k, span] == lane).astype(jnp.int32)
        for s in range(cap):
            slot = d * cap + s
            copies.append(
                pltpu.make_async_copy(store_ref.at[pick_ref[slot]], blocks[d].at[s], sem.at[slot])
            )
            copies[-1].start()
    for copy in copies:
        copy.wait()


def fetch(asked, store, n_lanes, cap):
    block = jax.ShapeDtypeStruct((cap,) + store.shape[1:], store.dtype)
    others = n_lanes - 1
    return pl.pallas_call(
        functools.partial(fetch_kernel, n_lanes, cap),
        out_shape=[block] * others,
        in_specs=[SMEM] * others + [ANY],
        out_specs=[VMEM] * others,
        scratch_shapes=[
            pltpu.SMEM((others * cap + 1,), jnp.int32),
            pltpu.SemaphoreType.DMA((others * cap,)),
        ],
        compiler_params=params(16),
        cost_estimate=SMALL,
        name="fetch",
    )(*asked, store)


def encode_pairs(width):
    step = 2 * ENCODER_HEAD_DIM
    return [(start, min(start + step, width)) for start in range(0, width, step)]


def spread(states, start, stop):
    part = states[:, start:stop]
    heads = (stop - start) // ENCODER_HEAD_DIM
    if heads == 1:
        return part
    rows = jnp.concatenate([part] * heads, axis=0)
    return jnp.where(own_cells(rows.shape, part.shape[0]), rows, jnp.zeros_like(rows))


def own_cells(shape, keys):
    row = lax.broadcasted_iota(jnp.int32, shape, 0)
    col = lax.broadcasted_iota(jnp.int32, shape, 1)
    return (row >= keys) == (col >= ENCODER_HEAD_DIM)


def softmax_top(logits, keys):
    if logits.shape[1] == keys:
        return jnp.max(logits, axis=1, keepdims=True)
    first = lax.broadcasted_iota(jnp.int32, logits.shape, 1) < keys
    low = jnp.max(jnp.where(first, logits, -jnp.inf), axis=1, keepdims=True)
    high = jnp.max(jnp.where(first, -jnp.inf, logits), axis=1, keepdims=True)
    return jnp.where(first, low, high)


def encode_block(block, out_ref, first, req_ref, states_ref, fanout, span_len):
    scale = ENCODER_HEAD_DIM ** (-0.5)
    runs = encode_pairs(states_ref.shape[1])
    units = []
    for s in range(block.shape[0]):
        span = lax.div(req_ref[first + s], fanout)
        states = states_ref[pl.ds(pl.multiple_of(span * span_len, span_len), span_len), :]
        units += [(s, start, stop, spread(states, start, stop)) for start, stop in runs]
    logits = [dot_t(block[s, :, start:stop], keys) for s, start, stop, keys in units]
    tops = [softmax_top(part, span_len) for part in logits]
    weights = [jnp.exp((part - top) * scale).astype(BF16) for part, top in zip(logits, tops)]
    mixed = [dot(part, keys) for part, (_, _, _, keys) in zip(weights, units)]
    sums = []
    for part, (_, start, stop, keys) in zip(weights, units):
        ones = jnp.ones(keys.shape, BF16)
        if stop - start > ENCODER_HEAD_DIM:
            ones = jnp.where(own_cells(keys.shape, span_len), ones, jnp.zeros_like(ones))
        sums.append(dot(part, ones))
    for (s, start, stop, _), top, bottom in zip(units, mixed, sums):
        token = block[s, :, start:stop].astype(F32)
        out_ref[s, :, start:stop] = (token + top / bottom).astype(BF16)


def encode_kernel(first, cap, fanout, span_len, req_ref, states_ref, *refs):
    blocks, out_ref = refs[:-1], refs[-1]
    for i, block in enumerate(blocks):
        out = out_ref.at[i * cap : (i + 1) * cap]
        encode_block(block, out, (first + i) * cap, req_ref, states_ref, fanout, span_len)


def encode(req, span_states, blocks, first, fanout, span_len):
    cap, tokens, width = blocks[0].shape
    return pl.pallas_call(
        functools.partial(encode_kernel, first, cap, fanout, span_len),
        out_shape=jax.ShapeDtypeStruct((len(blocks) * cap, tokens, width), BF16),
        in_specs=[SMEM, VMEM] + [VMEM] * len(blocks),
        out_specs=VMEM,
        compiler_params=params(16),
        cost_estimate=SMALL,
        name="encode",
    )(req, span_states, *blocks)


def encode_local_kernel(n_lanes, cap, span_len, own_ref, states_ref, store_ref, *refs):
    out_ref, req_ref, slot_ref, pick_ref, count_ref, tokens_ref, sem = refs
    lane = lax.axis_index("lanes")
    fanout, spans = own_ref.shape[0] // 2, own_ref.shape[1]
    for i in range(n_lanes):
        count_ref[i] = 0
    for i in range(n_lanes * cap):
        pick_ref[i] = 0
        req_ref[i] = 0
    for j in range(fanout * spans):
        span, k = j // fanout, j % fanout
        d = apart(n_lanes, lane, own_ref[k, span])
        rank = count_ref[d]
        count_ref[d] = rank + 1
        slot = d * cap + rank
        pick_ref[slot] = own_ref[fanout + k, span]
        req_ref[slot] = j
        slot_ref[j] = slot
    copies = [
        pltpu.make_async_copy(store_ref.at[pick_ref[s]], tokens_ref.at[s], sem.at[s]) for s in range(cap)
    ]
    for copy in copies:
        copy.start()
    for copy in copies:
        copy.wait()
    encode_block(tokens_ref, out_ref, 0, req_ref, states_ref, fanout, span_len)


def encode_local(own, span_states, store, n_lanes, cap, span_len):
    block = (cap,) + store.shape[1:]
    return pl.pallas_call(
        functools.partial(encode_local_kernel, n_lanes, cap, span_len),
        out_shape=(
            jax.ShapeDtypeStruct(block, BF16),
            jax.ShapeDtypeStruct((n_lanes * cap,), jnp.int32),
            jax.ShapeDtypeStruct((own.size // 2,), jnp.int32),
        ),
        in_specs=[SMEM, VMEM, ANY],
        out_specs=(VMEM, SMEM, SMEM),
        scratch_shapes=[
            pltpu.SMEM((n_lanes * cap,), jnp.int32),
            pltpu.SMEM((n_lanes,), jnp.int32),
            pltpu.VMEM(block, BF16),
            pltpu.SemaphoreType.DMA((cap,)),
        ],
        compiler_params=params(16),
        cost_estimate=SMALL,
        name="encode_local",
    )(own, span_states, store)


def project_into(kv_ref, first, pieces, wk_ref, wv_ref):
    n, slots, tokens, width = pieces[0].shape
    rows = jnp.concatenate([piece[...].reshape(n * slots * tokens, width) for piece in pieces], axis=0)
    cols = wk_ref.shape[1]
    for side, weight in enumerate((wk_ref, wv_ref)):
        made = dot(rows, weight[...]).astype(BF16)
        for p in range(n * len(pieces)):
            part = made[p * slots * tokens : (p + 1) * slots * tokens]
            kv_ref[first : first + slots, p, :, side * cols : (side + 1) * cols] = part.reshape(
                slots, tokens, cols
            )


def project_kernel(n_pieces, *refs):
    pieces, (wk_ref, wv_ref, kv_ref) = refs[:n_pieces], refs[n_pieces:]
    project_into(kv_ref, 0, pieces, wk_ref, wv_ref)


def project(pieces, w_key, w_value):
    n, slots, tokens, _ = pieces[0].shape
    shape = (slots, n * len(pieces), tokens, 2 * w_key.shape[1])
    return pl.pallas_call(
        functools.partial(project_kernel, len(pieces)),
        out_shape=jax.ShapeDtypeStruct(shape, BF16),
        in_specs=[VMEM] * (len(pieces) + 2),
        out_specs=VMEM,
        compiler_params=params(32),
        cost_estimate=SMALL,
        name="project",
    )(*pieces, w_key, w_value)


def attend_kernel(firsts, n_pieces, n_heads, n_rep, turns, fanout, spans, slot_ref, q_ref, *refs):
    n_ready = len(firsts) - 1
    ready, refs = refs[:n_ready], refs[n_ready:]
    pieces, refs = refs[:n_pieces], refs[n_pieces:]
    wk_ref, wv_ref = refs[:2]
    outs = refs[2 : 2 + n_rep]
    kv_ref, sem = refs[2 + n_rep :]
    copies = [
        pltpu.make_async_copy(ref, kv_ref.at[pl.ds(first, ref.shape[0])], sem.at[i])
        for i, (ref, first) in enumerate(zip(ready, firsts))
    ]
    for copy in copies:
        copy.start()
    project_into(kv_ref, firsts[-1], pieces, wk_ref, wv_ref)
    for copy in copies:
        copy.wait()
    heads_at, rep_at = lax.axis_index("heads"), lax.axis_index("rep")
    cols = wk_ref.shape[1]
    span_len = q_ref.shape[0] // spans
    block = spans // (n_heads * n_rep)
    tokens = kv_ref.shape[1] * kv_ref.shape[2]
    heads = [slice(h * HD, (h + 1) * HD) for h in range(cols // HD)]
    for at, t in enumerate(turns):
        for s in range(n_rep):
            owner = lax.rem(heads_at + t, n_heads) * n_rep + lax.rem(rep_at + s, n_rep)
            for i in range(block):
                span = owner * block + i
                slots = [slot_ref[span * fanout + k] for k in range(fanout)]
                rows = pl.ds(pl.multiple_of(span * span_len, span_len), span_len)

                def side(lanes):
                    return jnp.concatenate(
                        [kv_ref[slot, :, :, lanes].reshape(tokens, HD) for slot in slots], axis=0
                    )

                logits = [dot_t(q_ref[rows, lanes], side(lanes)) for lanes in heads]
                tops = [jnp.max(part, axis=1, keepdims=True) for part in logits]
                weights = [jnp.exp((part - top) * HD ** (-0.5)) for part, top in zip(logits, tops)]
                scales = [1.0 / jnp.sum(part, axis=1, keepdims=True) for part in weights]
                mixed = [
                    dot(part.astype(BF16), side(slice(cols + lanes.start, cols + lanes.stop)))
                    for part, lanes in zip(weights, heads)
                ]
                for part, scale, lanes in zip(mixed, scales, heads):
                    outs[s][at, i * span_len : (i + 1) * span_len, lanes] = (part * scale).astype(BF16)


def attend(slot, queries, ready, pieces, w_key, w_value, n_heads, n_rep, turns, fanout, spans):
    firsts = [0]
    for kv in ready:
        firsts.append(firsts[-1] + kv.shape[0])
    n, slots, tokens, _ = pieces[0].shape
    cols = w_key.shape[1]
    rows = queries.shape[0] // (n_heads * n_rep)
    kv_shape = (firsts[-1] + slots, n * len(pieces), tokens, 2 * cols)
    return pl.pallas_call(
        functools.partial(attend_kernel, firsts, len(pieces), n_heads, n_rep, turns, fanout, spans),
        out_shape=[jax.ShapeDtypeStruct((len(turns), rows, cols), BF16)] * n_rep,
        in_specs=[SMEM, VMEM] + [ANY] * len(ready) + [VMEM] * (len(pieces) + 2),
        out_specs=[VMEM] * n_rep,
        scratch_shapes=[pltpu.VMEM(kv_shape, BF16), pltpu.SemaphoreType.DMA((max(1, len(ready)),))],
        compiler_params=params(40),
        cost_estimate=SMALL,
        name="attend",
    )(slot, queries, *ready, *pieces, w_key, w_value)


def out_kernel(n_rep, *refs):
    mixed, weights, out_ref = refs[:n_rep], refs[n_rep:-1], refs[-1]
    out_ref[...] = sum(dot(a[0], w[...]) for a, w in zip(mixed, weights)).astype(BF16)


def out_project(mixed, weights, t, start, stop, tile):
    _, rows, depth = mixed[0].shape
    base = start // tile
    return pl.pallas_call(
        functools.partial(out_kernel, len(mixed)),
        grid=((stop - start) // tile,),
        out_shape=jax.ShapeDtypeStruct((rows, stop - start), BF16),
        in_specs=[pl.BlockSpec((1, rows, depth), lambda j: (t, 0, 0))] * len(mixed)
        + [pl.BlockSpec((depth, tile), lambda j: (0, base + j))] * len(mixed),
        out_specs=pl.BlockSpec((rows, tile), lambda j: (0, j)),
        compiler_params=params(16),
        cost_estimate=SMALL,
        name="out_project",
    )(*mixed, *weights)


def after(values, *earlier):
    return lax.optimization_barrier((values, earlier))[0]


def shards(queries, span_states, store, entry_ids, owners, w_key, w_value, w_out):
    n_lanes, n_heads, n_rep = (lax.axis_size(name) for name in ("lanes", "heads", "rep"))
    spans, fanout = entry_ids.shape
    requests = spans * fanout
    cap = max(2, (requests + n_lanes - 1) // n_lanes)
    span_len = queries.shape[0] // spans

    def over_heads(array):
        return [array] + [lax.ppermute(array, "heads", shift_pairs(n_heads, s)) for s in range(1, n_heads)]

    def over_rep(array):
        return [array] + [lax.ppermute(array, "rep", shift_pairs(n_rep, s)) for s in range(1, n_rep)]

    own = jnp.concatenate([owners.T, entry_ids.T], axis=0)
    asked = [lax.ppermute(own, "lanes", lane_pairs(n_lanes, d, False)) for d in range(1, n_lanes)]
    w_outs = over_rep(w_out)
    encoded, req, slot = encode_local(own, span_states, store, n_lanes, cap, span_len)
    asked = after(asked, req, w_outs)
    blocks = [None] + list(fetch(asked, store, n_lanes, cap))

    def send(distances, *earlier):
        ready = after([blocks[d] for d in distances], *earlier)
        return [
            lax.ppermute(block, "lanes", lane_pairs(n_lanes, d, True))
            for block, d in zip(ready, distances)
        ]

    cut = 1 + (2 * (n_lanes - 1) + 2) // 3
    parts = [list(range(1, cut)), list(range(cut, n_lanes))]
    parts = [part for part in parts if part]

    crossed = over_heads(encoded)
    arrived = send(parts[0]) if parts else []
    stacked, kvs = jnp.stack(crossed), []
    for i, part in enumerate(parts):
        later = parts[i + 1] if i + 1 < len(parts) else []
        next_arrived = send(later, arrived) if later else []
        encoded = encode(req, span_states, after(arrived, stacked, kvs), part[0], fanout, span_len)
        crossed = over_heads(encoded)
        kvs.append(project(after(over_rep(stacked), encoded), w_key, w_value))
        stacked = jnp.stack(after(crossed, kvs))
        arrived = next_arrived
    pieces = over_rep(stacked)

    def mix(turns, q):
        outs = attend(slot, q, kvs, pieces, w_key, w_value, n_heads, n_rep, turns, fanout, spans)
        return [outs[0]] + [
            lax.ppermute(outs[s], "rep", shift_pairs(n_rep, s)) for s in range(1, n_rep)
        ]

    width = w_out.shape[1]
    tile = min(COL_TILE, width)
    cuts = sorted({0, width // 2 // tile * tile, width - tile, width})
    mixed = mix(list(range(1, n_heads)), queries)
    received = []
    for t in range(1, n_heads):
        sent = []
        for start, stop in zip(cuts, cuts[1:]):
            partial = out_project(mixed, w_outs, t - 1, start, stop, tile)
            partial, mixed = lax.optimization_barrier((partial, mixed))
            sent.append(lax.ppermute(partial, "heads", shift_pairs(n_heads, t)))
        received.append(jnp.concatenate(sent, axis=1))
    total = out_project(mix([0], after(queries, mixed)), w_outs, 0, 0, width, tile).astype(F32)
    for part in received:
        total = total + part.astype(F32)
    return total.astype(BF16)


def solution(mesh):
    return jax.shard_map(
        shards,
        mesh=mesh,
        in_specs=(
            P(("groups", "lanes"), ("heads", "rep")),
            P(("groups", "lanes"), None),
            P(("groups", "lanes"), ("heads", "rep"), None),
            P(("groups", "lanes"), None),
            P(("groups", "lanes"), None),
            P(None, ("heads", "rep")),
            P(None, ("heads", "rep")),
            P(("heads", "rep"), None),
        ),
        out_specs=P(("groups", "lanes", "heads", "rep"), None),
        check_vma=False,
    )
```

time: 89 us -> 97.6 us (1.097)
  the two profiles are of different devices: /device:TPU:28 before, /device:TPU:0 now
where the time goes in v3:
time: 97.6 us; the launch traced here: 97.4 us
  waiting for transfers between devices  56.4 us (58%)
  Pallas kernels  23.6 us (24%)
  starting transfers between devices  12.7 us (13%)
  local copies, waits for them, and re-layouts  2.39 us (2%)
  other arithmetic  2.13 us (2%)
    ppermute x3, waiting for transfers between devices, send(): lax.ppermute(block, 'lanes', lane_pairs(n_lanes, d, True))  20.9 us
    ppermute x3, waiting for transfers between devices, shards(): sent.append(lax.ppermute(partial, 'heads', shift_pairs(n_heads, t)))  13.7 us
    ppermute x3, waiting for transfers between devices, over_heads(): lax.ppermute(array, 'heads', shift_pairs(n_heads, s))  13.2 us
    pallas_call x2, Pallas kernels, attend(): pl.pallas_call(functools.partial(attend_kernel, firsts, len(pieces), n_he...  6.8 us
    pallas_call x4, Pallas kernels, out_project(): pl.pallas_call(functools.partial(out_kernel, len(mixed)), grid=((stop - s...  6.53 us
    ppermute x3, waiting for transfers between devices, shards(): lax.ppermute(own, 'lanes', lane_pairs(n_lanes, d, False))  5.16 us
    ppermute x3, starting transfers between devices, shards(): lax.ppermute(own, 'lanes', lane_pairs(n_lanes, d, False))  4.39 us
    ppermute x3, starting transfers between devices, over_heads(): lax.ppermute(array, 'heads', shift_pairs(n_heads, s))  3.75 us
  transfers between devices with their start and end apart: 18, of which 11 were waited for; matrix products, arithmetic and copies ran while one was open for 1% of the time, Pallas kernels for 19%

profile of v3, /device:TPU:0, one launch (start us, length us, event | category | flops | bytes accessed | tf_op | source)
XLA Modules:
  0.0 97.4 jit_solution(299935465012976352)
XLA Ops:
  0.0 0.5 collective-permute-start.5
  0.5 0.7 pad_add_fusion.own_ref
  1.2 1.2 %copy-done.3 = bf16[512,896]{1,0:T(8,128)(2,1)S(1)} copy-done((bf16[512,896]{1,0:T(8,128)(2,1)S(1)}, bf16[512,896]{1,0:T(8,128)(2,1)}, u32[]{:S(2)}) %copy-start.3) | copy-done | bytes 917528
  2.3 1.2 %copy-done.5 = bf16[16,32,896]{2,1,0:T(8,128)(2,1)S(1)} copy-done((bf16[16,32,896]{2,1,0:T(8,128)(2,1)S(1)}, bf16[16,32,896]{2,1,0:T(8,128)(2,1)}, u32[]{:S(2)}) %copy-start.5) | copy-done | bytes 917528
  3.5 1.7 %encode_local.1 = (bf16[4,32,896]{2,1,0:T(8,128)(2,1)S(1)}, s32[16]{0:T(128)S(1)}, s32[16]{0:T(128)S(1)}) custom-call(s32[4,8]{1,0:T(4,128)S(1)} %pad_add_fusion.own_ref, bf16[512,896]{1,0:T(8,128)(2,1)S(1)} %copy-done.3, bf16[16,32,896]{2,1,0:T(8,128)(2,1)S(1)} %copy-done.5), custom_call_target="tpu_custom_call" | custom-call | flops 1024 | bytes 1024 | tf_op jit(solution)/shard_map/encode_local/pallas_call | solution.py:197
  5.3 0.0 copy-start.1
  5.3 0.0 copy-start.2
  5.3 2.6 %collective-permute-start = (bf16[4,32,896]{2,1,0:T(8,128)(2,1)S(1)}, bf16[4,32,896]{2,1,0:T(8,128)(2,1)S(1)}, u32[]{:S(2)}, u32[]{:S(2)}) collective-permute-start(bf16[4,32,896]{2,1,0:T(8,128)(2,1)S(1)} %get-tuple-element.40), channel_id=1, source_target_pairs={{0,2},{2,0},{1,3},{3,1},{4,6},{6,4},{5,7},{7,5},{8,10},{10,8},{9,1... | collective-permute-start | bytes 688136 | tf_op jit(solution)/shard_map/ppermute | solution.py:350
  7.8 1.6 %collective-permute-start.2 = (s32[4,8]{1,0:T(4,128)S(1)}, s32[4,8]{1,0:T(4,128)S(1)}, u32[]{:S(2)}, u32[]{:S(2)}) collective-permute-start(s32[4,8]{1,0:T(4,128)S(1)} %pad_add_fusion.own_ref), channel_id=1, source_target_pairs={{0,4},{4,0},{8,12},{12,8},{1,5},{5,1},{9,13},{13,9},{2,6},{6,2},{1... | collective-permute-start | bytes 392 | tf_op jit(solution)/shard_map/ppermute | solution.py:356
  9.4 2.6 %collective-permute-start.3 = (s32[4,8]{1,0:T(4,128)S(1)}, s32[4,8]{1,0:T(4,128)S(1)}, u32[]{:S(2)}, u32[]{:S(2)}) collective-permute-start(s32[4,8]{1,0:T(4,128)S(1)} %pad_add_fusion.own_ref), channel_id=1, source_target_pairs={{0,8},{4,12},{8,0},{12,4},{1,9},{5,13},{9,1},{13,5},{2,10},{6,14},... | collective-permute-start | bytes 392 | tf_op jit(solution)/shard_map/ppermute | solution.py:356
  12.0 0.2 collective-permute-start.4
  12.2 1.7 %collective-permute-done.3.refs_1_ = s32[4,8]{1,0:T(4,128)S(1)} collective-permute-done((s32[4,8]{1,0:T(4,128)S(1)}, s32[4,8]{1,0:T(4,128)S(1)}, u32[]{:S(2)}, u32[]{:S(2)}) %collective-permute-start.3) | collective-permute-done | bytes 160 | tf_op jit(solution)/shard_map/ppermute | solution.py:356
  13.9 3.5 %collective-permute-done.4.refs_2_ = s32[4,8]{1,0:T(4,128)S(1)} collective-permute-done((s32[4,8]{1,0:T(4,128)S(1)}, s32[4,8]{1,0:T(4,128)S(1)}, u32[]{:S(2)}, u32[]{:S(2)}) %collective-permute-start.4) | collective-permute-done | bytes 160 | tf_op jit(solution)/shard_map/ppermute | solution.py:356
  17.4 1.8 %fetch.1 = (bf16[4,32,896]{2,1,0:T(8,128)(2,1)S(1)}, bf16[4,32,896]{2,1,0:T(8,128)(2,1)S(1)}, bf16[4,32,896]{2,1,0:T(8,128)(2,1)S(1)}) custom-call(s32[4,8]{1,0:T(4,128)S(1)} %collective-permute-done.2.refs_0_, s32[4,8]{1,0:T(4,128)S(1)} %collective-permute-done.3.refs_1_, s32[4,8]{1,0:T(4,128)S(1)} %collective-permute-done.4.refs_2_, ...), custom_call_target="tpu_custom_call" | custom-call | flops 1024 | bytes 1024 | tf_op jit(solution)/shard_map/fetch/pallas_call | solution.py:80
  19.2 0.1 collective-permute-start.6
  19.3 0.8 collective-permute-start.7
  20.1 0.1 collective-permute-start.1
  20.2 7.9 %collective-permute-done.6.refs_0_ = bf16[4,32,896]{2,1,0:T(8,128)(2,1)S(1)} collective-permute-done((bf16[4,32,896]{2,1,0:T(8,128)(2,1)S(1)}, bf16[4,32,896]{2,1,0:T(8,128)(2,1)S(1)}, u32[]{:S(2)}, u32[]{:S(2)}) %collective-permute-start.6) | collective-permute-done | bytes 229408 | tf_op jit(solution)/shard_map/ppermute | solution.py:365
  28.1 3.1 %collective-permute-done.7.refs_1_ = bf16[4,32,896]{2,1,0:T(8,128)(2,1)S(1)} collective-permute-done((bf16[4,32,896]{2,1,0:T(8,128)(2,1)S(1)}, bf16[4,32,896]{2,1,0:T(8,128)(2,1)S(1)}, u32[]{:S(2)}, u32[]{:S(2)}) %collective-permute-start.7) | collective-permute-done | bytes 229408 | tf_op jit(solution)/shard_map/ppermute | solution.py:365
  31.3 1.8 %encode.2 = bf16[8,32,896]{2,1,0:T(8,128)(2,1)S(1)} custom-call(s32[16]{0:T(128)S(1)} %get-tuple-element.41.req_ref, bf16[512,896]{1,0:T(8,128)(2,1)S(1)} %copy-done.4, bf16[4,32,896]{2,1,0:T(8,128)(2,1)S(1)} %collective-permute-done.6.refs_0_, bf16[4,32,896]{2,1,0:T(8,128)(2,1)S(1)} %collective-permute-done.7.refs_1_), custom_call_target="tpu_custom_call" | custom-call | flops 1024 | bytes 1024 | tf_op jit(solution)/shard_map/encode/pallas_call | solution.py:156
  33.1 0.6 collective-permute-start.8
  33.7 1.2 %project.2.refs_0_ = bf16[4,4,32,1024]{3,2,1,0:T(8,128)(2,1)S(1)} custom-call(bf16[2,4,32,896]{3,2,1,0:T(8,128)(2,1)S(1)} %pad_maximum_fusion.1.refs_0_, bf16[2,4,32,896]{3,2,1,0:T(8,128)(2,1)S(1)} %collective-permute-done.1.refs_1_, bf16[896,512]{1,0:T(8,128)(2,1)S(1)} %copy-done.1, bf16[896,512]{1,0:T(8,128)(2,1)S(1)} %copy-done.2), custom_call_target="tpu_custom_call" | custom-call | flops 1024 | bytes 1024 | tf_op jit(solution)/shard_map/project/pallas_call | solution.py:239
  35.0 8.9 %collective-permute-done.8 = bf16[8,32,896]{2,1,0:T(8,128)(2,1)S(1)} collective-permute-done((bf16[8,32,896]{2,1,0:T(8,128)(2,1)S(1)}, bf16[8,32,896]{2,1,0:T(8,128)(2,1)S(1)}, u32[]{:S(2)}, u32[]{:S(2)}) %collective-permute-start.8) | collective-permute-done | bytes 458784 | tf_op jit(solution)/shard_map/ppermute | solution.py:350
  43.9 0.1 pad_maximum_fusion.refs_0_
  44.0 0.1 collective-permute-start.9
  44.1 0.1 collective-permute-start.10
  44.2 9.8 %collective-permute-done.10.refs_0_ = bf16[4,32,896]{2,1,0:T(8,128)(2,1)S(1)} collective-permute-done((bf16[4,32,896]{2,1,0:T(8,128)(2,1)S(1)}, bf16[4,32,896]{2,1,0:T(8,128)(2,1)S(1)}, u32[]{:S(2)}, u32[]{:S(2)}) %collective-permute-start.10) | collective-permute-done | bytes 229408 | tf_op jit(solution)/shard_map/ppermute | solution.py:365
  54.0 1.3 %encode.3 = bf16[4,32,896]{2,1,0:T(8,128)(2,1)S(1)} custom-call(s32[16]{0:T(128)S(1)} %get-tuple-element.41.req_ref, bf16[512,896]{1,0:T(8,128)(2,1)S(1)} %copy-done.4, bf16[4,32,896]{2,1,0:T(8,128)(2,1)S(1)} %collective-permute-done.10.refs_0_), custom_call_target="tpu_custom_call" | custom-call | flops 1024 | bytes 1024 | tf_op jit(solution)/shard_map/encode/pallas_call | solution.py:156
  55.3 0.6 collective-permute-start.11
  55.9 2.3 %project.3.refs_1_ = bf16[8,4,32,1024]{3,2,1,0:T(8,128)(2,1)S(1)} custom-call(bf16[2,8,32,896]{3,2,1,0:T(8,128)(2,1)S(1)} %pad_maximum_fusion.refs_0_, bf16[2,8,32,896]{3,2,1,0:T(8,128)(2,1)S(1)} %collective-permute-done.9.refs_1_, bf16[896,512]{1,0:T(8,128)(2,1)S(1)} %copy-done.1, bf16[896,512]{1,0:T(8,128)(2,1)S(1)} %copy-done.2), custom_call_target="tpu_custom_call" | custom-call | flops 1024 | bytes 1024 | tf_op jit(solution)/shard_map/project/pallas_call | solution.py:239
  58.2 4.2 %collective-permute-done.11 = bf16[4,32,896]{2,1,0:T(8,128)(2,1)S(1)} collective-permute-done((bf16[4,32,896]{2,1,0:T(8,128)(2,1)S(1)}, bf16[4,32,896]{2,1,0:T(8,128)(2,1)S(1)}, u32[]{:S(2)}, u32[]{:S(2)}) %collective-permute-start.11) | collective-permute-done | bytes 229408 | tf_op jit(solution)/shard_map/ppermute | solution.py:350
  62.5 0.1 collective-permute-start.12
  62.6 1.8 %collective-permute-done.12.refs_3_ = bf16[2,4,32,896]{3,2,1,0:T(8,128)(2,1)S(1)} collective-permute-done((bf16[2,4,32,896]{3,2,1,0:T(8,128)(2,1)S(1)}, bf16[2,4,32,896]{3,2,1,0:T(8,128)(2,1)S(1)}, u32[]{:S(2)}, u32[]{:S(2)}) %collective-permute-start.12) | collective-permute-done | bytes 458784 | tf_op jit(solution)/shard_map/ppermute | solution.py:353
  64.4 3.4 %attend.3 = (bf16[1,128,512]{2,1,0:T(8,128)(2,1)S(1)}, bf16[1,128,512]{2,1,0:T(8,128)(2,1)S(1)}) custom-call(s32[16]{0:T(128)S(1)} %get-tuple-element.39.slot_ref, bf16[512,512]{1,0:T(8,128)(2,1)S(1)} %copy-done.7, bf16[4,4,32,1024]{3,2,1,0:T(8,128)(2,1)S(1)} %project.2.refs_0_, bf16[8,4,32,1024]{3,2,1,0:T(8,128)(2,1)S(1)} %project.3.refs_1_, ...), custom_call_target="tpu_custom_call" | custom-call | flops 1024 | bytes 1024 | tf_op jit(solution)/shard_map/attend/pallas_call | solution.py:305
  67.8 0.2 collective-permute-start.14
  68.0 1.2 %collective-permute-done.14.refs_1_ = bf16[1,128,512]{2,1,0:T(8,128)(2,1)S(1)} collective-permute-done((bf16[1,128,512]{2,1,0:T(8,128)(2,1)S(1)}, bf16[1,128,512]{2,1,0:T(8,128)(2,1)S(1)}, u32[]{:S(2)}, u32[]{:S(2)}) %collective-permute-start.14) | collective-permute-done | bytes 131104 | tf_op jit(solution)/shard_map/ppermute | solution.py:389
  69.2 1.7 %out_project.5 = bf16[128,2048]{1,0:T(8,128)(2,1)S(1)} custom-call(bf16[1,128,512]{2,1,0:T(8,128)(2,1)S(1)} %get-tuple-element.70.refs_0_, bf16[1,128,512]{2,1,0:T(8,128)(2,1)S(1)} %collective-permute-done.14.refs_1_, bf16[512,4096]{1,0:T(8,128)(2,1)S(1)} %copy-done, bf16[512,4096]{1,0:T(8,128)(2,1)S(1)} %collective-permute-done.5.refs_3_), custom_call_target="tpu_custom_call" | custom-call | flops 1024 | bytes 1024 | tf_op jit(solution)/shard_map/out_project/pallas_call | solution.py:325
  70.9 0.6 collective-permute-start.15
  71.5 1.3 %out_project.6 = bf16[128,1536]{1,0:T(8,128)(2,1)S(1)} custom-call(bf16[1,128,512]{2,1,0:T(8,128)(2,1)S(1)} %get-tuple-element.70.refs_0_, bf16[1,128,512]{2,1,0:T(8,128)(2,1)S(1)} %collective-permute-done.14.refs_1_, bf16[512,4096]{1,0:T(8,128)(2,1)S(1)} %copy-done, bf16[512,4096]{1,0:T(8,128)(2,1)S(1)} %collective-permute-done.5.refs_3_), custom_call_target="tpu_custom_call" | custom-call | flops 1024 | bytes 1024 | tf_op jit(solution)/shard_map/out_project/pallas_call | solution.py:325
  72.8 1.6 %collective-permute-start.16 = (bf16[128,1536]{1,0:T(8,128)(2,1)S(1)}, bf16[128,1536]{1,0:T(8,128)(2,1)S(1)}, u32[]{:S(2)}, u32[]{:S(2)}) collective-permute-start(bf16[128,1536]{1,0:T(8,128)(2,1)S(1)} %out_project.6), channel_id=1, source_target_pairs={{0,2},{2,0},{1,3},{3,1},{4,6},{6,4},{5,7},{7,5},{8,10},{10,8},{9,1... | collective-permute-start | bytes 1179656 | tf_op jit(solution)/shard_map/ppermute | solution.py:402
  74.3 3.4 %attend.2 = (bf16[1,128,512]{2,1,0:T(8,128)(2,1)S(1)}, bf16[1,128,512]{2,1,0:T(8,128)(2,1)S(1)}) custom-call(s32[16]{0:T(128)S(1)} %get-tuple-element.39.slot_ref, bf16[512,512]{1,0:T(8,128)(2,1)S(1)} %copy-done.7, bf16[4,4,32,1024]{3,2,1,0:T(8,128)(2,1)S(1)} %project.2.refs_0_, bf16[8,4,32,1024]{3,2,1,0:T(8,128)(2,1)S(1)} %project.3.refs_1_, ...), custom_call_target="tpu_custom_call" | custom-call | flops 1024 | bytes 1024 | tf_op jit(solution)/shard_map/attend/pallas_call | solution.py:305
  77.7 0.1 collective-permute-start.13
  77.8 0.3 out_project.7
  78.1 0.6 collective-permute-start.17
  78.7 0.4 collective-permute-done.13.refs_1_
  79.2 3.3 %out_project.4 = bf16[128,4096]{1,0:T(8,128)(2,1)S(1)} custom-call(bf16[1,128,512]{2,1,0:T(8,128)(2,1)S(1)} %get-tuple-element.62.refs_0_, bf16[1,128,512]{2,1,0:T(8,128)(2,1)S(1)} %collective-permute-done.13.refs_1_, bf16[512,4096]{1,0:T(8,128)(2,1)S(1)} %copy-done, bf16[512,4096]{1,0:T(8,128)(2,1)S(1)} %collective-permute-done.5.refs_3_), custom_call_target="tpu_custom_call" | custom-call | flops 1024 | bytes 1024 | tf_op jit(solution)/shard_map/out_project/pallas_call | solution.py:325
  82.4 13.7 %collective-permute-done.17 = bf16[128,512]{1,0:T(8,128)(2,1)S(1)} collective-permute-done((bf16[128,512]{1,0:T(8,128)(2,1)S(1)}, bf16[128,512]{1,0:T(8,128)(2,1)S(1)}, u32[]{:S(2)}, u32[]{:S(2)}) %collective-permute-start.17) | collective-permute-done | bytes 131104 | tf_op jit(solution)/shard_map/ppermute | solution.py:402
  96.2 1.2 %add_convert_fusion = bf16[128,4096]{1,0:T(8,128)(2,1)} fusion(bf16[128,4096]{1,0:T(8,128)(2,1)S(1)} %out_project.4, bf16[128,512]{1,0:T(8,128)(2,1)S(1)} %collective-permute-done.17, bf16[128,1536]{1,0:T(8,128)(2,1)S(1)} %collective-permute-done.16, bf16[128,2048]{1,0:T(8,128)(2,1)S(1)} %collective-permute-done.15), kind=kLoop, calls=%fused_computation | loop fusion | flops 4718592 | bytes 3145728 | tf_op jit(solution)/shard_map/convert_element_type | solution.py:407
  (21 shorter events, 0.1 us)
Async XLA Ops:
  0.0 17.4 %collective-permute-start.5 = (bf16[512,4096]{1,0:T(8,128)(2,1)}, bf16[512,4096]{1,0:T(8,128)(2,1)S(1)}, u32[]{:S(2)}, u32[]{:S(2)}) collective-permute-start(bf16[512,4096]{1,0:T(8,128)(2,1)} %refs_2_.11), channel_id=1, source_target_pairs={{0,1},{1,0},{2,3},{3,2},{4,5},{5,4},{6,7},{7,6},{8,9},{9,8},{10,11... | collective-permute-start | bytes 12582920 | tf_op jit(solution)/shard_map/ppermute | solution.py:353
  1.2 1.2 %copy-start.3 = (bf16[512,896]{1,0:T(8,128)(2,1)S(1)}, bf16[512,896]{1,0:T(8,128)(2,1)}, u32[]{:S(2)}) copy-start(bf16[512,896]{1,0:T(8,128)(2,1)} %states_ref.5) | copy-start | bytes 2752516
  2.3 1.2 %copy-start.5 = (bf16[16,32,896]{2,1,0:T(8,128)(2,1)S(1)}, bf16[16,32,896]{2,1,0:T(8,128)(2,1)}, u32[]{:S(2)}) copy-start(bf16[16,32,896]{2,1,0:T(8,128)(2,1)} %refs_3_.3) | copy-start | bytes 2752516
  3.5 13.9 %copy-start.6 = (bf16[16,32,896]{2,1,0:T(8,128)(2,1)S(1)}, bf16[16,32,896]{2,1,0:T(8,128)(2,1)}, u32[]{:S(2)}) copy-start(bf16[16,32,896]{2,1,0:T(8,128)(2,1)} %refs_3_.3) | copy-start | bytes 2752516
  3.5 27.7 %copy-start.4 = (bf16[512,896]{1,0:T(8,128)(2,1)S(1)}, bf16[512,896]{1,0:T(8,128)(2,1)}, u32[]{:S(2)}) copy-start(bf16[512,896]{1,0:T(8,128)(2,1)} %states_ref.5) | copy-start | bytes 2752516
  5.3 28.4 %copy-start.1 = (bf16[896,512]{1,0:T(8,128)(2,1)S(1)}, bf16[896,512]{1,0:T(8,128)(2,1)}, u32[]{:S(2)}) copy-start(bf16[896,512]{1,0:T(8,128)(2,1)} %refs_4_.3) | copy-start | bytes 2752516
  5.3 28.4 %copy-start.2 = (bf16[896,512]{1,0:T(8,128)(2,1)S(1)}, bf16[896,512]{1,0:T(8,128)(2,1)}, u32[]{:S(2)}) copy-start(bf16[896,512]{1,0:T(8,128)(2,1)} %refs_5_.3) | copy-start | bytes 2752516
  5.3 14.8 %collective-permute-start = (bf16[4,32,896]{2,1,0:T(8,128)(2,1)S(1)}, bf16[4,32,896]{2,1,0:T(8,128)(2,1)S(1)}, u32[]{:S(2)}, u32[]{:S(2)}) collective-permute-start(bf16[4,32,896]{2,1,0:T(8,128)(2,1)S(1)} %get-tuple-element.40), channel_id=1, source_target_pairs={{0,2},{2,0},{1,3},{3,1},{4,6},{6,4},{5,7},{7,5},{8,10},{10,8},{9,1... | collective-permute-start | bytes 688136 | tf_op jit(solution)/shard_map/ppermute | solution.py:350
  7.8 4.4 %collective-permute-start.2 = (s32[4,8]{1,0:T(4,128)S(1)}, s32[4,8]{1,0:T(4,128)S(1)}, u32[]{:S(2)}, u32[]{:S(2)}) collective-permute-start(s32[4,8]{1,0:T(4,128)S(1)} %pad_add_fusion.own_ref), channel_id=1, source_target_pairs={{0,4},{4,0},{8,12},{12,8},{1,5},{5,1},{9,13},{13,9},{2,6},{6,2},{1... | collective-permute-start | bytes 392 | tf_op jit(solution)/shard_map/ppermute | solution.py:356
  9.4 4.5 %collective-permute-start.3 = (s32[4,8]{1,0:T(4,128)S(1)}, s32[4,8]{1,0:T(4,128)S(1)}, u32[]{:S(2)}, u32[]{:S(2)}) collective-permute-start(s32[4,8]{1,0:T(4,128)S(1)} %pad_add_fusion.own_ref), channel_id=1, source_target_pairs={{0,8},{4,12},{8,0},{12,4},{1,9},{5,13},{9,1},{13,5},{2,10},{6,14},... | collective-permute-start | bytes 392 | tf_op jit(solution)/shard_map/ppermute | solution.py:356
  12.0 5.4 %collective-permute-start.4 = (s32[4,8]{1,0:T(4,128)S(1)}, s32[4,8]{1,0:T(4,128)S(1)}, u32[]{:S(2)}, u32[]{:S(2)}) collective-permute-start(s32[4,8]{1,0:T(4,128)S(1)} %pad_add_fusion.own_ref), channel_id=1, source_target_pairs={{0,12},{4,8},{8,4},{12,0},{1,13},{5,9},{9,5},{13,1},{2,14},{6,10},... | collective-permute-start | bytes 392 | tf_op jit(solution)/shard_map/ppermute | solution.py:356
  19.2 8.9 %collective-permute-start.6 = (bf16[4,32,896]{2,1,0:T(8,128)(2,1)S(1)}, bf16[4,32,896]{2,1,0:T(8,128)(2,1)S(1)}, u32[]{:S(2)}, u32[]{:S(2)}) collective-permute-start(bf16[4,32,896]{2,1,0:T(8,128)(2,1)S(1)} %get-tuple-element.47), channel_id=1, source_target_pairs={{0,4},{4,0},{8,12},{12,8},{1,5},{5,1},{9,13},{13,9},{2,6},{6,2},{1... | collective-permute-start | bytes 688136 | tf_op jit(solution)/shard_map/ppermute | solution.py:365
  19.3 12.0 %collective-permute-start.7 = (bf16[4,32,896]{2,1,0:T(8,128)(2,1)S(1)}, bf16[4,32,896]{2,1,0:T(8,128)(2,1)S(1)}, u32[]{:S(2)}, u32[]{:S(2)}) collective-permute-start(bf16[4,32,896]{2,1,0:T(8,128)(2,1)S(1)} %get-tuple-element.48), channel_id=1, source_target_pairs={{0,8},{4,12},{8,0},{12,4},{1,9},{5,13},{9,1},{13,5},{2,10},{6,14},... | collective-permute-start | bytes 688136 | tf_op jit(solution)/shard_map/ppermute | solution.py:365
  20.1 13.6 %collective-permute-start.1 = (bf16[2,4,32,896]{3,2,1,0:T(8,128)(2,1)S(1)}, bf16[2,4,32,896]{3,2,1,0:T(8,128)(2,1)S(1)}, u32[]{:S(2)}, u32[]{:S(2)}) collective-permute-start(bf16[2,4,32,896]{3,2,1,0:T(8,128)(2,1)S(1)} %pad_maximum_fusion.1.refs_0_), channel_id=1, source_target_pairs={{0,1},{1,0},{2,3},{3,2},{4,5},{5,4},{6,7},{7,6},{8,9},{9,8},{10,11... | collective-permute-start | bytes 1376264 | tf_op jit(solution)/shard_map/ppermute | solution.py:353
  33.1 10.8 %collective-permute-start.8 = (bf16[8,32,896]{2,1,0:T(8,128)(2,1)S(1)}, bf16[8,32,896]{2,1,0:T(8,128)(2,1)S(1)}, u32[]{:S(2)}, u32[]{:S(2)}) collective-permute-start(bf16[8,32,896]{2,1,0:T(8,128)(2,1)S(1)} %encode.2), channel_id=1, source_target_pairs={{0,2},{2,0},{1,3},{3,1},{4,6},{6,4},{5,7},{7,5},{8,10},{10,8},{9,1... | collective-permute-start | bytes 1376264 | tf_op jit(solution)/shard_map/ppermute | solution.py:350
  44.0 11.9 %collective-permute-start.9 = (bf16[2,8,32,896]{3,2,1,0:T(8,128)(2,1)S(1)}, bf16[2,8,32,896]{3,2,1,0:T(8,128)(2,1)S(1)}, u32[]{:S(2)}, u32[]{:S(2)}) collective-permute-start(bf16[2,8,32,896]{3,2,1,0:T(8,128)(2,1)S(1)} %pad_maximum_fusion.refs_0_), channel_id=1, source_target_pairs={{0,1},{1,0},{2,3},{3,2},{4,5},{5,4},{6,7},{7,6},{8,9},{9,8},{10,11... | collective-permute-start | bytes 2752520 | tf_op jit(solution)/shard_map/ppermute | solution.py:353
  44.1 9.9 %collective-permute-start.10 = (bf16[4,32,896]{2,1,0:T(8,128)(2,1)S(1)}, bf16[4,32,896]{2,1,0:T(8,128)(2,1)S(1)}, u32[]{:S(2)}, u32[]{:S(2)}) collective-permute-start(bf16[4,32,896]{2,1,0:T(8,128)(2,1)S(1)} %get-tuple-element.56), channel_id=1, source_target_pairs={{0,12},{4,8},{8,4},{12,0},{1,13},{5,9},{9,5},{13,1},{2,14},{6,10},... | collective-permute-start | bytes 688136 | tf_op jit(solution)/shard_map/ppermute | solution.py:365
  55.3 9.1 %copy-start.7 = (bf16[512,512]{1,0:T(8,128)(2,1)S(1)}, bf16[512,512]{1,0:T(8,128)(2,1)}, u32[]{:S(2)}) copy-start(bf16[512,512]{1,0:T(8,128)(2,1)} %q_ref.2) | copy-start | bytes 1572868
  55.3 7.2 %collective-permute-start.11 = (bf16[4,32,896]{2,1,0:T(8,128)(2,1)S(1)}, bf16[4,32,896]{2,1,0:T(8,128)(2,1)S(1)}, u32[]{:S(2)}, u32[]{:S(2)}) collective-permute-start(bf16[4,32,896]{2,1,0:T(8,128)(2,1)S(1)} %encode.3), channel_id=1, source_target_pairs={{0,2},{2,0},{1,3},{3,1},{4,6},{6,4},{5,7},{7,5},{8,10},{10,8},{9,1... | collective-permute-start | bytes 688136 | tf_op jit(solution)/shard_map/ppermute | solution.py:350
  62.5 1.9 %collective-permute-start.12 = (bf16[2,4,32,896]{3,2,1,0:T(8,128)(2,1)S(1)}, bf16[2,4,32,896]{3,2,1,0:T(8,128)(2,1)S(1)}, u32[]{:S(2)}, u32[]{:S(2)}) collective-permute-start(bf16[2,4,32,896]{3,2,1,0:T(8,128)(2,1)S(1)} %pad_maximum_fusion.2.refs_2_), channel_id=1, source_target_pairs={{0,1},{1,0},{2,3},{3,2},{4,5},{5,4},{6,7},{7,6},{8,9},{9,8},{10,11... | collective-permute-start | bytes 1376264 | tf_op jit(solution)/shard_map/ppermute | solution.py:353
  64.4 4.8 %copy-start = (bf16[512,4096]{1,0:T(8,128)(2,1)S(1)}, bf16[512,4096]{1,0:T(8,128)(2,1)}, u32[]{:S(2)}) copy-start(bf16[512,4096]{1,0:T(8,128)(2,1)} %refs_2_.11) | copy-start | bytes 12582916
  67.8 1.4 %collective-permute-start.14 = (bf16[1,128,512]{2,1,0:T(8,128)(2,1)S(1)}, bf16[1,128,512]{2,1,0:T(8,128)(2,1)S(1)}, u32[]{:S(2)}, u32[]{:S(2)}) collective-permute-start(bf16[1,128,512]{2,1,0:T(8,128)(2,1)S(1)} %get-tuple-element.65), channel_id=1, source_target_pairs={{0,1},{1,0},{2,3},{3,2},{4,5},{5,4},{6,7},{7,6},{8,9},{9,8},{10,11... | collective-permute-start | bytes 393224 | tf_op jit(solution)/shard_map/ppermute | solution.py:389
  70.9 25.3 %collective-permute-start.15 = (bf16[128,2048]{1,0:T(8,128)(2,1)S(1)}, bf16[128,2048]{1,0:T(8,128)(2,1)S(1)}, u32[]{:S(2)}, u32[]{:S(2)}) collective-permute-start(bf16[128,2048]{1,0:T(8,128)(2,1)S(1)} %out_project.5), channel_id=1, source_target_pairs={{0,2},{2,0},{1,3},{3,1},{4,6},{6,4},{5,7},{7,5},{8,10},{10,8},{9,1... | collective-permute-start | bytes 1572872 | tf_op jit(solution)/shard_map/ppermute | solution.py:402
  72.8 23.4 %collective-permute-start.16 = (bf16[128,1536]{1,0:T(8,128)(2,1)S(1)}, bf16[128,1536]{1,0:T(8,128)(2,1)S(1)}, u32[]{:S(2)}, u32[]{:S(2)}) collective-permute-start(bf16[128,1536]{1,0:T(8,128)(2,1)S(1)} %out_project.6), channel_id=1, source_target_pairs={{0,2},{2,0},{1,3},{3,1},{4,6},{6,4},{5,7},{7,5},{8,10},{10,8},{9,1... | collective-permute-start | bytes 1179656 | tf_op jit(solution)/shard_map/ppermute | solution.py:402
  77.7 1.4 %collective-permute-start.13 = (bf16[1,128,512]{2,1,0:T(8,128)(2,1)S(1)}, bf16[1,128,512]{2,1,0:T(8,128)(2,1)S(1)}, u32[]{:S(2)}, u32[]{:S(2)}) collective-permute-start(bf16[1,128,512]{2,1,0:T(8,128)(2,1)S(1)} %get-tuple-element.63), channel_id=1, source_target_pairs={{0,1},{1,0},{2,3},{3,2},{4,5},{5,4},{6,7},{7,6},{8,9},{9,8},{10,11... | collective-permute-start | bytes 393224 | tf_op jit(solution)/shard_map/ppermute | solution.py:389
  78.1 18.0 %collective-permute-start.17 = (bf16[128,512]{1,0:T(8,128)(2,1)S(1)}, bf16[128,512]{1,0:T(8,128)(2,1)S(1)}, u32[]{:S(2)}, u32[]{:S(2)}) collective-permute-start(bf16[128,512]{1,0:T(8,128)(2,1)S(1)} %out_project.7), channel_id=1, source_target_pairs={{0,2},{2,0},{1,3},{3,1},{4,6},{6,4},{5,7},{7,5},{8,10},{10,8},{9,1... | collective-permute-start | bytes 393224 | tf_op jit(solution)/shard_map/ppermute | solution.py:402

commit v4 on v3

--- a/solution.py
+++ b/solution.py
@@ -22,7 +22,8 @@
     return pltpu.CompilerParams(vmem_limit_bytes=mib * 2**20)
 
 
-SMALL = pl.CostEstimate(flops=1024, bytes_accessed=1024, transcendentals=0)
+def cost(gflops):
+    return pl.CostEstimate(flops=int(gflops * 10**9), bytes_accessed=1024, transcendentals=0)
 
 
 def apart(n, a, b):
@@ -87,7 +88,7 @@
             pltpu.SemaphoreType.DMA((others * cap,)),
         ],
         compiler_params=params(16),
-        cost_estimate=SMALL,
+        cost_estimate=cost(10),
         name="fetch",
     )(*asked, store)
 
@@ -159,7 +160,7 @@
         in_specs=[SMEM, VMEM] + [VMEM] * len(blocks),
         out_specs=VMEM,
         compiler_params=params(16),
-        cost_estimate=SMALL,
+        cost_estimate=cost(10),
         name="encode",
     )(req, span_states, *blocks)
 
@@ -210,7 +211,7 @@
             pltpu.SemaphoreType.DMA((cap,)),
         ],
         compiler_params=params(16),
-        cost_estimate=SMALL,
+        cost_estimate=cost(10),
         name="encode_local",
     )(own, span_states, store)
 
@@ -242,7 +243,7 @@
         in_specs=[VMEM] * (len(pieces) + 2),
         out_specs=VMEM,
         compiler_params=params(32),
-        cost_estimate=SMALL,
+        cost_estimate=cost(0.1),
         name="project",
     )(*pieces, w_key, w_value)
 
@@ -309,7 +310,7 @@
         out_specs=[VMEM] * n_rep,
         scratch_shapes=[pltpu.VMEM(kv_shape, BF16), pltpu.SemaphoreType.DMA((max(1, len(ready)),))],
         compiler_params=params(40),
-        cost_estimate=SMALL,
+        cost_estimate=cost(0.001),
         name="attend",
     )(slot, queries, *ready, *pieces, w_key, w_value)
 
@@ -330,7 +331,7 @@
         + [pl.BlockSpec((depth, tile), lambda j: (0, base + j))] * len(mixed),
         out_specs=pl.BlockSpec((rows, tile), lambda j: (0, j)),
         compiler_params=params(16),
-        cost_estimate=SMALL,
+        cost_estimate=cost(0.001),
         name="out_project",
     )(*mixed, *weights)
 
@@ -372,16 +373,16 @@
 
     crossed = over_heads(encoded)
     arrived = send(parts[0]) if parts else []
-    stacked, kvs = jnp.stack(crossed), []
+    stacked, kvs = jnp.stack(after(crossed, blocks[1:])), []
     for i, part in enumerate(parts):
         later = parts[i + 1] if i + 1 < len(parts) else []
         next_arrived = send(later, arrived) if later else []
         encoded = encode(req, span_states, after(arrived, stacked, kvs), part[0], fanout, span_len)
-        crossed = over_heads(encoded)
+        if i:
+            stacked = jnp.stack(after(crossed, encoded))
         kvs.append(project(after(over_rep(stacked), encoded), w_key, w_value))
-        stacked = jnp.stack(after(crossed, kvs))
-        arrived = next_arrived
-    pieces = over_rep(stacked)
+        crossed, arrived = over_heads(encoded), next_arrived
+    pieces = over_rep(jnp.stack(after(crossed, kvs)) if parts else stacked)
 
     def mix(turns, q):
         outs = attend(slot, q, kvs, pieces, w_key, w_value, n_heads, n_rep, turns, fanout, spans)
@@ -393,15 +394,16 @@
     tile = min(COL_TILE, width)
     cuts = sorted({0, width // 2 // tile * tile, width - tile, width})
     mixed = mix(list(range(1, n_heads)), queries)
-    received = []
+    received, partials = [], []
     for t in range(1, n_heads):
         sent = []
         for start, stop in zip(cuts, cuts[1:]):
             partial = out_project(mixed, w_outs, t - 1, start, stop, tile)
             partial, mixed = lax.optimization_barrier((partial, mixed))
+            partials.append(partial)
             sent.append(lax.ppermute(partial, "heads", shift_pairs(n_heads, t)))
         received.append(jnp.concatenate(sent, axis=1))
-    total = out_project(mix([0], after(queries, mixed)), w_outs, 0, 0, width, tile).astype(F32)
+    total = out_project(mix([0], after(queries, partials)), w_outs, 0, 0, width, tile).astype(F32)
     for part in received:
         total = total + part.astype(F32)
     return total.astype(BF16)

time: 97.6 us -> 86.7 us (0.89)
  waiting for transfers between devices: 56.4 us -> 39.6 us
  starting transfers between devices: 12.7 us -> 18.6 us
    ppermute x3, waiting for transfers between devices: 20.9 us -> 11.3 us  [send(): lax.ppermute(block, 'lanes', lane_pairs(n_lanes, d, True))]
    ppermute x3, starting transfers between devices: 0.91 us -> 6.77 us  [send(): lax.ppermute(block, 'lanes', lane_pairs(n_lanes, d, True))]
    ppermute x3, waiting for transfers between devices: 5.16 us -> 0.01 us  [shards(): lax.ppermute(own, 'lanes', lane_pairs(n_lanes, d, False))]
    ppermute x3, waiting for transfers between devices: 13.2 us -> 9.27 us  [over_heads(): lax.ppermute(array, 'heads', shift_pairs(n_heads, s))]
    ppermute x4, waiting for transfers between devices: 1.81 us -> 3.67 us  [over_rep(): lax.ppermute(array, 'rep', shift_pairs(n_rep, s))]
  transfers between devices with their start and end apart: 18 -> 18, of which waited for: 11 -> 10; matrix products, arithmetic and copies ran while one was open for 1% -> 1% of each run, Pallas kernels for 19% -> 21%
where the time goes in v4:
time: 86.7 us; the launch traced here: 86.5 us
  waiting for transfers between devices  39.6 us (46%)
  Pallas kernels  23.6 us (27%)
  starting transfers between devices  18.6 us (21%)
  local copies, waits for them, and re-layouts  2.39 us (3%)
  other arithmetic  2.12 us (2%)
    ppermute x3, waiting for transfers between devices, shards(): sent.append(lax.ppermute(partial, 'heads', shift_pairs(n_heads, t)))  13.4 us
    ppermute x3, waiting for transfers between devices, send(): lax.ppermute(block, 'lanes', lane_pairs(n_lanes, d, True))  11.3 us
    ppermute x3, waiting for transfers between devices, over_heads(): lax.ppermute(array, 'heads', shift_pairs(n_heads, s))  9.27 us
    pallas_call x2, Pallas kernels, attend(): pl.pallas_call(functools.partial(attend_kernel, firsts, len(pieces), n_he...  6.8 us
    ppermute x3, starting transfers between devices, send(): lax.ppermute(block, 'lanes', lane_pairs(n_lanes, d, True))  6.77 us
    pallas_call x4, Pallas kernels, out_project(): pl.pallas_call(functools.partial(out_kernel, len(mixed)), grid=((stop - s...  6.54 us
    ppermute x3, starting transfers between devices, shards(): lax.ppermute(own, 'lanes', lane_pairs(n_lanes, d, False))  5.17 us
    ppermute x4, waiting for transfers between devices, over_rep(): lax.ppermute(array, 'rep', shift_pairs(n_rep, s))  3.67 us
  transfers between devices with their start and end apart: 18, of which 10 were waited for; matrix products, arithmetic and copies ran while one was open for 1% of the time, Pallas kernels for 21%

profile of v4, /device:TPU:0, one launch (start us, length us, event | category | flops | bytes accessed | tf_op | source)
XLA Modules:
  0.0 86.5 jit_solution(12659384943965893002)
XLA Ops:
  0.0 0.5 collective-permute-start.4
  0.5 0.7 pad_add_fusion.own_ref
  1.2 2.6 %collective-permute-start.1 = (s32[4,8]{1,0:T(4,128)S(1)}, s32[4,8]{1,0:T(4,128)S(1)}, u32[]{:S(2)}, u32[]{:S(2)}) collective-permute-start(s32[4,8]{1,0:T(4,128)S(1)} %pad_add_fusion.own_ref), channel_id=1, source_target_pairs={{0,4},{4,0},{8,12},{12,8},{1,5},{5,1},{9,13},{13,9},{2,6},{6,2},{1... | collective-permute-start | bytes 392 | tf_op jit(solution)/shard_map/ppermute | solution.py:357
  3.7 2.6 %collective-permute-start.2 = (s32[4,8]{1,0:T(4,128)S(1)}, s32[4,8]{1,0:T(4,128)S(1)}, u32[]{:S(2)}, u32[]{:S(2)}) collective-permute-start(s32[4,8]{1,0:T(4,128)S(1)} %pad_add_fusion.own_ref), channel_id=1, source_target_pairs={{0,8},{4,12},{8,0},{12,4},{1,9},{5,13},{9,1},{13,5},{2,10},{6,14},... | collective-permute-start | bytes 392 | tf_op jit(solution)/shard_map/ppermute | solution.py:357
  6.3 1.2 %copy-done.4 = bf16[16,32,896]{2,1,0:T(8,128)(2,1)S(1)} copy-done((bf16[16,32,896]{2,1,0:T(8,128)(2,1)S(1)}, bf16[16,32,896]{2,1,0:T(8,128)(2,1)}, u32[]{:S(2)}) %copy-start.4) | copy-done | bytes 917528
  7.5 1.2 %copy-done.6 = bf16[512,896]{1,0:T(8,128)(2,1)S(1)} copy-done((bf16[512,896]{1,0:T(8,128)(2,1)S(1)}, bf16[512,896]{1,0:T(8,128)(2,1)}, u32[]{:S(2)}) %copy-start.6) | copy-done | bytes 917528
  8.7 1.7 %encode_local.1 = (bf16[4,32,896]{2,1,0:T(8,128)(2,1)S(1)}, s32[16]{0:T(128)S(1)}, s32[16]{0:T(128)S(1)}) custom-call(s32[4,8]{1,0:T(4,128)S(1)} %pad_add_fusion.own_ref, bf16[512,896]{1,0:T(8,128)(2,1)S(1)} %copy-done.6, bf16[16,32,896]{2,1,0:T(8,128)(2,1)S(1)} %copy-done.4), custom_call_target="tpu_custom_call" | custom-call | flops 10000000000 | bytes 1024 | tf_op jit(solution)/shard_map/encode_local/pallas_call | solution.py:198
  10.4 1.8 %collective-permute-start = (bf16[4,32,896]{2,1,0:T(8,128)(2,1)S(1)}, bf16[4,32,896]{2,1,0:T(8,128)(2,1)S(1)}, u32[]{:S(2)}, u32[]{:S(2)}) collective-permute-start(bf16[4,32,896]{2,1,0:T(8,128)(2,1)S(1)} %get-tuple-element.51), channel_id=1, source_target_pairs={{0,2},{2,0},{1,3},{3,1},{4,6},{6,4},{5,7},{7,5},{8,10},{10,8},{9,1... | collective-permute-start | bytes 688136 | tf_op jit(solution)/shard_map/ppermute | solution.py:351
  12.2 1.8 %fetch.1 = (bf16[4,32,896]{2,1,0:T(8,128)(2,1)S(1)}, bf16[4,32,896]{2,1,0:T(8,128)(2,1)S(1)}, bf16[4,32,896]{2,1,0:T(8,128)(2,1)S(1)}) custom-call(s32[4,8]{1,0:T(4,128)S(1)} %collective-permute-done.1.refs_0_, s32[4,8]{1,0:T(4,128)S(1)} %collective-permute-done.2.refs_1_, s32[4,8]{1,0:T(4,128)S(1)} %collective-permute-done.3.refs_2_, ...), custom_call_target="tpu_custom_call" | custom-call | flops 10000000000 | bytes 1024 | tf_op jit(solution)/shard_map/fetch/pallas_call | solution.py:81
  14.1 0.7 collective-permute-start.6
  14.8 3.5 %collective-permute-start.7 = (bf16[4,32,896]{2,1,0:T(8,128)(2,1)S(1)}, bf16[4,32,896]{2,1,0:T(8,128)(2,1)S(1)}, u32[]{:S(2)}, u32[]{:S(2)}) collective-permute-start(bf16[4,32,896]{2,1,0:T(8,128)(2,1)S(1)} %get-tuple-element.54), channel_id=1, source_target_pairs={{0,8},{4,12},{8,0},{12,4},{1,9},{5,13},{9,1},{13,5},{2,10},{6,14},... | collective-permute-start | bytes 688136 | tf_op jit(solution)/shard_map/ppermute | solution.py:366
  18.3 0.0 copy-start.1
  18.4 0.0 copy-start.2
  18.4 0.1 collective-permute-start.5
  18.4 7.3 %collective-permute-done.6.refs_0_ = bf16[4,32,896]{2,1,0:T(8,128)(2,1)S(1)} collective-permute-done((bf16[4,32,896]{2,1,0:T(8,128)(2,1)S(1)}, bf16[4,32,896]{2,1,0:T(8,128)(2,1)S(1)}, u32[]{:S(2)}, u32[]{:S(2)}) %collective-permute-start.6) | collective-permute-done | bytes 229408 | tf_op jit(solution)/shard_map/ppermute | solution.py:366
  25.8 2.4 %collective-permute-done.7.refs_1_ = bf16[4,32,896]{2,1,0:T(8,128)(2,1)S(1)} collective-permute-done((bf16[4,32,896]{2,1,0:T(8,128)(2,1)S(1)}, bf16[4,32,896]{2,1,0:T(8,128)(2,1)S(1)}, u32[]{:S(2)}, u32[]{:S(2)}) %collective-permute-start.7) | collective-permute-done | bytes 229408 | tf_op jit(solution)/shard_map/ppermute | solution.py:366
  28.1 2.5 %collective-permute-start.9 = (bf16[4,32,896]{2,1,0:T(8,128)(2,1)S(1)}, bf16[4,32,896]{2,1,0:T(8,128)(2,1)S(1)}, u32[]{:S(2)}, u32[]{:S(2)}) collective-permute-start(bf16[4,32,896]{2,1,0:T(8,128)(2,1)S(1)} %get-tuple-element.59), channel_id=1, source_target_pairs={{0,12},{4,8},{8,4},{12,0},{1,13},{5,9},{9,5},{13,1},{2,14},{6,10},... | collective-permute-start | bytes 688136 | tf_op jit(solution)/shard_map/ppermute | solution.py:366
  30.7 1.8 %encode.2 = bf16[8,32,896]{2,1,0:T(8,128)(2,1)S(1)} custom-call(s32[16]{0:T(128)S(1)} %get-tuple-element.44.req_ref, bf16[512,896]{1,0:T(8,128)(2,1)S(1)} %copy-done.6, bf16[4,32,896]{2,1,0:T(8,128)(2,1)S(1)} %collective-permute-done.6.refs_0_, bf16[4,32,896]{2,1,0:T(8,128)(2,1)S(1)} %collective-permute-done.7.refs_1_), custom_call_target="tpu_custom_call" | custom-call | flops 10000000000 | bytes 1024 | tf_op jit(solution)/shard_map/encode/pallas_call | solution.py:157
  32.5 0.0 copy-start.7
  32.5 0.6 collective-permute-start.8
  33.1 1.2 %project.2.refs_0_ = bf16[4,4,32,1024]{3,2,1,0:T(8,128)(2,1)S(1)} custom-call(bf16[2,4,32,896]{3,2,1,0:T(8,128)(2,1)S(1)} %pad_maximum_fusion.1.refs_0_, bf16[2,4,32,896]{3,2,1,0:T(8,128)(2,1)S(1)} %collective-permute-done.5.refs_1_, bf16[896,512]{1,0:T(8,128)(2,1)S(1)} %copy-done.1, bf16[896,512]{1,0:T(8,128)(2,1)S(1)} %copy-done.2), custom_call_target="tpu_custom_call" | custom-call | flops 100000000 | bytes 1024 | tf_op jit(solution)/shard_map/project/pallas_call | solution.py:240
  34.4 1.6 %collective-permute-done.9.refs_0_ = bf16[4,32,896]{2,1,0:T(8,128)(2,1)S(1)} collective-permute-done((bf16[4,32,896]{2,1,0:T(8,128)(2,1)S(1)}, bf16[4,32,896]{2,1,0:T(8,128)(2,1)S(1)}, u32[]{:S(2)}, u32[]{:S(2)}) %collective-permute-start.9) | collective-permute-done | bytes 229408 | tf_op jit(solution)/shard_map/ppermute | solution.py:366
  36.0 1.3 %encode.3 = bf16[4,32,896]{2,1,0:T(8,128)(2,1)S(1)} custom-call(s32[16]{0:T(128)S(1)} %get-tuple-element.44.req_ref, bf16[512,896]{1,0:T(8,128)(2,1)S(1)} %copy-done.7, bf16[4,32,896]{2,1,0:T(8,128)(2,1)S(1)} %collective-permute-done.9.refs_0_), custom_call_target="tpu_custom_call" | custom-call | flops 10000000000 | bytes 1024 | tf_op jit(solution)/shard_map/encode/pallas_call | solution.py:157
  37.3 6.0 %collective-permute-done.8 = bf16[8,32,896]{2,1,0:T(8,128)(2,1)S(1)} collective-permute-done((bf16[8,32,896]{2,1,0:T(8,128)(2,1)S(1)}, bf16[8,32,896]{2,1,0:T(8,128)(2,1)S(1)}, u32[]{:S(2)}, u32[]{:S(2)}) %collective-permute-start.8) | collective-permute-done | bytes 458784 | tf_op jit(solution)/shard_map/ppermute | solution.py:351
  43.4 0.1 pad_maximum_fusion.refs_0_
  43.5 0.0 copy-start.3
  43.5 0.1 collective-permute-start.10
  43.5 0.6 collective-permute-start.11
  44.1 1.9 %collective-permute-done.10.refs_1_ = bf16[2,8,32,896]{3,2,1,0:T(8,128)(2,1)S(1)} collective-permute-done((bf16[2,8,32,896]{3,2,1,0:T(8,128)(2,1)S(1)}, bf16[2,8,32,896]{3,2,1,0:T(8,128)(2,1)S(1)}, u32[]{:S(2)}, u32[]{:S(2)}) %collective-permute-start.10) | collective-permute-done | bytes 917536 | tf_op jit(solution)/shard_map/ppermute | solution.py:354
  46.0 2.3 %project.3.refs_1_ = bf16[8,4,32,1024]{3,2,1,0:T(8,128)(2,1)S(1)} custom-call(bf16[2,8,32,896]{3,2,1,0:T(8,128)(2,1)S(1)} %pad_maximum_fusion.refs_0_, bf16[2,8,32,896]{3,2,1,0:T(8,128)(2,1)S(1)} %collective-permute-done.10.refs_1_, bf16[896,512]{1,0:T(8,128)(2,1)S(1)} %copy-done.1, bf16[896,512]{1,0:T(8,128)(2,1)S(1)} %copy-done.2), custom_call_target="tpu_custom_call" | custom-call | flops 100000000 | bytes 1024 | tf_op jit(solution)/shard_map/project/pallas_call | solution.py:240
  48.3 3.2 %collective-permute-done.11 = bf16[4,32,896]{2,1,0:T(8,128)(2,1)S(1)} collective-permute-done((bf16[4,32,896]{2,1,0:T(8,128)(2,1)S(1)}, bf16[4,32,896]{2,1,0:T(8,128)(2,1)S(1)}, u32[]{:S(2)}, u32[]{:S(2)}) %collective-permute-start.11) | collective-permute-done | bytes 229408 | tf_op jit(solution)/shard_map/ppermute | solution.py:351
  51.6 0.1 collective-permute-start.12
  51.7 1.8 %collective-permute-done.12.refs_3_ = bf16[2,4,32,896]{3,2,1,0:T(8,128)(2,1)S(1)} collective-permute-done((bf16[2,4,32,896]{3,2,1,0:T(8,128)(2,1)S(1)}, bf16[2,4,32,896]{3,2,1,0:T(8,128)(2,1)S(1)}, u32[]{:S(2)}, u32[]{:S(2)}) %collective-permute-start.12) | collective-permute-done | bytes 458784 | tf_op jit(solution)/shard_map/ppermute | solution.py:354
  53.5 3.4 %attend.2 = (bf16[1,128,512]{2,1,0:T(8,128)(2,1)S(1)}, bf16[1,128,512]{2,1,0:T(8,128)(2,1)S(1)}) custom-call(s32[16]{0:T(128)S(1)} %get-tuple-element.42.slot_ref, bf16[512,512]{1,0:T(8,128)(2,1)S(1)} %copy-done.3, bf16[4,4,32,1024]{3,2,1,0:T(8,128)(2,1)S(1)} %project.2.refs_0_, bf16[8,4,32,1024]{3,2,1,0:T(8,128)(2,1)S(1)} %project.3.refs_1_, ...), custom_call_target="tpu_custom_call" | custom-call | flops 1000000 | bytes 1024 | tf_op jit(solution)/shard_map/attend/pallas_call | solution.py:306
  56.9 0.2 collective-permute-start.13
  57.1 1.2 %collective-permute-done.13.refs_1_ = bf16[1,128,512]{2,1,0:T(8,128)(2,1)S(1)} collective-permute-done((bf16[1,128,512]{2,1,0:T(8,128)(2,1)S(1)}, bf16[1,128,512]{2,1,0:T(8,128)(2,1)S(1)}, u32[]{:S(2)}, u32[]{:S(2)}) %collective-permute-start.13) | collective-permute-done | bytes 131104 | tf_op jit(solution)/shard_map/ppermute | solution.py:390
  58.3 1.7 %out_project.4 = bf16[128,2048]{1,0:T(8,128)(2,1)S(1)} custom-call(bf16[1,128,512]{2,1,0:T(8,128)(2,1)S(1)} %get-tuple-element.73.refs_0_, bf16[1,128,512]{2,1,0:T(8,128)(2,1)S(1)} %collective-permute-done.13.refs_1_, bf16[512,4096]{1,0:T(8,128)(2,1)S(1)} %copy-done, bf16[512,4096]{1,0:T(8,128)(2,1)S(1)} %collective-permute-done.4.refs_3_), custom_call_target="tpu_custom_call" | custom-call | flops 1000000 | bytes 1024 | tf_op jit(solution)/shard_map/out_project/pallas_call | solution.py:326
  60.0 0.6 collective-permute-start.15
  60.6 1.3 %out_project.5 = bf16[128,1536]{1,0:T(8,128)(2,1)S(1)} custom-call(bf16[1,128,512]{2,1,0:T(8,128)(2,1)S(1)} %get-tuple-element.73.refs_0_, bf16[1,128,512]{2,1,0:T(8,128)(2,1)S(1)} %collective-permute-done.13.refs_1_, bf16[512,4096]{1,0:T(8,128)(2,1)S(1)} %copy-done, bf16[512,4096]{1,0:T(8,128)(2,1)S(1)} %collective-permute-done.4.refs_3_), custom_call_target="tpu_custom_call" | custom-call | flops 1000000 | bytes 1024 | tf_op jit(solution)/shard_map/out_project/pallas_call | solution.py:326
  61.9 1.6 %collective-permute-start.16 = (bf16[128,1536]{1,0:T(8,128)(2,1)S(1)}, bf16[128,1536]{1,0:T(8,128)(2,1)S(1)}, u32[]{:S(2)}, u32[]{:S(2)}) collective-permute-start(bf16[128,1536]{1,0:T(8,128)(2,1)S(1)} %out_project.5), channel_id=1, source_target_pairs={{0,2},{2,0},{1,3},{3,1},{4,6},{6,4},{5,7},{7,5},{8,10},{10,8},{9,1... | collective-permute-start | bytes 1179656 | tf_op jit(solution)/shard_map/ppermute | solution.py:404
  63.4 0.3 out_project.6
  63.8 3.4 %attend.3 = (bf16[1,128,512]{2,1,0:T(8,128)(2,1)S(1)}, bf16[1,128,512]{2,1,0:T(8,128)(2,1)S(1)}) custom-call(s32[16]{0:T(128)S(1)} %get-tuple-element.42.slot_ref, bf16[512,512]{1,0:T(8,128)(2,1)S(1)} %copy-done.3, bf16[4,4,32,1024]{3,2,1,0:T(8,128)(2,1)S(1)} %project.2.refs_0_, bf16[8,4,32,1024]{3,2,1,0:T(8,128)(2,1)S(1)} %project.3.refs_1_, ...), custom_call_target="tpu_custom_call" | custom-call | flops 1000000 | bytes 1024 | tf_op jit(solution)/shard_map/attend/pallas_call | solution.py:306
  67.2 0.1 collective-permute-start.14
  67.2 0.6 collective-permute-start.17
  67.9 0.7 collective-permute-done.14.refs_1_
  68.6 3.3 %out_project.7 = bf16[128,4096]{1,0:T(8,128)(2,1)S(1)} custom-call(bf16[1,128,512]{2,1,0:T(8,128)(2,1)S(1)} %get-tuple-element.77.refs_0_, bf16[1,128,512]{2,1,0:T(8,128)(2,1)S(1)} %collective-permute-done.14.refs_1_, bf16[512,4096]{1,0:T(8,128)(2,1)S(1)} %copy-done, bf16[512,4096]{1,0:T(8,128)(2,1)S(1)} %collective-permute-done.4.refs_3_), custom_call_target="tpu_custom_call" | custom-call | flops 1000000 | bytes 1024 | tf_op jit(solution)/shard_map/out_project/pallas_call | solution.py:326
  71.9 13.4 %collective-permute-done.17 = bf16[128,512]{1,0:T(8,128)(2,1)S(1)} collective-permute-done((bf16[128,512]{1,0:T(8,128)(2,1)S(1)}, bf16[128,512]{1,0:T(8,128)(2,1)S(1)}, u32[]{:S(2)}, u32[]{:S(2)}) %collective-permute-start.17) | collective-permute-done | bytes 131104 | tf_op jit(solution)/shard_map/ppermute | solution.py:404
  85.3 1.2 %add_convert_fusion = bf16[128,4096]{1,0:T(8,128)(2,1)} fusion(bf16[128,4096]{1,0:T(8,128)(2,1)S(1)} %out_project.7, bf16[128,512]{1,0:T(8,128)(2,1)S(1)} %collective-permute-done.17, bf16[128,1536]{1,0:T(8,128)(2,1)S(1)} %collective-permute-done.16, bf16[128,2048]{1,0:T(8,128)(2,1)S(1)} %collective-permute-done.15), kind=kLoop, calls=%fused_computation | loop fusion | flops 4718592 | bytes 3145728 | tf_op jit(solution)/shard_map/convert_element_type | solution.py:409
  (21 shorter events, 0.1 us)
Async XLA Ops:
  0.0 12.2 %collective-permute-start.4 = (bf16[512,4096]{1,0:T(8,128)(2,1)}, bf16[512,4096]{1,0:T(8,128)(2,1)S(1)}, u32[]{:S(2)}, u32[]{:S(2)}) collective-permute-start(bf16[512,4096]{1,0:T(8,128)(2,1)} %refs_2_.11), channel_id=1, source_target_pairs={{0,1},{1,0},{2,3},{3,2},{4,5},{5,4},{6,7},{7,6},{8,9},{9,8},{10,11... | collective-permute-start | bytes 12582920 | tf_op jit(solution)/shard_map/ppermute | solution.py:354
  1.2 11.1 %collective-permute-start.1 = (s32[4,8]{1,0:T(4,128)S(1)}, s32[4,8]{1,0:T(4,128)S(1)}, u32[]{:S(2)}, u32[]{:S(2)}) collective-permute-start(s32[4,8]{1,0:T(4,128)S(1)} %pad_add_fusion.own_ref), channel_id=1, source_target_pairs={{0,4},{4,0},{8,12},{12,8},{1,5},{5,1},{9,13},{13,9},{2,6},{6,2},{1... | collective-permute-start | bytes 392 | tf_op jit(solution)/shard_map/ppermute | solution.py:357
  3.7 8.5 %collective-permute-start.2 = (s32[4,8]{1,0:T(4,128)S(1)}, s32[4,8]{1,0:T(4,128)S(1)}, u32[]{:S(2)}, u32[]{:S(2)}) collective-permute-start(s32[4,8]{1,0:T(4,128)S(1)} %pad_add_fusion.own_ref), channel_id=1, source_target_pairs={{0,8},{4,12},{8,0},{12,4},{1,9},{5,13},{9,1},{13,5},{2,10},{6,14},... | collective-permute-start | bytes 392 | tf_op jit(solution)/shard_map/ppermute | solution.py:357
  6.3 5.9 %collective-permute-start.3 = (s32[4,8]{1,0:T(4,128)S(1)}, s32[4,8]{1,0:T(4,128)S(1)}, u32[]{:S(2)}, u32[]{:S(2)}) collective-permute-start(s32[4,8]{1,0:T(4,128)S(1)} %pad_add_fusion.own_ref), channel_id=1, source_target_pairs={{0,12},{4,8},{8,4},{12,0},{1,13},{5,9},{9,5},{13,1},{2,14},{6,10},... | collective-permute-start | bytes 392 | tf_op jit(solution)/shard_map/ppermute | solution.py:357
  6.3 1.2 %copy-start.4 = (bf16[16,32,896]{2,1,0:T(8,128)(2,1)S(1)}, bf16[16,32,896]{2,1,0:T(8,128)(2,1)}, u32[]{:S(2)}) copy-start(bf16[16,32,896]{2,1,0:T(8,128)(2,1)} %refs_3_.3) | copy-start | bytes 2752516
  7.5 1.2 %copy-start.6 = (bf16[512,896]{1,0:T(8,128)(2,1)S(1)}, bf16[512,896]{1,0:T(8,128)(2,1)}, u32[]{:S(2)}) copy-start(bf16[512,896]{1,0:T(8,128)(2,1)} %states_ref.5) | copy-start | bytes 2752516
  8.7 3.5 %copy-start.5 = (bf16[16,32,896]{2,1,0:T(8,128)(2,1)S(1)}, bf16[16,32,896]{2,1,0:T(8,128)(2,1)}, u32[]{:S(2)}) copy-start(bf16[16,32,896]{2,1,0:T(8,128)(2,1)} %refs_3_.3) | copy-start | bytes 2752516
  10.4 7.9 %collective-permute-start = (bf16[4,32,896]{2,1,0:T(8,128)(2,1)S(1)}, bf16[4,32,896]{2,1,0:T(8,128)(2,1)S(1)}, u32[]{:S(2)}, u32[]{:S(2)}) collective-permute-start(bf16[4,32,896]{2,1,0:T(8,128)(2,1)S(1)} %get-tuple-element.51), channel_id=1, source_target_pairs={{0,2},{2,0},{1,3},{3,1},{4,6},{6,4},{5,7},{7,5},{8,10},{10,8},{9,1... | collective-permute-start | bytes 688136 | tf_op jit(solution)/shard_map/ppermute | solution.py:351
  14.1 11.7 %collective-permute-start.6 = (bf16[4,32,896]{2,1,0:T(8,128)(2,1)S(1)}, bf16[4,32,896]{2,1,0:T(8,128)(2,1)S(1)}, u32[]{:S(2)}, u32[]{:S(2)}) collective-permute-start(bf16[4,32,896]{2,1,0:T(8,128)(2,1)S(1)} %get-tuple-element.53), channel_id=1, source_target_pairs={{0,4},{4,0},{8,12},{12,8},{1,5},{5,1},{9,13},{13,9},{2,6},{6,2},{1... | collective-permute-start | bytes 688136 | tf_op jit(solution)/shard_map/ppermute | solution.py:366
  14.8 13.3 %collective-permute-start.7 = (bf16[4,32,896]{2,1,0:T(8,128)(2,1)S(1)}, bf16[4,32,896]{2,1,0:T(8,128)(2,1)S(1)}, u32[]{:S(2)}, u32[]{:S(2)}) collective-permute-start(bf16[4,32,896]{2,1,0:T(8,128)(2,1)S(1)} %get-tuple-element.54), channel_id=1, source_target_pairs={{0,8},{4,12},{8,0},{12,4},{1,9},{5,13},{9,1},{13,5},{2,10},{6,14},... | collective-permute-start | bytes 688136 | tf_op jit(solution)/shard_map/ppermute | solution.py:366
  18.3 14.8 %copy-start.1 = (bf16[896,512]{1,0:T(8,128)(2,1)S(1)}, bf16[896,512]{1,0:T(8,128)(2,1)}, u32[]{:S(2)}) copy-start(bf16[896,512]{1,0:T(8,128)(2,1)} %refs_4_.3) | copy-start | bytes 2752516
  18.4 14.8 %copy-start.2 = (bf16[896,512]{1,0:T(8,128)(2,1)S(1)}, bf16[896,512]{1,0:T(8,128)(2,1)}, u32[]{:S(2)}) copy-start(bf16[896,512]{1,0:T(8,128)(2,1)} %refs_5_.3) | copy-start | bytes 2752516
  18.4 14.8 %collective-permute-start.5 = (bf16[2,4,32,896]{3,2,1,0:T(8,128)(2,1)S(1)}, bf16[2,4,32,896]{3,2,1,0:T(8,128)(2,1)S(1)}, u32[]{:S(2)}, u32[]{:S(2)}) collective-permute-start(bf16[2,4,32,896]{3,2,1,0:T(8,128)(2,1)S(1)} %pad_maximum_fusion.1.refs_0_), channel_id=1, source_target_pairs={{0,1},{1,0},{2,3},{3,2},{4,5},{5,4},{6,7},{7,6},{8,9},{9,8},{10,11... | collective-permute-start | bytes 1376264 | tf_op jit(solution)/shard_map/ppermute | solution.py:354
  28.1 7.9 %collective-permute-start.9 = (bf16[4,32,896]{2,1,0:T(8,128)(2,1)S(1)}, bf16[4,32,896]{2,1,0:T(8,128)(2,1)S(1)}, u32[]{:S(2)}, u32[]{:S(2)}) collective-permute-start(bf16[4,32,896]{2,1,0:T(8,128)(2,1)S(1)} %get-tuple-element.59), channel_id=1, source_target_pairs={{0,12},{4,8},{8,4},{12,0},{1,13},{5,9},{9,5},{13,1},{2,14},{6,10},... | collective-permute-start | bytes 688136 | tf_op jit(solution)/shard_map/ppermute | solution.py:366
  32.5 3.5 %copy-start.7 = (bf16[512,896]{1,0:T(8,128)(2,1)S(1)}, bf16[512,896]{1,0:T(8,128)(2,1)}, u32[]{:S(2)}) copy-start(bf16[512,896]{1,0:T(8,128)(2,1)} %states_ref.5) | copy-start | bytes 2752516
  32.5 10.8 %collective-permute-start.8 = (bf16[8,32,896]{2,1,0:T(8,128)(2,1)S(1)}, bf16[8,32,896]{2,1,0:T(8,128)(2,1)S(1)}, u32[]{:S(2)}, u32[]{:S(2)}) collective-permute-start(bf16[8,32,896]{2,1,0:T(8,128)(2,1)S(1)} %encode.2), channel_id=1, source_target_pairs={{0,2},{2,0},{1,3},{3,1},{4,6},{6,4},{5,7},{7,5},{8,10},{10,8},{9,1... | collective-permute-start | bytes 1376264 | tf_op jit(solution)/shard_map/ppermute | solution.py:351
  43.5 10.0 %copy-start.3 = (bf16[512,512]{1,0:T(8,128)(2,1)S(1)}, bf16[512,512]{1,0:T(8,128)(2,1)}, u32[]{:S(2)}) copy-start(bf16[512,512]{1,0:T(8,128)(2,1)} %q_ref.2) | copy-start | bytes 1572868
  43.5 2.5 %collective-permute-start.10 = (bf16[2,8,32,896]{3,2,1,0:T(8,128)(2,1)S(1)}, bf16[2,8,32,896]{3,2,1,0:T(8,128)(2,1)S(1)}, u32[]{:S(2)}, u32[]{:S(2)}) collective-permute-start(bf16[2,8,32,896]{3,2,1,0:T(8,128)(2,1)S(1)} %pad_maximum_fusion.refs_0_), channel_id=1, source_target_pairs={{0,1},{1,0},{2,3},{3,2},{4,5},{5,4},{6,7},{7,6},{8,9},{9,8},{10,11... | collective-permute-start | bytes 2752520 | tf_op jit(solution)/shard_map/ppermute | solution.py:354
  43.5 8.0 %collective-permute-start.11 = (bf16[4,32,896]{2,1,0:T(8,128)(2,1)S(1)}, bf16[4,32,896]{2,1,0:T(8,128)(2,1)S(1)}, u32[]{:S(2)}, u32[]{:S(2)}) collective-permute-start(bf16[4,32,896]{2,1,0:T(8,128)(2,1)S(1)} %encode.3), channel_id=1, source_target_pairs={{0,2},{2,0},{1,3},{3,1},{4,6},{6,4},{5,7},{7,5},{8,10},{10,8},{9,1... | collective-permute-start | bytes 688136 | tf_op jit(solution)/shard_map/ppermute | solution.py:351
  51.6 1.9 %collective-permute-start.12 = (bf16[2,4,32,896]{3,2,1,0:T(8,128)(2,1)S(1)}, bf16[2,4,32,896]{3,2,1,0:T(8,128)(2,1)S(1)}, u32[]{:S(2)}, u32[]{:S(2)}) collective-permute-start(bf16[2,4,32,896]{3,2,1,0:T(8,128)(2,1)S(1)} %pad_maximum_fusion.2.refs_2_), channel_id=1, source_target_pairs={{0,1},{1,0},{2,3},{3,2},{4,5},{5,4},{6,7},{7,6},{8,9},{9,8},{10,11... | collective-permute-start | bytes 1376264 | tf_op jit(solution)/shard_map/ppermute | solution.py:354
  53.5 4.8 %copy-start = (bf16[512,4096]{1,0:T(8,128)(2,1)S(1)}, bf16[512,4096]{1,0:T(8,128)(2,1)}, u32[]{:S(2)}) copy-start(bf16[512,4096]{1,0:T(8,128)(2,1)} %refs_2_.11) | copy-start | bytes 12582916
  56.9 1.4 %collective-permute-start.13 = (bf16[1,128,512]{2,1,0:T(8,128)(2,1)S(1)}, bf16[1,128,512]{2,1,0:T(8,128)(2,1)S(1)}, u32[]{:S(2)}, u32[]{:S(2)}) collective-permute-start(bf16[1,128,512]{2,1,0:T(8,128)(2,1)S(1)} %get-tuple-element.68), channel_id=1, source_target_pairs={{0,1},{1,0},{2,3},{3,2},{4,5},{5,4},{6,7},{7,6},{8,9},{9,8},{10,11... | collective-permute-start | bytes 393224 | tf_op jit(solution)/shard_map/ppermute | solution.py:390
  60.0 25.3 %collective-permute-start.15 = (bf16[128,2048]{1,0:T(8,128)(2,1)S(1)}, bf16[128,2048]{1,0:T(8,128)(2,1)S(1)}, u32[]{:S(2)}, u32[]{:S(2)}) collective-permute-start(bf16[128,2048]{1,0:T(8,128)(2,1)S(1)} %out_project.4), channel_id=1, source_target_pairs={{0,2},{2,0},{1,3},{3,1},{4,6},{6,4},{5,7},{7,5},{8,10},{10,8},{9,1... | collective-permute-start | bytes 1572872 | tf_op jit(solution)/shard_map/ppermute | solution.py:404
  61.9 23.4 %collective-permute-start.16 = (bf16[128,1536]{1,0:T(8,128)(2,1)S(1)}, bf16[128,1536]{1,0:T(8,128)(2,1)S(1)}, u32[]{:S(2)}, u32[]{:S(2)}) collective-permute-start(bf16[128,1536]{1,0:T(8,128)(2,1)S(1)} %out_project.5), channel_id=1, source_target_pairs={{0,2},{2,0},{1,3},{3,1},{4,6},{6,4},{5,7},{7,5},{8,10},{10,8},{9,1... | collective-permute-start | bytes 1179656 | tf_op jit(solution)/shard_map/ppermute | solution.py:404
  67.2 1.4 %collective-permute-start.14 = (bf16[1,128,512]{2,1,0:T(8,128)(2,1)S(1)}, bf16[1,128,512]{2,1,0:T(8,128)(2,1)S(1)}, u32[]{:S(2)}, u32[]{:S(2)}) collective-permute-start(bf16[1,128,512]{2,1,0:T(8,128)(2,1)S(1)} %get-tuple-element.78), channel_id=1, source_target_pairs={{0,1},{1,0},{2,3},{3,2},{4,5},{5,4},{6,7},{7,6},{8,9},{9,8},{10,11... | collective-permute-start | bytes 393224 | tf_op jit(solution)/shard_map/ppermute | solution.py:390
  67.2 18.0 %collective-permute-start.17 = (bf16[128,512]{1,0:T(8,128)(2,1)S(1)}, bf16[128,512]{1,0:T(8,128)(2,1)S(1)}, u32[]{:S(2)}, u32[]{:S(2)}) collective-permute-start(bf16[128,512]{1,0:T(8,128)(2,1)S(1)} %out_project.6), channel_id=1, source_target_pairs={{0,2},{2,0},{1,3},{3,1},{4,6},{6,4},{5,7},{7,5},{8,10},{10,8},{9,1... | collective-permute-start | bytes 393224 | tf_op jit(solution)/shard_map/ppermute | solution.py:404

commit v5 on v4

--- a/solution.py
+++ b/solution.py
@@ -11,7 +11,8 @@
 ENCODER_HEAD_DIM = 128
 F32 = jnp.float32
 BF16 = jnp.bfloat16
-COL_TILE = 512
+LATER_GROUPS = 4
+COL_TILE = 256
 
 VMEM = pl.BlockSpec(memory_space=pltpu.VMEM)
 SMEM = pl.BlockSpec(memory_space=pltpu.SMEM)
@@ -50,43 +51,68 @@
     return jnp.dot(a, b, preferred_element_type=F32)
 
 
-def fetch_kernel(n_lanes, cap, *refs):
-    others = n_lanes - 1
+def plan_kernel(n_lanes, cap, own_ref, req_ref, slot_ref, pick_ref, count_ref):
+    lane = lax.axis_index("lanes")
+    fanout, spans = own_ref.shape[0] // 2, own_ref.shape[1]
+    for i in range(n_lanes):
+        count_ref[i] = 0
+    for i in range(n_lanes * cap):
+        pick_ref[i] = 0
+        req_ref[i] = 0
+    for j in range(fanout * spans):
+        span, k = j // fanout, j % fanout
+        d = apart(n_lanes, lane, own_ref[k, span])
+        rank = count_ref[d]
+        count_ref[d] = rank + 1
+        slot = d * cap + rank
+        pick_ref[slot] = own_ref[fanout + k, span]
+        req_ref[slot] = j
+        slot_ref[j] = slot
+
+
+def plan(own, n_lanes, cap):
+    table = jax.ShapeDtypeStruct((n_lanes * cap,), jnp.int32)
+    return pl.pallas_call(
+        functools.partial(plan_kernel, n_lanes, cap),
+        out_shape=(table, jax.ShapeDtypeStruct((own.size // 2,), jnp.int32), table),
+        in_specs=[SMEM],
+        out_specs=(SMEM, SMEM, SMEM),
+        scratch_shapes=[pltpu.SMEM((n_lanes,), jnp.int32)],
+        compiler_params=params(16),
+        cost_estimate=cost(10),
+        name="plan",
+    )(own)
+
+
+def fetch_kernel(items, cap, *refs):
+    others = items[-1][0]
     asked, store_ref, refs = refs[:others], refs[others], refs[others + 1 :]
-    blocks, (pick_ref, sem) = refs[:others], refs[others:]
+    blocks, pick_ref = refs[:-1], refs[-1]
     lane = lax.axis_index("lanes")
     fanout, spans = asked[0].shape[0] // 2, asked[0].shape[1]
     for i in range(others * cap):
         pick_ref[i] = 0
-    copies = []
     for d in range(others):
         place = d * cap
         for span in range(spans):
             for k in range(fanout):
                 pick_ref[place] = asked[d][fanout + k, span]
                 place = place + (asked[d][k, span] == lane).astype(jnp.int32)
-        for s in range(cap):
-            slot = d * cap + s
-            copies.append(
-                pltpu.make_async_copy(store_ref.at[pick_ref[slot]], blocks[d].at[s], sem.at[slot])
-            )
-            copies[-1].start()
-    for copy in copies:
-        copy.wait()
-
-
-def fetch(asked, store, n_lanes, cap):
-    block = jax.ShapeDtypeStruct((cap,) + store.shape[1:], store.dtype)
-    others = n_lanes - 1
-    return pl.pallas_call(
-        functools.partial(fetch_kernel, n_lanes, cap),
-        out_shape=[block] * others,
-        in_specs=[SMEM] * others + [ANY],
-        out_specs=[VMEM] * others,
-        scratch_shapes=[
-            pltpu.SMEM((others * cap + 1,), jnp.int32),
-            pltpu.SemaphoreType.DMA((others * cap,)),
+    for block, (d, low, high) in zip(blocks, items):
+        for s in range(low, high):
+            block[s - low] = store_ref[pick_ref[(d - 1) * cap + s]]
+
+
+def fetch(asked, store, items, cap):
+    others = len(asked)
+    return pl.pallas_call(
+        functools.partial(fetch_kernel, items, cap),
+        out_shape=[
+            jax.ShapeDtypeStruct((high - low,) + store.shape[1:], store.dtype) for _, low, high in items
         ],
+        in_specs=[SMEM] * others + [VMEM],
+        out_specs=[VMEM] * len(items),
+        scratch_shapes=[pltpu.SMEM((others * cap + 1,), jnp.int32)],
         compiler_params=params(16),
         cost_estimate=cost(10),
         name="fetch",
@@ -145,18 +171,20 @@
         out_ref[s, :, start:stop] = (token + top / bottom).astype(BF16)
 
 
-def encode_kernel(first, cap, fanout, span_len, req_ref, states_ref, *refs):
+def encode_kernel(first, fanout, span_len, req_ref, states_ref, *refs):
     blocks, out_ref = refs[:-1], refs[-1]
-    for i, block in enumerate(blocks):
-        out = out_ref.at[i * cap : (i + 1) * cap]
-        encode_block(block, out, (first + i) * cap, req_ref, states_ref, fanout, span_len)
+    at = 0
+    for block in blocks:
+        stop = at + block.shape[0]
+        encode_block(block, out_ref.at[at:stop], first + at, req_ref, states_ref, fanout, span_len)
+        at = stop
 
 
 def encode(req, span_states, blocks, first, fanout, span_len):
-    cap, tokens, width = blocks[0].shape
-    return pl.pallas_call(
-        functools.partial(encode_kernel, first, cap, fanout, span_len),
-        out_shape=jax.ShapeDtypeStruct((len(blocks) * cap, tokens, width), BF16),
+    slots = sum(block.shape[0] for block in blocks)
+    return pl.pallas_call(
+        functools.partial(encode_kernel, first, fanout, span_len),
+        out_shape=jax.ShapeDtypeStruct((slots,) + blocks[0].shape[1:], BF16),
         in_specs=[SMEM, VMEM] + [VMEM] * len(blocks),
         out_specs=VMEM,
         compiler_params=params(16),
@@ -165,55 +193,24 @@
     )(req, span_states, *blocks)
 
 
-def encode_local_kernel(n_lanes, cap, span_len, own_ref, states_ref, store_ref, *refs):
-    out_ref, req_ref, slot_ref, pick_ref, count_ref, tokens_ref, sem = refs
-    lane = lax.axis_index("lanes")
-    fanout, spans = own_ref.shape[0] // 2, own_ref.shape[1]
-    for i in range(n_lanes):
-        count_ref[i] = 0
-    for i in range(n_lanes * cap):
-        pick_ref[i] = 0
-        req_ref[i] = 0
-    for j in range(fanout * spans):
-        span, k = j // fanout, j % fanout
-        d = apart(n_lanes, lane, own_ref[k, span])
-        rank = count_ref[d]
-        count_ref[d] = rank + 1
-        slot = d * cap + rank
-        pick_ref[slot] = own_ref[fanout + k, span]
-        req_ref[slot] = j
-        slot_ref[j] = slot
-    copies = [
-        pltpu.make_async_copy(store_ref.at[pick_ref[s]], tokens_ref.at[s], sem.at[s]) for s in range(cap)
-    ]
-    for copy in copies:
-        copy.start()
-    for copy in copies:
-        copy.wait()
+def encode_local_kernel(fanout, span_len, req_ref, pick_ref, states_ref, store_ref, out_ref, tokens_ref):
+    for s in range(out_ref.shape[0]):
+        tokens_ref[s] = store_ref[pick_ref[s]]
     encode_block(tokens_ref, out_ref, 0, req_ref, states_ref, fanout, span_len)
 
 
-def encode_local(own, span_states, store, n_lanes, cap, span_len):
+def encode_local(req, pick, span_states, store, cap, fanout, span_len):
     block = (cap,) + store.shape[1:]
     return pl.pallas_call(
-        functools.partial(encode_local_kernel, n_lanes, cap, span_len),
-        out_shape=(
-            jax.ShapeDtypeStruct(block, BF16),
-            jax.ShapeDtypeStruct((n_lanes * cap,), jnp.int32),
-            jax.ShapeDtypeStruct((own.size // 2,), jnp.int32),
-        ),
-        in_specs=[SMEM, VMEM, ANY],
-        out_specs=(VMEM, SMEM, SMEM),
-        scratch_shapes=[
-            pltpu.SMEM((n_lanes * cap,), jnp.int32),
-            pltpu.SMEM((n_lanes,), jnp.int32),
-            pltpu.VMEM(block, BF16),
-            pltpu.SemaphoreType.DMA((cap,)),
-        ],
+        functools.partial(encode_local_kernel, fanout, span_len),
+        out_shape=jax.ShapeDtypeStruct(block, BF16),
+        in_specs=[SMEM, SMEM, VMEM, VMEM],
+        out_specs=VMEM,
+        scratch_shapes=[pltpu.VMEM(block, BF16)],
         compiler_params=params(16),
         cost_estimate=cost(10),
         name="encode_local",
-    )(own, span_states, store)
+    )(req, pick, span_states, store)
 
 
 def project_into(kv_ref, first, pieces, wk_ref, wv_ref):
@@ -353,36 +350,43 @@
     def over_rep(array):
         return [array] + [lax.ppermute(array, "rep", shift_pairs(n_rep, s)) for s in range(1, n_rep)]
 
+    items = [(d, 0, cap) for d in range(1, n_lanes - 1)]
+    items += [(n_lanes - 1, 0, cap // 2), (n_lanes - 1, cap // 2, cap)]
+    size = -(-len(items) // LATER_GROUPS)
+    parts = [range(i, min(i + size, len(items))) for i in range(0, len(items), size)]
+
     own = jnp.concatenate([owners.T, entry_ids.T], axis=0)
     asked = [lax.ppermute(own, "lanes", lane_pairs(n_lanes, d, False)) for d in range(1, n_lanes)]
     w_outs = over_rep(w_out)
-    encoded, req, slot = encode_local(own, span_states, store, n_lanes, cap, span_len)
-    asked = after(asked, req, w_outs)
-    blocks = [None] + list(fetch(asked, store, n_lanes, cap))
-
-    def send(distances, *earlier):
-        ready = after([blocks[d] for d in distances], *earlier)
+    req, slot, pick = plan(own, n_lanes, cap)
+    encoded = encode_local(req, pick, span_states, store, cap, fanout, span_len)
+    blocks = fetch(after(asked, w_outs, encoded), store, items, cap)
+
+    def send(part, *earlier):
+        ready = after([blocks[i] for i in part], *earlier)
         return [
-            lax.ppermute(block, "lanes", lane_pairs(n_lanes, d, True))
-            for block, d in zip(ready, distances)
+            lax.ppermute(block, "lanes", lane_pairs(n_lanes, items[i][0], True))
+            for block, i in zip(ready, part)
         ]
 
-    cut = 1 + (2 * (n_lanes - 1) + 2) // 3
-    parts = [list(range(1, cut)), list(range(cut, n_lanes))]
-    parts = [part for part in parts if part]
-
-    crossed = over_heads(encoded)
-    arrived = send(parts[0]) if parts else []
-    stacked, kvs = jnp.stack(after(crossed, blocks[1:])), []
-    for i, part in enumerate(parts):
-        later = parts[i + 1] if i + 1 < len(parts) else []
-        next_arrived = send(later, arrived) if later else []
-        encoded = encode(req, span_states, after(arrived, stacked, kvs), part[0], fanout, span_len)
-        if i:
-            stacked = jnp.stack(after(crossed, encoded))
-        kvs.append(project(after(over_rep(stacked), encoded), w_key, w_value))
-        crossed, arrived = over_heads(encoded), next_arrived
-    pieces = over_rep(jnp.stack(after(crossed, kvs)) if parts else stacked)
+    crossed, pieces, kvs = [over_heads(encoded)], [], []
+    arrived = [None] + [send(part) for part in parts[:2]]
+    last = blocks
+    for i, part in enumerate(parts, 1):
+        if i + 2 <= len(parts):
+            arrived.append(send(parts[i + 1], arrived[i], last))
+        first = items[part[0]][0] * cap + items[part[0]][1]
+        encoded = encode(req, span_states, after(arrived[i], last), first, fanout, span_len)
+        crossed.append(over_heads(encoded))
+        last = encoded
+        if i >= 2:
+            last = project(after(pieces[i - 2], last), w_key, w_value)
+            kvs.append(last)
+        if i < len(parts):
+            last = jnp.stack(after(crossed[i - 1], last))
+            pieces.append(over_rep(last))
+    ends = [jnp.concatenate(pair, axis=0) for pair in zip(*after(crossed[-2:], kvs))]
+    pieces = over_rep(jnp.stack(ends))
 
     def mix(turns, q):
         outs = attend(slot, q, kvs, pieces, w_key, w_value, n_heads, n_rep, turns, fanout, spans)
@@ -392,7 +396,7 @@
 
     width = w_out.shape[1]
     tile = min(COL_TILE, width)
-    cuts = sorted({0, width // 2 // tile * tile, width - tile, width})
+    cuts = [width // tile * part // 16 * tile for part in (0, 6, 11, 14)] + [width]
     mixed = mix(list(range(1, n_heads)), queries)
     received, partials = [], []
     for t in range(1, n_heads):

time: 86.7 us -> 81.6 us (0.941)
  waiting for transfers between devices: 39.6 us -> 25.4 us
  starting transfers between devices: 18.6 us -> 24.4 us
  Pallas kernels: 23.6 us -> 29.2 us
  local copies, waits for them, and re-layouts: 2.39 us -> 0.03 us
    ppermute x3 -> x5, waiting for transfers between devices: 9.27 us -> 2.54 us  [over_heads(): lax.ppermute(array, 'heads', shift_pairs(n_heads, s))]
    ppermute x3 -> x4, waiting for transfers between devices: 13.4 us -> 7.85 us  [shards(): sent.append(lax.ppermute(partial, 'heads', shift_pairs(n_heads, t)))]
    pallas_call x4 -> x5, Pallas kernels: 6.54 us -> 10.6 us  [out_project(): pl.pallas_call(functools.partial(out_kernel, len(mixed)), grid=((stop - s...]
    ppermute x3 -> x5, starting transfers between devices: 2.98 us -> 6.69 us  [over_heads(): lax.ppermute(array, 'heads', shift_pairs(n_heads, s))]
    unnamed x16 -> x12, local copies, waits for them, and re-layouts: 2.39 us -> 0.03 us
    ppermute x4 -> x5, waiting for transfers between devices: 3.67 us -> 1.81 us  [over_rep(): lax.ppermute(array, 'rep', shift_pairs(n_rep, s))]
    ppermute x3 -> x4, waiting for transfers between devices: 11.3 us -> 9.73 us  [send(): lax.ppermute(block, 'lanes', lane_pairs(n_lanes, items[i][0], True))]
    ppermute x3 -> x4, starting transfers between devices: 2.76 us -> 4.31 us  [shards(): sent.append(lax.ppermute(partial, 'heads', shift_pairs(n_heads, t)))]
  transfers between devices with their start and end apart: 18 -> 23, of which waited for: 10 -> 9; matrix products, arithmetic and copies ran while one was open for 1% -> 1% of each run, Pallas kernels for 21% -> 28%
where the time goes in v5:
time: 81.6 us; the launch traced here: 81.4 us
  Pallas kernels  29.2 us (36%)
  waiting for transfers between devices  25.4 us (31%)
  starting transfers between devices  24.4 us (30%)
  other arithmetic  2.18 us (3%)
    pallas_call x5, Pallas kernels, out_project(): pl.pallas_call(functools.partial(out_kernel, len(mixed)), grid=((stop - s...  10.6 us
    ppermute x4, waiting for transfers between devices, send(): lax.ppermute(block, 'lanes', lane_pairs(n_lanes, items[i][0], True))  9.73 us
    ppermute x4, waiting for transfers between devices, shards(): sent.append(lax.ppermute(partial, 'heads', shift_pairs(n_heads, t)))  7.85 us
    ppermute x4, starting transfers between devices, send(): lax.ppermute(block, 'lanes', lane_pairs(n_lanes, items[i][0], True))  7.03 us
    pallas_call x2, Pallas kernels, attend(): pl.pallas_call(functools.partial(attend_kernel, firsts, len(pieces), n_he...  6.83 us
    ppermute x5, starting transfers between devices, over_heads(): lax.ppermute(array, 'heads', shift_pairs(n_heads, s))  6.69 us
    ppermute x3, starting transfers between devices, shards(): lax.ppermute(own, 'lanes', lane_pairs(n_lanes, d, False))  5.31 us
    pallas_call x4, Pallas kernels, encode(): pl.pallas_call(functools.partial(encode_kernel, first, fanout, span_len),...  4.64 us
  transfers between devices with their start and end apart: 23, of which 9 were waited for; matrix products, arithmetic and copies ran while one was open for 1% of the time, Pallas kernels for 28%

profile of v5, /device:TPU:0, one launch (start us, length us, event | category | flops | bytes accessed | tf_op | source)
XLA Modules:
  0.0 81.4 jit_solution(9771442867422919995)
XLA Ops:
  0.0 0.5 collective-permute-start.4
  0.5 0.7 pad_add_fusion.own_ref
  1.2 4.7 %collective-permute-start.3 = (s32[4,8]{1,0:T(4,128)S(1)}, s32[4,8]{1,0:T(4,128)S(1)}, u32[]{:S(2)}, u32[]{:S(2)}) collective-permute-start(s32[4,8]{1,0:T(4,128)S(1)} %pad_add_fusion.own_ref), channel_id=1, source_target_pairs={{0,12},{4,8},{8,4},{12,0},{1,13},{5,9},{9,5},{13,1},{2,14},{6,10},... | collective-permute-start | bytes 392 | tf_op jit(solution)/shard_map/ppermute | solution.py:359
  5.8 0.6 collective-permute-start.1
  6.5 1.3 %plan.1 = (s32[16]{0:T(128)S(1)}, s32[16]{0:T(128)S(1)}, s32[16]{0:T(128)S(1)}) custom-call(s32[4,8]{1,0:T(4,128)S(1)} %pad_add_fusion.own_ref), custom_call_target="tpu_custom_call" | custom-call | flops 10000000000 | bytes 1024 | tf_op jit(solution)/shard_map/plan/pallas_call | solution.py:75
  7.8 1.3 %encode_local.1 = bf16[4,32,896]{2,1,0:T(8,128)(2,1)S(1)} custom-call(s32[16]{0:T(128)S(1)} %get-tuple-element.53.req_ref, s32[16]{0:T(128)S(1)} %get-tuple-element.54.pick_ref, bf16[512,896]{1,0:T(8,128)(2,1)S(1)} %copy-done.5, bf16[16,32,896]{2,1,0:T(8,128)(2,1)S(1)} %copy-done.4), custom_call_target="tpu_custom_call" | custom-call | flops 10000000000 | bytes 1024 | tf_op jit(solution)/shard_map/encode_local/pallas_call | solution.py:204
  9.1 1.3 %collective-permute-done.2.refs_1_ = s32[4,8]{1,0:T(4,128)S(1)} collective-permute-done((s32[4,8]{1,0:T(4,128)S(1)}, s32[4,8]{1,0:T(4,128)S(1)}, u32[]{:S(2)}, u32[]{:S(2)}) %collective-permute-start.2) | collective-permute-done | bytes 160 | tf_op jit(solution)/shard_map/ppermute | solution.py:359
  10.3 0.8 fetch.1
  11.1 0.2 collective-permute-start.5
  11.4 1.5 %collective-permute-start = (bf16[4,32,896]{2,1,0:T(8,128)(2,1)S(1)}, bf16[4,32,896]{2,1,0:T(8,128)(2,1)S(1)}, u32[]{:S(2)}, u32[]{:S(2)}) collective-permute-start(bf16[4,32,896]{2,1,0:T(8,128)(2,1)S(1)} %encode_local.1), channel_id=1, source_target_pairs={{0,2},{2,0},{1,3},{3,1},{4,6},{6,4},{5,7},{7,5},{8,10},{10,8},{9,1... | collective-permute-start | bytes 688136 | tf_op jit(solution)/shard_map/ppermute | solution.py:348
  12.8 2.9 %collective-permute-start.7 = (bf16[4,32,896]{2,1,0:T(8,128)(2,1)S(1)}, bf16[4,32,896]{2,1,0:T(8,128)(2,1)S(1)}, u32[]{:S(2)}, u32[]{:S(2)}) collective-permute-start(bf16[4,32,896]{2,1,0:T(8,128)(2,1)S(1)} %get-tuple-element.59), channel_id=1, source_target_pairs={{0,8},{4,12},{8,0},{12,4},{1,9},{5,13},{9,1},{13,5},{2,10},{6,14},... | collective-permute-start | bytes 688136 | tf_op jit(solution)/shard_map/ppermute | solution.py:368
  15.8 5.6 %collective-permute-done.5.refs_0_ = bf16[4,32,896]{2,1,0:T(8,128)(2,1)S(1)} collective-permute-done((bf16[4,32,896]{2,1,0:T(8,128)(2,1)S(1)}, bf16[4,32,896]{2,1,0:T(8,128)(2,1)S(1)}, u32[]{:S(2)}, u32[]{:S(2)}) %collective-permute-start.5) | collective-permute-done | bytes 229408 | tf_op jit(solution)/shard_map/ppermute | solution.py:368
  21.4 1.3 %encode.4 = bf16[4,32,896]{2,1,0:T(8,128)(2,1)S(1)} custom-call(s32[16]{0:T(128)S(1)} %get-tuple-element.53.req_ref, bf16[512,896]{1,0:T(8,128)(2,1)S(1)} %copy-done.5, bf16[4,32,896]{2,1,0:T(8,128)(2,1)S(1)} %collective-permute-done.5.refs_0_), custom_call_target="tpu_custom_call" | custom-call | flops 10000000000 | bytes 1024 | tf_op jit(solution)/shard_map/encode/pallas_call | solution.py:185
  22.6 2.5 %collective-permute-start.8 = (bf16[4,32,896]{2,1,0:T(8,128)(2,1)S(1)}, bf16[4,32,896]{2,1,0:T(8,128)(2,1)S(1)}, u32[]{:S(2)}, u32[]{:S(2)}) collective-permute-start(bf16[4,32,896]{2,1,0:T(8,128)(2,1)S(1)} %encode.4), channel_id=1, source_target_pairs={{0,2},{2,0},{1,3},{3,1},{4,6},{6,4},{5,7},{7,5},{8,10},{10,8},{9,1... | collective-permute-start | bytes 688136 | tf_op jit(solution)/shard_map/ppermute | solution.py:348
  25.2 0.1 collective-permute-start.6
  25.3 0.4 collective-permute-done.7.refs_0_
  25.7 1.3 %encode.5 = bf16[4,32,896]{2,1,0:T(8,128)(2,1)S(1)} custom-call(s32[16]{0:T(128)S(1)} %get-tuple-element.53.req_ref, bf16[512,896]{1,0:T(8,128)(2,1)S(1)} %copy-done.5, bf16[4,32,896]{2,1,0:T(8,128)(2,1)S(1)} %collective-permute-done.7.refs_0_), custom_call_target="tpu_custom_call" | custom-call | flops 10000000000 | bytes 1024 | tf_op jit(solution)/shard_map/encode/pallas_call | solution.py:185
  27.0 2.5 %collective-permute-start.13 = (bf16[2,32,896]{2,1,0:T(8,128)(2,1)S(1)}, bf16[2,32,896]{2,1,0:T(8,128)(2,1)S(1)}, u32[]{:S(2)}, u32[]{:S(2)}) collective-permute-start(bf16[2,32,896]{2,1,0:T(8,128)(2,1)S(1)} %get-tuple-element.76), channel_id=1, source_target_pairs={{0,12},{4,8},{8,4},{12,0},{1,13},{5,9},{9,5},{13,1},{2,14},{6,10},... | collective-permute-start | bytes 344072 | tf_op jit(solution)/shard_map/ppermute | solution.py:368
  29.5 1.4 %collective-permute-start.10 = (bf16[2,32,896]{2,1,0:T(8,128)(2,1)S(1)}, bf16[2,32,896]{2,1,0:T(8,128)(2,1)S(1)}, u32[]{:S(2)}, u32[]{:S(2)}) collective-permute-start(bf16[2,32,896]{2,1,0:T(8,128)(2,1)S(1)} %get-tuple-element.70), channel_id=1, source_target_pairs={{0,12},{4,8},{8,4},{12,0},{1,13},{5,9},{9,5},{13,1},{2,14},{6,10},... | collective-permute-start | bytes 344072 | tf_op jit(solution)/shard_map/ppermute | solution.py:368
  30.9 0.5 collective-permute-start.11
  31.4 1.3 %project.3.refs_0_ = bf16[4,4,32,1024]{3,2,1,0:T(8,128)(2,1)S(1)} custom-call(bf16[2,4,32,896]{3,2,1,0:T(8,128)(2,1)S(1)} %pad_maximum_fusion.refs_0_, bf16[2,4,32,896]{3,2,1,0:T(8,128)(2,1)S(1)} %collective-permute-done.6.refs_1_, bf16[896,512]{1,0:T(8,128)(2,1)S(1)} %copy-done.1, bf16[896,512]{1,0:T(8,128)(2,1)S(1)} %copy-done.2), custom_call_target="tpu_custom_call" | custom-call | flops 100000000 | bytes 1024 | tf_op jit(solution)/shard_map/project/pallas_call | solution.py:237
  32.8 3.7 %collective-permute-done.10.refs_0_ = bf16[2,32,896]{2,1,0:T(8,128)(2,1)S(1)} collective-permute-done((bf16[2,32,896]{2,1,0:T(8,128)(2,1)S(1)}, bf16[2,32,896]{2,1,0:T(8,128)(2,1)S(1)}, u32[]{:S(2)}, u32[]{:S(2)}) %collective-permute-start.10) | collective-permute-done | bytes 114720 | tf_op jit(solution)/shard_map/ppermute | solution.py:368
  36.6 1.1 %encode.6 = bf16[2,32,896]{2,1,0:T(8,128)(2,1)S(1)} custom-call(s32[16]{0:T(128)S(1)} %get-tuple-element.53.req_ref, bf16[512,896]{1,0:T(8,128)(2,1)S(1)} %copy-done.5, bf16[2,32,896]{2,1,0:T(8,128)(2,1)S(1)} %collective-permute-done.10.refs_0_), custom_call_target="tpu_custom_call" | custom-call | flops 10000000000 | bytes 1024 | tf_op jit(solution)/shard_map/encode/pallas_call | solution.py:185
  37.6 0.2 collective-permute-start.14
  37.8 1.3 %project.4.refs_1_ = bf16[4,4,32,1024]{3,2,1,0:T(8,128)(2,1)S(1)} custom-call(bf16[2,4,32,896]{3,2,1,0:T(8,128)(2,1)S(1)} %pad_maximum_fusion.1.refs_0_, bf16[2,4,32,896]{3,2,1,0:T(8,128)(2,1)S(1)} %collective-permute-done.9.refs_1_, bf16[896,512]{1,0:T(8,128)(2,1)S(1)} %copy-done.1, bf16[896,512]{1,0:T(8,128)(2,1)S(1)} %copy-done.2), custom_call_target="tpu_custom_call" | custom-call | flops 100000000 | bytes 1024 | tf_op jit(solution)/shard_map/project/pallas_call | solution.py:237
  39.3 1.1 %encode.7 = bf16[2,32,896]{2,1,0:T(8,128)(2,1)S(1)} custom-call(s32[16]{0:T(128)S(1)} %get-tuple-element.53.req_ref, bf16[512,896]{1,0:T(8,128)(2,1)S(1)} %copy-done.5, bf16[2,32,896]{2,1,0:T(8,128)(2,1)S(1)} %collective-permute-done.13.refs_0_), custom_call_target="tpu_custom_call" | custom-call | flops 10000000000 | bytes 1024 | tf_op jit(solution)/shard_map/encode/pallas_call | solution.py:185
  40.3 2.0 %collective-permute-start.15 = (bf16[2,32,896]{2,1,0:T(8,128)(2,1)S(1)}, bf16[2,32,896]{2,1,0:T(8,128)(2,1)S(1)}, u32[]{:S(2)}, u32[]{:S(2)}) collective-permute-start(bf16[2,32,896]{2,1,0:T(8,128)(2,1)S(1)} %encode.7), channel_id=1, source_target_pairs={{0,2},{2,0},{1,3},{3,1},{4,6},{6,4},{5,7},{7,5},{8,10},{10,8},{9,1... | collective-permute-start | bytes 344072 | tf_op jit(solution)/shard_map/ppermute | solution.py:348
  42.3 1.2 %project.5.refs_2_ = bf16[4,4,32,1024]{3,2,1,0:T(8,128)(2,1)S(1)} custom-call(bf16[2,4,32,896]{3,2,1,0:T(8,128)(2,1)S(1)} %pad_maximum_fusion.2.refs_0_, bf16[2,4,32,896]{3,2,1,0:T(8,128)(2,1)S(1)} %collective-permute-done.12.refs_1_, bf16[896,512]{1,0:T(8,128)(2,1)S(1)} %copy-done.1, bf16[896,512]{1,0:T(8,128)(2,1)S(1)} %copy-done.2), custom_call_target="tpu_custom_call" | custom-call | flops 100000000 | bytes 1024 | tf_op jit(solution)/shard_map/project/pallas_call | solution.py:237
  43.6 2.5 %collective-permute-done.15 = bf16[2,32,896]{2,1,0:T(8,128)(2,1)S(1)} collective-permute-done((bf16[2,32,896]{2,1,0:T(8,128)(2,1)S(1)}, bf16[2,32,896]{2,1,0:T(8,128)(2,1)S(1)}, u32[]{:S(2)}, u32[]{:S(2)}) %collective-permute-start.15) | collective-permute-done | bytes 114720 | tf_op jit(solution)/shard_map/ppermute | solution.py:348
  46.2 0.1 collective-permute-start.16
  46.3 1.8 %collective-permute-done.16.refs_4_ = bf16[2,4,32,896]{3,2,1,0:T(8,128)(2,1)S(1)} collective-permute-done((bf16[2,4,32,896]{3,2,1,0:T(8,128)(2,1)S(1)}, bf16[2,4,32,896]{3,2,1,0:T(8,128)(2,1)S(1)}, u32[]{:S(2)}, u32[]{:S(2)}) %collective-permute-start.16) | collective-permute-done | bytes 458784 | tf_op jit(solution)/shard_map/ppermute | solution.py:351
  48.1 3.4 %attend.2 = (bf16[1,128,512]{2,1,0:T(8,128)(2,1)S(1)}, bf16[1,128,512]{2,1,0:T(8,128)(2,1)S(1)}) custom-call(s32[16]{0:T(128)S(1)} %get-tuple-element.52.slot_ref, bf16[512,512]{1,0:T(8,128)(2,1)S(1)} %copy-done.3, bf16[4,4,32,1024]{3,2,1,0:T(8,128)(2,1)S(1)} %project.3.refs_0_, bf16[4,4,32,1024]{3,2,1,0:T(8,128)(2,1)S(1)} %project.4.refs_1_, ...), custom_call_target="tpu_custom_call" | custom-call | flops 1000000 | bytes 1024 | tf_op jit(solution)/shard_map/attend/pallas_call | solution.py:303
  51.5 0.2 collective-permute-start.17
  51.7 1.2 %collective-permute-done.17.refs_1_ = bf16[1,128,512]{2,1,0:T(8,128)(2,1)S(1)} collective-permute-done((bf16[1,128,512]{2,1,0:T(8,128)(2,1)S(1)}, bf16[1,128,512]{2,1,0:T(8,128)(2,1)S(1)}, u32[]{:S(2)}, u32[]{:S(2)}) %collective-permute-start.17) | collective-permute-done | bytes 131104 | tf_op jit(solution)/shard_map/ppermute | solution.py:394
  52.9 2.0 %out_project.5 = bf16[128,1536]{1,0:T(8,128)(2,1)S(1)} custom-call(bf16[1,128,512]{2,1,0:T(8,128)(2,1)S(1)} %get-tuple-element.93.refs_0_, bf16[1,128,512]{2,1,0:T(8,128)(2,1)S(1)} %collective-permute-done.17.refs_1_, bf16[512,4096]{1,0:T(8,128)(2,1)S(1)} %copy-done, bf16[512,4096]{1,0:T(8,128)(2,1)S(1)} %collective-permute-done.4.refs_3_), custom_call_target="tpu_custom_call" | custom-call | flops 1000000 | bytes 1024 | tf_op jit(solution)/shard_map/out_project/pallas_call | solution.py:323
  54.9 1.8 %collective-permute-start.19 = (bf16[128,1536]{1,0:T(8,128)(2,1)S(1)}, bf16[128,1536]{1,0:T(8,128)(2,1)S(1)}, u32[]{:S(2)}, u32[]{:S(2)}) collective-permute-start(bf16[128,1536]{1,0:T(8,128)(2,1)S(1)} %out_project.5), channel_id=1, source_target_pairs={{0,2},{2,0},{1,3},{3,1},{4,6},{6,4},{5,7},{7,5},{8,10},{10,8},{9,1... | collective-permute-start | bytes 1179656 | tf_op jit(solution)/shard_map/ppermute | solution.py:408
  56.7 1.7 %out_project.6 = bf16[128,1280]{1,0:T(8,128)(2,1)S(1)} custom-call(bf16[1,128,512]{2,1,0:T(8,128)(2,1)S(1)} %get-tuple-element.93.refs_0_, bf16[1,128,512]{2,1,0:T(8,128)(2,1)S(1)} %collective-permute-done.17.refs_1_, bf16[512,4096]{1,0:T(8,128)(2,1)S(1)} %copy-done, bf16[512,4096]{1,0:T(8,128)(2,1)S(1)} %collective-permute-done.4.refs_3_), custom_call_target="tpu_custom_call" | custom-call | flops 1000000 | bytes 1024 | tf_op jit(solution)/shard_map/out_project/pallas_call | solution.py:323
  58.4 0.3 collective-permute-start.20
  58.8 1.0 %out_project.7 = bf16[128,768]{1,0:T(8,128)(2,1)S(1)} custom-call(bf16[1,128,512]{2,1,0:T(8,128)(2,1)S(1)} %get-tuple-element.93.refs_0_, bf16[1,128,512]{2,1,0:T(8,128)(2,1)S(1)} %collective-permute-done.17.refs_1_, bf16[512,4096]{1,0:T(8,128)(2,1)S(1)} %copy-done, bf16[512,4096]{1,0:T(8,128)(2,1)S(1)} %collective-permute-done.4.refs_3_), custom_call_target="tpu_custom_call" | custom-call | flops 1000000 | bytes 1024 | tf_op jit(solution)/shard_map/out_project/pallas_call | solution.py:323
  59.8 1.8 %collective-permute-start.21 = (bf16[128,768]{1,0:T(8,128)(2,1)S(1)}, bf16[128,768]{1,0:T(8,128)(2,1)S(1)}, u32[]{:S(2)}, u32[]{:S(2)}) collective-permute-start(bf16[128,768]{1,0:T(8,128)(2,1)S(1)} %out_project.7), channel_id=1, source_target_pairs={{0,2},{2,0},{1,3},{3,1},{4,6},{6,4},{5,7},{7,5},{8,10},{10,8},{9,1... | collective-permute-start | bytes 589832 | tf_op jit(solution)/shard_map/ppermute | solution.py:408
  61.6 0.7 out_project.8
  62.3 3.4 %attend.3 = (bf16[1,128,512]{2,1,0:T(8,128)(2,1)S(1)}, bf16[1,128,512]{2,1,0:T(8,128)(2,1)S(1)}) custom-call(s32[16]{0:T(128)S(1)} %get-tuple-element.52.slot_ref, bf16[512,512]{1,0:T(8,128)(2,1)S(1)} %copy-done.3, bf16[4,4,32,1024]{3,2,1,0:T(8,128)(2,1)S(1)} %project.3.refs_0_, bf16[4,4,32,1024]{3,2,1,0:T(8,128)(2,1)S(1)} %project.4.refs_1_, ...), custom_call_target="tpu_custom_call" | custom-call | flops 1000000 | bytes 1024 | tf_op jit(solution)/shard_map/attend/pallas_call | solution.py:303
  65.7 0.1 collective-permute-start.18
  65.8 0.3 collective-permute-start.22
  66.1 1.0 %collective-permute-done.18.refs_1_ = bf16[1,128,512]{2,1,0:T(8,128)(2,1)S(1)} collective-permute-done((bf16[1,128,512]{2,1,0:T(8,128)(2,1)S(1)}, bf16[1,128,512]{2,1,0:T(8,128)(2,1)S(1)}, u32[]{:S(2)}, u32[]{:S(2)}) %collective-permute-start.18) | collective-permute-done | bytes 131104 | tf_op jit(solution)/shard_map/ppermute | solution.py:394
  67.1 5.2 %out_project.9 = bf16[128,4096]{1,0:T(8,128)(2,1)S(1)} custom-call(bf16[1,128,512]{2,1,0:T(8,128)(2,1)S(1)} %get-tuple-element.97.refs_0_, bf16[1,128,512]{2,1,0:T(8,128)(2,1)S(1)} %collective-permute-done.18.refs_1_, bf16[512,4096]{1,0:T(8,128)(2,1)S(1)} %copy-done, bf16[512,4096]{1,0:T(8,128)(2,1)S(1)} %collective-permute-done.4.refs_3_), custom_call_target="tpu_custom_call" | custom-call | flops 1000000 | bytes 1024 | tf_op jit(solution)/shard_map/out_project/pallas_call | solution.py:323
  72.4 7.8 %collective-permute-done.22 = bf16[128,512]{1,0:T(8,128)(2,1)S(1)} collective-permute-done((bf16[128,512]{1,0:T(8,128)(2,1)S(1)}, bf16[128,512]{1,0:T(8,128)(2,1)S(1)}, u32[]{:S(2)}, u32[]{:S(2)}) %collective-permute-start.22) | collective-permute-done | bytes 131104 | tf_op jit(solution)/shard_map/ppermute | solution.py:408
  80.2 1.2 %add_convert_fusion = bf16[128,4096]{1,0:T(8,128)(2,1)} fusion(bf16[128,4096]{1,0:T(8,128)(2,1)S(1)} %out_project.9, bf16[128,512]{1,0:T(8,128)(2,1)S(1)} %collective-permute-done.22, bf16[128,768]{1,0:T(8,128)(2,1)S(1)} %collective-permute-done.21, bf16[128,1280]{1,0:T(8,128)(2,1)S(1)} %collective-permute-done.20, bf16[128,1536]{1,0:T(8,128)(2,1)S(1)} %collective-permute-done.19), kind=kLoop, calls=%fused_computation | loop fusion | flops 5767168 | bytes 3145728 | tf_op jit(solution)/shard_map/convert_element_type | solution.py:413
  (34 shorter events, 0.5 us)
Async XLA Ops:
  0.0 10.3 %collective-permute-start.4 = (bf16[512,4096]{1,0:T(8,128)(2,1)}, bf16[512,4096]{1,0:T(8,128)(2,1)S(1)}, u32[]{:S(2)}, u32[]{:S(2)}) collective-permute-start(bf16[512,4096]{1,0:T(8,128)(2,1)} %refs_2_.15), channel_id=1, source_target_pairs={{0,1},{1,0},{2,3},{3,2},{4,5},{5,4},{6,7},{7,6},{8,9},{9,8},{10,11... | collective-permute-start | bytes 12582920 | tf_op jit(solution)/shard_map/ppermute | solution.py:351
  1.2 6.6 %copy-start.4 = (bf16[16,32,896]{2,1,0:T(8,128)(2,1)S(1)}, bf16[16,32,896]{2,1,0:T(8,128)(2,1)}, u32[]{:S(2)}) copy-start(bf16[16,32,896]{2,1,0:T(8,128)(2,1)} %refs_3_.4) | copy-start | bytes 2752516
  1.2 6.6 %copy-start.5 = (bf16[512,896]{1,0:T(8,128)(2,1)S(1)}, bf16[512,896]{1,0:T(8,128)(2,1)}, u32[]{:S(2)}) copy-start(bf16[512,896]{1,0:T(8,128)(2,1)} %states_ref.9) | copy-start | bytes 2752516
  1.2 7.9 %collective-permute-start.3 = (s32[4,8]{1,0:T(4,128)S(1)}, s32[4,8]{1,0:T(4,128)S(1)}, u32[]{:S(2)}, u32[]{:S(2)}) collective-permute-start(s32[4,8]{1,0:T(4,128)S(1)} %pad_add_fusion.own_ref), channel_id=1, source_target_pairs={{0,12},{4,8},{8,4},{12,0},{1,13},{5,9},{9,5},{13,1},{2,14},{6,10},... | collective-permute-start | bytes 392 | tf_op jit(solution)/shard_map/ppermute | solution.py:359
  5.8 4.5 %collective-permute-start.2 = (s32[4,8]{1,0:T(4,128)S(1)}, s32[4,8]{1,0:T(4,128)S(1)}, u32[]{:S(2)}, u32[]{:S(2)}) collective-permute-start(s32[4,8]{1,0:T(4,128)S(1)} %pad_add_fusion.own_ref), channel_id=1, source_target_pairs={{0,8},{4,12},{8,0},{12,4},{1,9},{5,13},{9,1},{13,5},{2,10},{6,14},... | collective-permute-start | bytes 392 | tf_op jit(solution)/shard_map/ppermute | solution.py:359
  5.8 4.5 %collective-permute-start.1 = (s32[4,8]{1,0:T(4,128)S(1)}, s32[4,8]{1,0:T(4,128)S(1)}, u32[]{:S(2)}, u32[]{:S(2)}) collective-permute-start(s32[4,8]{1,0:T(4,128)S(1)} %pad_add_fusion.own_ref), channel_id=1, source_target_pairs={{0,4},{4,0},{8,12},{12,8},{1,5},{5,1},{9,13},{13,9},{2,6},{6,2},{1... | collective-permute-start | bytes 392 | tf_op jit(solution)/shard_map/ppermute | solution.py:359
  11.1 10.2 %collective-permute-start.5 = (bf16[4,32,896]{2,1,0:T(8,128)(2,1)S(1)}, bf16[4,32,896]{2,1,0:T(8,128)(2,1)S(1)}, u32[]{:S(2)}, u32[]{:S(2)}) collective-permute-start(bf16[4,32,896]{2,1,0:T(8,128)(2,1)S(1)} %get-tuple-element.58), channel_id=1, source_target_pairs={{0,4},{4,0},{8,12},{12,8},{1,5},{5,1},{9,13},{13,9},{2,6},{6,2},{1... | collective-permute-start | bytes 688136 | tf_op jit(solution)/shard_map/ppermute | solution.py:368
  11.4 13.8 %collective-permute-start = (bf16[4,32,896]{2,1,0:T(8,128)(2,1)S(1)}, bf16[4,32,896]{2,1,0:T(8,128)(2,1)S(1)}, u32[]{:S(2)}, u32[]{:S(2)}) collective-permute-start(bf16[4,32,896]{2,1,0:T(8,128)(2,1)S(1)} %encode_local.1), channel_id=1, source_target_pairs={{0,2},{2,0},{1,3},{3,1},{4,6},{6,4},{5,7},{7,5},{8,10},{10,8},{9,1... | collective-permute-start | bytes 688136 | tf_op jit(solution)/shard_map/ppermute | solution.py:348
  12.8 12.9 %collective-permute-start.7 = (bf16[4,32,896]{2,1,0:T(8,128)(2,1)S(1)}, bf16[4,32,896]{2,1,0:T(8,128)(2,1)S(1)}, u32[]{:S(2)}, u32[]{:S(2)}) collective-permute-start(bf16[4,32,896]{2,1,0:T(8,128)(2,1)S(1)} %get-tuple-element.59), channel_id=1, source_target_pairs={{0,8},{4,12},{8,0},{12,4},{1,9},{5,13},{9,1},{13,5},{2,10},{6,14},... | collective-permute-start | bytes 688136 | tf_op jit(solution)/shard_map/ppermute | solution.py:368
  22.6 10.0 %collective-permute-start.8 = (bf16[4,32,896]{2,1,0:T(8,128)(2,1)S(1)}, bf16[4,32,896]{2,1,0:T(8,128)(2,1)S(1)}, u32[]{:S(2)}, u32[]{:S(2)}) collective-permute-start(bf16[4,32,896]{2,1,0:T(8,128)(2,1)S(1)} %encode.4), channel_id=1, source_target_pairs={{0,2},{2,0},{1,3},{3,1},{4,6},{6,4},{5,7},{7,5},{8,10},{10,8},{9,1... | collective-permute-start | bytes 688136 | tf_op jit(solution)/shard_map/ppermute | solution.py:348
  25.2 6.2 %copy-start.1 = (bf16[896,512]{1,0:T(8,128)(2,1)S(1)}, bf16[896,512]{1,0:T(8,128)(2,1)}, u32[]{:S(2)}) copy-start(bf16[896,512]{1,0:T(8,128)(2,1)} %refs_5_.3) | copy-start | bytes 2752516
  25.2 6.2 %copy-start.2 = (bf16[896,512]{1,0:T(8,128)(2,1)S(1)}, bf16[896,512]{1,0:T(8,128)(2,1)}, u32[]{:S(2)}) copy-start(bf16[896,512]{1,0:T(8,128)(2,1)} %refs_6_.3) | copy-start | bytes 2752516
  25.2 6.2 %collective-permute-start.6 = (bf16[2,4,32,896]{3,2,1,0:T(8,128)(2,1)S(1)}, bf16[2,4,32,896]{3,2,1,0:T(8,128)(2,1)S(1)}, u32[]{:S(2)}, u32[]{:S(2)}) collective-permute-start(bf16[2,4,32,896]{3,2,1,0:T(8,128)(2,1)S(1)} %pad_maximum_fusion.refs_0_), channel_id=1, source_target_pairs={{0,1},{1,0},{2,3},{3,2},{4,5},{5,4},{6,7},{7,6},{8,9},{9,8},{10,11... | collective-permute-start | bytes 1376264 | tf_op jit(solution)/shard_map/ppermute | solution.py:351
  27.0 12.3 %collective-permute-start.13 = (bf16[2,32,896]{2,1,0:T(8,128)(2,1)S(1)}, bf16[2,32,896]{2,1,0:T(8,128)(2,1)S(1)}, u32[]{:S(2)}, u32[]{:S(2)}) collective-permute-start(bf16[2,32,896]{2,1,0:T(8,128)(2,1)S(1)} %get-tuple-element.76), channel_id=1, source_target_pairs={{0,12},{4,8},{8,4},{12,0},{1,13},{5,9},{9,5},{13,1},{2,14},{6,10},... | collective-permute-start | bytes 344072 | tf_op jit(solution)/shard_map/ppermute | solution.py:368
  29.5 7.0 %collective-permute-start.10 = (bf16[2,32,896]{2,1,0:T(8,128)(2,1)S(1)}, bf16[2,32,896]{2,1,0:T(8,128)(2,1)S(1)}, u32[]{:S(2)}, u32[]{:S(2)}) collective-permute-start(bf16[2,32,896]{2,1,0:T(8,128)(2,1)S(1)} %get-tuple-element.70), channel_id=1, source_target_pairs={{0,12},{4,8},{8,4},{12,0},{1,13},{5,9},{9,5},{13,1},{2,14},{6,10},... | collective-permute-start | bytes 344072 | tf_op jit(solution)/shard_map/ppermute | solution.py:368
  30.9 8.2 %collective-permute-start.11 = (bf16[4,32,896]{2,1,0:T(8,128)(2,1)S(1)}, bf16[4,32,896]{2,1,0:T(8,128)(2,1)S(1)}, u32[]{:S(2)}, u32[]{:S(2)}) collective-permute-start(bf16[4,32,896]{2,1,0:T(8,128)(2,1)S(1)} %encode.5), channel_id=1, source_target_pairs={{0,2},{2,0},{1,3},{3,1},{4,6},{6,4},{5,7},{7,5},{8,10},{10,8},{9,1... | collective-permute-start | bytes 688136 | tf_op jit(solution)/shard_map/ppermute | solution.py:348
  32.7 5.1 %collective-permute-start.9 = (bf16[2,4,32,896]{3,2,1,0:T(8,128)(2,1)S(1)}, bf16[2,4,32,896]{3,2,1,0:T(8,128)(2,1)S(1)}, u32[]{:S(2)}, u32[]{:S(2)}) collective-permute-start(bf16[2,4,32,896]{3,2,1,0:T(8,128)(2,1)S(1)} %pad_maximum_fusion.1.refs_0_), channel_id=1, source_target_pairs={{0,1},{1,0},{2,3},{3,2},{4,5},{5,4},{6,7},{7,6},{8,9},{9,8},{10,11... | collective-permute-start | bytes 1376264 | tf_op jit(solution)/shard_map/ppermute | solution.py:351
  37.6 5.9 %collective-permute-start.14 = (bf16[2,32,896]{2,1,0:T(8,128)(2,1)S(1)}, bf16[2,32,896]{2,1,0:T(8,128)(2,1)S(1)}, u32[]{:S(2)}, u32[]{:S(2)}) collective-permute-start(bf16[2,32,896]{2,1,0:T(8,128)(2,1)S(1)} %encode.6), channel_id=1, source_target_pairs={{0,2},{2,0},{1,3},{3,1},{4,6},{6,4},{5,7},{7,5},{8,10},{10,8},{9,1... | collective-permute-start | bytes 344072 | tf_op jit(solution)/shard_map/ppermute | solution.py:348
  39.2 3.1 %collective-permute-start.12 = (bf16[2,4,32,896]{3,2,1,0:T(8,128)(2,1)S(1)}, bf16[2,4,32,896]{3,2,1,0:T(8,128)(2,1)S(1)}, u32[]{:S(2)}, u32[]{:S(2)}) collective-permute-start(bf16[2,4,32,896]{3,2,1,0:T(8,128)(2,1)S(1)} %pad_maximum_fusion.2.refs_0_), channel_id=1, source_target_pairs={{0,1},{1,0},{2,3},{3,2},{4,5},{5,4},{6,7},{7,6},{8,9},{9,8},{10,11... | collective-permute-start | bytes 1376264 | tf_op jit(solution)/shard_map/ppermute | solution.py:351
  40.3 7.8 %copy-start.3 = (bf16[512,512]{1,0:T(8,128)(2,1)S(1)}, bf16[512,512]{1,0:T(8,128)(2,1)}, u32[]{:S(2)}) copy-start(bf16[512,512]{1,0:T(8,128)(2,1)} %q_ref.2) | copy-start | bytes 1572868
  40.3 5.8 %collective-permute-start.15 = (bf16[2,32,896]{2,1,0:T(8,128)(2,1)S(1)}, bf16[2,32,896]{2,1,0:T(8,128)(2,1)S(1)}, u32[]{:S(2)}, u32[]{:S(2)}) collective-permute-start(bf16[2,32,896]{2,1,0:T(8,128)(2,1)S(1)} %encode.7), channel_id=1, source_target_pairs={{0,2},{2,0},{1,3},{3,1},{4,6},{6,4},{5,7},{7,5},{8,10},{10,8},{9,1... | collective-permute-start | bytes 344072 | tf_op jit(solution)/shard_map/ppermute | solution.py:348
  46.2 1.9 %collective-permute-start.16 = (bf16[2,4,32,896]{3,2,1,0:T(8,128)(2,1)S(1)}, bf16[2,4,32,896]{3,2,1,0:T(8,128)(2,1)S(1)}, u32[]{:S(2)}, u32[]{:S(2)}) collective-permute-start(bf16[2,4,32,896]{3,2,1,0:T(8,128)(2,1)S(1)} %pad_maximum_fusion.3.refs_3_), channel_id=1, source_target_pairs={{0,1},{1,0},{2,3},{3,2},{4,5},{5,4},{6,7},{7,6},{8,9},{9,8},{10,11... | collective-permute-start | bytes 1376264 | tf_op jit(solution)/shard_map/ppermute | solution.py:351
  48.1 4.8 %copy-start = (bf16[512,4096]{1,0:T(8,128)(2,1)S(1)}, bf16[512,4096]{1,0:T(8,128)(2,1)}, u32[]{:S(2)}) copy-start(bf16[512,4096]{1,0:T(8,128)(2,1)} %refs_2_.15) | copy-start | bytes 12582916
  51.5 1.4 %collective-permute-start.17 = (bf16[1,128,512]{2,1,0:T(8,128)(2,1)S(1)}, bf16[1,128,512]{2,1,0:T(8,128)(2,1)S(1)}, u32[]{:S(2)}, u32[]{:S(2)}) collective-permute-start(bf16[1,128,512]{2,1,0:T(8,128)(2,1)S(1)} %get-tuple-element.85), channel_id=1, source_target_pairs={{0,1},{1,0},{2,3},{3,2},{4,5},{5,4},{6,7},{7,6},{8,9},{9,8},{10,11... | collective-permute-start | bytes 393224 | tf_op jit(solution)/shard_map/ppermute | solution.py:394
  54.9 25.3 %collective-permute-start.19 = (bf16[128,1536]{1,0:T(8,128)(2,1)S(1)}, bf16[128,1536]{1,0:T(8,128)(2,1)S(1)}, u32[]{:S(2)}, u32[]{:S(2)}) collective-permute-start(bf16[128,1536]{1,0:T(8,128)(2,1)S(1)} %out_project.5), channel_id=1, source_target_pairs={{0,2},{2,0},{1,3},{3,1},{4,6},{6,4},{5,7},{7,5},{8,10},{10,8},{9,1... | collective-permute-start | bytes 1179656 | tf_op jit(solution)/shard_map/ppermute | solution.py:408
  58.4 21.8 %collective-permute-start.20 = (bf16[128,1280]{1,0:T(8,128)(2,1)S(1)}, bf16[128,1280]{1,0:T(8,128)(2,1)S(1)}, u32[]{:S(2)}, u32[]{:S(2)}) collective-permute-start(bf16[128,1280]{1,0:T(8,128)(2,1)S(1)} %out_project.6), channel_id=1, source_target_pairs={{0,2},{2,0},{1,3},{3,1},{4,6},{6,4},{5,7},{7,5},{8,10},{10,8},{9,1... | collective-permute-start | bytes 983048 | tf_op jit(solution)/shard_map/ppermute | solution.py:408
  59.8 20.4 %collective-permute-start.21 = (bf16[128,768]{1,0:T(8,128)(2,1)S(1)}, bf16[128,768]{1,0:T(8,128)(2,1)S(1)}, u32[]{:S(2)}, u32[]{:S(2)}) collective-permute-start(bf16[128,768]{1,0:T(8,128)(2,1)S(1)} %out_project.7), channel_id=1, source_target_pairs={{0,2},{2,0},{1,3},{3,1},{4,6},{6,4},{5,7},{7,5},{8,10},{10,8},{9,1... | collective-permute-start | bytes 589832 | tf_op jit(solution)/shard_map/ppermute | solution.py:408
  65.7 1.4 %collective-permute-start.18 = (bf16[1,128,512]{2,1,0:T(8,128)(2,1)S(1)}, bf16[1,128,512]{2,1,0:T(8,128)(2,1)S(1)}, u32[]{:S(2)}, u32[]{:S(2)}) collective-permute-start(bf16[1,128,512]{2,1,0:T(8,128)(2,1)S(1)} %get-tuple-element.98), channel_id=1, source_target_pairs={{0,1},{1,0},{2,3},{3,2},{4,5},{5,4},{6,7},{7,6},{8,9},{9,8},{10,11... | collective-permute-start | bytes 393224 | tf_op jit(solution)/shard_map/ppermute | solution.py:394
  65.8 14.4 %collective-permute-start.22 = (bf16[128,512]{1,0:T(8,128)(2,1)S(1)}, bf16[128,512]{1,0:T(8,128)(2,1)S(1)}, u32[]{:S(2)}, u32[]{:S(2)}) collective-permute-start(bf16[128,512]{1,0:T(8,128)(2,1)S(1)} %out_project.8), channel_id=1, source_target_pairs={{0,2},{2,0},{1,3},{3,1},{4,6},{6,4},{5,7},{7,5},{8,10},{10,8},{9,1... | collective-permute-start | bytes 393224 | tf_op jit(solution)/shard_map/ppermute | solution.py:408

commit v6 on v5

--- a/solution.py
+++ b/solution.py
@@ -11,8 +11,9 @@
 ENCODER_HEAD_DIM = 128
 F32 = jnp.float32
 BF16 = jnp.bfloat16
-LATER_GROUPS = 4
+LATER_GROUPS = 3
 COL_TILE = 256
+ENCODE_COST = (None, 0.1, 10, 10, 10)
 
 VMEM = pl.BlockSpec(memory_space=pltpu.VMEM)
 SMEM = pl.BlockSpec(memory_space=pltpu.SMEM)
@@ -180,7 +181,7 @@
         at = stop
 
 
-def encode(req, span_states, blocks, first, fanout, span_len):
+def encode(req, span_states, blocks, first, fanout, span_len, gflops):
     slots = sum(block.shape[0] for block in blocks)
     return pl.pallas_call(
         functools.partial(encode_kernel, first, fanout, span_len),
@@ -188,7 +189,7 @@
         in_specs=[SMEM, VMEM] + [VMEM] * len(blocks),
         out_specs=VMEM,
         compiler_params=params(16),
-        cost_estimate=cost(10),
+        cost_estimate=cost(gflops),
         name="encode",
     )(req, span_states, *blocks)
 
@@ -350,10 +351,13 @@
     def over_rep(array):
         return [array] + [lax.ppermute(array, "rep", shift_pairs(n_rep, s)) for s in range(1, n_rep)]
 
-    items = [(d, 0, cap) for d in range(1, n_lanes - 1)]
-    items += [(n_lanes - 1, 0, cap // 2), (n_lanes - 1, cap // 2, cap)]
-    size = -(-len(items) // LATER_GROUPS)
-    parts = [range(i, min(i + size, len(items))) for i in range(0, len(items), size)]
+    items = []
+    for d in range(1, n_lanes):
+        cuts = (0, cap // 2, cap) if d in (1, n_lanes - 1) else (0, cap)
+        items += [(d, low, high) for low, high in zip(cuts, cuts[1:])]
+    size = max(1, -(-(len(items) - 2) // LATER_GROUPS))
+    cuts = [0] + list(range(2, len(items), size)) + [len(items)]
+    parts = [range(low, high) for low, high in zip(cuts, cuts[1:])]
 
     own = jnp.concatenate([owners.T, entry_ids.T], axis=0)
     asked = [lax.ppermute(own, "lanes", lane_pairs(n_lanes, d, False)) for d in range(1, n_lanes)]
@@ -376,7 +380,7 @@
         if i + 2 <= len(parts):
             arrived.append(send(parts[i + 1], arrived[i], last))
         first = items[part[0]][0] * cap + items[part[0]][1]
-        encoded = encode(req, span_states, after(arrived[i], last), first, fanout, span_len)
+        encoded = encode(req, span_states, after(arrived[i], last), first, fanout, span_len, ENCODE_COST[i])
         crossed.append(over_heads(encoded))
         last = encoded
         if i >= 2:

time: 81.6 us -> 81.6 us (level)
  waiting for transfers between devices: 25.4 us -> 22.9 us
  starting transfers between devices: 24.4 us -> 26.7 us
    ppermute x4 -> x5, starting transfers between devices: 7.03 us -> 10.8 us  [send(): lax.ppermute(block, 'lanes', lane_pairs(n_lanes, items[i][0], True))]
    ppermute x4 -> x5, waiting for transfers between devices: 9.73 us -> 7.2 us  [send(): lax.ppermute(block, 'lanes', lane_pairs(n_lanes, items[i][0], True))]
    ppermute x5, starting transfers between devices: 6.69 us -> 5.21 us  [over_heads(): lax.ppermute(array, 'heads', shift_pairs(n_heads, s))]
    ppermute x3, waiting for transfers between devices: 1.26 us -> 0.01 us  [shards(): lax.ppermute(own, 'lanes', lane_pairs(n_lanes, d, False))]
    ppermute x5, waiting for transfers between devices: 2.54 us -> 3.79 us  [over_heads(): lax.ppermute(array, 'heads', shift_pairs(n_heads, s))]
    ppermute x4, waiting for transfers between devices: 7.85 us -> 8.83 us  [shards(): sent.append(lax.ppermute(partial, 'heads', shift_pairs(n_heads, t)))]
    ppermute x2, waiting for transfers between devices: 2.19 us -> 1.22 us  [mix(): lax.ppermute(outs[s], 'rep', shift_pairs(n_rep, s))]
  transfers between devices with their start and end apart: 23 -> 24, of which waited for: 9 -> 7; matrix products, arithmetic and copies ran while one was open for 1% -> 1% of each run, Pallas kernels for 28% -> 29%
where the time goes in v6:
time: 81.6 us; the launch traced here: 81.5 us
  Pallas kernels  29.4 us (36%)
  starting transfers between devices  26.7 us (33%)
  waiting for transfers between devices  22.9 us (28%)
  other arithmetic  2.18 us (3%)
    ppermute x5, starting transfers between devices, send(): lax.ppermute(block, 'lanes', lane_pairs(n_lanes, items[i][0], True))  10.8 us
    pallas_call x5, Pallas kernels, out_project(): pl.pallas_call(functools.partial(out_kernel, len(mixed)), grid=((stop - s...  10.6 us
    ppermute x4, waiting for transfers between devices, shards(): sent.append(lax.ppermute(partial, 'heads', shift_pairs(n_heads, t)))  8.83 us
    ppermute x5, waiting for transfers between devices, send(): lax.ppermute(block, 'lanes', lane_pairs(n_lanes, items[i][0], True))  7.2 us
    pallas_call x2, Pallas kernels, attend(): pl.pallas_call(functools.partial(attend_kernel, firsts, len(pieces), n_he...  6.83 us
    ppermute x3, starting transfers between devices, shards(): lax.ppermute(own, 'lanes', lane_pairs(n_lanes, d, False))  5.31 us
    ppermute x5, starting transfers between devices, over_heads(): lax.ppermute(array, 'heads', shift_pairs(n_heads, s))  5.21 us
    pallas_call x4, Pallas kernels, encode(): pl.pallas_call(functools.partial(encode_kernel, first, fanout, span_len),...  4.85 us
  transfers between devices with their start and end apart: 24, of which 7 were waited for; matrix products, arithmetic and copies ran while one was open for 1% of the time, Pallas kernels for 29%

profile of v6, /device:TPU:0, one launch (start us, length us, event | category | flops | bytes accessed | tf_op | source)
XLA Modules:
  0.0 81.5 jit_solution(1379052795929722474)
XLA Ops:
  0.0 0.5 collective-permute-start.4
  0.5 0.7 pad_add_fusion.own_ref
  1.2 4.7 %collective-permute-start.3 = (s32[4,8]{1,0:T(4,128)S(1)}, s32[4,8]{1,0:T(4,128)S(1)}, u32[]{:S(2)}, u32[]{:S(2)}) collective-permute-start(s32[4,8]{1,0:T(4,128)S(1)} %pad_add_fusion.own_ref), channel_id=1, source_target_pairs={{0,12},{4,8},{8,4},{12,0},{1,13},{5,9},{9,5},{13,1},{2,14},{6,10},... | collective-permute-start | bytes 392 | tf_op jit(solution)/shard_map/ppermute | solution.py:363
  5.8 0.6 collective-permute-start.1
  6.5 1.3 %plan.1 = (s32[16]{0:T(128)S(1)}, s32[16]{0:T(128)S(1)}, s32[16]{0:T(128)S(1)}) custom-call(s32[4,8]{1,0:T(4,128)S(1)} %pad_add_fusion.own_ref), custom_call_target="tpu_custom_call" | custom-call | flops 10000000000 | bytes 1024 | tf_op jit(solution)/shard_map/plan/pallas_call | solution.py:76
  7.8 1.3 %encode_local.1 = bf16[4,32,896]{2,1,0:T(8,128)(2,1)S(1)} custom-call(s32[16]{0:T(128)S(1)} %get-tuple-element.57.req_ref, s32[16]{0:T(128)S(1)} %get-tuple-element.58.pick_ref, bf16[512,896]{1,0:T(8,128)(2,1)S(1)} %copy-done.4, bf16[16,32,896]{2,1,0:T(8,128)(2,1)S(1)} %copy-done.5), custom_call_target="tpu_custom_call" | custom-call | flops 10000000000 | bytes 1024 | tf_op jit(solution)/shard_map/encode_local/pallas_call | solution.py:205
  9.1 1.7 %collective-permute-start = (bf16[4,32,896]{2,1,0:T(8,128)(2,1)S(1)}, bf16[4,32,896]{2,1,0:T(8,128)(2,1)S(1)}, u32[]{:S(2)}, u32[]{:S(2)}) collective-permute-start(bf16[4,32,896]{2,1,0:T(8,128)(2,1)S(1)} %encode_local.1), channel_id=1, source_target_pairs={{0,2},{2,0},{1,3},{3,1},{4,6},{6,4},{5,7},{7,5},{8,10},{10,8},{9,1... | collective-permute-start | bytes 688136 | tf_op jit(solution)/shard_map/ppermute | solution.py:349
  10.8 0.8 fetch.1
  11.6 1.3 %collective-permute-start.5 = (bf16[2,32,896]{2,1,0:T(8,128)(2,1)S(1)}, bf16[2,32,896]{2,1,0:T(8,128)(2,1)S(1)}, u32[]{:S(2)}, u32[]{:S(2)}) collective-permute-start(bf16[2,32,896]{2,1,0:T(8,128)(2,1)S(1)} %get-tuple-element.64), channel_id=1, source_target_pairs={{0,4},{4,0},{8,12},{12,8},{1,5},{5,1},{9,13},{13,9},{2,6},{6,2},{1... | collective-permute-start | bytes 344072 | tf_op jit(solution)/shard_map/ppermute | solution.py:372
  12.9 0.8 collective-permute-start.6
  13.7 2.2 %collective-permute-start.8 = (bf16[4,32,896]{2,1,0:T(8,128)(2,1)S(1)}, bf16[4,32,896]{2,1,0:T(8,128)(2,1)S(1)}, u32[]{:S(2)}, u32[]{:S(2)}) collective-permute-start(bf16[4,32,896]{2,1,0:T(8,128)(2,1)S(1)} %get-tuple-element.66), channel_id=1, source_target_pairs={{0,8},{4,12},{8,0},{12,4},{1,9},{5,13},{9,1},{13,5},{2,10},{6,14},... | collective-permute-start | bytes 688136 | tf_op jit(solution)/shard_map/ppermute | solution.py:372
  15.9 6.0 %collective-permute-done.5.refs_0_ = bf16[2,32,896]{2,1,0:T(8,128)(2,1)S(1)} collective-permute-done((bf16[2,32,896]{2,1,0:T(8,128)(2,1)S(1)}, bf16[2,32,896]{2,1,0:T(8,128)(2,1)S(1)}, u32[]{:S(2)}, u32[]{:S(2)}) %collective-permute-start.5) | collective-permute-done | bytes 114720 | tf_op jit(solution)/shard_map/ppermute | solution.py:372
  21.9 1.2 %collective-permute-done.6.refs_1_ = bf16[2,32,896]{2,1,0:T(8,128)(2,1)S(1)} collective-permute-done((bf16[2,32,896]{2,1,0:T(8,128)(2,1)S(1)}, bf16[2,32,896]{2,1,0:T(8,128)(2,1)S(1)}, u32[]{:S(2)}, u32[]{:S(2)}) %collective-permute-start.6) | collective-permute-done | bytes 114720 | tf_op jit(solution)/shard_map/ppermute | solution.py:372
  23.1 1.5 %encode.4 = bf16[4,32,896]{2,1,0:T(8,128)(2,1)S(1)} custom-call(s32[16]{0:T(128)S(1)} %get-tuple-element.57.req_ref, bf16[512,896]{1,0:T(8,128)(2,1)S(1)} %copy-done.4, bf16[2,32,896]{2,1,0:T(8,128)(2,1)S(1)} %collective-permute-done.5.refs_0_, bf16[2,32,896]{2,1,0:T(8,128)(2,1)S(1)} %collective-permute-done.6.refs_1_), custom_call_target="tpu_custom_call" | custom-call | flops 100000000 | bytes 1024 | tf_op jit(solution)/shard_map/encode/pallas_call | solution.py:186
  24.6 0.8 collective-permute-start.9
  25.3 1.2 %collective-permute-start.11 = (bf16[2,32,896]{2,1,0:T(8,128)(2,1)S(1)}, bf16[2,32,896]{2,1,0:T(8,128)(2,1)S(1)}, u32[]{:S(2)}, u32[]{:S(2)}) collective-permute-start(bf16[2,32,896]{2,1,0:T(8,128)(2,1)S(1)} %get-tuple-element.78), channel_id=1, source_target_pairs={{0,12},{4,8},{8,4},{12,0},{1,13},{5,9},{9,5},{13,1},{2,14},{6,10},... | collective-permute-start | bytes 344072 | tf_op jit(solution)/shard_map/ppermute | solution.py:372
  26.6 0.1 collective-permute-start.7
  26.7 1.3 %encode.5 = bf16[4,32,896]{2,1,0:T(8,128)(2,1)S(1)} custom-call(s32[16]{0:T(128)S(1)} %get-tuple-element.57.req_ref, bf16[512,896]{1,0:T(8,128)(2,1)S(1)} %copy-done.4, bf16[4,32,896]{2,1,0:T(8,128)(2,1)S(1)} %collective-permute-done.8.refs_0_), custom_call_target="tpu_custom_call" | custom-call | flops 10000000000 | bytes 1024 | tf_op jit(solution)/shard_map/encode/pallas_call | solution.py:186
  27.9 5.3 %collective-permute-start.14 = (bf16[2,32,896]{2,1,0:T(8,128)(2,1)S(1)}, bf16[2,32,896]{2,1,0:T(8,128)(2,1)S(1)}, u32[]{:S(2)}, u32[]{:S(2)}) collective-permute-start(bf16[2,32,896]{2,1,0:T(8,128)(2,1)S(1)} %get-tuple-element.84), channel_id=1, source_target_pairs={{0,12},{4,8},{8,4},{12,0},{1,13},{5,9},{9,5},{13,1},{2,14},{6,10},... | collective-permute-start | bytes 344072 | tf_op jit(solution)/shard_map/ppermute | solution.py:372
  33.3 0.5 collective-permute-start.12
  33.8 1.3 %project.3.refs_0_ = bf16[4,4,32,1024]{3,2,1,0:T(8,128)(2,1)S(1)} custom-call(bf16[2,4,32,896]{3,2,1,0:T(8,128)(2,1)S(1)} %pad_maximum_fusion.refs_0_, bf16[2,4,32,896]{3,2,1,0:T(8,128)(2,1)S(1)} %collective-permute-done.7.refs_1_, bf16[896,512]{1,0:T(8,128)(2,1)S(1)} %copy-done.1, bf16[896,512]{1,0:T(8,128)(2,1)S(1)} %copy-done.2), custom_call_target="tpu_custom_call" | custom-call | flops 100000000 | bytes 1024 | tf_op jit(solution)/shard_map/project/pallas_call | solution.py:238
  35.1 0.1 collective-permute-start.10
  35.2 1.1 %encode.6 = bf16[2,32,896]{2,1,0:T(8,128)(2,1)S(1)} custom-call(s32[16]{0:T(128)S(1)} %get-tuple-element.57.req_ref, bf16[512,896]{1,0:T(8,128)(2,1)S(1)} %copy-done.4, bf16[2,32,896]{2,1,0:T(8,128)(2,1)S(1)} %collective-permute-done.11.refs_0_), custom_call_target="tpu_custom_call" | custom-call | flops 10000000000 | bytes 1024 | tf_op jit(solution)/shard_map/encode/pallas_call | solution.py:186
  36.3 1.6 %collective-permute-start.15 = (bf16[2,32,896]{2,1,0:T(8,128)(2,1)S(1)}, bf16[2,32,896]{2,1,0:T(8,128)(2,1)S(1)}, u32[]{:S(2)}, u32[]{:S(2)}) collective-permute-start(bf16[2,32,896]{2,1,0:T(8,128)(2,1)S(1)} %encode.6), channel_id=1, source_target_pairs={{0,2},{2,0},{1,3},{3,1},{4,6},{6,4},{5,7},{7,5},{8,10},{10,8},{9,1... | collective-permute-start | bytes 344072 | tf_op jit(solution)/shard_map/ppermute | solution.py:349
  37.9 1.3 %project.4.refs_1_ = bf16[4,4,32,1024]{3,2,1,0:T(8,128)(2,1)S(1)} custom-call(bf16[2,4,32,896]{3,2,1,0:T(8,128)(2,1)S(1)} %pad_maximum_fusion.1.refs_0_, bf16[2,4,32,896]{3,2,1,0:T(8,128)(2,1)S(1)} %collective-permute-done.10.refs_1_, bf16[896,512]{1,0:T(8,128)(2,1)S(1)} %copy-done.1, bf16[896,512]{1,0:T(8,128)(2,1)S(1)} %copy-done.2), custom_call_target="tpu_custom_call" | custom-call | flops 100000000 | bytes 1024 | tf_op jit(solution)/shard_map/project/pallas_call | solution.py:238
  39.1 0.1 collective-permute-done.12
  39.3 0.1 collective-permute-start.13
  39.5 1.1 %encode.7 = bf16[2,32,896]{2,1,0:T(8,128)(2,1)S(1)} custom-call(s32[16]{0:T(128)S(1)} %get-tuple-element.57.req_ref, bf16[512,896]{1,0:T(8,128)(2,1)S(1)} %copy-done.4, bf16[2,32,896]{2,1,0:T(8,128)(2,1)S(1)} %collective-permute-done.14.refs_0_), custom_call_target="tpu_custom_call" | custom-call | flops 10000000000 | bytes 1024 | tf_op jit(solution)/shard_map/encode/pallas_call | solution.py:186
  40.6 0.7 collective-permute-start.16
  41.2 1.2 %project.5.refs_2_ = bf16[4,4,32,1024]{3,2,1,0:T(8,128)(2,1)S(1)} custom-call(bf16[2,4,32,896]{3,2,1,0:T(8,128)(2,1)S(1)} %pad_maximum_fusion.2.refs_0_, bf16[2,4,32,896]{3,2,1,0:T(8,128)(2,1)S(1)} %collective-permute-done.13.refs_1_, bf16[896,512]{1,0:T(8,128)(2,1)S(1)} %copy-done.1, bf16[896,512]{1,0:T(8,128)(2,1)S(1)} %copy-done.2), custom_call_target="tpu_custom_call" | custom-call | flops 100000000 | bytes 1024 | tf_op jit(solution)/shard_map/project/pallas_call | solution.py:238
  42.5 3.6 %collective-permute-done.16 = bf16[2,32,896]{2,1,0:T(8,128)(2,1)S(1)} collective-permute-done((bf16[2,32,896]{2,1,0:T(8,128)(2,1)S(1)}, bf16[2,32,896]{2,1,0:T(8,128)(2,1)S(1)}, u32[]{:S(2)}, u32[]{:S(2)}) %collective-permute-start.16) | collective-permute-done | bytes 114720 | tf_op jit(solution)/shard_map/ppermute | solution.py:349
  46.3 1.8 %collective-permute-done.17.refs_4_ = bf16[2,4,32,896]{3,2,1,0:T(8,128)(2,1)S(1)} collective-permute-done((bf16[2,4,32,896]{3,2,1,0:T(8,128)(2,1)S(1)}, bf16[2,4,32,896]{3,2,1,0:T(8,128)(2,1)S(1)}, u32[]{:S(2)}, u32[]{:S(2)}) %collective-permute-start.17) | collective-permute-done | bytes 458784 | tf_op jit(solution)/shard_map/ppermute | solution.py:352
  48.1 3.4 %attend.2 = (bf16[1,128,512]{2,1,0:T(8,128)(2,1)S(1)}, bf16[1,128,512]{2,1,0:T(8,128)(2,1)S(1)}) custom-call(s32[16]{0:T(128)S(1)} %get-tuple-element.56.slot_ref, bf16[512,512]{1,0:T(8,128)(2,1)S(1)} %copy-done.3, bf16[4,4,32,1024]{3,2,1,0:T(8,128)(2,1)S(1)} %project.3.refs_0_, bf16[4,4,32,1024]{3,2,1,0:T(8,128)(2,1)S(1)} %project.4.refs_1_, ...), custom_call_target="tpu_custom_call" | custom-call | flops 1000000 | bytes 1024 | tf_op jit(solution)/shard_map/attend/pallas_call | solution.py:304
  51.6 0.2 collective-permute-start.18
  51.8 1.2 %collective-permute-done.18.refs_1_ = bf16[1,128,512]{2,1,0:T(8,128)(2,1)S(1)} collective-permute-done((bf16[1,128,512]{2,1,0:T(8,128)(2,1)S(1)}, bf16[1,128,512]{2,1,0:T(8,128)(2,1)S(1)}, u32[]{:S(2)}, u32[]{:S(2)}) %collective-permute-start.18) | collective-permute-done | bytes 131104 | tf_op jit(solution)/shard_map/ppermute | solution.py:398
  53.0 2.0 %out_project.5 = bf16[128,1536]{1,0:T(8,128)(2,1)S(1)} custom-call(bf16[1,128,512]{2,1,0:T(8,128)(2,1)S(1)} %get-tuple-element.101.refs_0_, bf16[1,128,512]{2,1,0:T(8,128)(2,1)S(1)} %collective-permute-done.18.refs_1_, bf16[512,4096]{1,0:T(8,128)(2,1)S(1)} %copy-done, bf16[512,4096]{1,0:T(8,128)(2,1)S(1)} %collective-permute-done.4.refs_3_), custom_call_target="tpu_custom_call" | custom-call | flops 1000000 | bytes 1024 | tf_op jit(solution)/shard_map/out_project/pallas_call | solution.py:324
  55.0 0.6 collective-permute-start.20
  55.5 1.7 %out_project.6 = bf16[128,1280]{1,0:T(8,128)(2,1)S(1)} custom-call(bf16[1,128,512]{2,1,0:T(8,128)(2,1)S(1)} %get-tuple-element.101.refs_0_, bf16[1,128,512]{2,1,0:T(8,128)(2,1)S(1)} %collective-permute-done.18.refs_1_, bf16[512,4096]{1,0:T(8,128)(2,1)S(1)} %copy-done, bf16[512,4096]{1,0:T(8,128)(2,1)S(1)} %collective-permute-done.4.refs_3_), custom_call_target="tpu_custom_call" | custom-call | flops 1000000 | bytes 1024 | tf_op jit(solution)/shard_map/out_project/pallas_call | solution.py:324
  57.2 1.6 %collective-permute-start.21 = (bf16[128,1280]{1,0:T(8,128)(2,1)S(1)}, bf16[128,1280]{1,0:T(8,128)(2,1)S(1)}, u32[]{:S(2)}, u32[]{:S(2)}) collective-permute-start(bf16[128,1280]{1,0:T(8,128)(2,1)S(1)} %out_project.6), channel_id=1, source_target_pairs={{0,2},{2,0},{1,3},{3,1},{4,6},{6,4},{5,7},{7,5},{8,10},{10,8},{9,1... | collective-permute-start | bytes 983048 | tf_op jit(solution)/shard_map/ppermute | solution.py:412
  58.8 1.0 %out_project.7 = bf16[128,768]{1,0:T(8,128)(2,1)S(1)} custom-call(bf16[1,128,512]{2,1,0:T(8,128)(2,1)S(1)} %get-tuple-element.101.refs_0_, bf16[1,128,512]{2,1,0:T(8,128)(2,1)S(1)} %collective-permute-done.18.refs_1_, bf16[512,4096]{1,0:T(8,128)(2,1)S(1)} %copy-done, bf16[512,4096]{1,0:T(8,128)(2,1)S(1)} %collective-permute-done.4.refs_3_), custom_call_target="tpu_custom_call" | custom-call | flops 1000000 | bytes 1024 | tf_op jit(solution)/shard_map/out_project/pallas_call | solution.py:324
  59.8 0.6 collective-permute-start.22
  60.4 0.7 out_project.8
  61.1 3.4 %attend.3 = (bf16[1,128,512]{2,1,0:T(8,128)(2,1)S(1)}, bf16[1,128,512]{2,1,0:T(8,128)(2,1)S(1)}) custom-call(s32[16]{0:T(128)S(1)} %get-tuple-element.56.slot_ref, bf16[512,512]{1,0:T(8,128)(2,1)S(1)} %copy-done.3, bf16[4,4,32,1024]{3,2,1,0:T(8,128)(2,1)S(1)} %project.3.refs_0_, bf16[4,4,32,1024]{3,2,1,0:T(8,128)(2,1)S(1)} %project.4.refs_1_, ...), custom_call_target="tpu_custom_call" | custom-call | flops 1000000 | bytes 1024 | tf_op jit(solution)/shard_map/attend/pallas_call | solution.py:304
  64.5 0.1 collective-permute-start.19
  64.6 1.6 %collective-permute-start.23 = (bf16[128,512]{1,0:T(8,128)(2,1)S(1)}, bf16[128,512]{1,0:T(8,128)(2,1)S(1)}, u32[]{:S(2)}, u32[]{:S(2)}) collective-permute-start(bf16[128,512]{1,0:T(8,128)(2,1)S(1)} %out_project.8), channel_id=1, source_target_pairs={{0,2},{2,0},{1,3},{3,1},{4,6},{6,4},{5,7},{7,5},{8,10},{10,8},{9,1... | collective-permute-start | bytes 393224 | tf_op jit(solution)/shard_map/ppermute | solution.py:412
  66.2 5.2 %out_project.9 = bf16[128,4096]{1,0:T(8,128)(2,1)S(1)} custom-call(bf16[1,128,512]{2,1,0:T(8,128)(2,1)S(1)} %get-tuple-element.105.refs_0_, bf16[1,128,512]{2,1,0:T(8,128)(2,1)S(1)} %collective-permute-done.19.refs_1_, bf16[512,4096]{1,0:T(8,128)(2,1)S(1)} %copy-done, bf16[512,4096]{1,0:T(8,128)(2,1)S(1)} %collective-permute-done.4.refs_3_), custom_call_target="tpu_custom_call" | custom-call | flops 1000000 | bytes 1024 | tf_op jit(solution)/shard_map/out_project/pallas_call | solution.py:324
  71.4 8.8 %collective-permute-done.23 = bf16[128,512]{1,0:T(8,128)(2,1)S(1)} collective-permute-done((bf16[128,512]{1,0:T(8,128)(2,1)S(1)}, bf16[128,512]{1,0:T(8,128)(2,1)S(1)}, u32[]{:S(2)}, u32[]{:S(2)}) %collective-permute-start.23) | collective-permute-done | bytes 131104 | tf_op jit(solution)/shard_map/ppermute | solution.py:412
  80.3 1.2 %add_convert_fusion = bf16[128,4096]{1,0:T(8,128)(2,1)} fusion(bf16[128,4096]{1,0:T(8,128)(2,1)S(1)} %out_project.9, bf16[128,512]{1,0:T(8,128)(2,1)S(1)} %collective-permute-done.23, bf16[128,768]{1,0:T(8,128)(2,1)S(1)} %collective-permute-done.22, bf16[128,1280]{1,0:T(8,128)(2,1)S(1)} %collective-permute-done.21, bf16[128,1536]{1,0:T(8,128)(2,1)S(1)} %collective-permute-done.20), kind=kLoop, calls=%fused_computation | loop fusion | flops 5767168 | bytes 3145728 | tf_op jit(solution)/shard_map/convert_element_type | solution.py:417
  (36 shorter events, 0.4 us)
Async XLA Ops:
  0.0 10.8 %collective-permute-start.4 = (bf16[512,4096]{1,0:T(8,128)(2,1)}, bf16[512,4096]{1,0:T(8,128)(2,1)S(1)}, u32[]{:S(2)}, u32[]{:S(2)}) collective-permute-start(bf16[512,4096]{1,0:T(8,128)(2,1)} %refs_2_.15), channel_id=1, source_target_pairs={{0,1},{1,0},{2,3},{3,2},{4,5},{5,4},{6,7},{7,6},{8,9},{9,8},{10,11... | collective-permute-start | bytes 12582920 | tf_op jit(solution)/shard_map/ppermute | solution.py:352
  1.2 6.6 %copy-start.4 = (bf16[512,896]{1,0:T(8,128)(2,1)S(1)}, bf16[512,896]{1,0:T(8,128)(2,1)}, u32[]{:S(2)}) copy-start(bf16[512,896]{1,0:T(8,128)(2,1)} %states_ref.9) | copy-start | bytes 2752516
  1.2 6.6 %copy-start.5 = (bf16[16,32,896]{2,1,0:T(8,128)(2,1)S(1)}, bf16[16,32,896]{2,1,0:T(8,128)(2,1)}, u32[]{:S(2)}) copy-start(bf16[16,32,896]{2,1,0:T(8,128)(2,1)} %refs_3_.4) | copy-start | bytes 2752516
  1.2 9.6 %collective-permute-start.3 = (s32[4,8]{1,0:T(4,128)S(1)}, s32[4,8]{1,0:T(4,128)S(1)}, u32[]{:S(2)}, u32[]{:S(2)}) collective-permute-start(s32[4,8]{1,0:T(4,128)S(1)} %pad_add_fusion.own_ref), channel_id=1, source_target_pairs={{0,12},{4,8},{8,4},{12,0},{1,13},{5,9},{9,5},{13,1},{2,14},{6,10},... | collective-permute-start | bytes 392 | tf_op jit(solution)/shard_map/ppermute | solution.py:363
  5.8 4.9 %collective-permute-start.2 = (s32[4,8]{1,0:T(4,128)S(1)}, s32[4,8]{1,0:T(4,128)S(1)}, u32[]{:S(2)}, u32[]{:S(2)}) collective-permute-start(s32[4,8]{1,0:T(4,128)S(1)} %pad_add_fusion.own_ref), channel_id=1, source_target_pairs={{0,8},{4,12},{8,0},{12,4},{1,9},{5,13},{9,1},{13,5},{2,10},{6,14},... | collective-permute-start | bytes 392 | tf_op jit(solution)/shard_map/ppermute | solution.py:363
  5.8 4.9 %collective-permute-start.1 = (s32[4,8]{1,0:T(4,128)S(1)}, s32[4,8]{1,0:T(4,128)S(1)}, u32[]{:S(2)}, u32[]{:S(2)}) collective-permute-start(s32[4,8]{1,0:T(4,128)S(1)} %pad_add_fusion.own_ref), channel_id=1, source_target_pairs={{0,4},{4,0},{8,12},{12,8},{1,5},{5,1},{9,13},{13,9},{2,6},{6,2},{1... | collective-permute-start | bytes 392 | tf_op jit(solution)/shard_map/ppermute | solution.py:363
  9.1 16.3 %collective-permute-start = (bf16[4,32,896]{2,1,0:T(8,128)(2,1)S(1)}, bf16[4,32,896]{2,1,0:T(8,128)(2,1)S(1)}, u32[]{:S(2)}, u32[]{:S(2)}) collective-permute-start(bf16[4,32,896]{2,1,0:T(8,128)(2,1)S(1)} %encode_local.1), channel_id=1, source_target_pairs={{0,2},{2,0},{1,3},{3,1},{4,6},{6,4},{5,7},{7,5},{8,10},{10,8},{9,1... | collective-permute-start | bytes 688136 | tf_op jit(solution)/shard_map/ppermute | solution.py:349
  11.6 10.3 %collective-permute-start.5 = (bf16[2,32,896]{2,1,0:T(8,128)(2,1)S(1)}, bf16[2,32,896]{2,1,0:T(8,128)(2,1)S(1)}, u32[]{:S(2)}, u32[]{:S(2)}) collective-permute-start(bf16[2,32,896]{2,1,0:T(8,128)(2,1)S(1)} %get-tuple-element.64), channel_id=1, source_target_pairs={{0,4},{4,0},{8,12},{12,8},{1,5},{5,1},{9,13},{13,9},{2,6},{6,2},{1... | collective-permute-start | bytes 344072 | tf_op jit(solution)/shard_map/ppermute | solution.py:372
  12.9 10.2 %collective-permute-start.6 = (bf16[2,32,896]{2,1,0:T(8,128)(2,1)S(1)}, bf16[2,32,896]{2,1,0:T(8,128)(2,1)S(1)}, u32[]{:S(2)}, u32[]{:S(2)}) collective-permute-start(bf16[2,32,896]{2,1,0:T(8,128)(2,1)S(1)} %get-tuple-element.65), channel_id=1, source_target_pairs={{0,4},{4,0},{8,12},{12,8},{1,5},{5,1},{9,13},{13,9},{2,6},{6,2},{1... | collective-permute-start | bytes 344072 | tf_op jit(solution)/shard_map/ppermute | solution.py:372
  13.7 13.0 %collective-permute-start.8 = (bf16[4,32,896]{2,1,0:T(8,128)(2,1)S(1)}, bf16[4,32,896]{2,1,0:T(8,128)(2,1)S(1)}, u32[]{:S(2)}, u32[]{:S(2)}) collective-permute-start(bf16[4,32,896]{2,1,0:T(8,128)(2,1)S(1)} %get-tuple-element.66), channel_id=1, source_target_pairs={{0,8},{4,12},{8,0},{12,4},{1,9},{5,13},{9,1},{13,5},{2,10},{6,14},... | collective-permute-start | bytes 688136 | tf_op jit(solution)/shard_map/ppermute | solution.py:372
  24.6 10.5 %collective-permute-start.9 = (bf16[4,32,896]{2,1,0:T(8,128)(2,1)S(1)}, bf16[4,32,896]{2,1,0:T(8,128)(2,1)S(1)}, u32[]{:S(2)}, u32[]{:S(2)}) collective-permute-start(bf16[4,32,896]{2,1,0:T(8,128)(2,1)S(1)} %encode.4), channel_id=1, source_target_pairs={{0,2},{2,0},{1,3},{3,1},{4,6},{6,4},{5,7},{7,5},{8,10},{10,8},{9,1... | collective-permute-start | bytes 688136 | tf_op jit(solution)/shard_map/ppermute | solution.py:349
  25.3 9.9 %collective-permute-start.11 = (bf16[2,32,896]{2,1,0:T(8,128)(2,1)S(1)}, bf16[2,32,896]{2,1,0:T(8,128)(2,1)S(1)}, u32[]{:S(2)}, u32[]{:S(2)}) collective-permute-start(bf16[2,32,896]{2,1,0:T(8,128)(2,1)S(1)} %get-tuple-element.78), channel_id=1, source_target_pairs={{0,12},{4,8},{8,4},{12,0},{1,13},{5,9},{9,5},{13,1},{2,14},{6,10},... | collective-permute-start | bytes 344072 | tf_op jit(solution)/shard_map/ppermute | solution.py:372
  26.5 7.2 %copy-start.1 = (bf16[896,512]{1,0:T(8,128)(2,1)S(1)}, bf16[896,512]{1,0:T(8,128)(2,1)}, u32[]{:S(2)}) copy-start(bf16[896,512]{1,0:T(8,128)(2,1)} %refs_5_.3) | copy-start | bytes 2752516
  26.5 7.2 %copy-start.2 = (bf16[896,512]{1,0:T(8,128)(2,1)S(1)}, bf16[896,512]{1,0:T(8,128)(2,1)}, u32[]{:S(2)}) copy-start(bf16[896,512]{1,0:T(8,128)(2,1)} %refs_6_.3) | copy-start | bytes 2752516
  26.6 7.2 %collective-permute-start.7 = (bf16[2,4,32,896]{3,2,1,0:T(8,128)(2,1)S(1)}, bf16[2,4,32,896]{3,2,1,0:T(8,128)(2,1)S(1)}, u32[]{:S(2)}, u32[]{:S(2)}) collective-permute-start(bf16[2,4,32,896]{3,2,1,0:T(8,128)(2,1)S(1)} %pad_maximum_fusion.refs_0_), channel_id=1, source_target_pairs={{0,1},{1,0},{2,3},{3,2},{4,5},{5,4},{6,7},{7,6},{8,9},{9,8},{10,11... | collective-permute-start | bytes 1376264 | tf_op jit(solution)/shard_map/ppermute | solution.py:352
  27.9 11.6 %collective-permute-start.14 = (bf16[2,32,896]{2,1,0:T(8,128)(2,1)S(1)}, bf16[2,32,896]{2,1,0:T(8,128)(2,1)S(1)}, u32[]{:S(2)}, u32[]{:S(2)}) collective-permute-start(bf16[2,32,896]{2,1,0:T(8,128)(2,1)S(1)} %get-tuple-element.84), channel_id=1, source_target_pairs={{0,12},{4,8},{8,4},{12,0},{1,13},{5,9},{9,5},{13,1},{2,14},{6,10},... | collective-permute-start | bytes 344072 | tf_op jit(solution)/shard_map/ppermute | solution.py:372
  33.3 6.0 %collective-permute-start.12 = (bf16[4,32,896]{2,1,0:T(8,128)(2,1)S(1)}, bf16[4,32,896]{2,1,0:T(8,128)(2,1)S(1)}, u32[]{:S(2)}, u32[]{:S(2)}) collective-permute-start(bf16[4,32,896]{2,1,0:T(8,128)(2,1)S(1)} %encode.5), channel_id=1, source_target_pairs={{0,2},{2,0},{1,3},{3,1},{4,6},{6,4},{5,7},{7,5},{8,10},{10,8},{9,1... | collective-permute-start | bytes 688136 | tf_op jit(solution)/shard_map/ppermute | solution.py:349
  35.1 2.8 %collective-permute-start.10 = (bf16[2,4,32,896]{3,2,1,0:T(8,128)(2,1)S(1)}, bf16[2,4,32,896]{3,2,1,0:T(8,128)(2,1)S(1)}, u32[]{:S(2)}, u32[]{:S(2)}) collective-permute-start(bf16[2,4,32,896]{3,2,1,0:T(8,128)(2,1)S(1)} %pad_maximum_fusion.1.refs_0_), channel_id=1, source_target_pairs={{0,1},{1,0},{2,3},{3,2},{4,5},{5,4},{6,7},{7,6},{8,9},{9,8},{10,11... | collective-permute-start | bytes 1376264 | tf_op jit(solution)/shard_map/ppermute | solution.py:352
  36.3 6.2 %collective-permute-start.15 = (bf16[2,32,896]{2,1,0:T(8,128)(2,1)S(1)}, bf16[2,32,896]{2,1,0:T(8,128)(2,1)S(1)}, u32[]{:S(2)}, u32[]{:S(2)}) collective-permute-start(bf16[2,32,896]{2,1,0:T(8,128)(2,1)S(1)} %encode.6), channel_id=1, source_target_pairs={{0,2},{2,0},{1,3},{3,1},{4,6},{6,4},{5,7},{7,5},{8,10},{10,8},{9,1... | collective-permute-start | bytes 344072 | tf_op jit(solution)/shard_map/ppermute | solution.py:349
  39.3 1.9 %collective-permute-start.13 = (bf16[2,4,32,896]{3,2,1,0:T(8,128)(2,1)S(1)}, bf16[2,4,32,896]{3,2,1,0:T(8,128)(2,1)S(1)}, u32[]{:S(2)}, u32[]{:S(2)}) collective-permute-start(bf16[2,4,32,896]{3,2,1,0:T(8,128)(2,1)S(1)} %pad_maximum_fusion.2.refs_0_), channel_id=1, source_target_pairs={{0,1},{1,0},{2,3},{3,2},{4,5},{5,4},{6,7},{7,6},{8,9},{9,8},{10,11... | collective-permute-start | bytes 1376264 | tf_op jit(solution)/shard_map/ppermute | solution.py:352
  40.6 7.6 %copy-start.3 = (bf16[512,512]{1,0:T(8,128)(2,1)S(1)}, bf16[512,512]{1,0:T(8,128)(2,1)}, u32[]{:S(2)}) copy-start(bf16[512,512]{1,0:T(8,128)(2,1)} %q_ref.2) | copy-start | bytes 1572868
  40.6 5.6 %collective-permute-start.16 = (bf16[2,32,896]{2,1,0:T(8,128)(2,1)S(1)}, bf16[2,32,896]{2,1,0:T(8,128)(2,1)S(1)}, u32[]{:S(2)}, u32[]{:S(2)}) collective-permute-start(bf16[2,32,896]{2,1,0:T(8,128)(2,1)S(1)} %encode.7), channel_id=1, source_target_pairs={{0,2},{2,0},{1,3},{3,1},{4,6},{6,4},{5,7},{7,5},{8,10},{10,8},{9,1... | collective-permute-start | bytes 344072 | tf_op jit(solution)/shard_map/ppermute | solution.py:349
  46.2 1.9 %collective-permute-start.17 = (bf16[2,4,32,896]{3,2,1,0:T(8,128)(2,1)S(1)}, bf16[2,4,32,896]{3,2,1,0:T(8,128)(2,1)S(1)}, u32[]{:S(2)}, u32[]{:S(2)}) collective-permute-start(bf16[2,4,32,896]{3,2,1,0:T(8,128)(2,1)S(1)} %pad_maximum_fusion.3.refs_3_), channel_id=1, source_target_pairs={{0,1},{1,0},{2,3},{3,2},{4,5},{5,4},{6,7},{7,6},{8,9},{9,8},{10,11... | collective-permute-start | bytes 1376264 | tf_op jit(solution)/shard_map/ppermute | solution.py:352
  48.1 4.8 %copy-start = (bf16[512,4096]{1,0:T(8,128)(2,1)S(1)}, bf16[512,4096]{1,0:T(8,128)(2,1)}, u32[]{:S(2)}) copy-start(bf16[512,4096]{1,0:T(8,128)(2,1)} %refs_2_.15) | copy-start | bytes 12582916
  51.6 1.4 %collective-permute-start.18 = (bf16[1,128,512]{2,1,0:T(8,128)(2,1)S(1)}, bf16[1,128,512]{2,1,0:T(8,128)(2,1)S(1)}, u32[]{:S(2)}, u32[]{:S(2)}) collective-permute-start(bf16[1,128,512]{2,1,0:T(8,128)(2,1)S(1)} %get-tuple-element.93), channel_id=1, source_target_pairs={{0,1},{1,0},{2,3},{3,2},{4,5},{5,4},{6,7},{7,6},{8,9},{9,8},{10,11... | collective-permute-start | bytes 393224 | tf_op jit(solution)/shard_map/ppermute | solution.py:398
  55.0 25.3 %collective-permute-start.20 = (bf16[128,1536]{1,0:T(8,128)(2,1)S(1)}, bf16[128,1536]{1,0:T(8,128)(2,1)S(1)}, u32[]{:S(2)}, u32[]{:S(2)}) collective-permute-start(bf16[128,1536]{1,0:T(8,128)(2,1)S(1)} %out_project.5), channel_id=1, source_target_pairs={{0,2},{2,0},{1,3},{3,1},{4,6},{6,4},{5,7},{7,5},{8,10},{10,8},{9,1... | collective-permute-start | bytes 1179656 | tf_op jit(solution)/shard_map/ppermute | solution.py:412
  57.2 23.0 %collective-permute-start.21 = (bf16[128,1280]{1,0:T(8,128)(2,1)S(1)}, bf16[128,1280]{1,0:T(8,128)(2,1)S(1)}, u32[]{:S(2)}, u32[]{:S(2)}) collective-permute-start(bf16[128,1280]{1,0:T(8,128)(2,1)S(1)} %out_project.6), channel_id=1, source_target_pairs={{0,2},{2,0},{1,3},{3,1},{4,6},{6,4},{5,7},{7,5},{8,10},{10,8},{9,1... | collective-permute-start | bytes 983048 | tf_op jit(solution)/shard_map/ppermute | solution.py:412
  59.8 20.4 %collective-permute-start.22 = (bf16[128,768]{1,0:T(8,128)(2,1)S(1)}, bf16[128,768]{1,0:T(8,128)(2,1)S(1)}, u32[]{:S(2)}, u32[]{:S(2)}) collective-permute-start(bf16[128,768]{1,0:T(8,128)(2,1)S(1)} %out_project.7), channel_id=1, source_target_pairs={{0,2},{2,0},{1,3},{3,1},{4,6},{6,4},{5,7},{7,5},{8,10},{10,8},{9,1... | collective-permute-start | bytes 589832 | tf_op jit(solution)/shard_map/ppermute | solution.py:412
  64.5 1.7 %collective-permute-start.19 = (bf16[1,128,512]{2,1,0:T(8,128)(2,1)S(1)}, bf16[1,128,512]{2,1,0:T(8,128)(2,1)S(1)}, u32[]{:S(2)}, u32[]{:S(2)}) collective-permute-start(bf16[1,128,512]{2,1,0:T(8,128)(2,1)S(1)} %get-tuple-element.106), channel_id=1, source_target_pairs={{0,1},{1,0},{2,3},{3,2},{4,5},{5,4},{6,7},{7,6},{8,9},{9,8},{10,11... | collective-permute-start | bytes 393224 | tf_op jit(solution)/shard_map/ppermute | solution.py:398
  64.6 15.7 %collective-permute-start.23 = (bf16[128,512]{1,0:T(8,128)(2,1)S(1)}, bf16[128,512]{1,0:T(8,128)(2,1)S(1)}, u32[]{:S(2)}, u32[]{:S(2)}) collective-permute-start(bf16[128,512]{1,0:T(8,128)(2,1)S(1)} %out_project.8), channel_id=1, source_target_pairs={{0,2},{2,0},{1,3},{3,1},{4,6},{6,4},{5,7},{7,5},{8,10},{10,8},{9,1... | collective-permute-start | bytes 393224 | tf_op jit(solution)/shard_map/ppermute | solution.py:412

commit v7 on v6

--- a/solution.py
+++ b/solution.py
@@ -11,9 +11,9 @@
 ENCODER_HEAD_DIM = 128
 F32 = jnp.float32
 BF16 = jnp.bfloat16
-LATER_GROUPS = 3
-COL_TILE = 256
-ENCODE_COST = (None, 0.1, 10, 10, 10)
+LATER_GROUPS = 2
+COL_TILE = 512
+ENCODE_COST = (None, 0.1, 10, 10)
 
 VMEM = pl.BlockSpec(memory_space=pltpu.VMEM)
 SMEM = pl.BlockSpec(memory_space=pltpu.SMEM)
@@ -52,33 +52,33 @@
     return jnp.dot(a, b, preferred_element_type=F32)
 
 
-def plan_kernel(n_lanes, cap, own_ref, req_ref, slot_ref, pick_ref, count_ref):
+def plan_kernel(order, cap, own_ref, req_ref, slot_ref, pick_ref, next_ref):
+    n_lanes = len(order)
     lane = lax.axis_index("lanes")
     fanout, spans = own_ref.shape[0] // 2, own_ref.shape[1]
-    for i in range(n_lanes):
-        count_ref[i] = 0
+    for i, d in enumerate(order):
+        next_ref[d] = i * cap
     for i in range(n_lanes * cap):
         pick_ref[i] = 0
         req_ref[i] = 0
     for j in range(fanout * spans):
         span, k = j // fanout, j % fanout
         d = apart(n_lanes, lane, own_ref[k, span])
-        rank = count_ref[d]
-        count_ref[d] = rank + 1
-        slot = d * cap + rank
+        slot = next_ref[d]
+        next_ref[d] = slot + 1
         pick_ref[slot] = own_ref[fanout + k, span]
         req_ref[slot] = j
         slot_ref[j] = slot
 
 
-def plan(own, n_lanes, cap):
-    table = jax.ShapeDtypeStruct((n_lanes * cap,), jnp.int32)
-    return pl.pallas_call(
-        functools.partial(plan_kernel, n_lanes, cap),
+def plan(own, order, cap):
+    table = jax.ShapeDtypeStruct((len(order) * cap,), jnp.int32)
+    return pl.pallas_call(
+        functools.partial(plan_kernel, order, cap),
         out_shape=(table, jax.ShapeDtypeStruct((own.size // 2,), jnp.int32), table),
         in_specs=[SMEM],
         out_specs=(SMEM, SMEM, SMEM),
-        scratch_shapes=[pltpu.SMEM((n_lanes,), jnp.int32)],
+        scratch_shapes=[pltpu.SMEM((len(order),), jnp.int32)],
         compiler_params=params(16),
         cost_estimate=cost(10),
         name="plan",
@@ -86,7 +86,7 @@
 
 
 def fetch_kernel(items, cap, *refs):
-    others = items[-1][0]
+    others = max(d for d, _, _ in items)
     asked, store_ref, refs = refs[:others], refs[others], refs[others + 1 :]
     blocks, pick_ref = refs[:-1], refs[-1]
     lane = lax.axis_index("lanes")
@@ -241,7 +241,7 @@
         in_specs=[VMEM] * (len(pieces) + 2),
         out_specs=VMEM,
         compiler_params=params(32),
-        cost_estimate=cost(0.1),
+        cost_estimate=cost(10),
         name="project",
     )(*pieces, w_key, w_value)
 
@@ -351,9 +351,10 @@
     def over_rep(array):
         return [array] + [lax.ppermute(array, "rep", shift_pairs(n_rep, s)) for s in range(1, n_rep)]
 
+    order = list(range(n_lanes))
     items = []
-    for d in range(1, n_lanes):
-        cuts = (0, cap // 2, cap) if d in (1, n_lanes - 1) else (0, cap)
+    for d in order[1:]:
+        cuts = (0, cap // 2, cap) if d == 1 else (0, cap)
         items += [(d, low, high) for low, high in zip(cuts, cuts[1:])]
     size = max(1, -(-(len(items) - 2) // LATER_GROUPS))
     cuts = [0] + list(range(2, len(items), size)) + [len(items)]
@@ -362,7 +363,7 @@
     own = jnp.concatenate([owners.T, entry_ids.T], axis=0)
     asked = [lax.ppermute(own, "lanes", lane_pairs(n_lanes, d, False)) for d in range(1, n_lanes)]
     w_outs = over_rep(w_out)
-    req, slot, pick = plan(own, n_lanes, cap)
+    req, slot, pick = plan(own, order, cap)
     encoded = encode_local(req, pick, span_states, store, cap, fanout, span_len)
     blocks = fetch(after(asked, w_outs, encoded), store, items, cap)
 
@@ -373,24 +374,26 @@
             for block, i in zip(ready, part)
         ]
 
-    crossed, pieces, kvs = [over_heads(encoded)], [], []
+    crossed, pieces = [over_heads(encoded)], []
     arrived = [None] + [send(part) for part in parts[:2]]
     last = blocks
     for i, part in enumerate(parts, 1):
         if i + 2 <= len(parts):
             arrived.append(send(parts[i + 1], arrived[i], last))
         first = items[part[0]][0] * cap + items[part[0]][1]
-        encoded = encode(req, span_states, after(arrived[i], last), first, fanout, span_len, ENCODE_COST[i])
+        encoded = encode(
+            req, span_states, after(arrived[i], last), first, fanout, span_len, ENCODE_COST[i]
+        )
         crossed.append(over_heads(encoded))
         last = encoded
-        if i >= 2:
-            last = project(after(pieces[i - 2], last), w_key, w_value)
-            kvs.append(last)
-        if i < len(parts):
-            last = jnp.stack(after(crossed[i - 1], last))
+        while i > 1 and len(pieces) < i:
+            last = jnp.stack(after(crossed[len(pieces)], last))
             pieces.append(over_rep(last))
-    ends = [jnp.concatenate(pair, axis=0) for pair in zip(*after(crossed[-2:], kvs))]
-    pieces = over_rep(jnp.stack(ends))
+    kvs = []
+    while len(kvs) < len(pieces):
+        last = project(after(pieces[len(kvs)], last), w_key, w_value)
+        kvs.append(last)
+    pieces = over_rep(jnp.stack(after(crossed[-1], kvs)))
 
     def mix(turns, q):
         outs = attend(slot, q, kvs, pieces, w_key, w_value, n_heads, n_rep, turns, fanout, spans)
@@ -400,7 +403,7 @@
 
     width = w_out.shape[1]
     tile = min(COL_TILE, width)
-    cuts = [width // tile * part // 16 * tile for part in (0, 6, 11, 14)] + [width]
+    cuts = [width // tile * part // 8 * tile for part in (0, 3, 5, 7)] + [width]
     mixed = mix(list(range(1, n_heads)), queries)
     received, partials = [], []
     for t in range(1, n_heads):

time: 81.6 us -> 78.6 us (0.963)
  waiting for transfers between devices: 22.9 us -> 31.9 us
  starting transfers between devices: 26.7 us -> 18.9 us
  Pallas kernels: 29.4 us -> 24.5 us
    ppermute x5 -> x4, starting transfers between devices: 10.8 us -> 4.12 us  [send(): lax.ppermute(block, 'lanes', lane_pairs(n_lanes, items[i][0], True))]
    pallas_call x5, Pallas kernels: 10.6 us -> 6.58 us  [out_project(): pl.pallas_call(functools.partial(out_kernel, len(mixed)), grid=((stop - s...]
    ppermute x5 -> x4, waiting for transfers between devices: 3.79 us -> 7.06 us  [over_heads(): lax.ppermute(array, 'heads', shift_pairs(n_heads, s))]
    ppermute x4, waiting for transfers between devices: 8.83 us -> 11.8 us  [shards(): sent.append(lax.ppermute(partial, 'heads', shift_pairs(n_heads, t)))]
    ppermute x3, waiting for transfers between devices: 0.01 us -> 1.29 us  [shards(): lax.ppermute(own, 'lanes', lane_pairs(n_lanes, d, False))]
    ppermute x5 -> x4, waiting for transfers between devices: 7.2 us -> 8.31 us  [send(): lax.ppermute(block, 'lanes', lane_pairs(n_lanes, items[i][0], True))]
    ppermute x5 -> x4, starting transfers between devices: 5.21 us -> 4.25 us  [over_heads(): lax.ppermute(array, 'heads', shift_pairs(n_heads, s))]
    pallas_call x4 -> x3, Pallas kernels: 4.85 us -> 3.97 us  [encode(): pl.pallas_call(functools.partial(encode_kernel, first, fanout, span_len),...]
  transfers between devices with their start and end apart: 24 -> 22, of which waited for: 7 -> 10; matrix products, arithmetic and copies ran while one was open for 1% -> 1% of each run, Pallas kernels for 29% -> 24%
where the time goes in v7:
time: 78.6 us; the launch traced here: 77.7 us
  waiting for transfers between devices  31.9 us (41%)
  Pallas kernels  24.5 us (31%)
  starting transfers between devices  18.9 us (24%)
  other arithmetic  2.11 us (3%)
    ppermute x4, waiting for transfers between devices, shards(): sent.append(lax.ppermute(partial, 'heads', shift_pairs(n_heads, t)))  11.8 us
    ppermute x4, waiting for transfers between devices, send(): lax.ppermute(block, 'lanes', lane_pairs(n_lanes, items[i][0], True))  8.31 us
    ppermute x4, waiting for transfers between devices, over_heads(): lax.ppermute(array, 'heads', shift_pairs(n_heads, s))  7.06 us
    pallas_call x2, Pallas kernels, attend(): pl.pallas_call(functools.partial(attend_kernel, firsts, len(pieces), n_he...  6.83 us
    pallas_call x5, Pallas kernels, out_project(): pl.pallas_call(functools.partial(out_kernel, len(mixed)), grid=((stop - s...  6.58 us
    ppermute x3, starting transfers between devices, shards(): lax.ppermute(own, 'lanes', lane_pairs(n_lanes, d, False))  5.31 us
    ppermute x4, starting transfers between devices, over_heads(): lax.ppermute(array, 'heads', shift_pairs(n_heads, s))  4.25 us
    ppermute x4, starting transfers between devices, shards(): sent.append(lax.ppermute(partial, 'heads', shift_pairs(n_heads, t)))  4.25 us
  transfers between devices with their start and end apart: 22, of which 10 were waited for; matrix products, arithmetic and copies ran while one was open for 1% of the time, Pallas kernels for 24%

profile of v7, /device:TPU:0, one launch (start us, length us, event | category | flops | bytes accessed | tf_op | source)
XLA Modules:
  0.0 77.7 jit_solution(11966268351057154111)
XLA Ops:
  0.0 0.5 collective-permute-start.4
  0.5 0.7 pad_add_fusion.own_ref
  1.2 4.7 %collective-permute-start.3 = (s32[4,8]{1,0:T(4,128)S(1)}, s32[4,8]{1,0:T(4,128)S(1)}, u32[]{:S(2)}, u32[]{:S(2)}) collective-permute-start(s32[4,8]{1,0:T(4,128)S(1)} %pad_add_fusion.own_ref), channel_id=1, source_target_pairs={{0,12},{4,8},{8,4},{12,0},{1,13},{5,9},{9,5},{13,1},{2,14},{6,10},... | collective-permute-start | bytes 392 | tf_op jit(solution)/shard_map/ppermute | solution.py:364
  5.8 0.6 collective-permute-start.1
  6.5 1.3 %plan.1 = (s32[16]{0:T(128)S(1)}, s32[16]{0:T(128)S(1)}, s32[16]{0:T(128)S(1)}) custom-call(s32[4,8]{1,0:T(4,128)S(1)} %pad_add_fusion.own_ref), custom_call_target="tpu_custom_call" | custom-call | flops 10000000000 | bytes 1024 | tf_op jit(solution)/shard_map/plan/pallas_call | solution.py:76
  7.8 1.3 %encode_local.1 = bf16[4,32,896]{2,1,0:T(8,128)(2,1)S(1)} custom-call(s32[16]{0:T(128)S(1)} %get-tuple-element.52.req_ref, s32[16]{0:T(128)S(1)} %get-tuple-element.53.pick_ref, bf16[512,896]{1,0:T(8,128)(2,1)S(1)} %copy-done.4, bf16[16,32,896]{2,1,0:T(8,128)(2,1)S(1)} %copy-done.5), custom_call_target="tpu_custom_call" | custom-call | flops 10000000000 | bytes 1024 | tf_op jit(solution)/shard_map/encode_local/pallas_call | solution.py:205
  9.0 1.3 %collective-permute-done.2.refs_1_ = s32[4,8]{1,0:T(4,128)S(1)} collective-permute-done((s32[4,8]{1,0:T(4,128)S(1)}, s32[4,8]{1,0:T(4,128)S(1)}, u32[]{:S(2)}, u32[]{:S(2)}) %collective-permute-start.2) | collective-permute-done | bytes 160 | tf_op jit(solution)/shard_map/ppermute | solution.py:364
  10.3 0.8 %fetch.1 = (bf16[2,32,896]{2,1,0:T(8,128)(2,1)S(1)}, bf16[2,32,896]{2,1,0:T(8,128)(2,1)S(1)}, bf16[4,32,896]{2,1,0:T(8,128)(2,1)S(1)}, bf16[4,32,896]{2,1,0:T(8,128)(2,1)S(1)}) custom-call(s32[4,8]{1,0:T(4,128)S(1)} %collective-permute-done.1.refs_0_, s32[4,8]{1,0:T(4,128)S(1)} %collective-permute-done.2.refs_1_, s32[4,8]{1,0:T(4,128)S(1)} %collective-permute-done.3.refs_2_, ...), custom_call_target="tpu_custom_call" | custom-call | flops 10000000000 | bytes 1024 | tf_op jit(solution)/shard_map/fetch/pallas_call | solution.py:109
  11.1 2.1 %collective-permute-start.5 = (bf16[4,32,896]{2,1,0:T(8,128)(2,1)S(1)}, bf16[4,32,896]{2,1,0:T(8,128)(2,1)S(1)}, u32[]{:S(2)}, u32[]{:S(2)}) collective-permute-start(bf16[4,32,896]{2,1,0:T(8,128)(2,1)S(1)} %get-tuple-element.57), channel_id=1, source_target_pairs={{0,8},{4,12},{8,0},{12,4},{1,9},{5,13},{9,1},{13,5},{2,10},{6,14},... | collective-permute-start | bytes 688136 | tf_op jit(solution)/shard_map/ppermute | solution.py:373
  13.2 1.0 %collective-permute-start.6 = (bf16[2,32,896]{2,1,0:T(8,128)(2,1)S(1)}, bf16[2,32,896]{2,1,0:T(8,128)(2,1)S(1)}, u32[]{:S(2)}, u32[]{:S(2)}) collective-permute-start(bf16[2,32,896]{2,1,0:T(8,128)(2,1)S(1)} %get-tuple-element.60), channel_id=1, source_target_pairs={{0,4},{4,0},{8,12},{12,8},{1,5},{5,1},{9,13},{13,9},{2,6},{6,2},{1... | collective-permute-start | bytes 344072 | tf_op jit(solution)/shard_map/ppermute | solution.py:373
  14.3 1.0 %collective-permute-start.7 = (bf16[2,32,896]{2,1,0:T(8,128)(2,1)S(1)}, bf16[2,32,896]{2,1,0:T(8,128)(2,1)S(1)}, u32[]{:S(2)}, u32[]{:S(2)}) collective-permute-start(bf16[2,32,896]{2,1,0:T(8,128)(2,1)S(1)} %get-tuple-element.61), channel_id=1, source_target_pairs={{0,4},{4,0},{8,12},{12,8},{1,5},{5,1},{9,13},{13,9},{2,6},{6,2},{1... | collective-permute-start | bytes 344072 | tf_op jit(solution)/shard_map/ppermute | solution.py:373
  15.3 1.5 %collective-permute-start = (bf16[4,32,896]{2,1,0:T(8,128)(2,1)S(1)}, bf16[4,32,896]{2,1,0:T(8,128)(2,1)S(1)}, u32[]{:S(2)}, u32[]{:S(2)}) collective-permute-start(bf16[4,32,896]{2,1,0:T(8,128)(2,1)S(1)} %encode_local.1), channel_id=1, source_target_pairs={{0,2},{2,0},{1,3},{3,1},{4,6},{6,4},{5,7},{7,5},{8,10},{10,8},{9,1... | collective-permute-start | bytes 688136 | tf_op jit(solution)/shard_map/ppermute | solution.py:349
  16.7 4.4 %collective-permute-done.6.refs_0_ = bf16[2,32,896]{2,1,0:T(8,128)(2,1)S(1)} collective-permute-done((bf16[2,32,896]{2,1,0:T(8,128)(2,1)S(1)}, bf16[2,32,896]{2,1,0:T(8,128)(2,1)S(1)}, u32[]{:S(2)}, u32[]{:S(2)}) %collective-permute-start.6) | collective-permute-done | bytes 114720 | tf_op jit(solution)/shard_map/ppermute | solution.py:373
  21.2 2.8 %collective-permute-done.7.refs_1_ = bf16[2,32,896]{2,1,0:T(8,128)(2,1)S(1)} collective-permute-done((bf16[2,32,896]{2,1,0:T(8,128)(2,1)S(1)}, bf16[2,32,896]{2,1,0:T(8,128)(2,1)S(1)}, u32[]{:S(2)}, u32[]{:S(2)}) %collective-permute-start.7) | collective-permute-done | bytes 114720 | tf_op jit(solution)/shard_map/ppermute | solution.py:373
  24.0 1.5 %encode.3 = bf16[4,32,896]{2,1,0:T(8,128)(2,1)S(1)} custom-call(s32[16]{0:T(128)S(1)} %get-tuple-element.52.req_ref, bf16[512,896]{1,0:T(8,128)(2,1)S(1)} %copy-done.4, bf16[2,32,896]{2,1,0:T(8,128)(2,1)S(1)} %collective-permute-done.6.refs_0_, bf16[2,32,896]{2,1,0:T(8,128)(2,1)S(1)} %collective-permute-done.7.refs_1_), custom_call_target="tpu_custom_call" | custom-call | flops 100000000 | bytes 1024 | tf_op jit(solution)/shard_map/encode/pallas_call | solution.py:186
  25.4 1.6 %collective-permute-start.11 = (bf16[4,32,896]{2,1,0:T(8,128)(2,1)S(1)}, bf16[4,32,896]{2,1,0:T(8,128)(2,1)S(1)}, u32[]{:S(2)}, u32[]{:S(2)}) collective-permute-start(bf16[4,32,896]{2,1,0:T(8,128)(2,1)S(1)} %encode.3), channel_id=1, source_target_pairs={{0,2},{2,0},{1,3},{3,1},{4,6},{6,4},{5,7},{7,5},{8,10},{10,8},{9,1... | collective-permute-start | bytes 688136 | tf_op jit(solution)/shard_map/ppermute | solution.py:349
  27.0 1.3 %encode.4 = bf16[4,32,896]{2,1,0:T(8,128)(2,1)S(1)} custom-call(s32[16]{0:T(128)S(1)} %get-tuple-element.52.req_ref, bf16[512,896]{1,0:T(8,128)(2,1)S(1)} %copy-done.4, bf16[4,32,896]{2,1,0:T(8,128)(2,1)S(1)} %collective-permute-done.5.refs_0_), custom_call_target="tpu_custom_call" | custom-call | flops 10000000000 | bytes 1024 | tf_op jit(solution)/shard_map/encode/pallas_call | solution.py:186
  28.3 0.6 collective-permute-start.9
  28.9 0.1 collective-permute-start.8
  29.0 4.7 %collective-permute-done.11 = bf16[4,32,896]{2,1,0:T(8,128)(2,1)S(1)} collective-permute-done((bf16[4,32,896]{2,1,0:T(8,128)(2,1)S(1)}, bf16[4,32,896]{2,1,0:T(8,128)(2,1)S(1)}, u32[]{:S(2)}, u32[]{:S(2)}) %collective-permute-start.11) | collective-permute-done | bytes 229408 | tf_op jit(solution)/shard_map/ppermute | solution.py:349
  33.8 0.1 collective-permute-start.12
  33.8 1.1 %collective-permute-done.10.refs_0_ = bf16[4,32,896]{2,1,0:T(8,128)(2,1)S(1)} collective-permute-done((bf16[4,32,896]{2,1,0:T(8,128)(2,1)S(1)}, bf16[4,32,896]{2,1,0:T(8,128)(2,1)S(1)}, u32[]{:S(2)}, u32[]{:S(2)}) %collective-permute-start.10) | collective-permute-done | bytes 229408 | tf_op jit(solution)/shard_map/ppermute | solution.py:373
  34.9 1.3 %encode.5 = bf16[4,32,896]{2,1,0:T(8,128)(2,1)S(1)} custom-call(s32[16]{0:T(128)S(1)} %get-tuple-element.52.req_ref, bf16[512,896]{1,0:T(8,128)(2,1)S(1)} %copy-done.4, bf16[4,32,896]{2,1,0:T(8,128)(2,1)S(1)} %collective-permute-done.10.refs_0_), custom_call_target="tpu_custom_call" | custom-call | flops 10000000000 | bytes 1024 | tf_op jit(solution)/shard_map/encode/pallas_call | solution.py:186
  36.2 0.6 collective-permute-start.14
  36.8 0.1 collective-permute-start.13
  36.9 1.3 %project.3.refs_0_ = bf16[4,4,32,1024]{3,2,1,0:T(8,128)(2,1)S(1)} custom-call(bf16[2,4,32,896]{3,2,1,0:T(8,128)(2,1)S(1)} %pad_maximum_fusion.refs_0_, bf16[2,4,32,896]{3,2,1,0:T(8,128)(2,1)S(1)} %collective-permute-done.8.refs_1_, bf16[896,512]{1,0:T(8,128)(2,1)S(1)} %copy-done.1, bf16[896,512]{1,0:T(8,128)(2,1)S(1)} %copy-done.2), custom_call_target="tpu_custom_call" | custom-call | flops 10000000000 | bytes 1024 | tf_op jit(solution)/shard_map/project/pallas_call | solution.py:238
  38.2 1.3 %project.4.refs_1_ = bf16[4,4,32,1024]{3,2,1,0:T(8,128)(2,1)S(1)} custom-call(bf16[2,4,32,896]{3,2,1,0:T(8,128)(2,1)S(1)} %pad_maximum_fusion.1.refs_0_, bf16[2,4,32,896]{3,2,1,0:T(8,128)(2,1)S(1)} %collective-permute-done.12.refs_1_, bf16[896,512]{1,0:T(8,128)(2,1)S(1)} %copy-done.1, bf16[896,512]{1,0:T(8,128)(2,1)S(1)} %copy-done.2), custom_call_target="tpu_custom_call" | custom-call | flops 10000000000 | bytes 1024 | tf_op jit(solution)/shard_map/project/pallas_call | solution.py:238
  39.5 1.3 %project.5.refs_2_ = bf16[4,4,32,1024]{3,2,1,0:T(8,128)(2,1)S(1)} custom-call(bf16[2,4,32,896]{3,2,1,0:T(8,128)(2,1)S(1)} %pad_maximum_fusion.2.refs_0_, bf16[2,4,32,896]{3,2,1,0:T(8,128)(2,1)S(1)} %collective-permute-done.13.refs_1_, bf16[896,512]{1,0:T(8,128)(2,1)S(1)} %copy-done.1, bf16[896,512]{1,0:T(8,128)(2,1)S(1)} %copy-done.2), custom_call_target="tpu_custom_call" | custom-call | flops 10000000000 | bytes 1024 | tf_op jit(solution)/shard_map/project/pallas_call | solution.py:238
  40.8 2.4 %collective-permute-done.14 = bf16[4,32,896]{2,1,0:T(8,128)(2,1)S(1)} collective-permute-done((bf16[4,32,896]{2,1,0:T(8,128)(2,1)S(1)}, bf16[4,32,896]{2,1,0:T(8,128)(2,1)S(1)}, u32[]{:S(2)}, u32[]{:S(2)}) %collective-permute-start.14) | collective-permute-done | bytes 229408 | tf_op jit(solution)/shard_map/ppermute | solution.py:349
  43.2 0.1 collective-permute-start.15
  43.3 1.8 %collective-permute-done.15.refs_4_ = bf16[2,4,32,896]{3,2,1,0:T(8,128)(2,1)S(1)} collective-permute-done((bf16[2,4,32,896]{3,2,1,0:T(8,128)(2,1)S(1)}, bf16[2,4,32,896]{3,2,1,0:T(8,128)(2,1)S(1)}, u32[]{:S(2)}, u32[]{:S(2)}) %collective-permute-start.15) | collective-permute-done | bytes 458784 | tf_op jit(solution)/shard_map/ppermute | solution.py:352
  45.1 3.4 %attend.2 = (bf16[1,128,512]{2,1,0:T(8,128)(2,1)S(1)}, bf16[1,128,512]{2,1,0:T(8,128)(2,1)S(1)}) custom-call(s32[16]{0:T(128)S(1)} %get-tuple-element.51.slot_ref, bf16[512,512]{1,0:T(8,128)(2,1)S(1)} %copy-done.3, bf16[4,4,32,1024]{3,2,1,0:T(8,128)(2,1)S(1)} %project.3.refs_0_, bf16[4,4,32,1024]{3,2,1,0:T(8,128)(2,1)S(1)} %project.4.refs_1_, ...), custom_call_target="tpu_custom_call" | custom-call | flops 1000000 | bytes 1024 | tf_op jit(solution)/shard_map/attend/pallas_call | solution.py:304
  48.5 0.2 collective-permute-start.16
  48.7 1.2 %collective-permute-done.16.refs_1_ = bf16[1,128,512]{2,1,0:T(8,128)(2,1)S(1)} collective-permute-done((bf16[1,128,512]{2,1,0:T(8,128)(2,1)S(1)}, bf16[1,128,512]{2,1,0:T(8,128)(2,1)S(1)}, u32[]{:S(2)}, u32[]{:S(2)}) %collective-permute-start.16) | collective-permute-done | bytes 131104 | tf_op jit(solution)/shard_map/ppermute | solution.py:401
  50.0 1.3 %out_project.5 = bf16[128,1536]{1,0:T(8,128)(2,1)S(1)} custom-call(bf16[1,128,512]{2,1,0:T(8,128)(2,1)S(1)} %get-tuple-element.91.refs_0_, bf16[1,128,512]{2,1,0:T(8,128)(2,1)S(1)} %collective-permute-done.16.refs_1_, bf16[512,4096]{1,0:T(8,128)(2,1)S(1)} %copy-done, bf16[512,4096]{1,0:T(8,128)(2,1)S(1)} %collective-permute-done.4.refs_3_), custom_call_target="tpu_custom_call" | custom-call | flops 1000000 | bytes 1024 | tf_op jit(solution)/shard_map/out_project/pallas_call | solution.py:324
  51.2 1.2 %collective-permute-start.18 = (bf16[128,1536]{1,0:T(8,128)(2,1)S(1)}, bf16[128,1536]{1,0:T(8,128)(2,1)S(1)}, u32[]{:S(2)}, u32[]{:S(2)}) collective-permute-start(bf16[128,1536]{1,0:T(8,128)(2,1)S(1)} %out_project.5), channel_id=1, source_target_pairs={{0,2},{2,0},{1,3},{3,1},{4,6},{6,4},{5,7},{7,5},{8,10},{10,8},{9,1... | collective-permute-start | bytes 1179656 | tf_op jit(solution)/shard_map/ppermute | solution.py:415
  52.4 0.9 %out_project.6 = bf16[128,1024]{1,0:T(8,128)(2,1)S(1)} custom-call(bf16[1,128,512]{2,1,0:T(8,128)(2,1)S(1)} %get-tuple-element.91.refs_0_, bf16[1,128,512]{2,1,0:T(8,128)(2,1)S(1)} %collective-permute-done.16.refs_1_, bf16[512,4096]{1,0:T(8,128)(2,1)S(1)} %copy-done, bf16[512,4096]{1,0:T(8,128)(2,1)S(1)} %collective-permute-done.4.refs_3_), custom_call_target="tpu_custom_call" | custom-call | flops 1000000 | bytes 1024 | tf_op jit(solution)/shard_map/out_project/pallas_call | solution.py:324
  53.3 0.9 %out_project.7 = bf16[128,1024]{1,0:T(8,128)(2,1)S(1)} custom-call(bf16[1,128,512]{2,1,0:T(8,128)(2,1)S(1)} %get-tuple-element.91.refs_0_, bf16[1,128,512]{2,1,0:T(8,128)(2,1)S(1)} %collective-permute-done.16.refs_1_, bf16[512,4096]{1,0:T(8,128)(2,1)S(1)} %copy-done, bf16[512,4096]{1,0:T(8,128)(2,1)S(1)} %collective-permute-done.4.refs_3_), custom_call_target="tpu_custom_call" | custom-call | flops 1000000 | bytes 1024 | tf_op jit(solution)/shard_map/out_project/pallas_call | solution.py:324
  54.1 1.0 %collective-permute-start.20 = (bf16[128,1024]{1,0:T(8,128)(2,1)S(1)}, bf16[128,1024]{1,0:T(8,128)(2,1)S(1)}, u32[]{:S(2)}, u32[]{:S(2)}) collective-permute-start(bf16[128,1024]{1,0:T(8,128)(2,1)S(1)} %out_project.7), channel_id=1, source_target_pairs={{0,2},{2,0},{1,3},{3,1},{4,6},{6,4},{5,7},{7,5},{8,10},{10,8},{9,1... | collective-permute-start | bytes 786440 | tf_op jit(solution)/shard_map/ppermute | solution.py:415
  55.1 1.1 %collective-permute-start.19 = (bf16[128,1024]{1,0:T(8,128)(2,1)S(1)}, bf16[128,1024]{1,0:T(8,128)(2,1)S(1)}, u32[]{:S(2)}, u32[]{:S(2)}) collective-permute-start(bf16[128,1024]{1,0:T(8,128)(2,1)S(1)} %out_project.6), channel_id=1, source_target_pairs={{0,2},{2,0},{1,3},{3,1},{4,6},{6,4},{5,7},{7,5},{8,10},{10,8},{9,1... | collective-permute-start | bytes 786440 | tf_op jit(solution)/shard_map/ppermute | solution.py:415
  56.2 0.3 out_project.8
  56.6 3.4 %attend.3 = (bf16[1,128,512]{2,1,0:T(8,128)(2,1)S(1)}, bf16[1,128,512]{2,1,0:T(8,128)(2,1)S(1)}) custom-call(s32[16]{0:T(128)S(1)} %get-tuple-element.51.slot_ref, bf16[512,512]{1,0:T(8,128)(2,1)S(1)} %copy-done.3, bf16[4,4,32,1024]{3,2,1,0:T(8,128)(2,1)S(1)} %project.3.refs_0_, bf16[4,4,32,1024]{3,2,1,0:T(8,128)(2,1)S(1)} %project.4.refs_1_, ...), custom_call_target="tpu_custom_call" | custom-call | flops 1000000 | bytes 1024 | tf_op jit(solution)/shard_map/attend/pallas_call | solution.py:304
  60.0 0.1 collective-permute-start.17
  60.1 1.0 %collective-permute-start.21 = (bf16[128,512]{1,0:T(8,128)(2,1)S(1)}, bf16[128,512]{1,0:T(8,128)(2,1)S(1)}, u32[]{:S(2)}, u32[]{:S(2)}) collective-permute-start(bf16[128,512]{1,0:T(8,128)(2,1)S(1)} %out_project.8), channel_id=1, source_target_pairs={{0,2},{2,0},{1,3},{3,1},{4,6},{6,4},{5,7},{7,5},{8,10},{10,8},{9,1... | collective-permute-start | bytes 393224 | tf_op jit(solution)/shard_map/ppermute | solution.py:415
  61.0 0.4 collective-permute-done.17.refs_1_
  61.4 3.3 %out_project.9 = bf16[128,4096]{1,0:T(8,128)(2,1)S(1)} custom-call(bf16[1,128,512]{2,1,0:T(8,128)(2,1)S(1)} %get-tuple-element.95.refs_0_, bf16[1,128,512]{2,1,0:T(8,128)(2,1)S(1)} %collective-permute-done.17.refs_1_, bf16[512,4096]{1,0:T(8,128)(2,1)S(1)} %copy-done, bf16[512,4096]{1,0:T(8,128)(2,1)S(1)} %collective-permute-done.4.refs_3_), custom_call_target="tpu_custom_call" | custom-call | flops 1000000 | bytes 1024 | tf_op jit(solution)/shard_map/out_project/pallas_call | solution.py:324
  64.7 11.8 %collective-permute-done.21 = bf16[128,512]{1,0:T(8,128)(2,1)S(1)} collective-permute-done((bf16[128,512]{1,0:T(8,128)(2,1)S(1)}, bf16[128,512]{1,0:T(8,128)(2,1)S(1)}, u32[]{:S(2)}, u32[]{:S(2)}) %collective-permute-start.21) | collective-permute-done | bytes 131104 | tf_op jit(solution)/shard_map/ppermute | solution.py:415
  76.5 1.2 %add_convert_fusion = bf16[128,4096]{1,0:T(8,128)(2,1)} fusion(bf16[128,4096]{1,0:T(8,128)(2,1)S(1)} %out_project.9, bf16[128,512]{1,0:T(8,128)(2,1)S(1)} %collective-permute-done.21, bf16[128,1024]{1,0:T(8,128)(2,1)S(1)} %collective-permute-done.20, bf16[128,1024]{1,0:T(8,128)(2,1)S(1)} %collective-permute-done.19, ...), kind=kLoop, calls=%fused_computation | loop fusion | flops 5767168 | bytes 3145728 | tf_op jit(solution)/shard_map/convert_element_type | solution.py:420
  (30 shorter events, 0.3 us)
Async XLA Ops:
  0.0 10.3 %collective-permute-start.4 = (bf16[512,4096]{1,0:T(8,128)(2,1)}, bf16[512,4096]{1,0:T(8,128)(2,1)S(1)}, u32[]{:S(2)}, u32[]{:S(2)}) collective-permute-start(bf16[512,4096]{1,0:T(8,128)(2,1)} %refs_2_.15), channel_id=1, source_target_pairs={{0,1},{1,0},{2,3},{3,2},{4,5},{5,4},{6,7},{7,6},{8,9},{9,8},{10,11... | collective-permute-start | bytes 12582920 | tf_op jit(solution)/shard_map/ppermute | solution.py:352
  1.2 6.6 %copy-start.4 = (bf16[512,896]{1,0:T(8,128)(2,1)S(1)}, bf16[512,896]{1,0:T(8,128)(2,1)}, u32[]{:S(2)}) copy-start(bf16[512,896]{1,0:T(8,128)(2,1)} %states_ref.7) | copy-start | bytes 2752516
  1.2 6.6 %copy-start.5 = (bf16[16,32,896]{2,1,0:T(8,128)(2,1)S(1)}, bf16[16,32,896]{2,1,0:T(8,128)(2,1)}, u32[]{:S(2)}) copy-start(bf16[16,32,896]{2,1,0:T(8,128)(2,1)} %refs_3_.4) | copy-start | bytes 2752516
  1.2 7.9 %collective-permute-start.3 = (s32[4,8]{1,0:T(4,128)S(1)}, s32[4,8]{1,0:T(4,128)S(1)}, u32[]{:S(2)}, u32[]{:S(2)}) collective-permute-start(s32[4,8]{1,0:T(4,128)S(1)} %pad_add_fusion.own_ref), channel_id=1, source_target_pairs={{0,12},{4,8},{8,4},{12,0},{1,13},{5,9},{9,5},{13,1},{2,14},{6,10},... | collective-permute-start | bytes 392 | tf_op jit(solution)/shard_map/ppermute | solution.py:364
  5.8 4.5 %collective-permute-start.2 = (s32[4,8]{1,0:T(4,128)S(1)}, s32[4,8]{1,0:T(4,128)S(1)}, u32[]{:S(2)}, u32[]{:S(2)}) collective-permute-start(s32[4,8]{1,0:T(4,128)S(1)} %pad_add_fusion.own_ref), channel_id=1, source_target_pairs={{0,8},{4,12},{8,0},{12,4},{1,9},{5,13},{9,1},{13,5},{2,10},{6,14},... | collective-permute-start | bytes 392 | tf_op jit(solution)/shard_map/ppermute | solution.py:364
  5.8 4.5 %collective-permute-start.1 = (s32[4,8]{1,0:T(4,128)S(1)}, s32[4,8]{1,0:T(4,128)S(1)}, u32[]{:S(2)}, u32[]{:S(2)}) collective-permute-start(s32[4,8]{1,0:T(4,128)S(1)} %pad_add_fusion.own_ref), channel_id=1, source_target_pairs={{0,4},{4,0},{8,12},{12,8},{1,5},{5,1},{9,13},{13,9},{2,6},{6,2},{1... | collective-permute-start | bytes 392 | tf_op jit(solution)/shard_map/ppermute | solution.py:364
  11.1 15.9 %collective-permute-start.5 = (bf16[4,32,896]{2,1,0:T(8,128)(2,1)S(1)}, bf16[4,32,896]{2,1,0:T(8,128)(2,1)S(1)}, u32[]{:S(2)}, u32[]{:S(2)}) collective-permute-start(bf16[4,32,896]{2,1,0:T(8,128)(2,1)S(1)} %get-tuple-element.57), channel_id=1, source_target_pairs={{0,8},{4,12},{8,0},{12,4},{1,9},{5,13},{9,1},{13,5},{2,10},{6,14},... | collective-permute-start | bytes 688136 | tf_op jit(solution)/shard_map/ppermute | solution.py:373
  13.2 7.9 %collective-permute-start.6 = (bf16[2,32,896]{2,1,0:T(8,128)(2,1)S(1)}, bf16[2,32,896]{2,1,0:T(8,128)(2,1)S(1)}, u32[]{:S(2)}, u32[]{:S(2)}) collective-permute-start(bf16[2,32,896]{2,1,0:T(8,128)(2,1)S(1)} %get-tuple-element.60), channel_id=1, source_target_pairs={{0,4},{4,0},{8,12},{12,8},{1,5},{5,1},{9,13},{13,9},{2,6},{6,2},{1... | collective-permute-start | bytes 344072 | tf_op jit(solution)/shard_map/ppermute | solution.py:373
  14.3 9.7 %collective-permute-start.7 = (bf16[2,32,896]{2,1,0:T(8,128)(2,1)S(1)}, bf16[2,32,896]{2,1,0:T(8,128)(2,1)S(1)}, u32[]{:S(2)}, u32[]{:S(2)}) collective-permute-start(bf16[2,32,896]{2,1,0:T(8,128)(2,1)S(1)} %get-tuple-element.61), channel_id=1, source_target_pairs={{0,4},{4,0},{8,12},{12,8},{1,5},{5,1},{9,13},{13,9},{2,6},{6,2},{1... | collective-permute-start | bytes 344072 | tf_op jit(solution)/shard_map/ppermute | solution.py:373
  15.3 13.6 %collective-permute-start = (bf16[4,32,896]{2,1,0:T(8,128)(2,1)S(1)}, bf16[4,32,896]{2,1,0:T(8,128)(2,1)S(1)}, u32[]{:S(2)}, u32[]{:S(2)}) collective-permute-start(bf16[4,32,896]{2,1,0:T(8,128)(2,1)S(1)} %encode_local.1), channel_id=1, source_target_pairs={{0,2},{2,0},{1,3},{3,1},{4,6},{6,4},{5,7},{7,5},{8,10},{10,8},{9,1... | collective-permute-start | bytes 688136 | tf_op jit(solution)/shard_map/ppermute | solution.py:349
  25.4 8.2 %collective-permute-start.11 = (bf16[4,32,896]{2,1,0:T(8,128)(2,1)S(1)}, bf16[4,32,896]{2,1,0:T(8,128)(2,1)S(1)}, u32[]{:S(2)}, u32[]{:S(2)}) collective-permute-start(bf16[4,32,896]{2,1,0:T(8,128)(2,1)S(1)} %encode.3), channel_id=1, source_target_pairs={{0,2},{2,0},{1,3},{3,1},{4,6},{6,4},{5,7},{7,5},{8,10},{10,8},{9,1... | collective-permute-start | bytes 688136 | tf_op jit(solution)/shard_map/ppermute | solution.py:349
  27.0 7.9 %collective-permute-start.10 = (bf16[4,32,896]{2,1,0:T(8,128)(2,1)S(1)}, bf16[4,32,896]{2,1,0:T(8,128)(2,1)S(1)}, u32[]{:S(2)}, u32[]{:S(2)}) collective-permute-start(bf16[4,32,896]{2,1,0:T(8,128)(2,1)S(1)} %get-tuple-element.68), channel_id=1, source_target_pairs={{0,12},{4,8},{8,4},{12,0},{1,13},{5,9},{9,5},{13,1},{2,14},{6,10},... | collective-permute-start | bytes 688136 | tf_op jit(solution)/shard_map/ppermute | solution.py:373
  28.3 8.5 %collective-permute-start.9 = (bf16[4,32,896]{2,1,0:T(8,128)(2,1)S(1)}, bf16[4,32,896]{2,1,0:T(8,128)(2,1)S(1)}, u32[]{:S(2)}, u32[]{:S(2)}) collective-permute-start(bf16[4,32,896]{2,1,0:T(8,128)(2,1)S(1)} %encode.4), channel_id=1, source_target_pairs={{0,2},{2,0},{1,3},{3,1},{4,6},{6,4},{5,7},{7,5},{8,10},{10,8},{9,1... | collective-permute-start | bytes 688136 | tf_op jit(solution)/shard_map/ppermute | solution.py:349
  28.9 8.0 %collective-permute-start.8 = (bf16[2,4,32,896]{3,2,1,0:T(8,128)(2,1)S(1)}, bf16[2,4,32,896]{3,2,1,0:T(8,128)(2,1)S(1)}, u32[]{:S(2)}, u32[]{:S(2)}) collective-permute-start(bf16[2,4,32,896]{3,2,1,0:T(8,128)(2,1)S(1)} %pad_maximum_fusion.refs_0_), channel_id=1, source_target_pairs={{0,1},{1,0},{2,3},{3,2},{4,5},{5,4},{6,7},{7,6},{8,9},{9,8},{10,11... | collective-permute-start | bytes 1376264 | tf_op jit(solution)/shard_map/ppermute | solution.py:352
  33.7 3.2 %copy-start.1 = (bf16[896,512]{1,0:T(8,128)(2,1)S(1)}, bf16[896,512]{1,0:T(8,128)(2,1)}, u32[]{:S(2)}) copy-start(bf16[896,512]{1,0:T(8,128)(2,1)} %refs_5_.3) | copy-start | bytes 2752516
  33.7 3.2 %copy-start.2 = (bf16[896,512]{1,0:T(8,128)(2,1)S(1)}, bf16[896,512]{1,0:T(8,128)(2,1)}, u32[]{:S(2)}) copy-start(bf16[896,512]{1,0:T(8,128)(2,1)} %refs_6_.3) | copy-start | bytes 2752516
  33.8 4.5 %collective-permute-start.12 = (bf16[2,4,32,896]{3,2,1,0:T(8,128)(2,1)S(1)}, bf16[2,4,32,896]{3,2,1,0:T(8,128)(2,1)S(1)}, u32[]{:S(2)}, u32[]{:S(2)}) collective-permute-start(bf16[2,4,32,896]{3,2,1,0:T(8,128)(2,1)S(1)} %pad_maximum_fusion.1.refs_0_), channel_id=1, source_target_pairs={{0,1},{1,0},{2,3},{3,2},{4,5},{5,4},{6,7},{7,6},{8,9},{9,8},{10,11... | collective-permute-start | bytes 1376264 | tf_op jit(solution)/shard_map/ppermute | solution.py:352
  36.2 7.0 %collective-permute-start.14 = (bf16[4,32,896]{2,1,0:T(8,128)(2,1)S(1)}, bf16[4,32,896]{2,1,0:T(8,128)(2,1)S(1)}, u32[]{:S(2)}, u32[]{:S(2)}) collective-permute-start(bf16[4,32,896]{2,1,0:T(8,128)(2,1)S(1)} %encode.5), channel_id=1, source_target_pairs={{0,2},{2,0},{1,3},{3,1},{4,6},{6,4},{5,7},{7,5},{8,10},{10,8},{9,1... | collective-permute-start | bytes 688136 | tf_op jit(solution)/shard_map/ppermute | solution.py:349
  36.8 2.7 %collective-permute-start.13 = (bf16[2,4,32,896]{3,2,1,0:T(8,128)(2,1)S(1)}, bf16[2,4,32,896]{3,2,1,0:T(8,128)(2,1)S(1)}, u32[]{:S(2)}, u32[]{:S(2)}) collective-permute-start(bf16[2,4,32,896]{3,2,1,0:T(8,128)(2,1)S(1)} %pad_maximum_fusion.2.refs_0_), channel_id=1, source_target_pairs={{0,1},{1,0},{2,3},{3,2},{4,5},{5,4},{6,7},{7,6},{8,9},{9,8},{10,11... | collective-permute-start | bytes 1376264 | tf_op jit(solution)/shard_map/ppermute | solution.py:352
  39.5 5.6 %copy-start.3 = (bf16[512,512]{1,0:T(8,128)(2,1)S(1)}, bf16[512,512]{1,0:T(8,128)(2,1)}, u32[]{:S(2)}) copy-start(bf16[512,512]{1,0:T(8,128)(2,1)} %q_ref.2) | copy-start | bytes 1572868
  43.2 1.9 %collective-permute-start.15 = (bf16[2,4,32,896]{3,2,1,0:T(8,128)(2,1)S(1)}, bf16[2,4,32,896]{3,2,1,0:T(8,128)(2,1)S(1)}, u32[]{:S(2)}, u32[]{:S(2)}) collective-permute-start(bf16[2,4,32,896]{3,2,1,0:T(8,128)(2,1)S(1)} %pad_maximum_fusion.3.refs_3_), channel_id=1, source_target_pairs={{0,1},{1,0},{2,3},{3,2},{4,5},{5,4},{6,7},{7,6},{8,9},{9,8},{10,11... | collective-permute-start | bytes 1376264 | tf_op jit(solution)/shard_map/ppermute | solution.py:352
  45.1 4.8 %copy-start = (bf16[512,4096]{1,0:T(8,128)(2,1)S(1)}, bf16[512,4096]{1,0:T(8,128)(2,1)}, u32[]{:S(2)}) copy-start(bf16[512,4096]{1,0:T(8,128)(2,1)} %refs_2_.15) | copy-start | bytes 12582916
  48.5 1.4 %collective-permute-start.16 = (bf16[1,128,512]{2,1,0:T(8,128)(2,1)S(1)}, bf16[1,128,512]{2,1,0:T(8,128)(2,1)S(1)}, u32[]{:S(2)}, u32[]{:S(2)}) collective-permute-start(bf16[1,128,512]{2,1,0:T(8,128)(2,1)S(1)} %get-tuple-element.83), channel_id=1, source_target_pairs={{0,1},{1,0},{2,3},{3,2},{4,5},{5,4},{6,7},{7,6},{8,9},{9,8},{10,11... | collective-permute-start | bytes 393224 | tf_op jit(solution)/shard_map/ppermute | solution.py:401
  51.2 25.3 %collective-permute-start.18 = (bf16[128,1536]{1,0:T(8,128)(2,1)S(1)}, bf16[128,1536]{1,0:T(8,128)(2,1)S(1)}, u32[]{:S(2)}, u32[]{:S(2)}) collective-permute-start(bf16[128,1536]{1,0:T(8,128)(2,1)S(1)} %out_project.5), channel_id=1, source_target_pairs={{0,2},{2,0},{1,3},{3,1},{4,6},{6,4},{5,7},{7,5},{8,10},{10,8},{9,1... | collective-permute-start | bytes 1179656 | tf_op jit(solution)/shard_map/ppermute | solution.py:415
  54.1 22.3 %collective-permute-start.20 = (bf16[128,1024]{1,0:T(8,128)(2,1)S(1)}, bf16[128,1024]{1,0:T(8,128)(2,1)S(1)}, u32[]{:S(2)}, u32[]{:S(2)}) collective-permute-start(bf16[128,1024]{1,0:T(8,128)(2,1)S(1)} %out_project.7), channel_id=1, source_target_pairs={{0,2},{2,0},{1,3},{3,1},{4,6},{6,4},{5,7},{7,5},{8,10},{10,8},{9,1... | collective-permute-start | bytes 786440 | tf_op jit(solution)/shard_map/ppermute | solution.py:415
  55.1 21.4 %collective-permute-start.19 = (bf16[128,1024]{1,0:T(8,128)(2,1)S(1)}, bf16[128,1024]{1,0:T(8,128)(2,1)S(1)}, u32[]{:S(2)}, u32[]{:S(2)}) collective-permute-start(bf16[128,1024]{1,0:T(8,128)(2,1)S(1)} %out_project.6), channel_id=1, source_target_pairs={{0,2},{2,0},{1,3},{3,1},{4,6},{6,4},{5,7},{7,5},{8,10},{10,8},{9,1... | collective-permute-start | bytes 786440 | tf_op jit(solution)/shard_map/ppermute | solution.py:415
  60.0 1.4 %collective-permute-start.17 = (bf16[1,128,512]{2,1,0:T(8,128)(2,1)S(1)}, bf16[1,128,512]{2,1,0:T(8,128)(2,1)S(1)}, u32[]{:S(2)}, u32[]{:S(2)}) collective-permute-start(bf16[1,128,512]{2,1,0:T(8,128)(2,1)S(1)} %get-tuple-element.96), channel_id=1, source_target_pairs={{0,1},{1,0},{2,3},{3,2},{4,5},{5,4},{6,7},{7,6},{8,9},{9,8},{10,11... | collective-permute-start | bytes 393224 | tf_op jit(solution)/shard_map/ppermute | solution.py:401
  60.1 16.4 %collective-permute-start.21 = (bf16[128,512]{1,0:T(8,128)(2,1)S(1)}, bf16[128,512]{1,0:T(8,128)(2,1)S(1)}, u32[]{:S(2)}, u32[]{:S(2)}) collective-permute-start(bf16[128,512]{1,0:T(8,128)(2,1)S(1)} %out_project.8), channel_id=1, source_target_pairs={{0,2},{2,0},{1,3},{3,1},{4,6},{6,4},{5,7},{7,5},{8,10},{10,8},{9,1... | collective-permute-start | bytes 393224 | tf_op jit(solution)/shard_map/ppermute | solution.py:415

commit v8 on v7

--- a/solution.py
+++ b/solution.py
@@ -313,25 +313,34 @@
     )(slot, queries, *ready, *pieces, w_key, w_value)
 
 
-def out_kernel(n_rep, *refs):
-    mixed, weights, out_ref = refs[:n_rep], refs[n_rep:-1], refs[-1]
-    out_ref[...] = sum(dot(a[0], w[...]) for a, w in zip(mixed, weights)).astype(BF16)
-
-
-def out_project(mixed, weights, t, start, stop, tile):
+def out_kernel(n_rep, n_received, *refs):
+    mixed, weights, received = refs[:n_rep], refs[n_rep : 2 * n_rep], refs[2 * n_rep : 2 * n_rep + n_received]
+    total = sum(dot(a[0], w[...]) for a, w in zip(mixed, weights))
+    for part in received:
+        total = total + part[...].astype(F32)
+    refs[-1][...] = total.astype(BF16)
+
+
+def out_project(mixed, weights, t, start, stop, tile, gflops, received=(), out=None, final=False):
     _, rows, depth = mixed[0].shape
+    width = weights[0].shape[1]
     base = start // tile
-    return pl.pallas_call(
-        functools.partial(out_kernel, len(mixed)),
+    n = len(mixed)
+    operands = [*mixed, *weights, *received] + ([] if out is None else [out])
+    return pl.pallas_call(
+        functools.partial(out_kernel, n, len(received)),
         grid=((stop - start) // tile,),
-        out_shape=jax.ShapeDtypeStruct((rows, stop - start), BF16),
-        in_specs=[pl.BlockSpec((1, rows, depth), lambda j: (t, 0, 0))] * len(mixed)
-        + [pl.BlockSpec((depth, tile), lambda j: (0, base + j))] * len(mixed),
-        out_specs=pl.BlockSpec((rows, tile), lambda j: (0, j)),
+        out_shape=jax.ShapeDtypeStruct((rows, width if final else stop - start), BF16),
+        in_specs=[pl.BlockSpec((1, rows, depth), lambda j: (t, 0, 0))] * n
+        + [pl.BlockSpec((depth, tile), lambda j: (0, base + j))] * n
+        + [pl.BlockSpec((rows, tile), lambda j: (0, j))] * len(received)
+        + [ANY] * (out is not None),
+        out_specs=pl.BlockSpec((rows, tile), lambda j: (0, (base if final else 0) + j)),
+        input_output_aliases={} if out is None else {len(operands) - 1: 0},
         compiler_params=params(16),
-        cost_estimate=cost(0.001),
-        name="out_project",
-    )(*mixed, *weights)
+        cost_estimate=cost(gflops),
+        name="out_final" if final else "out_project",
+    )(*operands)
 
 
 def after(values, *earlier):
@@ -362,10 +371,9 @@
 
     own = jnp.concatenate([owners.T, entry_ids.T], axis=0)
     asked = [lax.ppermute(own, "lanes", lane_pairs(n_lanes, d, False)) for d in range(1, n_lanes)]
-    w_outs = over_rep(w_out)
     req, slot, pick = plan(own, order, cap)
     encoded = encode_local(req, pick, span_states, store, cap, fanout, span_len)
-    blocks = fetch(after(asked, w_outs, encoded), store, items, cap)
+    blocks = fetch(after(asked, encoded), store, items, cap)
 
     def send(part, *earlier):
         ready = after([blocks[i] for i in part], *earlier)
@@ -389,7 +397,8 @@
         while i > 1 and len(pieces) < i:
             last = jnp.stack(after(crossed[len(pieces)], last))
             pieces.append(over_rep(last))
-    kvs = []
+    w_outs = over_rep(w_out)
+    kvs, last = [], after(last, w_outs)
     while len(kvs) < len(pieces):
         last = project(after(pieces[len(kvs)], last), w_key, w_value)
         kvs.append(last)
@@ -403,21 +412,21 @@
 
     width = w_out.shape[1]
     tile = min(COL_TILE, width)
-    cuts = [width // tile * part // 8 * tile for part in (0, 3, 5, 7)] + [width]
+    cuts = [width // tile * part // 8 * tile for part in (0, 2, 4, 6, 7)] + [width]
+    blocks = [(start, stop) for start, stop in zip(cuts, cuts[1:]) if stop > start]
     mixed = mix(list(range(1, n_heads)), queries)
-    received, partials = [], []
+    received, partials = [[] for _ in blocks], []
     for t in range(1, n_heads):
-        sent = []
-        for start, stop in zip(cuts, cuts[1:]):
-            partial = out_project(mixed, w_outs, t - 1, start, stop, tile)
+        for i, (start, stop) in enumerate(blocks):
+            partial = out_project(mixed, w_outs, t - 1, start, stop, tile, 0.001)
             partial, mixed = lax.optimization_barrier((partial, mixed))
             partials.append(partial)
-            sent.append(lax.ppermute(partial, "heads", shift_pairs(n_heads, t)))
-        received.append(jnp.concatenate(sent, axis=1))
-    total = out_project(mix([0], after(queries, partials)), w_outs, 0, 0, width, tile).astype(F32)
-    for part in received:
-        total = total + part.astype(F32)
-    return total.astype(BF16)
+            received[i].append(lax.ppermute(partial, "heads", shift_pairs(n_heads, t)))
+    mixed = mix([0], after(queries, partials))
+    out = None
+    for (start, stop), parts in zip(blocks, received):
+        out = out_project(mixed, w_outs, 0, start, stop, tile, 0.2, parts, out, True)
+    return out
 
 
 def solution(mesh):

time: 78.6 us -> 76.4 us (0.972)
  waiting for transfers between devices: 31.9 us -> 27.1 us
  Pallas kernels: 24.5 us -> 27.6 us
  starting transfers between devices: 18.9 us -> 20.2 us
  other arithmetic: 2.11 us -> 0.9 us
    ppermute x4 -> x5, waiting for transfers between devices: 11.8 us -> 8.39 us  [shards(): received[i].append(lax.ppermute(partial, 'heads', shift_pairs(n_heads, t)))]
    pallas_call x5 -> x10, Pallas kernels: 6.58 us -> 9.59 us  [out_project(): pl.pallas_call(functools.partial(out_kernel, n, len(received)), grid=((st...]
    ppermute x4 -> x5, starting transfers between devices: 4.25 us -> 5.58 us  [shards(): received[i].append(lax.ppermute(partial, 'heads', shift_pairs(n_heads, t)))]
    ppermute x4, waiting for transfers between devices: 7.06 us -> 5.8 us  [over_heads(): lax.ppermute(array, 'heads', shift_pairs(n_heads, s))]
    convert_element_type x1 -> x0, other arithmetic: 1.21 us -> none  [shards(): return total.astype(BF16)]
  transfers between devices with their start and end apart: 22 -> 23, of which waited for: 10 -> 12; matrix products, arithmetic and copies ran while one was open for 1% -> 0% of each run, Pallas kernels for 24% -> 33%
where the time goes in v8:
time: 76.4 us; the launch traced here: 76.2 us
  Pallas kernels  27.6 us (36%)
  waiting for transfers between devices  27.1 us (35%)
  starting transfers between devices  20.2 us (26%)
  other arithmetic  0.9 us (1%)
    pallas_call x10, Pallas kernels, out_project(): pl.pallas_call(functools.partial(out_kernel, n, len(received)), grid=((st...  9.59 us
    ppermute x4, waiting for transfers between devices, send(): lax.ppermute(block, 'lanes', lane_pairs(n_lanes, items[i][0], True))  8.6 us
    ppermute x5, waiting for transfers between devices, shards(): received[i].append(lax.ppermute(partial, 'heads', shift_pairs(n_heads, t)))  8.39 us
    pallas_call x2, Pallas kernels, attend(): pl.pallas_call(functools.partial(attend_kernel, firsts, len(pieces), n_he...  7.01 us
    ppermute x4, waiting for transfers between devices, over_heads(): lax.ppermute(array, 'heads', shift_pairs(n_heads, s))  5.8 us
    ppermute x3, starting transfers between devices, shards(): lax.ppermute(own, 'lanes', lane_pairs(n_lanes, d, False))  5.76 us
    ppermute x5, starting transfers between devices, shards(): received[i].append(lax.ppermute(partial, 'heads', shift_pairs(n_heads, t)))  5.58 us
    ppermute x4, starting transfers between devices, over_heads(): lax.ppermute(array, 'heads', shift_pairs(n_heads, s))  4.25 us
  transfers between devices with their start and end apart: 23, of which 12 were waited for; matrix products, arithmetic and copies ran while one was open for 0% of the time, Pallas kernels for 33%

profile of v8, /device:TPU:0, one launch (start us, length us, event | category | flops | bytes accessed | tf_op | source)
XLA Modules:
  0.0 76.2 jit_solution(18075427747766442204)
XLA Ops:
  0.0 0.7 pad_add_fusion.own_ref
  0.7 5.1 %collective-permute-start.3 = (s32[4,8]{1,0:T(4,128)S(1)}, s32[4,8]{1,0:T(4,128)S(1)}, u32[]{:S(2)}, u32[]{:S(2)}) collective-permute-start(s32[4,8]{1,0:T(4,128)S(1)} %pad_add_fusion.own_ref), channel_id=1, source_target_pairs={{0,12},{4,8},{8,4},{12,0},{1,13},{5,9},{9,5},{13,1},{2,14},{6,10},... | collective-permute-start | bytes 392 | tf_op jit(solution)/shard_map/ppermute | solution.py:373
  5.8 0.6 collective-permute-start.1
  6.5 1.3 %plan.1 = (s32[16]{0:T(128)S(1)}, s32[16]{0:T(128)S(1)}, s32[16]{0:T(128)S(1)}) custom-call(s32[4,8]{1,0:T(4,128)S(1)} %pad_add_fusion.own_ref), custom_call_target="tpu_custom_call" | custom-call | flops 10000000000 | bytes 1024 | tf_op jit(solution)/shard_map/plan/pallas_call | solution.py:76
  7.8 1.3 %encode_local.1 = bf16[4,32,896]{2,1,0:T(8,128)(2,1)S(1)} custom-call(s32[16]{0:T(128)S(1)} %get-tuple-element.55.req_ref, s32[16]{0:T(128)S(1)} %get-tuple-element.56.pick_ref, bf16[512,896]{1,0:T(8,128)(2,1)S(1)} %copy-done.4, bf16[16,32,896]{2,1,0:T(8,128)(2,1)S(1)} %copy-done.5), custom_call_target="tpu_custom_call" | custom-call | flops 10000000000 | bytes 1024 | tf_op jit(solution)/shard_map/encode_local/pallas_call | solution.py:205
  9.1 1.3 %collective-permute-done.2.refs_1_ = s32[4,8]{1,0:T(4,128)S(1)} collective-permute-done((s32[4,8]{1,0:T(4,128)S(1)}, s32[4,8]{1,0:T(4,128)S(1)}, u32[]{:S(2)}, u32[]{:S(2)}) %collective-permute-start.2) | collective-permute-done | bytes 160 | tf_op jit(solution)/shard_map/ppermute | solution.py:373
  10.3 0.8 %fetch.1 = (bf16[2,32,896]{2,1,0:T(8,128)(2,1)S(1)}, bf16[2,32,896]{2,1,0:T(8,128)(2,1)S(1)}, bf16[4,32,896]{2,1,0:T(8,128)(2,1)S(1)}, bf16[4,32,896]{2,1,0:T(8,128)(2,1)S(1)}) custom-call(s32[4,8]{1,0:T(4,128)S(1)} %collective-permute-done.1.refs_0_, s32[4,8]{1,0:T(4,128)S(1)} %collective-permute-done.2.refs_1_, s32[4,8]{1,0:T(4,128)S(1)} %collective-permute-done.3.refs_2_, ...), custom_call_target="tpu_custom_call" | custom-call | flops 10000000000 | bytes 1024 | tf_op jit(solution)/shard_map/fetch/pallas_call | solution.py:109
  11.1 2.1 %collective-permute-start.4 = (bf16[4,32,896]{2,1,0:T(8,128)(2,1)S(1)}, bf16[4,32,896]{2,1,0:T(8,128)(2,1)S(1)}, u32[]{:S(2)}, u32[]{:S(2)}) collective-permute-start(bf16[4,32,896]{2,1,0:T(8,128)(2,1)S(1)} %get-tuple-element.60), channel_id=1, source_target_pairs={{0,8},{4,12},{8,0},{12,4},{1,9},{5,13},{9,1},{13,5},{2,10},{6,14},... | collective-permute-start | bytes 688136 | tf_op jit(solution)/shard_map/ppermute | solution.py:381
  13.2 1.0 %collective-permute-start.5 = (bf16[2,32,896]{2,1,0:T(8,128)(2,1)S(1)}, bf16[2,32,896]{2,1,0:T(8,128)(2,1)S(1)}, u32[]{:S(2)}, u32[]{:S(2)}) collective-permute-start(bf16[2,32,896]{2,1,0:T(8,128)(2,1)S(1)} %get-tuple-element.63), channel_id=1, source_target_pairs={{0,4},{4,0},{8,12},{12,8},{1,5},{5,1},{9,13},{13,9},{2,6},{6,2},{1... | collective-permute-start | bytes 344072 | tf_op jit(solution)/shard_map/ppermute | solution.py:381
  14.3 1.0 %collective-permute-start.6 = (bf16[2,32,896]{2,1,0:T(8,128)(2,1)S(1)}, bf16[2,32,896]{2,1,0:T(8,128)(2,1)S(1)}, u32[]{:S(2)}, u32[]{:S(2)}) collective-permute-start(bf16[2,32,896]{2,1,0:T(8,128)(2,1)S(1)} %get-tuple-element.64), channel_id=1, source_target_pairs={{0,4},{4,0},{8,12},{12,8},{1,5},{5,1},{9,13},{13,9},{2,6},{6,2},{1... | collective-permute-start | bytes 344072 | tf_op jit(solution)/shard_map/ppermute | solution.py:381
  15.2 1.5 %collective-permute-start = (bf16[4,32,896]{2,1,0:T(8,128)(2,1)S(1)}, bf16[4,32,896]{2,1,0:T(8,128)(2,1)S(1)}, u32[]{:S(2)}, u32[]{:S(2)}) collective-permute-start(bf16[4,32,896]{2,1,0:T(8,128)(2,1)S(1)} %encode_local.1), channel_id=1, source_target_pairs={{0,2},{2,0},{1,3},{3,1},{4,6},{6,4},{5,7},{7,5},{8,10},{10,8},{9,1... | collective-permute-start | bytes 688136 | tf_op jit(solution)/shard_map/ppermute | solution.py:358
  16.7 3.5 %collective-permute-done.5.refs_0_ = bf16[2,32,896]{2,1,0:T(8,128)(2,1)S(1)} collective-permute-done((bf16[2,32,896]{2,1,0:T(8,128)(2,1)S(1)}, bf16[2,32,896]{2,1,0:T(8,128)(2,1)S(1)}, u32[]{:S(2)}, u32[]{:S(2)}) %collective-permute-start.5) | collective-permute-done | bytes 114720 | tf_op jit(solution)/shard_map/ppermute | solution.py:381
  20.3 3.3 %collective-permute-done.6.refs_1_ = bf16[2,32,896]{2,1,0:T(8,128)(2,1)S(1)} collective-permute-done((bf16[2,32,896]{2,1,0:T(8,128)(2,1)S(1)}, bf16[2,32,896]{2,1,0:T(8,128)(2,1)S(1)}, u32[]{:S(2)}, u32[]{:S(2)}) %collective-permute-start.6) | collective-permute-done | bytes 114720 | tf_op jit(solution)/shard_map/ppermute | solution.py:381
  23.6 1.5 %encode.3 = bf16[4,32,896]{2,1,0:T(8,128)(2,1)S(1)} custom-call(s32[16]{0:T(128)S(1)} %get-tuple-element.55.req_ref, bf16[512,896]{1,0:T(8,128)(2,1)S(1)} %copy-done.4, bf16[2,32,896]{2,1,0:T(8,128)(2,1)S(1)} %collective-permute-done.5.refs_0_, bf16[2,32,896]{2,1,0:T(8,128)(2,1)S(1)} %collective-permute-done.6.refs_1_), custom_call_target="tpu_custom_call" | custom-call | flops 100000000 | bytes 1024 | tf_op jit(solution)/shard_map/encode/pallas_call | solution.py:186
  25.1 1.6 %collective-permute-start.8 = (bf16[4,32,896]{2,1,0:T(8,128)(2,1)S(1)}, bf16[4,32,896]{2,1,0:T(8,128)(2,1)S(1)}, u32[]{:S(2)}, u32[]{:S(2)}) collective-permute-start(bf16[4,32,896]{2,1,0:T(8,128)(2,1)S(1)} %encode.3), channel_id=1, source_target_pairs={{0,2},{2,0},{1,3},{3,1},{4,6},{6,4},{5,7},{7,5},{8,10},{10,8},{9,1... | collective-permute-start | bytes 688136 | tf_op jit(solution)/shard_map/ppermute | solution.py:358
  26.6 1.3 %encode.4 = bf16[4,32,896]{2,1,0:T(8,128)(2,1)S(1)} custom-call(s32[16]{0:T(128)S(1)} %get-tuple-element.55.req_ref, bf16[512,896]{1,0:T(8,128)(2,1)S(1)} %copy-done.4, bf16[4,32,896]{2,1,0:T(8,128)(2,1)S(1)} %collective-permute-done.4.refs_0_), custom_call_target="tpu_custom_call" | custom-call | flops 10000000000 | bytes 1024 | tf_op jit(solution)/shard_map/encode/pallas_call | solution.py:186
  27.9 0.6 collective-permute-start.10
  28.6 4.0 %collective-permute-done.8 = bf16[4,32,896]{2,1,0:T(8,128)(2,1)S(1)} collective-permute-done((bf16[4,32,896]{2,1,0:T(8,128)(2,1)S(1)}, bf16[4,32,896]{2,1,0:T(8,128)(2,1)S(1)}, u32[]{:S(2)}, u32[]{:S(2)}) %collective-permute-start.8) | collective-permute-done | bytes 229408 | tf_op jit(solution)/shard_map/ppermute | solution.py:358
  32.8 1.7 %collective-permute-done.11.refs_0_ = bf16[4,32,896]{2,1,0:T(8,128)(2,1)S(1)} collective-permute-done((bf16[4,32,896]{2,1,0:T(8,128)(2,1)S(1)}, bf16[4,32,896]{2,1,0:T(8,128)(2,1)S(1)}, u32[]{:S(2)}, u32[]{:S(2)}) %collective-permute-start.11) | collective-permute-done | bytes 229408 | tf_op jit(solution)/shard_map/ppermute | solution.py:381
  34.6 1.3 %encode.5 = bf16[4,32,896]{2,1,0:T(8,128)(2,1)S(1)} custom-call(s32[16]{0:T(128)S(1)} %get-tuple-element.55.req_ref, bf16[512,896]{1,0:T(8,128)(2,1)S(1)} %copy-done.4, bf16[4,32,896]{2,1,0:T(8,128)(2,1)S(1)} %collective-permute-done.11.refs_0_), custom_call_target="tpu_custom_call" | custom-call | flops 10000000000 | bytes 1024 | tf_op jit(solution)/shard_map/encode/pallas_call | solution.py:186
  35.8 0.6 collective-permute-start.13
  36.6 1.2 %project.3.refs_0_ = bf16[4,4,32,1024]{3,2,1,0:T(8,128)(2,1)S(1)} custom-call(bf16[2,4,32,896]{3,2,1,0:T(8,128)(2,1)S(1)} %pad_maximum_fusion.refs_0_, bf16[2,4,32,896]{3,2,1,0:T(8,128)(2,1)S(1)} %collective-permute-done.7.refs_1_, bf16[896,512]{1,0:T(8,128)(2,1)S(1)} %copy-done.1, bf16[896,512]{1,0:T(8,128)(2,1)S(1)} %copy-done.2), custom_call_target="tpu_custom_call" | custom-call | flops 10000000000 | bytes 1024 | tf_op jit(solution)/shard_map/project/pallas_call | solution.py:238
  37.8 1.3 %project.4.refs_1_ = bf16[4,4,32,1024]{3,2,1,0:T(8,128)(2,1)S(1)} custom-call(bf16[2,4,32,896]{3,2,1,0:T(8,128)(2,1)S(1)} %pad_maximum_fusion.1.refs_0_, bf16[2,4,32,896]{3,2,1,0:T(8,128)(2,1)S(1)} %collective-permute-done.9.refs_1_, bf16[896,512]{1,0:T(8,128)(2,1)S(1)} %copy-done.1, bf16[896,512]{1,0:T(8,128)(2,1)S(1)} %copy-done.2), custom_call_target="tpu_custom_call" | custom-call | flops 10000000000 | bytes 1024 | tf_op jit(solution)/shard_map/project/pallas_call | solution.py:238
  39.1 1.2 %project.5.refs_2_ = bf16[4,4,32,1024]{3,2,1,0:T(8,128)(2,1)S(1)} custom-call(bf16[2,4,32,896]{3,2,1,0:T(8,128)(2,1)S(1)} %pad_maximum_fusion.2.refs_0_, bf16[2,4,32,896]{3,2,1,0:T(8,128)(2,1)S(1)} %collective-permute-done.12.refs_1_, bf16[896,512]{1,0:T(8,128)(2,1)S(1)} %copy-done.1, bf16[896,512]{1,0:T(8,128)(2,1)S(1)} %copy-done.2), custom_call_target="tpu_custom_call" | custom-call | flops 10000000000 | bytes 1024 | tf_op jit(solution)/shard_map/project/pallas_call | solution.py:238
  40.4 1.8 %collective-permute-done.13 = bf16[4,32,896]{2,1,0:T(8,128)(2,1)S(1)} collective-permute-done((bf16[4,32,896]{2,1,0:T(8,128)(2,1)S(1)}, bf16[4,32,896]{2,1,0:T(8,128)(2,1)S(1)}, u32[]{:S(2)}, u32[]{:S(2)}) %collective-permute-start.13) | collective-permute-done | bytes 229408 | tf_op jit(solution)/shard_map/ppermute | solution.py:358
  42.3 1.8 %collective-permute-done.14.refs_4_ = bf16[2,4,32,896]{3,2,1,0:T(8,128)(2,1)S(1)} collective-permute-done((bf16[2,4,32,896]{3,2,1,0:T(8,128)(2,1)S(1)}, bf16[2,4,32,896]{3,2,1,0:T(8,128)(2,1)S(1)}, u32[]{:S(2)}, u32[]{:S(2)}) %collective-permute-start.14) | collective-permute-done | bytes 458784 | tf_op jit(solution)/shard_map/ppermute | solution.py:361
  44.1 3.6 %attend.2 = (bf16[1,128,512]{2,1,0:T(8,128)(2,1)S(1)}, bf16[1,128,512]{2,1,0:T(8,128)(2,1)S(1)}) custom-call(s32[16]{0:T(128)S(1)} %get-tuple-element.54.slot_ref, bf16[512,512]{1,0:T(8,128)(2,1)S(1)} %copy-done.3, bf16[4,4,32,1024]{3,2,1,0:T(8,128)(2,1)S(1)} %project.3.refs_0_, bf16[4,4,32,1024]{3,2,1,0:T(8,128)(2,1)S(1)} %project.4.refs_1_, ...), custom_call_target="tpu_custom_call" | custom-call | flops 1000000 | bytes 1024 | tf_op jit(solution)/shard_map/attend/pallas_call | solution.py:304
  47.9 1.2 %collective-permute-done.15.refs_1_ = bf16[1,128,512]{2,1,0:T(8,128)(2,1)S(1)} collective-permute-done((bf16[1,128,512]{2,1,0:T(8,128)(2,1)S(1)}, bf16[1,128,512]{2,1,0:T(8,128)(2,1)S(1)}, u32[]{:S(2)}, u32[]{:S(2)}) %collective-permute-start.15) | collective-permute-done | bytes 131104 | tf_op jit(solution)/shard_map/ppermute | solution.py:410
  49.1 0.8 %out_project.5 = bf16[128,1024]{1,0:T(8,128)(2,1)S(1)} custom-call(bf16[1,128,512]{2,1,0:T(8,128)(2,1)S(1)} %get-tuple-element.97.refs_0_, bf16[1,128,512]{2,1,0:T(8,128)(2,1)S(1)} %collective-permute-done.15.refs_1_, bf16[512,4096]{1,0:T(8,128)(2,1)S(1)} %copy-done, bf16[512,4096]{1,0:T(8,128)(2,1)S(1)} %collective-permute-done.16.refs_3_), custom_call_target="tpu_custom_call" | custom-call | flops 1000000 | bytes 1024 | tf_op jit(solution)/shard_map/out_project/pallas_call | solution.py:330
  50.0 0.6 collective-permute-start.22
  50.6 0.8 %out_project.6 = bf16[128,1024]{1,0:T(8,128)(2,1)S(1)} custom-call(bf16[1,128,512]{2,1,0:T(8,128)(2,1)S(1)} %get-tuple-element.97.refs_0_, bf16[1,128,512]{2,1,0:T(8,128)(2,1)S(1)} %collective-permute-done.15.refs_1_, bf16[512,4096]{1,0:T(8,128)(2,1)S(1)} %copy-done, bf16[512,4096]{1,0:T(8,128)(2,1)S(1)} %collective-permute-done.16.refs_3_), custom_call_target="tpu_custom_call" | custom-call | flops 1000000 | bytes 1024 | tf_op jit(solution)/shard_map/out_project/pallas_call | solution.py:330
  51.4 1.6 %collective-permute-start.21 = (bf16[128,1024]{1,0:T(8,128)(2,1)S(1)}, bf16[128,1024]{1,0:T(8,128)(2,1)S(1)}, u32[]{:S(2)}, u32[]{:S(2)}) collective-permute-start(bf16[128,1024]{1,0:T(8,128)(2,1)S(1)} %out_project.6), channel_id=1, source_target_pairs={{0,2},{2,0},{1,3},{3,1},{4,6},{6,4},{5,7},{7,5},{8,10},{10,8},{9,1... | collective-permute-start | bytes 786440 | tf_op jit(solution)/shard_map/ppermute | solution.py:424
  53.0 0.8 %out_project.7 = bf16[128,1024]{1,0:T(8,128)(2,1)S(1)} custom-call(bf16[1,128,512]{2,1,0:T(8,128)(2,1)S(1)} %get-tuple-element.97.refs_0_, bf16[1,128,512]{2,1,0:T(8,128)(2,1)S(1)} %collective-permute-done.15.refs_1_, bf16[512,4096]{1,0:T(8,128)(2,1)S(1)} %copy-done, bf16[512,4096]{1,0:T(8,128)(2,1)S(1)} %collective-permute-done.16.refs_3_), custom_call_target="tpu_custom_call" | custom-call | flops 1000000 | bytes 1024 | tf_op jit(solution)/shard_map/out_project/pallas_call | solution.py:330
  53.8 0.6 collective-permute-start.20
  54.4 0.3 out_project.8
  54.8 0.3 out_project.9
  55.1 3.4 %attend.3 = (bf16[1,128,512]{2,1,0:T(8,128)(2,1)S(1)}, bf16[1,128,512]{2,1,0:T(8,128)(2,1)S(1)}) custom-call(s32[16]{0:T(128)S(1)} %get-tuple-element.54.slot_ref, bf16[512,512]{1,0:T(8,128)(2,1)S(1)} %copy-done.3, bf16[4,4,32,1024]{3,2,1,0:T(8,128)(2,1)S(1)} %project.3.refs_0_, bf16[4,4,32,1024]{3,2,1,0:T(8,128)(2,1)S(1)} %project.4.refs_1_, ...), custom_call_target="tpu_custom_call" | custom-call | flops 1000000 | bytes 1024 | tf_op jit(solution)/shard_map/attend/pallas_call | solution.py:304
  58.6 1.5 %collective-permute-start.19 = (bf16[128,512]{1,0:T(8,128)(2,1)S(1)}, bf16[128,512]{1,0:T(8,128)(2,1)S(1)}, u32[]{:S(2)}, u32[]{:S(2)}) collective-permute-start(bf16[128,512]{1,0:T(8,128)(2,1)S(1)} %out_project.8), channel_id=1, source_target_pairs={{0,2},{2,0},{1,3},{3,1},{4,6},{6,4},{5,7},{7,5},{8,10},{10,8},{9,1... | collective-permute-start | bytes 393224 | tf_op jit(solution)/shard_map/ppermute | solution.py:424
  60.1 1.3 %collective-permute-start.18 = (bf16[128,512]{1,0:T(8,128)(2,1)S(1)}, bf16[128,512]{1,0:T(8,128)(2,1)S(1)}, u32[]{:S(2)}, u32[]{:S(2)}) collective-permute-start(bf16[128,512]{1,0:T(8,128)(2,1)S(1)} %out_project.9), channel_id=1, source_target_pairs={{0,2},{2,0},{1,3},{3,1},{4,6},{6,4},{5,7},{7,5},{8,10},{10,8},{9,1... | collective-permute-start | bytes 393224 | tf_op jit(solution)/shard_map/ppermute | solution.py:424
  61.4 1.5 %out_final.5.refs_5_ = bf16[128,4096]{1,0:T(8,128)(2,1)} custom-call(bf16[1,128,512]{2,1,0:T(8,128)(2,1)S(1)} %get-tuple-element.101.refs_0_, bf16[1,128,512]{2,1,0:T(8,128)(2,1)S(1)} %collective-permute-done.17.refs_1_, bf16[512,4096]{1,0:T(8,128)(2,1)S(1)} %copy-done, bf16[512,4096]{1,0:T(8,128)(2,1)S(1)} %collective-permute-done.16.refs_3_, ...), custom_call_target="tpu_custom_call" | custom-call | flops 200000000 | bytes 1024 | tf_op jit(solution)/shard_map/out_final/pallas_call | solution.py:330
  62.9 1.9 %collective-permute-done.21.refs_4_ = bf16[128,1024]{1,0:T(8,128)(2,1)S(1)} collective-permute-done((bf16[128,1024]{1,0:T(8,128)(2,1)S(1)}, bf16[128,1024]{1,0:T(8,128)(2,1)S(1)}, u32[]{:S(2)}, u32[]{:S(2)}) %collective-permute-start.21) | collective-permute-done | bytes 262176 | tf_op jit(solution)/shard_map/ppermute | solution.py:424
  64.8 1.5 %out_final.6.refs_5_ = bf16[128,4096]{1,0:T(8,128)(2,1)} custom-call(bf16[1,128,512]{2,1,0:T(8,128)(2,1)S(1)} %get-tuple-element.101.refs_0_, bf16[1,128,512]{2,1,0:T(8,128)(2,1)S(1)} %collective-permute-done.17.refs_1_, bf16[512,4096]{1,0:T(8,128)(2,1)S(1)} %copy-done, ...), custom_call_target="tpu_custom_call", output_to_operand_aliasing={{}: (5, {})} | custom-call | flops 200000000 | bytes 1024 | tf_op jit(solution)/shard_map/out_final/pallas_call | solution.py:330
  66.3 4.1 %collective-permute-done.20.refs_4_ = bf16[128,1024]{1,0:T(8,128)(2,1)S(1)} collective-permute-done((bf16[128,1024]{1,0:T(8,128)(2,1)S(1)}, bf16[128,1024]{1,0:T(8,128)(2,1)S(1)}, u32[]{:S(2)}, u32[]{:S(2)}) %collective-permute-start.20) | collective-permute-done | bytes 262176 | tf_op jit(solution)/shard_map/ppermute | solution.py:424
  70.4 1.5 %out_final.7.refs_5_ = bf16[128,4096]{1,0:T(8,128)(2,1)} custom-call(bf16[1,128,512]{2,1,0:T(8,128)(2,1)S(1)} %get-tuple-element.101.refs_0_, bf16[1,128,512]{2,1,0:T(8,128)(2,1)S(1)} %collective-permute-done.17.refs_1_, bf16[512,4096]{1,0:T(8,128)(2,1)S(1)} %copy-done, ...), custom_call_target="tpu_custom_call", output_to_operand_aliasing={{}: (5, {})} | custom-call | flops 200000000 | bytes 1024 | tf_op jit(solution)/shard_map/out_final/pallas_call | solution.py:330
  71.9 1.3 %collective-permute-done.19.refs_4_ = bf16[128,512]{1,0:T(8,128)(2,1)S(1)} collective-permute-done((bf16[128,512]{1,0:T(8,128)(2,1)S(1)}, bf16[128,512]{1,0:T(8,128)(2,1)S(1)}, u32[]{:S(2)}, u32[]{:S(2)}) %collective-permute-start.19) | collective-permute-done | bytes 131104 | tf_op jit(solution)/shard_map/ppermute | solution.py:424
  73.2 1.0 %out_final.8.refs_5_ = bf16[128,4096]{1,0:T(8,128)(2,1)} custom-call(bf16[1,128,512]{2,1,0:T(8,128)(2,1)S(1)} %get-tuple-element.101.refs_0_, bf16[1,128,512]{2,1,0:T(8,128)(2,1)S(1)} %collective-permute-done.17.refs_1_, bf16[512,4096]{1,0:T(8,128)(2,1)S(1)} %copy-done, ...), custom_call_target="tpu_custom_call", output_to_operand_aliasing={{}: (5, {})} | custom-call | flops 200000000 | bytes 1024 | tf_op jit(solution)/shard_map/out_final/pallas_call | solution.py:330
  74.2 1.0 %collective-permute-done.18.refs_4_ = bf16[128,512]{1,0:T(8,128)(2,1)S(1)} collective-permute-done((bf16[128,512]{1,0:T(8,128)(2,1)S(1)}, bf16[128,512]{1,0:T(8,128)(2,1)S(1)}, u32[]{:S(2)}, u32[]{:S(2)}) %collective-permute-start.18) | collective-permute-done | bytes 131104 | tf_op jit(solution)/shard_map/ppermute | solution.py:424
  75.2 1.0 %out_final.9 = bf16[128,4096]{1,0:T(8,128)(2,1)} custom-call(bf16[1,128,512]{2,1,0:T(8,128)(2,1)S(1)} %get-tuple-element.101.refs_0_, bf16[1,128,512]{2,1,0:T(8,128)(2,1)S(1)} %collective-permute-done.17.refs_1_, bf16[512,4096]{1,0:T(8,128)(2,1)S(1)} %copy-done, ...), custom_call_target="tpu_custom_call", output_to_operand_aliasing={{}: (5, {})} | custom-call | flops 200000000 | bytes 1024 | tf_op jit(solution)/shard_map/out_final/pallas_call | solution.py:330
  (36 shorter events, 0.8 us)
Async XLA Ops:
  0.7 7.0 %copy-start.4 = (bf16[512,896]{1,0:T(8,128)(2,1)S(1)}, bf16[512,896]{1,0:T(8,128)(2,1)}, u32[]{:S(2)}) copy-start(bf16[512,896]{1,0:T(8,128)(2,1)} %states_ref.7) | copy-start | bytes 2752516
  0.7 7.0 %copy-start.5 = (bf16[16,32,896]{2,1,0:T(8,128)(2,1)S(1)}, bf16[16,32,896]{2,1,0:T(8,128)(2,1)}, u32[]{:S(2)}) copy-start(bf16[16,32,896]{2,1,0:T(8,128)(2,1)} %refs_3_.4) | copy-start | bytes 2752516
  0.7 8.3 %collective-permute-start.3 = (s32[4,8]{1,0:T(4,128)S(1)}, s32[4,8]{1,0:T(4,128)S(1)}, u32[]{:S(2)}, u32[]{:S(2)}) collective-permute-start(s32[4,8]{1,0:T(4,128)S(1)} %pad_add_fusion.own_ref), channel_id=1, source_target_pairs={{0,12},{4,8},{8,4},{12,0},{1,13},{5,9},{9,5},{13,1},{2,14},{6,10},... | collective-permute-start | bytes 392 | tf_op jit(solution)/shard_map/ppermute | solution.py:373
  5.8 4.5 %collective-permute-start.2 = (s32[4,8]{1,0:T(4,128)S(1)}, s32[4,8]{1,0:T(4,128)S(1)}, u32[]{:S(2)}, u32[]{:S(2)}) collective-permute-start(s32[4,8]{1,0:T(4,128)S(1)} %pad_add_fusion.own_ref), channel_id=1, source_target_pairs={{0,8},{4,12},{8,0},{12,4},{1,9},{5,13},{9,1},{13,5},{2,10},{6,14},... | collective-permute-start | bytes 392 | tf_op jit(solution)/shard_map/ppermute | solution.py:373
  5.8 4.5 %collective-permute-start.1 = (s32[4,8]{1,0:T(4,128)S(1)}, s32[4,8]{1,0:T(4,128)S(1)}, u32[]{:S(2)}, u32[]{:S(2)}) collective-permute-start(s32[4,8]{1,0:T(4,128)S(1)} %pad_add_fusion.own_ref), channel_id=1, source_target_pairs={{0,4},{4,0},{8,12},{12,8},{1,5},{5,1},{9,13},{13,9},{2,6},{6,2},{1... | collective-permute-start | bytes 392 | tf_op jit(solution)/shard_map/ppermute | solution.py:373
  9.0 7.7 %copy-start = (bf16[512,4096]{1,0:T(8,128)(2,1)S(1)}, bf16[512,4096]{1,0:T(8,128)(2,1)}, u32[]{:S(2)}) copy-start(bf16[512,4096]{1,0:T(8,128)(2,1)} %refs_2_.25) | copy-start | bytes 12582916
  11.1 15.5 %collective-permute-start.4 = (bf16[4,32,896]{2,1,0:T(8,128)(2,1)S(1)}, bf16[4,32,896]{2,1,0:T(8,128)(2,1)S(1)}, u32[]{:S(2)}, u32[]{:S(2)}) collective-permute-start(bf16[4,32,896]{2,1,0:T(8,128)(2,1)S(1)} %get-tuple-element.60), channel_id=1, source_target_pairs={{0,8},{4,12},{8,0},{12,4},{1,9},{5,13},{9,1},{13,5},{2,10},{6,14},... | collective-permute-start | bytes 688136 | tf_op jit(solution)/shard_map/ppermute | solution.py:381
  13.2 7.0 %collective-permute-start.5 = (bf16[2,32,896]{2,1,0:T(8,128)(2,1)S(1)}, bf16[2,32,896]{2,1,0:T(8,128)(2,1)S(1)}, u32[]{:S(2)}, u32[]{:S(2)}) collective-permute-start(bf16[2,32,896]{2,1,0:T(8,128)(2,1)S(1)} %get-tuple-element.63), channel_id=1, source_target_pairs={{0,4},{4,0},{8,12},{12,8},{1,5},{5,1},{9,13},{13,9},{2,6},{6,2},{1... | collective-permute-start | bytes 344072 | tf_op jit(solution)/shard_map/ppermute | solution.py:381
  14.3 9.4 %collective-permute-start.6 = (bf16[2,32,896]{2,1,0:T(8,128)(2,1)S(1)}, bf16[2,32,896]{2,1,0:T(8,128)(2,1)S(1)}, u32[]{:S(2)}, u32[]{:S(2)}) collective-permute-start(bf16[2,32,896]{2,1,0:T(8,128)(2,1)S(1)} %get-tuple-element.64), channel_id=1, source_target_pairs={{0,4},{4,0},{8,12},{12,8},{1,5},{5,1},{9,13},{13,9},{2,6},{6,2},{1... | collective-permute-start | bytes 344072 | tf_op jit(solution)/shard_map/ppermute | solution.py:381
  15.2 13.3 %collective-permute-start = (bf16[4,32,896]{2,1,0:T(8,128)(2,1)S(1)}, bf16[4,32,896]{2,1,0:T(8,128)(2,1)S(1)}, u32[]{:S(2)}, u32[]{:S(2)}) collective-permute-start(bf16[4,32,896]{2,1,0:T(8,128)(2,1)S(1)} %encode_local.1), channel_id=1, source_target_pairs={{0,2},{2,0},{1,3},{3,1},{4,6},{6,4},{5,7},{7,5},{8,10},{10,8},{9,1... | collective-permute-start | bytes 688136 | tf_op jit(solution)/shard_map/ppermute | solution.py:358
  16.7 32.4 %collective-permute-start.16 = (bf16[512,4096]{1,0:T(8,128)(2,1)S(1)}, bf16[512,4096]{1,0:T(8,128)(2,1)S(1)}, u32[]{:S(2)}, u32[]{:S(2)}) collective-permute-start(bf16[512,4096]{1,0:T(8,128)(2,1)S(1)} %copy-done), channel_id=1, source_target_pairs={{0,1},{1,0},{2,3},{3,2},{4,5},{5,4},{6,7},{7,6},{8,9},{9,8},{10,11... | collective-permute-start | bytes 12582920 | tf_op jit(solution)/shard_map/ppermute | solution.py:361
  25.1 7.6 %collective-permute-start.8 = (bf16[4,32,896]{2,1,0:T(8,128)(2,1)S(1)}, bf16[4,32,896]{2,1,0:T(8,128)(2,1)S(1)}, u32[]{:S(2)}, u32[]{:S(2)}) collective-permute-start(bf16[4,32,896]{2,1,0:T(8,128)(2,1)S(1)} %encode.3), channel_id=1, source_target_pairs={{0,2},{2,0},{1,3},{3,1},{4,6},{6,4},{5,7},{7,5},{8,10},{10,8},{9,1... | collective-permute-start | bytes 688136 | tf_op jit(solution)/shard_map/ppermute | solution.py:358
  26.6 7.9 %collective-permute-start.11 = (bf16[4,32,896]{2,1,0:T(8,128)(2,1)S(1)}, bf16[4,32,896]{2,1,0:T(8,128)(2,1)S(1)}, u32[]{:S(2)}, u32[]{:S(2)}) collective-permute-start(bf16[4,32,896]{2,1,0:T(8,128)(2,1)S(1)} %get-tuple-element.77), channel_id=1, source_target_pairs={{0,12},{4,8},{8,4},{12,0},{1,13},{5,9},{9,5},{13,1},{2,14},{6,10},... | collective-permute-start | bytes 688136 | tf_op jit(solution)/shard_map/ppermute | solution.py:381
  27.9 8.5 %collective-permute-start.10 = (bf16[4,32,896]{2,1,0:T(8,128)(2,1)S(1)}, bf16[4,32,896]{2,1,0:T(8,128)(2,1)S(1)}, u32[]{:S(2)}, u32[]{:S(2)}) collective-permute-start(bf16[4,32,896]{2,1,0:T(8,128)(2,1)S(1)} %encode.4), channel_id=1, source_target_pairs={{0,2},{2,0},{1,3},{3,1},{4,6},{6,4},{5,7},{7,5},{8,10},{10,8},{9,1... | collective-permute-start | bytes 688136 | tf_op jit(solution)/shard_map/ppermute | solution.py:358
  28.6 8.0 %collective-permute-start.7 = (bf16[2,4,32,896]{3,2,1,0:T(8,128)(2,1)S(1)}, bf16[2,4,32,896]{3,2,1,0:T(8,128)(2,1)S(1)}, u32[]{:S(2)}, u32[]{:S(2)}) collective-permute-start(bf16[2,4,32,896]{3,2,1,0:T(8,128)(2,1)S(1)} %pad_maximum_fusion.refs_0_), channel_id=1, source_target_pairs={{0,1},{1,0},{2,3},{3,2},{4,5},{5,4},{6,7},{7,6},{8,9},{9,8},{10,11... | collective-permute-start | bytes 1376264 | tf_op jit(solution)/shard_map/ppermute | solution.py:361
  32.7 3.8 %copy-start.1 = (bf16[896,512]{1,0:T(8,128)(2,1)S(1)}, bf16[896,512]{1,0:T(8,128)(2,1)}, u32[]{:S(2)}) copy-start(bf16[896,512]{1,0:T(8,128)(2,1)} %refs_5_.3) | copy-start | bytes 2752516
  32.7 3.8 %copy-start.2 = (bf16[896,512]{1,0:T(8,128)(2,1)S(1)}, bf16[896,512]{1,0:T(8,128)(2,1)}, u32[]{:S(2)}) copy-start(bf16[896,512]{1,0:T(8,128)(2,1)} %refs_6_.3) | copy-start | bytes 2752516
  32.7 5.1 %collective-permute-start.9 = (bf16[2,4,32,896]{3,2,1,0:T(8,128)(2,1)S(1)}, bf16[2,4,32,896]{3,2,1,0:T(8,128)(2,1)S(1)}, u32[]{:S(2)}, u32[]{:S(2)}) collective-permute-start(bf16[2,4,32,896]{3,2,1,0:T(8,128)(2,1)S(1)} %pad_maximum_fusion.1.refs_0_), channel_id=1, source_target_pairs={{0,1},{1,0},{2,3},{3,2},{4,5},{5,4},{6,7},{7,6},{8,9},{9,8},{10,11... | collective-permute-start | bytes 1376264 | tf_op jit(solution)/shard_map/ppermute | solution.py:361
  35.8 6.3 %collective-permute-start.13 = (bf16[4,32,896]{2,1,0:T(8,128)(2,1)S(1)}, bf16[4,32,896]{2,1,0:T(8,128)(2,1)S(1)}, u32[]{:S(2)}, u32[]{:S(2)}) collective-permute-start(bf16[4,32,896]{2,1,0:T(8,128)(2,1)S(1)} %encode.5), channel_id=1, source_target_pairs={{0,2},{2,0},{1,3},{3,1},{4,6},{6,4},{5,7},{7,5},{8,10},{10,8},{9,1... | collective-permute-start | bytes 688136 | tf_op jit(solution)/shard_map/ppermute | solution.py:358
  36.5 2.7 %collective-permute-start.12 = (bf16[2,4,32,896]{3,2,1,0:T(8,128)(2,1)S(1)}, bf16[2,4,32,896]{3,2,1,0:T(8,128)(2,1)S(1)}, u32[]{:S(2)}, u32[]{:S(2)}) collective-permute-start(bf16[2,4,32,896]{3,2,1,0:T(8,128)(2,1)S(1)} %pad_maximum_fusion.2.refs_0_), channel_id=1, source_target_pairs={{0,1},{1,0},{2,3},{3,2},{4,5},{5,4},{6,7},{7,6},{8,9},{9,8},{10,11... | collective-permute-start | bytes 1376264 | tf_op jit(solution)/shard_map/ppermute | solution.py:361
  39.1 5.0 %copy-start.3 = (bf16[512,512]{1,0:T(8,128)(2,1)S(1)}, bf16[512,512]{1,0:T(8,128)(2,1)}, u32[]{:S(2)}) copy-start(bf16[512,512]{1,0:T(8,128)(2,1)} %q_ref.2) | copy-start | bytes 1572868
  42.2 1.9 %collective-permute-start.14 = (bf16[2,4,32,896]{3,2,1,0:T(8,128)(2,1)S(1)}, bf16[2,4,32,896]{3,2,1,0:T(8,128)(2,1)S(1)}, u32[]{:S(2)}, u32[]{:S(2)}) collective-permute-start(bf16[2,4,32,896]{3,2,1,0:T(8,128)(2,1)S(1)} %pad_maximum_fusion.3.refs_3_), channel_id=1, source_target_pairs={{0,1},{1,0},{2,3},{3,2},{4,5},{5,4},{6,7},{7,6},{8,9},{9,8},{10,11... | collective-permute-start | bytes 1376264 | tf_op jit(solution)/shard_map/ppermute | solution.py:361
  47.7 1.4 %collective-permute-start.15 = (bf16[1,128,512]{2,1,0:T(8,128)(2,1)S(1)}, bf16[1,128,512]{2,1,0:T(8,128)(2,1)S(1)}, u32[]{:S(2)}, u32[]{:S(2)}) collective-permute-start(bf16[1,128,512]{2,1,0:T(8,128)(2,1)S(1)} %get-tuple-element.86), channel_id=1, source_target_pairs={{0,1},{1,0},{2,3},{3,2},{4,5},{5,4},{6,7},{7,6},{8,9},{9,8},{10,11... | collective-permute-start | bytes 393224 | tf_op jit(solution)/shard_map/ppermute | solution.py:410
  50.0 11.4 %collective-permute-start.22 = (bf16[128,1024]{1,0:T(8,128)(2,1)S(1)}, bf16[128,1024]{1,0:T(8,128)(2,1)S(1)}, u32[]{:S(2)}, u32[]{:S(2)}) collective-permute-start(bf16[128,1024]{1,0:T(8,128)(2,1)S(1)} %out_project.5), channel_id=1, source_target_pairs={{0,2},{2,0},{1,3},{3,1},{4,6},{6,4},{5,7},{7,5},{8,10},{10,8},{9,1... | collective-permute-start | bytes 786440 | tf_op jit(solution)/shard_map/ppermute | solution.py:424
  51.4 13.4 %collective-permute-start.21 = (bf16[128,1024]{1,0:T(8,128)(2,1)S(1)}, bf16[128,1024]{1,0:T(8,128)(2,1)S(1)}, u32[]{:S(2)}, u32[]{:S(2)}) collective-permute-start(bf16[128,1024]{1,0:T(8,128)(2,1)S(1)} %out_project.6), channel_id=1, source_target_pairs={{0,2},{2,0},{1,3},{3,1},{4,6},{6,4},{5,7},{7,5},{8,10},{10,8},{9,1... | collective-permute-start | bytes 786440 | tf_op jit(solution)/shard_map/ppermute | solution.py:424
  53.8 16.6 %collective-permute-start.20 = (bf16[128,1024]{1,0:T(8,128)(2,1)S(1)}, bf16[128,1024]{1,0:T(8,128)(2,1)S(1)}, u32[]{:S(2)}, u32[]{:S(2)}) collective-permute-start(bf16[128,1024]{1,0:T(8,128)(2,1)S(1)} %out_project.7), channel_id=1, source_target_pairs={{0,2},{2,0},{1,3},{3,1},{4,6},{6,4},{5,7},{7,5},{8,10},{10,8},{9,1... | collective-permute-start | bytes 786440 | tf_op jit(solution)/shard_map/ppermute | solution.py:424
  58.5 1.6 %collective-permute-start.17 = (bf16[1,128,512]{2,1,0:T(8,128)(2,1)S(1)}, bf16[1,128,512]{2,1,0:T(8,128)(2,1)S(1)}, u32[]{:S(2)}, u32[]{:S(2)}) collective-permute-start(bf16[1,128,512]{2,1,0:T(8,128)(2,1)S(1)} %get-tuple-element.102), channel_id=1, source_target_pairs={{0,1},{1,0},{2,3},{3,2},{4,5},{5,4},{6,7},{7,6},{8,9},{9,8},{10,11... | collective-permute-start | bytes 393224 | tf_op jit(solution)/shard_map/ppermute | solution.py:410
  58.6 14.6 %collective-permute-start.19 = (bf16[128,512]{1,0:T(8,128)(2,1)S(1)}, bf16[128,512]{1,0:T(8,128)(2,1)S(1)}, u32[]{:S(2)}, u32[]{:S(2)}) collective-permute-start(bf16[128,512]{1,0:T(8,128)(2,1)S(1)} %out_project.8), channel_id=1, source_target_pairs={{0,2},{2,0},{1,3},{3,1},{4,6},{6,4},{5,7},{7,5},{8,10},{10,8},{9,1... | collective-permute-start | bytes 393224 | tf_op jit(solution)/shard_map/ppermute | solution.py:424
  60.1 15.1 %collective-permute-start.18 = (bf16[128,512]{1,0:T(8,128)(2,1)S(1)}, bf16[128,512]{1,0:T(8,128)(2,1)S(1)}, u32[]{:S(2)}, u32[]{:S(2)}) collective-permute-start(bf16[128,512]{1,0:T(8,128)(2,1)S(1)} %out_project.9), channel_id=1, source_target_pairs={{0,2},{2,0},{1,3},{3,1},{4,6},{6,4},{5,7},{7,5},{8,10},{10,8},{9,1... | collective-permute-start | bytes 393224 | tf_op jit(solution)/shard_map/ppermute | solution.py:424

commit v9 on v8

--- a/solution.py
+++ b/solution.py
@@ -38,6 +38,18 @@
     if n & (n - 1) == 0:
         return [(i, i ^ d) for i in range(n)]
     return [(i, (i - d if reply else i + d) % n) for i in range(n)]
+
+
+def tables_of_lanes(own, n, meanwhile):
+    if n & (n - 1):
+        others = [lax.ppermute(own, "lanes", lane_pairs(n, d, False)) for d in range(1, n)]
+        return jnp.concatenate([own] + others, axis=0)
+    step, held = 1, own
+    while step < n:
+        other = lax.ppermute(held, "lanes", lane_pairs(n, step, False))
+        held = jnp.concatenate(after([held, other], meanwhile if step == 1 else ()), axis=0)
+        step *= 2
+    return held
 
 
 def shift_pairs(n, s):
@@ -85,39 +97,38 @@
     )(own)
 
 
-def fetch_kernel(items, cap, *refs):
-    others = max(d for d, _, _ in items)
-    asked, store_ref, refs = refs[:others], refs[others], refs[others + 1 :]
+def fetch_kernel(items, cap, fanout, tables_ref, store_ref, *refs):
     blocks, pick_ref = refs[:-1], refs[-1]
     lane = lax.axis_index("lanes")
-    fanout, spans = asked[0].shape[0] // 2, asked[0].shape[1]
+    spans = tables_ref.shape[1]
+    others = tables_ref.shape[0] // (2 * fanout) - 1
     for i in range(others * cap):
         pick_ref[i] = 0
     for d in range(others):
-        place = d * cap
+        place, row = d * cap, (d + 1) * 2 * fanout
         for span in range(spans):
             for k in range(fanout):
-                pick_ref[place] = asked[d][fanout + k, span]
-                place = place + (asked[d][k, span] == lane).astype(jnp.int32)
+                pick_ref[place] = tables_ref[row + fanout + k, span]
+                place = place + (tables_ref[row + k, span] == lane).astype(jnp.int32)
     for block, (d, low, high) in zip(blocks, items):
         for s in range(low, high):
             block[s - low] = store_ref[pick_ref[(d - 1) * cap + s]]
 
 
-def fetch(asked, store, items, cap):
-    others = len(asked)
-    return pl.pallas_call(
-        functools.partial(fetch_kernel, items, cap),
+def fetch(tables, store, items, cap, fanout):
+    others = tables.shape[0] // (2 * fanout) - 1
+    return pl.pallas_call(
+        functools.partial(fetch_kernel, items, cap, fanout),
         out_shape=[
             jax.ShapeDtypeStruct((high - low,) + store.shape[1:], store.dtype) for _, low, high in items
         ],
-        in_specs=[SMEM] * others + [VMEM],
+        in_specs=[SMEM, VMEM],
         out_specs=[VMEM] * len(items),
         scratch_shapes=[pltpu.SMEM((others * cap + 1,), jnp.int32)],
         compiler_params=params(16),
         cost_estimate=cost(10),
         name="fetch",
-    )(*asked, store)
+    )(tables, store)
 
 
 def encode_pairs(width):
@@ -246,71 +257,112 @@
     )(*pieces, w_key, w_value)
 
 
-def attend_kernel(firsts, n_pieces, n_heads, n_rep, turns, fanout, spans, slot_ref, q_ref, *refs):
-    n_ready = len(firsts) - 1
-    ready, refs = refs[:n_ready], refs[n_ready:]
-    pieces, refs = refs[:n_pieces], refs[n_pieces:]
-    wk_ref, wv_ref = refs[:2]
-    outs = refs[2 : 2 + n_rep]
-    kv_ref, sem = refs[2 + n_rep :]
-    copies = [
-        pltpu.make_async_copy(ref, kv_ref.at[pl.ds(first, ref.shape[0])], sem.at[i])
-        for i, (ref, first) in enumerate(zip(ready, firsts))
-    ]
-    for copy in copies:
-        copy.start()
-    project_into(kv_ref, firsts[-1], pieces, wk_ref, wv_ref)
-    for copy in copies:
-        copy.wait()
+def attend_kernel(firsts, n_heads, n_rep, targets, fanout, spans, n_rest, slot_ref, q_ref, *refs):
+    ready, (own_ref, *refs) = refs[: len(firsts) - 1], refs[len(firsts) - 1 :]
+    last = firsts[-1]
+    if n_rest:
+        pieces, (wk_ref, wv_ref, out_ref, rest_ref, kv_ref, sem) = refs[:n_rest], refs[n_rest:]
+    else:
+        rest_ref, out_ref, kv_ref, sem = refs
     heads_at, rep_at = lax.axis_index("heads"), lax.axis_index("rep")
-    cols = wk_ref.shape[1]
+    cols = q_ref.shape[1]
     span_len = q_ref.shape[0] // spans
     block = spans // (n_heads * n_rep)
     tokens = kv_ref.shape[1] * kv_ref.shape[2]
+    mine = own_ref.shape[1]
+    wanted = []
+    for t, s in targets:
+        owner = lax.rem(heads_at + t, n_heads) * n_rep + lax.rem(rep_at + s, n_rep)
+        for i in range(block):
+            wanted.append((owner * block + i, [slot_ref[(owner * block + i) * fanout + k] for k in range(fanout)]))
+    held = [(at * fanout + k, slots[k]) for at, (_, slots) in enumerate(wanted) for k in range(fanout)]
+
+    def whole(j, ref, index):
+        return pltpu.make_async_copy(ref.at[index], kv_ref.at[j], sem.at[j])
+
+    def part(j, index):
+        return pltpu.make_async_copy(own_ref.at[index], kv_ref.at[j, :mine], sem.at[j])
+
+    def other_part(j, index):
+        return pltpu.make_async_copy(rest_ref.at[index], kv_ref.at[j, mine:], sem.at[len(held) + j])
+
+    for j, slot in held:
+        for ref, low, high in zip(ready, firsts, firsts[1:]):
+
+            @pl.when(jnp.logical_and(slot >= low, slot < high))
+            def _(j=j, slot=slot, ref=ref, low=low):
+                whole(j, ref, slot - low).start()
+
+        @pl.when(slot >= last)
+        def _(j=j, slot=slot):
+            part(j, slot - last).start()
+            if not n_rest:
+                other_part(j, slot - last).start()
+
+    if n_rest:
+        project_into(rest_ref, 0, pieces, wk_ref, wv_ref)
+    for j, slot in held:
+
+        @pl.when(slot >= last)
+        def _(j=j, slot=slot):
+            if n_rest:
+                other_part(j, slot - last).start()
+            part(j, slot - last).wait()
+            other_part(j, slot - last).wait()
+
+        @pl.when(slot < last)
+        def _(j=j):
+            whole(j, ready[0], 0).wait()
+
     heads = [slice(h * HD, (h + 1) * HD) for h in range(cols // HD)]
-    for at, t in enumerate(turns):
-        for s in range(n_rep):
-            owner = lax.rem(heads_at + t, n_heads) * n_rep + lax.rem(rep_at + s, n_rep)
-            for i in range(block):
-                span = owner * block + i
-                slots = [slot_ref[span * fanout + k] for k in range(fanout)]
-                rows = pl.ds(pl.multiple_of(span * span_len, span_len), span_len)
-
-                def side(lanes):
-                    return jnp.concatenate(
-                        [kv_ref[slot, :, :, lanes].reshape(tokens, HD) for slot in slots], axis=0
-                    )
-
-                logits = [dot_t(q_ref[rows, lanes], side(lanes)) for lanes in heads]
-                tops = [jnp.max(part, axis=1, keepdims=True) for part in logits]
-                weights = [jnp.exp((part - top) * HD ** (-0.5)) for part, top in zip(logits, tops)]
-                scales = [1.0 / jnp.sum(part, axis=1, keepdims=True) for part in weights]
-                mixed = [
-                    dot(part.astype(BF16), side(slice(cols + lanes.start, cols + lanes.stop)))
-                    for part, lanes in zip(weights, heads)
-                ]
-                for part, scale, lanes in zip(mixed, scales, heads):
-                    outs[s][at, i * span_len : (i + 1) * span_len, lanes] = (part * scale).astype(BF16)
-
-
-def attend(slot, queries, ready, pieces, w_key, w_value, n_heads, n_rep, turns, fanout, spans):
+    for at, (span, _) in enumerate(wanted):
+        rows = pl.ds(pl.multiple_of(span * span_len, span_len), span_len)
+
+        def side(lanes):
+            return kv_ref[at * fanout : (at + 1) * fanout, :, :, lanes].reshape(fanout * tokens, HD)
+
+        logits = [dot_t(q_ref[rows, lanes], side(lanes)) for lanes in heads]
+        tops = [jnp.max(part, axis=1, keepdims=True) for part in logits]
+        weights = [jnp.exp((part - top) * HD ** (-0.5)) for part, top in zip(logits, tops)]
+        scales = [1.0 / jnp.sum(part, axis=1, keepdims=True) for part in weights]
+        mixed = [
+            dot(part.astype(BF16), side(slice(cols + lanes.start, cols + lanes.stop)))
+            for part, lanes in zip(weights, heads)
+        ]
+        into = slice(at % block * span_len, (at % block + 1) * span_len)
+        for part, scale, lanes in zip(mixed, scales, heads):
+            out_ref[at // block, into, lanes] = (part * scale).astype(BF16)
+
+
+def attend(slot, queries, ready, own, rest, weights, n_heads, n_rep, targets, fanout, spans):
     firsts = [0]
     for kv in ready:
         firsts.append(firsts[-1] + kv.shape[0])
-    n, slots, tokens, _ = pieces[0].shape
-    cols = w_key.shape[1]
+    cols = queries.shape[1]
     rows = queries.shape[0] // (n_heads * n_rep)
-    kv_shape = (firsts[-1] + slots, n * len(pieces), tokens, 2 * cols)
-    return pl.pallas_call(
-        functools.partial(attend_kernel, firsts, len(pieces), n_heads, n_rep, turns, fanout, spans),
-        out_shape=[jax.ShapeDtypeStruct((len(turns), rows, cols), BF16)] * n_rep,
-        in_specs=[SMEM, VMEM] + [ANY] * len(ready) + [VMEM] * (len(pieces) + 2),
-        out_specs=[VMEM] * n_rep,
-        scratch_shapes=[pltpu.VMEM(kv_shape, BF16), pltpu.SemaphoreType.DMA((max(1, len(ready)),))],
-        compiler_params=params(40),
+    todo = isinstance(rest, list)
+    slots, mine, tokens, width = own.shape
+    others = sum(piece.shape[0] for piece in rest) if todo else rest.shape[1]
+    held = len(targets) * (spans // (n_heads * n_rep)) * fanout
+    out_shape = [jax.ShapeDtypeStruct((len(targets), rows, cols), BF16)]
+    if todo:
+        out_shape.append(jax.ShapeDtypeStruct((slots, others, tokens, width), BF16))
+    operands = [*rest, *weights] if todo else [rest]
+    return pl.pallas_call(
+        functools.partial(
+            attend_kernel, firsts, n_heads, n_rep, targets, fanout, spans, len(rest) if todo else 0
+        ),
+        out_shape=out_shape,
+        in_specs=[SMEM, VMEM] + [ANY] * (len(ready) + 1) + [VMEM if todo else ANY] * len(operands),
+        out_specs=[VMEM] * len(out_shape),
+        scratch_shapes=[
+            pltpu.VMEM((held, mine + others, tokens, width), BF16),
+            pltpu.SemaphoreType.DMA((2 * held,)),
+        ],
+        compiler_params=params(32),
         cost_estimate=cost(0.001),
         name="attend",
-    )(slot, queries, *ready, *pieces, w_key, w_value)
+    )(slot, queries, *ready, own, *operands)
 
 
 def out_kernel(n_rep, n_received, *refs):
@@ -370,10 +422,10 @@
     parts = [range(low, high) for low, high in zip(cuts, cuts[1:])]
 
     own = jnp.concatenate([owners.T, entry_ids.T], axis=0)
-    asked = [lax.ppermute(own, "lanes", lane_pairs(n_lanes, d, False)) for d in range(1, n_lanes)]
     req, slot, pick = plan(own, order, cap)
+    tables = tables_of_lanes(own, n_lanes, req)
     encoded = encode_local(req, pick, span_states, store, cap, fanout, span_len)
-    blocks = fetch(after(asked, encoded), store, items, cap)
+    blocks = fetch(after(tables, encoded), store, items, cap, fanout)
 
     def send(part, *earlier):
         ready = after([blocks[i] for i in part], *earlier)
@@ -403,18 +455,26 @@
         last = project(after(pieces[len(kvs)], last), w_key, w_value)
         kvs.append(last)
     pieces = over_rep(jnp.stack(after(crossed[-1], kvs)))
-
-    def mix(turns, q):
-        outs = attend(slot, q, kvs, pieces, w_key, w_value, n_heads, n_rep, turns, fanout, spans)
-        return [outs[0]] + [
-            lax.ppermute(outs[s], "rep", shift_pairs(n_rep, s)) for s in range(1, n_rep)
-        ]
+    own_kv, rest = project(pieces[:1], w_key, w_value), pieces[1:]
+
+    def mix(turns, q, rest):
+        mixed = []
+        for s in range(1, n_rep):
+            given, *made = attend(
+                slot, q, kvs, own_kv, rest, (w_key, w_value), n_heads, n_rep, [(t, s) for t in turns], fanout, spans
+            )
+            rest = made[0] if made else rest
+            mixed.append(lax.ppermute(given, "rep", shift_pairs(n_rep, s)))
+        kept = attend(
+            slot, q, kvs, own_kv, rest, (w_key, w_value), n_heads, n_rep, [(t, 0) for t in turns], fanout, spans
+        )
+        return [kept[0]] + mixed, rest
 
     width = w_out.shape[1]
     tile = min(COL_TILE, width)
     cuts = [width // tile * part // 8 * tile for part in (0, 2, 4, 6, 7)] + [width]
     blocks = [(start, stop) for start, stop in zip(cuts, cuts[1:]) if stop > start]
-    mixed = mix(list(range(1, n_heads)), queries)
+    mixed, rest = mix(list(range(1, n_heads)), queries, rest)
     received, partials = [[] for _ in blocks], []
     for t in range(1, n_heads):
         for i, (start, stop) in enumerate(blocks):
@@ -422,7 +482,7 @@
             partial, mixed = lax.optimization_barrier((partial, mixed))
             partials.append(partial)
             received[i].append(lax.ppermute(partial, "heads", shift_pairs(n_heads, t)))
-    mixed = mix([0], after(queries, partials))
+    mixed, rest = mix([0], after(queries, partials), rest)
     out = None
     for (start, stop), parts in zip(blocks, received):
         out = out_project(mixed, w_outs, 0, start, stop, tile, 0.2, parts, out, True)

time: 76.4 us -> 75 us (0.982)
  waiting for transfers between devices: 27.1 us -> 22.7 us
  Pallas kernels: 27.6 us -> 29.6 us
  starting transfers between devices: 20.2 us -> 21.6 us
    ppermute x4, waiting for transfers between devices: 5.8 us -> 4.23 us  [over_heads(): lax.ppermute(array, 'heads', shift_pairs(n_heads, s))]
    ppermute x4, starting transfers between devices: 4.12 us -> 5.63 us  [send(): lax.ppermute(block, 'lanes', lane_pairs(n_lanes, items[i][0], True))]
    pallas_call x3 -> x5, Pallas kernels: 7.81 us -> 8.99 us  [the longest x4 8.16 us: attend(): pl.pallas_call(functools.partial(attend_kernel, firsts, n_heads, n_rep, t...]
    ppermute x5 -> x4, waiting for transfers between devices: 2.49 us -> 1.49 us  [the longest x2 0.87 us: mix(): mixed.append(lax.ppermute(given, 'rep', shift_pairs(n_rep, s)))]
    pallas_call x3 -> x4, Pallas kernels: 3.75 us -> 4.49 us  [project(): pl.pallas_call(functools.partial(project_kernel, len(pieces)), out_shape=...]
    ppermute x5 -> x4, starting transfers between devices: 6.02 us -> 6.32 us  [the longest x2 6.18 us: tables_of_lanes(): other = lax.ppermute(held, 'lanes', lane_pairs(n, step, False))]
  transfers between devices with their start and end apart: 23 -> 22, of which waited for: 12 -> 13; matrix products, arithmetic and copies ran while one was open for 0% -> 0% of each run, Pallas kernels for 33% -> 36%
where the time goes in v9:
time: 75 us; the launch traced here: 75.1 us
  Pallas kernels  29.6 us (39%)
  waiting for transfers between devices  22.7 us (30%)
  starting transfers between devices  21.6 us (29%)
  other arithmetic  0.91 us (1%)
    pallas_call x10, Pallas kernels, out_project(): pl.pallas_call(functools.partial(out_kernel, n, len(received)), grid=((st...  9.61 us
    pallas_call x4, Pallas kernels, attend(): pl.pallas_call(functools.partial(attend_kernel, firsts, n_heads, n_rep, t...  8.16 us
    ppermute x5, waiting for transfers between devices, shards(): received[i].append(lax.ppermute(partial, 'heads', shift_pairs(n_heads, t)))  8.02 us
    ppermute x4, waiting for transfers between devices, send(): lax.ppermute(block, 'lanes', lane_pairs(n_lanes, items[i][0], True))  7.87 us
    ppermute x2, starting transfers between devices, tables_of_lanes(): other = lax.ppermute(held, 'lanes', lane_pairs(n, step, False))  6.18 us
    ppermute x4, starting transfers between devices, send(): lax.ppermute(block, 'lanes', lane_pairs(n_lanes, items[i][0], True))  5.63 us
    ppermute x5, starting transfers between devices, shards(): received[i].append(lax.ppermute(partial, 'heads', shift_pairs(n_heads, t)))  5.07 us
    pallas_call x4, Pallas kernels, project(): pl.pallas_call(functools.partial(project_kernel, len(pieces)), out_shape=...  4.49 us
  transfers between devices with their start and end apart: 22, of which 13 were waited for; matrix products, arithmetic and copies ran while one was open for 0% of the time, Pallas kernels for 36%

profile of v9, /device:TPU:0, one launch (start us, length us, event | category | flops | bytes accessed | tf_op | source)
XLA Modules:
  0.0 75.1 jit_solution(6862789829080603017)
XLA Ops:
  0.0 0.7 pad_add_fusion.2.own_ref
  0.7 3.1 %collective-permute-start.1 = (s32[4,8]{1,0:T(4,128)S(1)}, s32[4,8]{1,0:T(4,128)S(1)}, u32[]{:S(2)}, u32[]{:S(2)}) collective-permute-start(s32[4,8]{1,0:T(4,128)S(1)} %pad_add_fusion.2.own_ref), channel_id=1, source_target_pairs={{0,4},{4,0},{8,12},{12,8},{1,5},{5,1},{9,13},{13,9},{2,6},{6,2},{1... | collective-permute-start | bytes 392 | tf_op jit(solution)/shard_map/ppermute | solution.py:49
  3.8 1.3 %plan.1 = (s32[16]{0:T(128)S(1)}, s32[16]{0:T(128)S(1)}, s32[16]{0:T(128)S(1)}) custom-call(s32[4,8]{1,0:T(4,128)S(1)} %pad_add_fusion.2.own_ref), custom_call_target="tpu_custom_call" | custom-call | flops 10000000000 | bytes 1024 | tf_op jit(solution)/shard_map/plan/pallas_call | solution.py:88
  5.4 3.1 %collective-permute-start.2 = (s32[8,8]{1,0:T(8,128)S(1)}, s32[8,8]{1,0:T(8,128)S(1)}, u32[]{:S(2)}, u32[]{:S(2)}) collective-permute-start(s32[8,8]{1,0:T(8,128)S(1)} %pad_add_fusion.1), channel_id=1, source_target_pairs={{0,8},{4,12},{8,0},{12,4},{1,9},{5,13},{9,1},{13,5},{2,10},{6,14},... | collective-permute-start | bytes 776 | tf_op jit(solution)/shard_map/ppermute | solution.py:49
  8.5 1.3 %encode_local.1 = bf16[4,32,896]{2,1,0:T(8,128)(2,1)S(1)} custom-call(s32[16]{0:T(128)S(1)} %get-tuple-element.55.req_ref, s32[16]{0:T(128)S(1)} %get-tuple-element.56.pick_ref, bf16[512,896]{1,0:T(8,128)(2,1)S(1)} %copy-done.4, bf16[16,32,896]{2,1,0:T(8,128)(2,1)S(1)} %copy-done.5), custom_call_target="tpu_custom_call" | custom-call | flops 10000000000 | bytes 1024 | tf_op jit(solution)/shard_map/encode_local/pallas_call | solution.py:216
  10.1 0.8 %fetch.1 = (bf16[2,32,896]{2,1,0:T(8,128)(2,1)S(1)}, bf16[2,32,896]{2,1,0:T(8,128)(2,1)S(1)}, bf16[4,32,896]{2,1,0:T(8,128)(2,1)S(1)}, bf16[4,32,896]{2,1,0:T(8,128)(2,1)S(1)}) custom-call(s32[16,8]{1,0:T(8,128)S(1)} %pad_add_fusion.tables_ref, bf16[16,32,896]{2,1,0:T(8,128)(2,1)S(1)} %copy-done.5), custom_call_target="tpu_custom_call" | custom-call | flops 10000000000 | bytes 1024 | tf_op jit(solution)/shard_map/fetch/pallas_call | solution.py:120
  10.9 3.0 %collective-permute-start.3 = (bf16[4,32,896]{2,1,0:T(8,128)(2,1)S(1)}, bf16[4,32,896]{2,1,0:T(8,128)(2,1)S(1)}, u32[]{:S(2)}, u32[]{:S(2)}) collective-permute-start(bf16[4,32,896]{2,1,0:T(8,128)(2,1)S(1)} %get-tuple-element.62), channel_id=1, source_target_pairs={{0,8},{4,12},{8,0},{12,4},{1,9},{5,13},{9,1},{13,5},{2,10},{6,14},... | collective-permute-start | bytes 688136 | tf_op jit(solution)/shard_map/ppermute | solution.py:433
  13.9 1.6 %collective-permute-start.4 = (bf16[2,32,896]{2,1,0:T(8,128)(2,1)S(1)}, bf16[2,32,896]{2,1,0:T(8,128)(2,1)S(1)}, u32[]{:S(2)}, u32[]{:S(2)}) collective-permute-start(bf16[2,32,896]{2,1,0:T(8,128)(2,1)S(1)} %get-tuple-element.65), channel_id=1, source_target_pairs={{0,4},{4,0},{8,12},{12,8},{1,5},{5,1},{9,13},{13,9},{2,6},{6,2},{1... | collective-permute-start | bytes 344072 | tf_op jit(solution)/shard_map/ppermute | solution.py:433
  15.9 1.5 %collective-permute-start = (bf16[4,32,896]{2,1,0:T(8,128)(2,1)S(1)}, bf16[4,32,896]{2,1,0:T(8,128)(2,1)S(1)}, u32[]{:S(2)}, u32[]{:S(2)}) collective-permute-start(bf16[4,32,896]{2,1,0:T(8,128)(2,1)S(1)} %encode_local.1), channel_id=1, source_target_pairs={{0,2},{2,0},{1,3},{3,1},{4,6},{6,4},{5,7},{7,5},{8,10},{10,8},{9,1... | collective-permute-start | bytes 688136 | tf_op jit(solution)/shard_map/ppermute | solution.py:410
  17.4 2.9 %collective-permute-done.4.refs_0_ = bf16[2,32,896]{2,1,0:T(8,128)(2,1)S(1)} collective-permute-done((bf16[2,32,896]{2,1,0:T(8,128)(2,1)S(1)}, bf16[2,32,896]{2,1,0:T(8,128)(2,1)S(1)}, u32[]{:S(2)}, u32[]{:S(2)}) %collective-permute-start.4) | collective-permute-done | bytes 114720 | tf_op jit(solution)/shard_map/ppermute | solution.py:433
  20.4 2.5 %collective-permute-done.5.refs_1_ = bf16[2,32,896]{2,1,0:T(8,128)(2,1)S(1)} collective-permute-done((bf16[2,32,896]{2,1,0:T(8,128)(2,1)S(1)}, bf16[2,32,896]{2,1,0:T(8,128)(2,1)S(1)}, u32[]{:S(2)}, u32[]{:S(2)}) %collective-permute-start.5) | collective-permute-done | bytes 114720 | tf_op jit(solution)/shard_map/ppermute | solution.py:433
  22.9 1.5 %encode.3 = bf16[4,32,896]{2,1,0:T(8,128)(2,1)S(1)} custom-call(s32[16]{0:T(128)S(1)} %get-tuple-element.55.req_ref, bf16[512,896]{1,0:T(8,128)(2,1)S(1)} %copy-done.4, bf16[2,32,896]{2,1,0:T(8,128)(2,1)S(1)} %collective-permute-done.4.refs_0_, bf16[2,32,896]{2,1,0:T(8,128)(2,1)S(1)} %collective-permute-done.5.refs_1_), custom_call_target="tpu_custom_call" | custom-call | flops 100000000 | bytes 1024 | tf_op jit(solution)/shard_map/encode/pallas_call | solution.py:197
  24.3 1.6 %collective-permute-start.7 = (bf16[4,32,896]{2,1,0:T(8,128)(2,1)S(1)}, bf16[4,32,896]{2,1,0:T(8,128)(2,1)S(1)}, u32[]{:S(2)}, u32[]{:S(2)}) collective-permute-start(bf16[4,32,896]{2,1,0:T(8,128)(2,1)S(1)} %encode.3), channel_id=1, source_target_pairs={{0,2},{2,0},{1,3},{3,1},{4,6},{6,4},{5,7},{7,5},{8,10},{10,8},{9,1... | collective-permute-start | bytes 688136 | tf_op jit(solution)/shard_map/ppermute | solution.py:410
  25.9 0.6 collective-permute-start.10
  26.5 1.3 %encode.4 = bf16[4,32,896]{2,1,0:T(8,128)(2,1)S(1)} custom-call(s32[16]{0:T(128)S(1)} %get-tuple-element.55.req_ref, bf16[512,896]{1,0:T(8,128)(2,1)S(1)} %copy-done.4, bf16[4,32,896]{2,1,0:T(8,128)(2,1)S(1)} %collective-permute-done.3.refs_0_), custom_call_target="tpu_custom_call" | custom-call | flops 10000000000 | bytes 1024 | tf_op jit(solution)/shard_map/encode/pallas_call | solution.py:197
  27.8 0.6 collective-permute-start.9
  28.5 2.7 %collective-permute-done.7 = bf16[4,32,896]{2,1,0:T(8,128)(2,1)S(1)} collective-permute-done((bf16[4,32,896]{2,1,0:T(8,128)(2,1)S(1)}, bf16[4,32,896]{2,1,0:T(8,128)(2,1)S(1)}, u32[]{:S(2)}, u32[]{:S(2)}) %collective-permute-start.7) | collective-permute-done | bytes 229408 | tf_op jit(solution)/shard_map/ppermute | solution.py:410
  31.4 2.4 %collective-permute-done.10.refs_0_ = bf16[4,32,896]{2,1,0:T(8,128)(2,1)S(1)} collective-permute-done((bf16[4,32,896]{2,1,0:T(8,128)(2,1)S(1)}, bf16[4,32,896]{2,1,0:T(8,128)(2,1)S(1)}, u32[]{:S(2)}, u32[]{:S(2)}) %collective-permute-start.10) | collective-permute-done | bytes 229408 | tf_op jit(solution)/shard_map/ppermute | solution.py:433
  33.8 1.3 %encode.5 = bf16[4,32,896]{2,1,0:T(8,128)(2,1)S(1)} custom-call(s32[16]{0:T(128)S(1)} %get-tuple-element.55.req_ref, bf16[512,896]{1,0:T(8,128)(2,1)S(1)} %copy-done.4, bf16[4,32,896]{2,1,0:T(8,128)(2,1)S(1)} %collective-permute-done.10.refs_0_), custom_call_target="tpu_custom_call" | custom-call | flops 10000000000 | bytes 1024 | tf_op jit(solution)/shard_map/encode/pallas_call | solution.py:197
  35.1 0.6 collective-permute-start.12
  35.9 1.3 %project.4.refs_0_ = bf16[4,4,32,1024]{3,2,1,0:T(8,128)(2,1)S(1)} custom-call(bf16[2,4,32,896]{3,2,1,0:T(8,128)(2,1)S(1)} %pad_maximum_fusion.refs_0_, bf16[2,4,32,896]{3,2,1,0:T(8,128)(2,1)S(1)} %collective-permute-done.6.refs_1_, bf16[896,512]{1,0:T(8,128)(2,1)S(1)} %copy-done.2, bf16[896,512]{1,0:T(8,128)(2,1)S(1)} %copy-done.3), custom_call_target="tpu_custom_call" | custom-call | flops 10000000000 | bytes 1024 | tf_op jit(solution)/shard_map/project/pallas_call | solution.py:249
  37.1 1.3 %project.5.refs_1_ = bf16[4,4,32,1024]{3,2,1,0:T(8,128)(2,1)S(1)} custom-call(bf16[2,4,32,896]{3,2,1,0:T(8,128)(2,1)S(1)} %pad_maximum_fusion.1.refs_0_, bf16[2,4,32,896]{3,2,1,0:T(8,128)(2,1)S(1)} %collective-permute-done.8.refs_1_, bf16[896,512]{1,0:T(8,128)(2,1)S(1)} %copy-done.2, bf16[896,512]{1,0:T(8,128)(2,1)S(1)} %copy-done.3), custom_call_target="tpu_custom_call" | custom-call | flops 10000000000 | bytes 1024 | tf_op jit(solution)/shard_map/project/pallas_call | solution.py:249
  38.4 1.3 %project.6.refs_2_ = bf16[4,4,32,1024]{3,2,1,0:T(8,128)(2,1)S(1)} custom-call(bf16[2,4,32,896]{3,2,1,0:T(8,128)(2,1)S(1)} %pad_maximum_fusion.2.refs_0_, bf16[2,4,32,896]{3,2,1,0:T(8,128)(2,1)S(1)} %collective-permute-done.11.refs_1_, bf16[896,512]{1,0:T(8,128)(2,1)S(1)} %copy-done.2, bf16[896,512]{1,0:T(8,128)(2,1)S(1)} %copy-done.3), custom_call_target="tpu_custom_call" | custom-call | flops 10000000000 | bytes 1024 | tf_op jit(solution)/shard_map/project/pallas_call | solution.py:249
  39.7 1.5 %collective-permute-done.12 = bf16[4,32,896]{2,1,0:T(8,128)(2,1)S(1)} collective-permute-done((bf16[4,32,896]{2,1,0:T(8,128)(2,1)S(1)}, bf16[4,32,896]{2,1,0:T(8,128)(2,1)S(1)}, u32[]{:S(2)}, u32[]{:S(2)}) %collective-permute-start.12) | collective-permute-done | bytes 229408 | tf_op jit(solution)/shard_map/ppermute | solution.py:410
  41.3 0.7 project.7.refs_3_
  42.0 1.1 %collective-permute-done.13.refs_4_ = bf16[2,4,32,896]{3,2,1,0:T(8,128)(2,1)S(1)} collective-permute-done((bf16[2,4,32,896]{3,2,1,0:T(8,128)(2,1)S(1)}, bf16[2,4,32,896]{3,2,1,0:T(8,128)(2,1)S(1)}, u32[]{:S(2)}, u32[]{:S(2)}) %collective-permute-start.13) | collective-permute-done | bytes 458784 | tf_op jit(solution)/shard_map/ppermute | solution.py:413
  43.1 2.6 %attend.4 = (bf16[1,128,512]{2,1,0:T(8,128)(2,1)S(1)}, bf16[4,2,32,1024]{3,2,1,0:T(8,128)(2,1)S(1)}) custom-call(s32[16]{0:T(128)S(1)} %get-tuple-element.54.slot_ref, bf16[512,512]{1,0:T(8,128)(2,1)S(1)} %copy-done.1, bf16[4,4,32,1024]{3,2,1,0:T(8,128)(2,1)S(1)} %project.4.refs_0_, bf16[4,4,32,1024]{3,2,1,0:T(8,128)(2,1)S(1)} %project.5.refs_1_, ...), custom_call_target="tpu_custom_call" | custom-call | flops 1000000 | bytes 1024 | tf_op jit(solution)/shard_map/attend/pallas_call | solution.py:351
  45.8 1.5 %attend.5.refs_0_ = bf16[1,128,512]{2,1,0:T(8,128)(2,1)S(1)} custom-call(s32[16]{0:T(128)S(1)} %get-tuple-element.54.slot_ref, bf16[512,512]{1,0:T(8,128)(2,1)S(1)} %copy-done.1, bf16[4,4,32,1024]{3,2,1,0:T(8,128)(2,1)S(1)} %project.4.refs_0_, bf16[4,4,32,1024]{3,2,1,0:T(8,128)(2,1)S(1)} %project.5.refs_1_, bf16[4,4,32,1024]{3,2,1,0:T(8,128)(2,1)S(1)} %project.6.refs_2_, ...), custom_call_target="tpu_custom_call" | custom-call | flops 1000000 | bytes 1024 | tf_op jit(solution)/shard_map/attend/pallas_call | solution.py:351
  47.4 0.9 %out_project.5 = bf16[128,1024]{1,0:T(8,128)(2,1)S(1)} custom-call(bf16[1,128,512]{2,1,0:T(8,128)(2,1)S(1)} %attend.5.refs_0_, bf16[1,128,512]{2,1,0:T(8,128)(2,1)S(1)} %collective-permute-done.14.refs_1_, bf16[512,4096]{1,0:T(8,128)(2,1)S(1)} %copy-done, bf16[512,4096]{1,0:T(8,128)(2,1)S(1)} %collective-permute-done.15.refs_3_), custom_call_target="tpu_custom_call" | custom-call | flops 1000000 | bytes 1024 | tf_op jit(solution)/shard_map/out_project/pallas_call | solution.py:382
  48.2 1.7 %collective-permute-start.21 = (bf16[128,1024]{1,0:T(8,128)(2,1)S(1)}, bf16[128,1024]{1,0:T(8,128)(2,1)S(1)}, u32[]{:S(2)}, u32[]{:S(2)}) collective-permute-start(bf16[128,1024]{1,0:T(8,128)(2,1)S(1)} %out_project.5), channel_id=1, source_target_pairs={{0,2},{2,0},{1,3},{3,1},{4,6},{6,4},{5,7},{7,5},{8,10},{10,8},{9,1... | collective-permute-start | bytes 786440 | tf_op jit(solution)/shard_map/ppermute | solution.py:484
  49.9 0.9 %out_project.6 = bf16[128,1024]{1,0:T(8,128)(2,1)S(1)} custom-call(bf16[1,128,512]{2,1,0:T(8,128)(2,1)S(1)} %attend.5.refs_0_, bf16[1,128,512]{2,1,0:T(8,128)(2,1)S(1)} %collective-permute-done.14.refs_1_, bf16[512,4096]{1,0:T(8,128)(2,1)S(1)} %copy-done, bf16[512,4096]{1,0:T(8,128)(2,1)S(1)} %collective-permute-done.15.refs_3_), custom_call_target="tpu_custom_call" | custom-call | flops 1000000 | bytes 1024 | tf_op jit(solution)/shard_map/out_project/pallas_call | solution.py:382
  50.8 0.5 collective-permute-start.20
  51.2 0.9 %out_project.7 = bf16[128,1024]{1,0:T(8,128)(2,1)S(1)} custom-call(bf16[1,128,512]{2,1,0:T(8,128)(2,1)S(1)} %attend.5.refs_0_, bf16[1,128,512]{2,1,0:T(8,128)(2,1)S(1)} %collective-permute-done.14.refs_1_, bf16[512,4096]{1,0:T(8,128)(2,1)S(1)} %copy-done, bf16[512,4096]{1,0:T(8,128)(2,1)S(1)} %collective-permute-done.15.refs_3_), custom_call_target="tpu_custom_call" | custom-call | flops 1000000 | bytes 1024 | tf_op jit(solution)/shard_map/out_project/pallas_call | solution.py:382
  52.1 1.7 %collective-permute-start.19 = (bf16[128,1024]{1,0:T(8,128)(2,1)S(1)}, bf16[128,1024]{1,0:T(8,128)(2,1)S(1)}, u32[]{:S(2)}, u32[]{:S(2)}) collective-permute-start(bf16[128,1024]{1,0:T(8,128)(2,1)S(1)} %out_project.7), channel_id=1, source_target_pairs={{0,2},{2,0},{1,3},{3,1},{4,6},{6,4},{5,7},{7,5},{8,10},{10,8},{9,1... | collective-permute-start | bytes 786440 | tf_op jit(solution)/shard_map/ppermute | solution.py:484
  54.4 1.9 %attend.7 = bf16[1,128,512]{2,1,0:T(8,128)(2,1)S(1)} custom-call(s32[16]{0:T(128)S(1)} %get-tuple-element.54.slot_ref, bf16[512,512]{1,0:T(8,128)(2,1)S(1)} %copy-done.1, bf16[4,4,32,1024]{3,2,1,0:T(8,128)(2,1)S(1)} %project.4.refs_0_, bf16[4,4,32,1024]{3,2,1,0:T(8,128)(2,1)S(1)} %project.5.refs_1_, bf16[4,4,32,1024]{3,2,1,0:T(8,128)(2,1)S(1)} %project.6.refs_2_, ...), custom_call_target="tpu_custom_call" | custom-call | flops 1000000 | bytes 1024 | tf_op jit(solution)/shard_map/attend/pallas_call | solution.py:351
  56.4 0.5 collective-permute-start.18
  56.8 0.9 %collective-permute-done.16.refs_1_ = bf16[1,128,512]{2,1,0:T(8,128)(2,1)S(1)} collective-permute-done((bf16[1,128,512]{2,1,0:T(8,128)(2,1)S(1)}, bf16[1,128,512]{2,1,0:T(8,128)(2,1)S(1)}, u32[]{:S(2)}, u32[]{:S(2)}) %collective-permute-start.16) | collective-permute-done | bytes 131104 | tf_op jit(solution)/shard_map/ppermute | solution.py:467
  57.7 0.8 %collective-permute-start.17 = (bf16[128,512]{1,0:T(8,128)(2,1)S(1)}, bf16[128,512]{1,0:T(8,128)(2,1)S(1)}, u32[]{:S(2)}, u32[]{:S(2)}) collective-permute-start(bf16[128,512]{1,0:T(8,128)(2,1)S(1)} %out_project.9), channel_id=1, source_target_pairs={{0,2},{2,0},{1,3},{3,1},{4,6},{6,4},{5,7},{7,5},{8,10},{10,8},{9,1... | collective-permute-start | bytes 393224 | tf_op jit(solution)/shard_map/ppermute | solution.py:484
  58.5 2.2 %attend.6.refs_0_ = bf16[1,128,512]{2,1,0:T(8,128)(2,1)S(1)} custom-call(s32[16]{0:T(128)S(1)} %get-tuple-element.54.slot_ref, bf16[512,512]{1,0:T(8,128)(2,1)S(1)} %copy-done.1, bf16[4,4,32,1024]{3,2,1,0:T(8,128)(2,1)S(1)} %project.4.refs_0_, bf16[4,4,32,1024]{3,2,1,0:T(8,128)(2,1)S(1)} %project.5.refs_1_, bf16[4,4,32,1024]{3,2,1,0:T(8,128)(2,1)S(1)} %project.6.refs_2_, ...), custom_call_target="tpu_custom_call" | custom-call | flops 1000000 | bytes 1024 | tf_op jit(solution)/shard_map/attend/pallas_call | solution.py:351
  60.7 1.5 %out_final.5.refs_5_ = bf16[128,4096]{1,0:T(8,128)(2,1)} custom-call(bf16[1,128,512]{2,1,0:T(8,128)(2,1)S(1)} %attend.6.refs_0_, bf16[1,128,512]{2,1,0:T(8,128)(2,1)S(1)} %collective-permute-done.16.refs_1_, bf16[512,4096]{1,0:T(8,128)(2,1)S(1)} %copy-done, bf16[512,4096]{1,0:T(8,128)(2,1)S(1)} %collective-permute-done.15.refs_3_, ...), custom_call_target="tpu_custom_call" | custom-call | flops 200000000 | bytes 1024 | tf_op jit(solution)/shard_map/out_final/pallas_call | solution.py:382
  62.2 0.9 %collective-permute-done.20.refs_4_ = bf16[128,1024]{1,0:T(8,128)(2,1)S(1)} collective-permute-done((bf16[128,1024]{1,0:T(8,128)(2,1)S(1)}, bf16[128,1024]{1,0:T(8,128)(2,1)S(1)}, u32[]{:S(2)}, u32[]{:S(2)}) %collective-permute-start.20) | collective-permute-done | bytes 262176 | tf_op jit(solution)/shard_map/ppermute | solution.py:484
  63.1 1.5 %out_final.6.refs_5_ = bf16[128,4096]{1,0:T(8,128)(2,1)} custom-call(bf16[1,128,512]{2,1,0:T(8,128)(2,1)S(1)} %attend.6.refs_0_, bf16[1,128,512]{2,1,0:T(8,128)(2,1)S(1)} %collective-permute-done.16.refs_1_, bf16[512,4096]{1,0:T(8,128)(2,1)S(1)} %copy-done, bf16[512,4096]{1,0:T(8,128)(2,1)S(1)} %collective-permute-done.15.refs_3_, ...), custom_call_target="tpu_custom_call", output_to_operand_aliasing={{}: (5, {})} | custom-call | flops 200000000 | bytes 1024 | tf_op jit(solution)/shard_map/out_final/pallas_call | solution.py:382
  64.6 4.1 %collective-permute-done.19.refs_4_ = bf16[128,1024]{1,0:T(8,128)(2,1)S(1)} collective-permute-done((bf16[128,1024]{1,0:T(8,128)(2,1)S(1)}, bf16[128,1024]{1,0:T(8,128)(2,1)S(1)}, u32[]{:S(2)}, u32[]{:S(2)}) %collective-permute-start.19) | collective-permute-done | bytes 262176 | tf_op jit(solution)/shard_map/ppermute | solution.py:484
  68.7 1.5 %out_final.7.refs_5_ = bf16[128,4096]{1,0:T(8,128)(2,1)} custom-call(bf16[1,128,512]{2,1,0:T(8,128)(2,1)S(1)} %attend.6.refs_0_, bf16[1,128,512]{2,1,0:T(8,128)(2,1)S(1)} %collective-permute-done.16.refs_1_, bf16[512,4096]{1,0:T(8,128)(2,1)S(1)} %copy-done, bf16[512,4096]{1,0:T(8,128)(2,1)S(1)} %collective-permute-done.15.refs_3_, ...), custom_call_target="tpu_custom_call", output_to_operand_aliasing={{}: (5, {})} | custom-call | flops 200000000 | bytes 1024 | tf_op jit(solution)/shard_map/out_final/pallas_call | solution.py:382
  70.2 1.3 %collective-permute-done.18.refs_4_ = bf16[128,512]{1,0:T(8,128)(2,1)S(1)} collective-permute-done((bf16[128,512]{1,0:T(8,128)(2,1)S(1)}, bf16[128,512]{1,0:T(8,128)(2,1)S(1)}, u32[]{:S(2)}, u32[]{:S(2)}) %collective-permute-start.18) | collective-permute-done | bytes 131104 | tf_op jit(solution)/shard_map/ppermute | solution.py:484
  71.5 1.0 %out_final.8.refs_5_ = bf16[128,4096]{1,0:T(8,128)(2,1)} custom-call(bf16[1,128,512]{2,1,0:T(8,128)(2,1)S(1)} %attend.6.refs_0_, bf16[1,128,512]{2,1,0:T(8,128)(2,1)S(1)} %collective-permute-done.16.refs_1_, bf16[512,4096]{1,0:T(8,128)(2,1)S(1)} %copy-done, bf16[512,4096]{1,0:T(8,128)(2,1)S(1)} %collective-permute-done.15.refs_3_, ...), custom_call_target="tpu_custom_call", output_to_operand_aliasing={{}: (5, {})} | custom-call | flops 200000000 | bytes 1024 | tf_op jit(solution)/shard_map/out_final/pallas_call | solution.py:382
  72.5 1.7 %collective-permute-done.17.refs_4_ = bf16[128,512]{1,0:T(8,128)(2,1)S(1)} collective-permute-done((bf16[128,512]{1,0:T(8,128)(2,1)S(1)}, bf16[128,512]{1,0:T(8,128)(2,1)S(1)}, u32[]{:S(2)}, u32[]{:S(2)}) %collective-permute-start.17) | collective-permute-done | bytes 131104 | tf_op jit(solution)/shard_map/ppermute | solution.py:484
  74.2 1.0 %out_final.9 = bf16[128,4096]{1,0:T(8,128)(2,1)} custom-call(bf16[1,128,512]{2,1,0:T(8,128)(2,1)S(1)} %attend.6.refs_0_, bf16[1,128,512]{2,1,0:T(8,128)(2,1)S(1)} %collective-permute-done.16.refs_1_, bf16[512,4096]{1,0:T(8,128)(2,1)S(1)} %copy-done, bf16[512,4096]{1,0:T(8,128)(2,1)S(1)} %collective-permute-done.15.refs_3_, ...), custom_call_target="tpu_custom_call", output_to_operand_aliasing={{}: (5, {})} | custom-call | flops 200000000 | bytes 1024 | tf_op jit(solution)/shard_map/out_final/pallas_call | solution.py:382
  (39 shorter events, 2.4 us)
Async XLA Ops:
  0.7 7.8 %copy-start.4 = (bf16[512,896]{1,0:T(8,128)(2,1)S(1)}, bf16[512,896]{1,0:T(8,128)(2,1)}, u32[]{:S(2)}) copy-start(bf16[512,896]{1,0:T(8,128)(2,1)} %states_ref.7) | copy-start | bytes 2752516
  0.7 7.8 %copy-start.5 = (bf16[16,32,896]{2,1,0:T(8,128)(2,1)S(1)}, bf16[16,32,896]{2,1,0:T(8,128)(2,1)}, u32[]{:S(2)}) copy-start(bf16[16,32,896]{2,1,0:T(8,128)(2,1)} %store_ref.3) | copy-start | bytes 2752516
  0.7 4.7 %collective-permute-start.1 = (s32[4,8]{1,0:T(4,128)S(1)}, s32[4,8]{1,0:T(4,128)S(1)}, u32[]{:S(2)}, u32[]{:S(2)}) collective-permute-start(s32[4,8]{1,0:T(4,128)S(1)} %pad_add_fusion.2.own_ref), channel_id=1, source_target_pairs={{0,4},{4,0},{8,12},{12,8},{1,5},{5,1},{9,13},{13,9},{2,6},{6,2},{1... | collective-permute-start | bytes 392 | tf_op jit(solution)/shard_map/ppermute | solution.py:49
  5.4 4.7 %collective-permute-start.2 = (s32[8,8]{1,0:T(8,128)S(1)}, s32[8,8]{1,0:T(8,128)S(1)}, u32[]{:S(2)}, u32[]{:S(2)}) collective-permute-start(s32[8,8]{1,0:T(8,128)S(1)} %pad_add_fusion.1), channel_id=1, source_target_pairs={{0,8},{4,12},{8,0},{12,4},{1,9},{5,13},{9,1},{13,5},{2,10},{6,14},... | collective-permute-start | bytes 776 | tf_op jit(solution)/shard_map/ppermute | solution.py:49
  10.1 7.4 %copy-start = (bf16[512,4096]{1,0:T(8,128)(2,1)S(1)}, bf16[512,4096]{1,0:T(8,128)(2,1)}, u32[]{:S(2)}) copy-start(bf16[512,4096]{1,0:T(8,128)(2,1)} %refs_2_.27) | copy-start | bytes 12582916
  10.9 15.6 %collective-permute-start.3 = (bf16[4,32,896]{2,1,0:T(8,128)(2,1)S(1)}, bf16[4,32,896]{2,1,0:T(8,128)(2,1)S(1)}, u32[]{:S(2)}, u32[]{:S(2)}) collective-permute-start(bf16[4,32,896]{2,1,0:T(8,128)(2,1)S(1)} %get-tuple-element.62), channel_id=1, source_target_pairs={{0,8},{4,12},{8,0},{12,4},{1,9},{5,13},{9,1},{13,5},{2,10},{6,14},... | collective-permute-start | bytes 688136 | tf_op jit(solution)/shard_map/ppermute | solution.py:433
  13.9 6.5 %collective-permute-start.4 = (bf16[2,32,896]{2,1,0:T(8,128)(2,1)S(1)}, bf16[2,32,896]{2,1,0:T(8,128)(2,1)S(1)}, u32[]{:S(2)}, u32[]{:S(2)}) collective-permute-start(bf16[2,32,896]{2,1,0:T(8,128)(2,1)S(1)} %get-tuple-element.65), channel_id=1, source_target_pairs={{0,4},{4,0},{8,12},{12,8},{1,5},{5,1},{9,13},{13,9},{2,6},{6,2},{1... | collective-permute-start | bytes 344072 | tf_op jit(solution)/shard_map/ppermute | solution.py:433
  15.5 7.4 %collective-permute-start.5 = (bf16[2,32,896]{2,1,0:T(8,128)(2,1)S(1)}, bf16[2,32,896]{2,1,0:T(8,128)(2,1)S(1)}, u32[]{:S(2)}, u32[]{:S(2)}) collective-permute-start(bf16[2,32,896]{2,1,0:T(8,128)(2,1)S(1)} %get-tuple-element.66), channel_id=1, source_target_pairs={{0,4},{4,0},{8,12},{12,8},{1,5},{5,1},{9,13},{13,9},{2,6},{6,2},{1... | collective-permute-start | bytes 344072 | tf_op jit(solution)/shard_map/ppermute | solution.py:433
  15.9 12.5 %collective-permute-start = (bf16[4,32,896]{2,1,0:T(8,128)(2,1)S(1)}, bf16[4,32,896]{2,1,0:T(8,128)(2,1)S(1)}, u32[]{:S(2)}, u32[]{:S(2)}) collective-permute-start(bf16[4,32,896]{2,1,0:T(8,128)(2,1)S(1)} %encode_local.1), channel_id=1, source_target_pairs={{0,2},{2,0},{1,3},{3,1},{4,6},{6,4},{5,7},{7,5},{8,10},{10,8},{9,1... | collective-permute-start | bytes 688136 | tf_op jit(solution)/shard_map/ppermute | solution.py:410
  17.4 29.9 %collective-permute-start.15 = (bf16[512,4096]{1,0:T(8,128)(2,1)S(1)}, bf16[512,4096]{1,0:T(8,128)(2,1)S(1)}, u32[]{:S(2)}, u32[]{:S(2)}) collective-permute-start(bf16[512,4096]{1,0:T(8,128)(2,1)S(1)} %copy-done), channel_id=1, source_target_pairs={{0,1},{1,0},{2,3},{3,2},{4,5},{5,4},{6,7},{7,6},{8,9},{9,8},{10,11... | collective-permute-start | bytes 12582920 | tf_op jit(solution)/shard_map/ppermute | solution.py:413
  24.3 6.9 %collective-permute-start.7 = (bf16[4,32,896]{2,1,0:T(8,128)(2,1)S(1)}, bf16[4,32,896]{2,1,0:T(8,128)(2,1)S(1)}, u32[]{:S(2)}, u32[]{:S(2)}) collective-permute-start(bf16[4,32,896]{2,1,0:T(8,128)(2,1)S(1)} %encode.3), channel_id=1, source_target_pairs={{0,2},{2,0},{1,3},{3,1},{4,6},{6,4},{5,7},{7,5},{8,10},{10,8},{9,1... | collective-permute-start | bytes 688136 | tf_op jit(solution)/shard_map/ppermute | solution.py:410
  25.9 7.9 %collective-permute-start.10 = (bf16[4,32,896]{2,1,0:T(8,128)(2,1)S(1)}, bf16[4,32,896]{2,1,0:T(8,128)(2,1)S(1)}, u32[]{:S(2)}, u32[]{:S(2)}) collective-permute-start(bf16[4,32,896]{2,1,0:T(8,128)(2,1)S(1)} %get-tuple-element.79), channel_id=1, source_target_pairs={{0,12},{4,8},{8,4},{12,0},{1,13},{5,9},{9,5},{13,1},{2,14},{6,10},... | collective-permute-start | bytes 688136 | tf_op jit(solution)/shard_map/ppermute | solution.py:433
  27.8 7.9 %collective-permute-start.9 = (bf16[4,32,896]{2,1,0:T(8,128)(2,1)S(1)}, bf16[4,32,896]{2,1,0:T(8,128)(2,1)S(1)}, u32[]{:S(2)}, u32[]{:S(2)}) collective-permute-start(bf16[4,32,896]{2,1,0:T(8,128)(2,1)S(1)} %encode.4), channel_id=1, source_target_pairs={{0,2},{2,0},{1,3},{3,1},{4,6},{6,4},{5,7},{7,5},{8,10},{10,8},{9,1... | collective-permute-start | bytes 688136 | tf_op jit(solution)/shard_map/ppermute | solution.py:410
  28.4 7.4 %collective-permute-start.6 = (bf16[2,4,32,896]{3,2,1,0:T(8,128)(2,1)S(1)}, bf16[2,4,32,896]{3,2,1,0:T(8,128)(2,1)S(1)}, u32[]{:S(2)}, u32[]{:S(2)}) collective-permute-start(bf16[2,4,32,896]{3,2,1,0:T(8,128)(2,1)S(1)} %pad_maximum_fusion.refs_0_), channel_id=1, source_target_pairs={{0,1},{1,0},{2,3},{3,2},{4,5},{5,4},{6,7},{7,6},{8,9},{9,8},{10,11... | collective-permute-start | bytes 1376264 | tf_op jit(solution)/shard_map/ppermute | solution.py:413
  31.3 4.5 %copy-start.2 = (bf16[896,512]{1,0:T(8,128)(2,1)S(1)}, bf16[896,512]{1,0:T(8,128)(2,1)}, u32[]{:S(2)}) copy-start(bf16[896,512]{1,0:T(8,128)(2,1)} %refs_5_.1) | copy-start | bytes 2752516
  31.3 4.5 %copy-start.3 = (bf16[896,512]{1,0:T(8,128)(2,1)S(1)}, bf16[896,512]{1,0:T(8,128)(2,1)}, u32[]{:S(2)}) copy-start(bf16[896,512]{1,0:T(8,128)(2,1)} %refs_6_.1) | copy-start | bytes 2752516
  31.3 5.8 %collective-permute-start.8 = (bf16[2,4,32,896]{3,2,1,0:T(8,128)(2,1)S(1)}, bf16[2,4,32,896]{3,2,1,0:T(8,128)(2,1)S(1)}, u32[]{:S(2)}, u32[]{:S(2)}) collective-permute-start(bf16[2,4,32,896]{3,2,1,0:T(8,128)(2,1)S(1)} %pad_maximum_fusion.1.refs_0_), channel_id=1, source_target_pairs={{0,1},{1,0},{2,3},{3,2},{4,5},{5,4},{6,7},{7,6},{8,9},{9,8},{10,11... | collective-permute-start | bytes 1376264 | tf_op jit(solution)/shard_map/ppermute | solution.py:413
  35.1 6.1 %collective-permute-start.12 = (bf16[4,32,896]{2,1,0:T(8,128)(2,1)S(1)}, bf16[4,32,896]{2,1,0:T(8,128)(2,1)S(1)}, u32[]{:S(2)}, u32[]{:S(2)}) collective-permute-start(bf16[4,32,896]{2,1,0:T(8,128)(2,1)S(1)} %encode.5), channel_id=1, source_target_pairs={{0,2},{2,0},{1,3},{3,1},{4,6},{6,4},{5,7},{7,5},{8,10},{10,8},{9,1... | collective-permute-start | bytes 688136 | tf_op jit(solution)/shard_map/ppermute | solution.py:410
  35.7 2.7 %collective-permute-start.11 = (bf16[2,4,32,896]{3,2,1,0:T(8,128)(2,1)S(1)}, bf16[2,4,32,896]{3,2,1,0:T(8,128)(2,1)S(1)}, u32[]{:S(2)}, u32[]{:S(2)}) collective-permute-start(bf16[2,4,32,896]{3,2,1,0:T(8,128)(2,1)S(1)} %pad_maximum_fusion.2.refs_0_), channel_id=1, source_target_pairs={{0,1},{1,0},{2,3},{3,2},{4,5},{5,4},{6,7},{7,6},{8,9},{9,8},{10,11... | collective-permute-start | bytes 1376264 | tf_op jit(solution)/shard_map/ppermute | solution.py:413
  41.2 1.9 %copy-start.1 = (bf16[512,512]{1,0:T(8,128)(2,1)S(1)}, bf16[512,512]{1,0:T(8,128)(2,1)}, u32[]{:S(2)}) copy-start(bf16[512,512]{1,0:T(8,128)(2,1)} %q_ref.5) | copy-start | bytes 1572868
  41.2 1.9 %collective-permute-start.13 = (bf16[2,4,32,896]{3,2,1,0:T(8,128)(2,1)S(1)}, bf16[2,4,32,896]{3,2,1,0:T(8,128)(2,1)S(1)}, u32[]{:S(2)}, u32[]{:S(2)}) collective-permute-start(bf16[2,4,32,896]{3,2,1,0:T(8,128)(2,1)S(1)} %pad_maximum_fusion.3.refs_0_), channel_id=1, source_target_pairs={{0,1},{1,0},{2,3},{3,2},{4,5},{5,4},{6,7},{7,6},{8,9},{9,8},{10,11... | collective-permute-start | bytes 1376264 | tf_op jit(solution)/shard_map/ppermute | solution.py:413
  45.7 1.6 %collective-permute-start.14 = (bf16[1,128,512]{2,1,0:T(8,128)(2,1)S(1)}, bf16[1,128,512]{2,1,0:T(8,128)(2,1)S(1)}, u32[]{:S(2)}, u32[]{:S(2)}) collective-permute-start(bf16[1,128,512]{2,1,0:T(8,128)(2,1)S(1)} %get-tuple-element.88), channel_id=1, source_target_pairs={{0,1},{1,0},{2,3},{3,2},{4,5},{5,4},{6,7},{7,6},{8,9},{9,8},{10,11... | collective-permute-start | bytes 393224 | tf_op jit(solution)/shard_map/ppermute | solution.py:467
  48.2 12.4 %collective-permute-start.21 = (bf16[128,1024]{1,0:T(8,128)(2,1)S(1)}, bf16[128,1024]{1,0:T(8,128)(2,1)S(1)}, u32[]{:S(2)}, u32[]{:S(2)}) collective-permute-start(bf16[128,1024]{1,0:T(8,128)(2,1)S(1)} %out_project.5), channel_id=1, source_target_pairs={{0,2},{2,0},{1,3},{3,1},{4,6},{6,4},{5,7},{7,5},{8,10},{10,8},{9,1... | collective-permute-start | bytes 786440 | tf_op jit(solution)/shard_map/ppermute | solution.py:484
  50.8 12.3 %collective-permute-start.20 = (bf16[128,1024]{1,0:T(8,128)(2,1)S(1)}, bf16[128,1024]{1,0:T(8,128)(2,1)S(1)}, u32[]{:S(2)}, u32[]{:S(2)}) collective-permute-start(bf16[128,1024]{1,0:T(8,128)(2,1)S(1)} %out_project.6), channel_id=1, source_target_pairs={{0,2},{2,0},{1,3},{3,1},{4,6},{6,4},{5,7},{7,5},{8,10},{10,8},{9,1... | collective-permute-start | bytes 786440 | tf_op jit(solution)/shard_map/ppermute | solution.py:484
  52.1 16.6 %collective-permute-start.19 = (bf16[128,1024]{1,0:T(8,128)(2,1)S(1)}, bf16[128,1024]{1,0:T(8,128)(2,1)S(1)}, u32[]{:S(2)}, u32[]{:S(2)}) collective-permute-start(bf16[128,1024]{1,0:T(8,128)(2,1)S(1)} %out_project.7), channel_id=1, source_target_pairs={{0,2},{2,0},{1,3},{3,1},{4,6},{6,4},{5,7},{7,5},{8,10},{10,8},{9,1... | collective-permute-start | bytes 786440 | tf_op jit(solution)/shard_map/ppermute | solution.py:484
  56.3 1.4 %collective-permute-start.16 = (bf16[1,128,512]{2,1,0:T(8,128)(2,1)S(1)}, bf16[1,128,512]{2,1,0:T(8,128)(2,1)S(1)}, u32[]{:S(2)}, u32[]{:S(2)}) collective-permute-start(bf16[1,128,512]{2,1,0:T(8,128)(2,1)S(1)} %attend.7), channel_id=1, source_target_pairs={{0,1},{1,0},{2,3},{3,2},{4,5},{5,4},{6,7},{7,6},{8,9},{9,8},{10,11... | collective-permute-start | bytes 393224 | tf_op jit(solution)/shard_map/ppermute | solution.py:467
  56.4 15.1 %collective-permute-start.18 = (bf16[128,512]{1,0:T(8,128)(2,1)S(1)}, bf16[128,512]{1,0:T(8,128)(2,1)S(1)}, u32[]{:S(2)}, u32[]{:S(2)}) collective-permute-start(bf16[128,512]{1,0:T(8,128)(2,1)S(1)} %out_project.8), channel_id=1, source_target_pairs={{0,2},{2,0},{1,3},{3,1},{4,6},{6,4},{5,7},{7,5},{8,10},{10,8},{9,1... | collective-permute-start | bytes 393224 | tf_op jit(solution)/shard_map/ppermute | solution.py:484
  57.7 16.5 %collective-permute-start.17 = (bf16[128,512]{1,0:T(8,128)(2,1)S(1)}, bf16[128,512]{1,0:T(8,128)(2,1)S(1)}, u32[]{:S(2)}, u32[]{:S(2)}) collective-permute-start(bf16[128,512]{1,0:T(8,128)(2,1)S(1)} %out_project.9), channel_id=1, source_target_pairs={{0,2},{2,0},{1,3},{3,1},{4,6},{6,4},{5,7},{7,5},{8,10},{10,8},{9,1... | collective-permute-start | bytes 393224 | tf_op jit(solution)/shard_map/ppermute | solution.py:484

commit v10 on v8

--- a/solution.py
+++ b/solution.py
@@ -246,71 +246,76 @@
     )(*pieces, w_key, w_value)
 
 
-def attend_kernel(firsts, n_pieces, n_heads, n_rep, turns, fanout, spans, slot_ref, q_ref, *refs):
-    n_ready = len(firsts) - 1
-    ready, refs = refs[:n_ready], refs[n_ready:]
-    pieces, refs = refs[:n_pieces], refs[n_pieces:]
-    wk_ref, wv_ref = refs[:2]
-    outs = refs[2 : 2 + n_rep]
-    kv_ref, sem = refs[2 + n_rep :]
-    copies = [
-        pltpu.make_async_copy(ref, kv_ref.at[pl.ds(first, ref.shape[0])], sem.at[i])
-        for i, (ref, first) in enumerate(zip(ready, firsts))
-    ]
-    for copy in copies:
-        copy.start()
-    project_into(kv_ref, firsts[-1], pieces, wk_ref, wv_ref)
-    for copy in copies:
-        copy.wait()
+def attend_kernel(firsts, n_heads, n_rep, targets, fanout, spans, n_rest, slot_ref, q_ref, *refs):
+    ready, (own_ref, *refs) = refs[: len(firsts) - 1], refs[len(firsts) - 1 :]
+    if n_rest:
+        pieces, (wk_ref, wv_ref, out_ref, rest_ref) = refs[:n_rest], refs[n_rest:]
+        project_into(rest_ref, 0, pieces, wk_ref, wv_ref)
+    else:
+        rest_ref, out_ref = refs
     heads_at, rep_at = lax.axis_index("heads"), lax.axis_index("rep")
-    cols = wk_ref.shape[1]
+    cols = q_ref.shape[1]
     span_len = q_ref.shape[0] // spans
     block = spans // (n_heads * n_rep)
-    tokens = kv_ref.shape[1] * kv_ref.shape[2]
+
+    def place(slot, first, count):
+        return jnp.clip(slot - first, 0, count - 1)
+
+    def held(slot, lanes):
+        at = place(slot, firsts[-1], own_ref.shape[0])
+        value = jnp.concatenate([own_ref[at, :, :, lanes], rest_ref[at, :, :, lanes]], axis=0)
+        for ref, first in reversed(list(zip(ready, firsts))):
+            there = slot < first + ref.shape[0]
+            value = jnp.where(there, ref[place(slot, first, ref.shape[0]), :, :, lanes], value)
+        return value.reshape(-1, HD)
+
     heads = [slice(h * HD, (h + 1) * HD) for h in range(cols // HD)]
-    for at, t in enumerate(turns):
-        for s in range(n_rep):
-            owner = lax.rem(heads_at + t, n_heads) * n_rep + lax.rem(rep_at + s, n_rep)
-            for i in range(block):
-                span = owner * block + i
-                slots = [slot_ref[span * fanout + k] for k in range(fanout)]
-                rows = pl.ds(pl.multiple_of(span * span_len, span_len), span_len)
-
-                def side(lanes):
-                    return jnp.concatenate(
-                        [kv_ref[slot, :, :, lanes].reshape(tokens, HD) for slot in slots], axis=0
-                    )
-
-                logits = [dot_t(q_ref[rows, lanes], side(lanes)) for lanes in heads]
-                tops = [jnp.max(part, axis=1, keepdims=True) for part in logits]
-                weights = [jnp.exp((part - top) * HD ** (-0.5)) for part, top in zip(logits, tops)]
-                scales = [1.0 / jnp.sum(part, axis=1, keepdims=True) for part in weights]
-                mixed = [
-                    dot(part.astype(BF16), side(slice(cols + lanes.start, cols + lanes.stop)))
-                    for part, lanes in zip(weights, heads)
-                ]
-                for part, scale, lanes in zip(mixed, scales, heads):
-                    outs[s][at, i * span_len : (i + 1) * span_len, lanes] = (part * scale).astype(BF16)
-
-
-def attend(slot, queries, ready, pieces, w_key, w_value, n_heads, n_rep, turns, fanout, spans):
+    for at, (t, s) in enumerate(targets):
+        owner = lax.rem(heads_at + t, n_heads) * n_rep + lax.rem(rep_at + s, n_rep)
+        for i in range(block):
+            span = owner * block + i
+            slots = [slot_ref[span * fanout + k] for k in range(fanout)]
+            rows = pl.ds(pl.multiple_of(span * span_len, span_len), span_len)
+
+            def side(lanes):
+                return jnp.concatenate([held(slot, lanes) for slot in slots], axis=0)
+
+            logits = [dot_t(q_ref[rows, lanes], side(lanes)) for lanes in heads]
+            tops = [jnp.max(part, axis=1, keepdims=True) for part in logits]
+            weights = [jnp.exp((part - top) * HD ** (-0.5)) for part, top in zip(logits, tops)]
+            scales = [1.0 / jnp.sum(part, axis=1, keepdims=True) for part in weights]
+            mixed = [
+                dot(part.astype(BF16), side(slice(cols + lanes.start, cols + lanes.stop)))
+                for part, lanes in zip(weights, heads)
+            ]
+            for part, scale, lanes in zip(mixed, scales, heads):
+                out_ref[at, i * span_len : (i + 1) * span_len, lanes] = (part * scale).astype(BF16)
+
+
+def attend(slot, queries, ready, own, rest, weights, n_heads, n_rep, targets, fanout, spans):
     firsts = [0]
     for kv in ready:
         firsts.append(firsts[-1] + kv.shape[0])
-    n, slots, tokens, _ = pieces[0].shape
-    cols = w_key.shape[1]
+    cols = queries.shape[1]
     rows = queries.shape[0] // (n_heads * n_rep)
-    kv_shape = (firsts[-1] + slots, n * len(pieces), tokens, 2 * cols)
-    return pl.pallas_call(
-        functools.partial(attend_kernel, firsts, len(pieces), n_heads, n_rep, turns, fanout, spans),
-        out_shape=[jax.ShapeDtypeStruct((len(turns), rows, cols), BF16)] * n_rep,
-        in_specs=[SMEM, VMEM] + [ANY] * len(ready) + [VMEM] * (len(pieces) + 2),
-        out_specs=[VMEM] * n_rep,
-        scratch_shapes=[pltpu.VMEM(kv_shape, BF16), pltpu.SemaphoreType.DMA((max(1, len(ready)),))],
-        compiler_params=params(40),
+    todo = isinstance(rest, list)
+    slots, _, tokens, width = own.shape
+    out_shape = [jax.ShapeDtypeStruct((len(targets), rows, cols), BF16)]
+    if todo:
+        others = sum(piece.shape[0] for piece in rest)
+        out_shape.append(jax.ShapeDtypeStruct((slots, others, tokens, width), BF16))
+    operands = [*rest, *weights] if todo else [rest]
+    return pl.pallas_call(
+        functools.partial(
+            attend_kernel, firsts, n_heads, n_rep, targets, fanout, spans, len(rest) if todo else 0
+        ),
+        out_shape=out_shape,
+        in_specs=[SMEM] + [VMEM] * (len(ready) + 2 + len(operands)),
+        out_specs=[VMEM] * len(out_shape),
+        compiler_params=params(32),
         cost_estimate=cost(0.001),
         name="attend",
-    )(slot, queries, *ready, *pieces, w_key, w_value)
+    )(slot, queries, *ready, own, *operands)
 
 
 def out_kernel(n_rep, n_received, *refs):
@@ -403,18 +408,26 @@
         last = project(after(pieces[len(kvs)], last), w_key, w_value)
         kvs.append(last)
     pieces = over_rep(jnp.stack(after(crossed[-1], kvs)))
-
-    def mix(turns, q):
-        outs = attend(slot, q, kvs, pieces, w_key, w_value, n_heads, n_rep, turns, fanout, spans)
-        return [outs[0]] + [
-            lax.ppermute(outs[s], "rep", shift_pairs(n_rep, s)) for s in range(1, n_rep)
-        ]
+    own_kv, rest = project(pieces[:1], w_key, w_value), pieces[1:]
+
+    def mix(turns, q, rest):
+        mixed = []
+        for s in range(1, n_rep):
+            given, *made = attend(
+                slot, q, kvs, own_kv, rest, (w_key, w_value), n_heads, n_rep, [(t, s) for t in turns], fanout, spans
+            )
+            rest = made[0] if made else rest
+            mixed.append(lax.ppermute(given, "rep", shift_pairs(n_rep, s)))
+        kept = attend(
+            slot, q, kvs, own_kv, rest, (w_key, w_value), n_heads, n_rep, [(t, 0) for t in turns], fanout, spans
+        )
+        return [kept[0]] + mixed, rest
 
     width = w_out.shape[1]
     tile = min(COL_TILE, width)
     cuts = [width // tile * part // 8 * tile for part in (0, 2, 4, 6, 7)] + [width]
     blocks = [(start, stop) for start, stop in zip(cuts, cuts[1:]) if stop > start]
-    mixed = mix(list(range(1, n_heads)), queries)
+    mixed, rest = mix(list(range(1, n_heads)), queries, rest)
     received, partials = [[] for _ in blocks], []
     for t in range(1, n_heads):
         for i, (start, stop) in enumerate(blocks):
@@ -422,7 +435,7 @@
             partial, mixed = lax.optimization_barrier((partial, mixed))
             partials.append(partial)
             received[i].append(lax.ppermute(partial, "heads", shift_pairs(n_heads, t)))
-    mixed = mix([0], after(queries, partials))
+    mixed, rest = mix([0], after(queries, partials), rest)
     out = None
     for (start, stop), parts in zip(blocks, received):
         out = out_project(mixed, w_outs, 0, start, stop, tile, 0.2, parts, out, True)

time: 76.4 us -> 75.7 us (level)
  waiting for transfers between devices: 27.1 us -> 25.7 us
    ppermute x2, waiting for transfers between devices: 1.22 us -> 0.01 us  [mix(): mixed.append(lax.ppermute(given, 'rep', shift_pairs(n_rep, s)))]
    pallas_call x3 -> x4, Pallas kernels: 3.75 us -> 4.49 us  [project(): pl.pallas_call(functools.partial(project_kernel, len(pieces)), out_shape=...]
    pallas_call x2 -> x4, Pallas kernels: 7.01 us -> 6.69 us  [attend(): pl.pallas_call(functools.partial(attend_kernel, firsts, n_heads, n_rep, t...]
  transfers between devices with their start and end apart: 23 -> 23, of which waited for: 12 -> 11; matrix products, arithmetic and copies ran while one was open for 0% -> 0% of each run, Pallas kernels for 33% -> 34%
where the time goes in v10:
time: 75.7 us; the launch traced here: 75.5 us
  Pallas kernels  28.3 us (37%)
  waiting for transfers between devices  25.7 us (34%)
  starting transfers between devices  20.3 us (27%)
  other arithmetic  0.9 us (1%)
    pallas_call x10, Pallas kernels, out_project(): pl.pallas_call(functools.partial(out_kernel, n, len(received)), grid=((st...  9.81 us
    ppermute x5, waiting for transfers between devices, shards(): received[i].append(lax.ppermute(partial, 'heads', shift_pairs(n_heads, t)))  8.97 us
    ppermute x4, waiting for transfers between devices, send(): lax.ppermute(block, 'lanes', lane_pairs(n_lanes, items[i][0], True))  8.6 us
    pallas_call x4, Pallas kernels, attend(): pl.pallas_call(functools.partial(attend_kernel, firsts, n_heads, n_rep, t...  6.69 us
    ppermute x4, waiting for transfers between devices, over_heads(): lax.ppermute(array, 'heads', shift_pairs(n_heads, s))  5.78 us
    ppermute x3, starting transfers between devices, shards(): lax.ppermute(own, 'lanes', lane_pairs(n_lanes, d, False))  5.76 us
    ppermute x5, starting transfers between devices, shards(): received[i].append(lax.ppermute(partial, 'heads', shift_pairs(n_heads, t)))  5.6 us
    pallas_call x4, Pallas kernels, project(): pl.pallas_call(functools.partial(project_kernel, len(pieces)), out_shape=...  4.49 us
  transfers between devices with their start and end apart: 23, of which 11 were waited for; matrix products, arithmetic and copies ran while one was open for 0% of the time, Pallas kernels for 34%

profile of v10, /device:TPU:0, one launch (start us, length us, event | category | flops | bytes accessed | tf_op | source)
XLA Modules:
  0.0 75.5 jit_solution(13115303783341873541)
XLA Ops:
  0.0 0.7 pad_add_fusion.own_ref
  0.7 5.1 %collective-permute-start.3 = (s32[4,8]{1,0:T(4,128)S(1)}, s32[4,8]{1,0:T(4,128)S(1)}, u32[]{:S(2)}, u32[]{:S(2)}) collective-permute-start(s32[4,8]{1,0:T(4,128)S(1)} %pad_add_fusion.own_ref), channel_id=1, source_target_pairs={{0,12},{4,8},{8,4},{12,0},{1,13},{5,9},{9,5},{13,1},{2,14},{6,10},... | collective-permute-start | bytes 392 | tf_op jit(solution)/shard_map/ppermute | solution.py:378
  5.8 0.6 collective-permute-start.1
  6.5 1.3 %plan.1 = (s32[16]{0:T(128)S(1)}, s32[16]{0:T(128)S(1)}, s32[16]{0:T(128)S(1)}) custom-call(s32[4,8]{1,0:T(4,128)S(1)} %pad_add_fusion.own_ref), custom_call_target="tpu_custom_call" | custom-call | flops 10000000000 | bytes 1024 | tf_op jit(solution)/shard_map/plan/pallas_call | solution.py:76
  7.8 1.3 %encode_local.1 = bf16[4,32,896]{2,1,0:T(8,128)(2,1)S(1)} custom-call(s32[16]{0:T(128)S(1)} %get-tuple-element.53.req_ref, s32[16]{0:T(128)S(1)} %get-tuple-element.54.pick_ref, bf16[512,896]{1,0:T(8,128)(2,1)S(1)} %copy-done.4, bf16[16,32,896]{2,1,0:T(8,128)(2,1)S(1)} %copy-done.5), custom_call_target="tpu_custom_call" | custom-call | flops 10000000000 | bytes 1024 | tf_op jit(solution)/shard_map/encode_local/pallas_call | solution.py:205
  9.1 1.3 %collective-permute-done.2.refs_1_ = s32[4,8]{1,0:T(4,128)S(1)} collective-permute-done((s32[4,8]{1,0:T(4,128)S(1)}, s32[4,8]{1,0:T(4,128)S(1)}, u32[]{:S(2)}, u32[]{:S(2)}) %collective-permute-start.2) | collective-permute-done | bytes 160 | tf_op jit(solution)/shard_map/ppermute | solution.py:378
  10.3 0.8 %fetch.1 = (bf16[2,32,896]{2,1,0:T(8,128)(2,1)S(1)}, bf16[2,32,896]{2,1,0:T(8,128)(2,1)S(1)}, bf16[4,32,896]{2,1,0:T(8,128)(2,1)S(1)}, bf16[4,32,896]{2,1,0:T(8,128)(2,1)S(1)}) custom-call(s32[4,8]{1,0:T(4,128)S(1)} %collective-permute-done.1.refs_0_, s32[4,8]{1,0:T(4,128)S(1)} %collective-permute-done.2.refs_1_, s32[4,8]{1,0:T(4,128)S(1)} %collective-permute-done.3.refs_2_, ...), custom_call_target="tpu_custom_call" | custom-call | flops 10000000000 | bytes 1024 | tf_op jit(solution)/shard_map/fetch/pallas_call | solution.py:109
  11.1 2.1 %collective-permute-start.4 = (bf16[4,32,896]{2,1,0:T(8,128)(2,1)S(1)}, bf16[4,32,896]{2,1,0:T(8,128)(2,1)S(1)}, u32[]{:S(2)}, u32[]{:S(2)}) collective-permute-start(bf16[4,32,896]{2,1,0:T(8,128)(2,1)S(1)} %get-tuple-element.58), channel_id=1, source_target_pairs={{0,8},{4,12},{8,0},{12,4},{1,9},{5,13},{9,1},{13,5},{2,10},{6,14},... | collective-permute-start | bytes 688136 | tf_op jit(solution)/shard_map/ppermute | solution.py:386
  13.2 1.0 %collective-permute-start.5 = (bf16[2,32,896]{2,1,0:T(8,128)(2,1)S(1)}, bf16[2,32,896]{2,1,0:T(8,128)(2,1)S(1)}, u32[]{:S(2)}, u32[]{:S(2)}) collective-permute-start(bf16[2,32,896]{2,1,0:T(8,128)(2,1)S(1)} %get-tuple-element.61), channel_id=1, source_target_pairs={{0,4},{4,0},{8,12},{12,8},{1,5},{5,1},{9,13},{13,9},{2,6},{6,2},{1... | collective-permute-start | bytes 344072 | tf_op jit(solution)/shard_map/ppermute | solution.py:386
  14.3 1.0 %collective-permute-start.6 = (bf16[2,32,896]{2,1,0:T(8,128)(2,1)S(1)}, bf16[2,32,896]{2,1,0:T(8,128)(2,1)S(1)}, u32[]{:S(2)}, u32[]{:S(2)}) collective-permute-start(bf16[2,32,896]{2,1,0:T(8,128)(2,1)S(1)} %get-tuple-element.62), channel_id=1, source_target_pairs={{0,4},{4,0},{8,12},{12,8},{1,5},{5,1},{9,13},{13,9},{2,6},{6,2},{1... | collective-permute-start | bytes 344072 | tf_op jit(solution)/shard_map/ppermute | solution.py:386
  15.2 1.5 %collective-permute-start = (bf16[4,32,896]{2,1,0:T(8,128)(2,1)S(1)}, bf16[4,32,896]{2,1,0:T(8,128)(2,1)S(1)}, u32[]{:S(2)}, u32[]{:S(2)}) collective-permute-start(bf16[4,32,896]{2,1,0:T(8,128)(2,1)S(1)} %encode_local.1), channel_id=1, source_target_pairs={{0,2},{2,0},{1,3},{3,1},{4,6},{6,4},{5,7},{7,5},{8,10},{10,8},{9,1... | collective-permute-start | bytes 688136 | tf_op jit(solution)/shard_map/ppermute | solution.py:363
  16.7 3.5 %collective-permute-done.5.refs_0_ = bf16[2,32,896]{2,1,0:T(8,128)(2,1)S(1)} collective-permute-done((bf16[2,32,896]{2,1,0:T(8,128)(2,1)S(1)}, bf16[2,32,896]{2,1,0:T(8,128)(2,1)S(1)}, u32[]{:S(2)}, u32[]{:S(2)}) %collective-permute-start.5) | collective-permute-done | bytes 114720 | tf_op jit(solution)/shard_map/ppermute | solution.py:386
  20.3 3.3 %collective-permute-done.6.refs_1_ = bf16[2,32,896]{2,1,0:T(8,128)(2,1)S(1)} collective-permute-done((bf16[2,32,896]{2,1,0:T(8,128)(2,1)S(1)}, bf16[2,32,896]{2,1,0:T(8,128)(2,1)S(1)}, u32[]{:S(2)}, u32[]{:S(2)}) %collective-permute-start.6) | collective-permute-done | bytes 114720 | tf_op jit(solution)/shard_map/ppermute | solution.py:386
  23.6 1.5 %encode.3 = bf16[4,32,896]{2,1,0:T(8,128)(2,1)S(1)} custom-call(s32[16]{0:T(128)S(1)} %get-tuple-element.53.req_ref, bf16[512,896]{1,0:T(8,128)(2,1)S(1)} %copy-done.4, bf16[2,32,896]{2,1,0:T(8,128)(2,1)S(1)} %collective-permute-done.5.refs_0_, bf16[2,32,896]{2,1,0:T(8,128)(2,1)S(1)} %collective-permute-done.6.refs_1_), custom_call_target="tpu_custom_call" | custom-call | flops 100000000 | bytes 1024 | tf_op jit(solution)/shard_map/encode/pallas_call | solution.py:186
  25.1 1.6 %collective-permute-start.8 = (bf16[4,32,896]{2,1,0:T(8,128)(2,1)S(1)}, bf16[4,32,896]{2,1,0:T(8,128)(2,1)S(1)}, u32[]{:S(2)}, u32[]{:S(2)}) collective-permute-start(bf16[4,32,896]{2,1,0:T(8,128)(2,1)S(1)} %encode.3), channel_id=1, source_target_pairs={{0,2},{2,0},{1,3},{3,1},{4,6},{6,4},{5,7},{7,5},{8,10},{10,8},{9,1... | collective-permute-start | bytes 688136 | tf_op jit(solution)/shard_map/ppermute | solution.py:363
  26.6 1.3 %encode.4 = bf16[4,32,896]{2,1,0:T(8,128)(2,1)S(1)} custom-call(s32[16]{0:T(128)S(1)} %get-tuple-element.53.req_ref, bf16[512,896]{1,0:T(8,128)(2,1)S(1)} %copy-done.4, bf16[4,32,896]{2,1,0:T(8,128)(2,1)S(1)} %collective-permute-done.4.refs_0_), custom_call_target="tpu_custom_call" | custom-call | flops 10000000000 | bytes 1024 | tf_op jit(solution)/shard_map/encode/pallas_call | solution.py:186
  27.9 0.6 collective-permute-start.10
  28.6 4.0 %collective-permute-done.8 = bf16[4,32,896]{2,1,0:T(8,128)(2,1)S(1)} collective-permute-done((bf16[4,32,896]{2,1,0:T(8,128)(2,1)S(1)}, bf16[4,32,896]{2,1,0:T(8,128)(2,1)S(1)}, u32[]{:S(2)}, u32[]{:S(2)}) %collective-permute-start.8) | collective-permute-done | bytes 229408 | tf_op jit(solution)/shard_map/ppermute | solution.py:363
  32.8 1.7 %collective-permute-done.11.refs_0_ = bf16[4,32,896]{2,1,0:T(8,128)(2,1)S(1)} collective-permute-done((bf16[4,32,896]{2,1,0:T(8,128)(2,1)S(1)}, bf16[4,32,896]{2,1,0:T(8,128)(2,1)S(1)}, u32[]{:S(2)}, u32[]{:S(2)}) %collective-permute-start.11) | collective-permute-done | bytes 229408 | tf_op jit(solution)/shard_map/ppermute | solution.py:386
  34.6 1.3 %encode.5 = bf16[4,32,896]{2,1,0:T(8,128)(2,1)S(1)} custom-call(s32[16]{0:T(128)S(1)} %get-tuple-element.53.req_ref, bf16[512,896]{1,0:T(8,128)(2,1)S(1)} %copy-done.4, bf16[4,32,896]{2,1,0:T(8,128)(2,1)S(1)} %collective-permute-done.11.refs_0_), custom_call_target="tpu_custom_call" | custom-call | flops 10000000000 | bytes 1024 | tf_op jit(solution)/shard_map/encode/pallas_call | solution.py:186
  35.8 0.6 collective-permute-start.13
  36.6 1.3 %project.4.refs_0_ = bf16[4,4,32,1024]{3,2,1,0:T(8,128)(2,1)S(1)} custom-call(bf16[2,4,32,896]{3,2,1,0:T(8,128)(2,1)S(1)} %pad_maximum_fusion.refs_0_, bf16[2,4,32,896]{3,2,1,0:T(8,128)(2,1)S(1)} %collective-permute-done.7.refs_1_, bf16[896,512]{1,0:T(8,128)(2,1)S(1)} %copy-done.2, bf16[896,512]{1,0:T(8,128)(2,1)S(1)} %copy-done.3), custom_call_target="tpu_custom_call" | custom-call | flops 10000000000 | bytes 1024 | tf_op jit(solution)/shard_map/project/pallas_call | solution.py:238
  37.9 1.3 %project.5.refs_1_ = bf16[4,4,32,1024]{3,2,1,0:T(8,128)(2,1)S(1)} custom-call(bf16[2,4,32,896]{3,2,1,0:T(8,128)(2,1)S(1)} %pad_maximum_fusion.1.refs_0_, bf16[2,4,32,896]{3,2,1,0:T(8,128)(2,1)S(1)} %collective-permute-done.9.refs_1_, bf16[896,512]{1,0:T(8,128)(2,1)S(1)} %copy-done.2, bf16[896,512]{1,0:T(8,128)(2,1)S(1)} %copy-done.3), custom_call_target="tpu_custom_call" | custom-call | flops 10000000000 | bytes 1024 | tf_op jit(solution)/shard_map/project/pallas_call | solution.py:238
  39.1 1.3 %project.6.refs_2_ = bf16[4,4,32,1024]{3,2,1,0:T(8,128)(2,1)S(1)} custom-call(bf16[2,4,32,896]{3,2,1,0:T(8,128)(2,1)S(1)} %pad_maximum_fusion.2.refs_0_, bf16[2,4,32,896]{3,2,1,0:T(8,128)(2,1)S(1)} %collective-permute-done.12.refs_1_, bf16[896,512]{1,0:T(8,128)(2,1)S(1)} %copy-done.2, bf16[896,512]{1,0:T(8,128)(2,1)S(1)} %copy-done.3), custom_call_target="tpu_custom_call" | custom-call | flops 10000000000 | bytes 1024 | tf_op jit(solution)/shard_map/project/pallas_call | solution.py:238
  40.4 1.8 %collective-permute-done.13 = bf16[4,32,896]{2,1,0:T(8,128)(2,1)S(1)} collective-permute-done((bf16[4,32,896]{2,1,0:T(8,128)(2,1)S(1)}, bf16[4,32,896]{2,1,0:T(8,128)(2,1)S(1)}, u32[]{:S(2)}, u32[]{:S(2)}) %collective-permute-start.13) | collective-permute-done | bytes 229408 | tf_op jit(solution)/shard_map/ppermute | solution.py:363
  42.3 0.7 project.7.refs_3_
  43.0 1.1 %collective-permute-done.14.refs_4_ = bf16[2,4,32,896]{3,2,1,0:T(8,128)(2,1)S(1)} collective-permute-done((bf16[2,4,32,896]{3,2,1,0:T(8,128)(2,1)S(1)}, bf16[2,4,32,896]{3,2,1,0:T(8,128)(2,1)S(1)}, u32[]{:S(2)}, u32[]{:S(2)}) %collective-permute-start.14) | collective-permute-done | bytes 458784 | tf_op jit(solution)/shard_map/ppermute | solution.py:366
  44.1 2.2 %attend.4 = (bf16[1,128,512]{2,1,0:T(8,128)(2,1)S(1)}, bf16[4,2,32,1024]{3,2,1,0:T(8,128)(2,1)S(1)}) custom-call(s32[16]{0:T(128)S(1)} %get-tuple-element.52.slot_ref, bf16[512,512]{1,0:T(8,128)(2,1)S(1)} %copy-done.1, bf16[4,4,32,1024]{3,2,1,0:T(8,128)(2,1)S(1)} %project.4.refs_0_, bf16[4,4,32,1024]{3,2,1,0:T(8,128)(2,1)S(1)} %project.5.refs_1_, ...), custom_call_target="tpu_custom_call" | custom-call | flops 1000000 | bytes 1024 | tf_op jit(solution)/shard_map/attend/pallas_call | solution.py:308
  46.5 1.5 %attend.5.refs_0_ = bf16[1,128,512]{2,1,0:T(8,128)(2,1)S(1)} custom-call(s32[16]{0:T(128)S(1)} %get-tuple-element.52.slot_ref, bf16[512,512]{1,0:T(8,128)(2,1)S(1)} %copy-done.1, bf16[4,4,32,1024]{3,2,1,0:T(8,128)(2,1)S(1)} %project.4.refs_0_, bf16[4,4,32,1024]{3,2,1,0:T(8,128)(2,1)S(1)} %project.5.refs_1_, bf16[4,4,32,1024]{3,2,1,0:T(8,128)(2,1)S(1)} %project.6.refs_2_, ...), custom_call_target="tpu_custom_call" | custom-call | flops 1000000 | bytes 1024 | tf_op jit(solution)/shard_map/attend/pallas_call | solution.py:308
  48.0 1.0 %out_project.5 = bf16[128,1024]{1,0:T(8,128)(2,1)S(1)} custom-call(bf16[1,128,512]{2,1,0:T(8,128)(2,1)S(1)} %attend.5.refs_0_, bf16[1,128,512]{2,1,0:T(8,128)(2,1)S(1)} %collective-permute-done.15.refs_1_, bf16[512,4096]{1,0:T(8,128)(2,1)S(1)} %copy-done, bf16[512,4096]{1,0:T(8,128)(2,1)S(1)} %collective-permute-done.16.refs_3_), custom_call_target="tpu_custom_call" | custom-call | flops 1000000 | bytes 1024 | tf_op jit(solution)/shard_map/out_project/pallas_call | solution.py:335
  49.1 0.6 collective-permute-start.22
  49.7 0.9 %out_project.6 = bf16[128,1024]{1,0:T(8,128)(2,1)S(1)} custom-call(bf16[1,128,512]{2,1,0:T(8,128)(2,1)S(1)} %attend.5.refs_0_, bf16[1,128,512]{2,1,0:T(8,128)(2,1)S(1)} %collective-permute-done.15.refs_1_, bf16[512,4096]{1,0:T(8,128)(2,1)S(1)} %copy-done, bf16[512,4096]{1,0:T(8,128)(2,1)S(1)} %collective-permute-done.16.refs_3_), custom_call_target="tpu_custom_call" | custom-call | flops 1000000 | bytes 1024 | tf_op jit(solution)/shard_map/out_project/pallas_call | solution.py:335
  50.5 1.6 %collective-permute-start.21 = (bf16[128,1024]{1,0:T(8,128)(2,1)S(1)}, bf16[128,1024]{1,0:T(8,128)(2,1)S(1)}, u32[]{:S(2)}, u32[]{:S(2)}) collective-permute-start(bf16[128,1024]{1,0:T(8,128)(2,1)S(1)} %out_project.6), channel_id=1, source_target_pairs={{0,2},{2,0},{1,3},{3,1},{4,6},{6,4},{5,7},{7,5},{8,10},{10,8},{9,1... | collective-permute-start | bytes 786440 | tf_op jit(solution)/shard_map/ppermute | solution.py:437
  52.1 0.9 %out_project.7 = bf16[128,1024]{1,0:T(8,128)(2,1)S(1)} custom-call(bf16[1,128,512]{2,1,0:T(8,128)(2,1)S(1)} %attend.5.refs_0_, bf16[1,128,512]{2,1,0:T(8,128)(2,1)S(1)} %collective-permute-done.15.refs_1_, bf16[512,4096]{1,0:T(8,128)(2,1)S(1)} %copy-done, bf16[512,4096]{1,0:T(8,128)(2,1)S(1)} %collective-permute-done.16.refs_3_), custom_call_target="tpu_custom_call" | custom-call | flops 1000000 | bytes 1024 | tf_op jit(solution)/shard_map/out_project/pallas_call | solution.py:335
  53.0 0.6 collective-permute-start.20
  54.2 1.5 %attend.7 = bf16[1,128,512]{2,1,0:T(8,128)(2,1)S(1)} custom-call(s32[16]{0:T(128)S(1)} %get-tuple-element.52.slot_ref, bf16[512,512]{1,0:T(8,128)(2,1)S(1)} %copy-done.1, bf16[4,4,32,1024]{3,2,1,0:T(8,128)(2,1)S(1)} %project.4.refs_0_, bf16[4,4,32,1024]{3,2,1,0:T(8,128)(2,1)S(1)} %project.5.refs_1_, bf16[4,4,32,1024]{3,2,1,0:T(8,128)(2,1)S(1)} %project.6.refs_2_, ...), custom_call_target="tpu_custom_call" | custom-call | flops 1000000 | bytes 1024 | tf_op jit(solution)/shard_map/attend/pallas_call | solution.py:308
  55.8 1.6 %collective-permute-start.19 = (bf16[128,512]{1,0:T(8,128)(2,1)S(1)}, bf16[128,512]{1,0:T(8,128)(2,1)S(1)}, u32[]{:S(2)}, u32[]{:S(2)}) collective-permute-start(bf16[128,512]{1,0:T(8,128)(2,1)S(1)} %out_project.8), channel_id=1, source_target_pairs={{0,2},{2,0},{1,3},{3,1},{4,6},{6,4},{5,7},{7,5},{8,10},{10,8},{9,1... | collective-permute-start | bytes 393224 | tf_op jit(solution)/shard_map/ppermute | solution.py:437
  57.3 1.3 %collective-permute-start.18 = (bf16[128,512]{1,0:T(8,128)(2,1)S(1)}, bf16[128,512]{1,0:T(8,128)(2,1)S(1)}, u32[]{:S(2)}, u32[]{:S(2)}) collective-permute-start(bf16[128,512]{1,0:T(8,128)(2,1)S(1)} %out_project.9), channel_id=1, source_target_pairs={{0,2},{2,0},{1,3},{3,1},{4,6},{6,4},{5,7},{7,5},{8,10},{10,8},{9,1... | collective-permute-start | bytes 393224 | tf_op jit(solution)/shard_map/ppermute | solution.py:437
  58.6 1.5 %attend.6.refs_0_ = bf16[1,128,512]{2,1,0:T(8,128)(2,1)S(1)} custom-call(s32[16]{0:T(128)S(1)} %get-tuple-element.52.slot_ref, bf16[512,512]{1,0:T(8,128)(2,1)S(1)} %copy-done.1, bf16[4,4,32,1024]{3,2,1,0:T(8,128)(2,1)S(1)} %project.4.refs_0_, bf16[4,4,32,1024]{3,2,1,0:T(8,128)(2,1)S(1)} %project.5.refs_1_, bf16[4,4,32,1024]{3,2,1,0:T(8,128)(2,1)S(1)} %project.6.refs_2_, ...), custom_call_target="tpu_custom_call" | custom-call | flops 1000000 | bytes 1024 | tf_op jit(solution)/shard_map/attend/pallas_call | solution.py:308
  60.1 1.5 %out_final.5.refs_5_ = bf16[128,4096]{1,0:T(8,128)(2,1)} custom-call(bf16[1,128,512]{2,1,0:T(8,128)(2,1)S(1)} %attend.6.refs_0_, bf16[1,128,512]{2,1,0:T(8,128)(2,1)S(1)} %collective-permute-done.17.refs_1_, bf16[512,4096]{1,0:T(8,128)(2,1)S(1)} %copy-done, bf16[512,4096]{1,0:T(8,128)(2,1)S(1)} %collective-permute-done.16.refs_3_, ...), custom_call_target="tpu_custom_call" | custom-call | flops 200000000 | bytes 1024 | tf_op jit(solution)/shard_map/out_final/pallas_call | solution.py:335
  61.6 2.2 %collective-permute-done.21.refs_4_ = bf16[128,1024]{1,0:T(8,128)(2,1)S(1)} collective-permute-done((bf16[128,1024]{1,0:T(8,128)(2,1)S(1)}, bf16[128,1024]{1,0:T(8,128)(2,1)S(1)}, u32[]{:S(2)}, u32[]{:S(2)}) %collective-permute-start.21) | collective-permute-done | bytes 262176 | tf_op jit(solution)/shard_map/ppermute | solution.py:437
  63.9 1.5 %out_final.6.refs_5_ = bf16[128,4096]{1,0:T(8,128)(2,1)} custom-call(bf16[1,128,512]{2,1,0:T(8,128)(2,1)S(1)} %attend.6.refs_0_, bf16[1,128,512]{2,1,0:T(8,128)(2,1)S(1)} %collective-permute-done.17.refs_1_, bf16[512,4096]{1,0:T(8,128)(2,1)S(1)} %copy-done, bf16[512,4096]{1,0:T(8,128)(2,1)S(1)} %collective-permute-done.16.refs_3_, ...), custom_call_target="tpu_custom_call", output_to_operand_aliasing={{}: (5, {})} | custom-call | flops 200000000 | bytes 1024 | tf_op jit(solution)/shard_map/out_final/pallas_call | solution.py:335
  65.4 4.1 %collective-permute-done.20.refs_4_ = bf16[128,1024]{1,0:T(8,128)(2,1)S(1)} collective-permute-done((bf16[128,1024]{1,0:T(8,128)(2,1)S(1)}, bf16[128,1024]{1,0:T(8,128)(2,1)S(1)}, u32[]{:S(2)}, u32[]{:S(2)}) %collective-permute-start.20) | collective-permute-done | bytes 262176 | tf_op jit(solution)/shard_map/ppermute | solution.py:437
  69.5 1.5 %out_final.7.refs_5_ = bf16[128,4096]{1,0:T(8,128)(2,1)} custom-call(bf16[1,128,512]{2,1,0:T(8,128)(2,1)S(1)} %attend.6.refs_0_, bf16[1,128,512]{2,1,0:T(8,128)(2,1)S(1)} %collective-permute-done.17.refs_1_, bf16[512,4096]{1,0:T(8,128)(2,1)S(1)} %copy-done, bf16[512,4096]{1,0:T(8,128)(2,1)S(1)} %collective-permute-done.16.refs_3_, ...), custom_call_target="tpu_custom_call", output_to_operand_aliasing={{}: (5, {})} | custom-call | flops 200000000 | bytes 1024 | tf_op jit(solution)/shard_map/out_final/pallas_call | solution.py:335
  71.0 1.3 %collective-permute-done.19.refs_4_ = bf16[128,512]{1,0:T(8,128)(2,1)S(1)} collective-permute-done((bf16[128,512]{1,0:T(8,128)(2,1)S(1)}, bf16[128,512]{1,0:T(8,128)(2,1)S(1)}, u32[]{:S(2)}, u32[]{:S(2)}) %collective-permute-start.19) | collective-permute-done | bytes 131104 | tf_op jit(solution)/shard_map/ppermute | solution.py:437
  72.3 1.0 %out_final.8.refs_5_ = bf16[128,4096]{1,0:T(8,128)(2,1)} custom-call(bf16[1,128,512]{2,1,0:T(8,128)(2,1)S(1)} %attend.6.refs_0_, bf16[1,128,512]{2,1,0:T(8,128)(2,1)S(1)} %collective-permute-done.17.refs_1_, bf16[512,4096]{1,0:T(8,128)(2,1)S(1)} %copy-done, bf16[512,4096]{1,0:T(8,128)(2,1)S(1)} %collective-permute-done.16.refs_3_, ...), custom_call_target="tpu_custom_call", output_to_operand_aliasing={{}: (5, {})} | custom-call | flops 200000000 | bytes 1024 | tf_op jit(solution)/shard_map/out_final/pallas_call | solution.py:335
  73.3 1.3 %collective-permute-done.18.refs_4_ = bf16[128,512]{1,0:T(8,128)(2,1)S(1)} collective-permute-done((bf16[128,512]{1,0:T(8,128)(2,1)S(1)}, bf16[128,512]{1,0:T(8,128)(2,1)S(1)}, u32[]{:S(2)}, u32[]{:S(2)}) %collective-permute-start.18) | collective-permute-done | bytes 131104 | tf_op jit(solution)/shard_map/ppermute | solution.py:437
  74.6 1.0 %out_final.9 = bf16[128,4096]{1,0:T(8,128)(2,1)} custom-call(bf16[1,128,512]{2,1,0:T(8,128)(2,1)S(1)} %attend.6.refs_0_, bf16[1,128,512]{2,1,0:T(8,128)(2,1)S(1)} %collective-permute-done.17.refs_1_, bf16[512,4096]{1,0:T(8,128)(2,1)S(1)} %copy-done, bf16[512,4096]{1,0:T(8,128)(2,1)S(1)} %collective-permute-done.16.refs_3_, ...), custom_call_target="tpu_custom_call", output_to_operand_aliasing={{}: (5, {})} | custom-call | flops 200000000 | bytes 1024 | tf_op jit(solution)/shard_map/out_final/pallas_call | solution.py:335
  (39 shorter events, 1.4 us)
Async XLA Ops:
  0.7 7.0 %copy-start.4 = (bf16[512,896]{1,0:T(8,128)(2,1)S(1)}, bf16[512,896]{1,0:T(8,128)(2,1)}, u32[]{:S(2)}) copy-start(bf16[512,896]{1,0:T(8,128)(2,1)} %states_ref.7) | copy-start | bytes 2752516
  0.7 7.0 %copy-start.5 = (bf16[16,32,896]{2,1,0:T(8,128)(2,1)S(1)}, bf16[16,32,896]{2,1,0:T(8,128)(2,1)}, u32[]{:S(2)}) copy-start(bf16[16,32,896]{2,1,0:T(8,128)(2,1)} %refs_3_.4) | copy-start | bytes 2752516
  0.7 8.3 %collective-permute-start.3 = (s32[4,8]{1,0:T(4,128)S(1)}, s32[4,8]{1,0:T(4,128)S(1)}, u32[]{:S(2)}, u32[]{:S(2)}) collective-permute-start(s32[4,8]{1,0:T(4,128)S(1)} %pad_add_fusion.own_ref), channel_id=1, source_target_pairs={{0,12},{4,8},{8,4},{12,0},{1,13},{5,9},{9,5},{13,1},{2,14},{6,10},... | collective-permute-start | bytes 392 | tf_op jit(solution)/shard_map/ppermute | solution.py:378
  5.8 4.5 %collective-permute-start.2 = (s32[4,8]{1,0:T(4,128)S(1)}, s32[4,8]{1,0:T(4,128)S(1)}, u32[]{:S(2)}, u32[]{:S(2)}) collective-permute-start(s32[4,8]{1,0:T(4,128)S(1)} %pad_add_fusion.own_ref), channel_id=1, source_target_pairs={{0,8},{4,12},{8,0},{12,4},{1,9},{5,13},{9,1},{13,5},{2,10},{6,14},... | collective-permute-start | bytes 392 | tf_op jit(solution)/shard_map/ppermute | solution.py:378
  5.8 4.5 %collective-permute-start.1 = (s32[4,8]{1,0:T(4,128)S(1)}, s32[4,8]{1,0:T(4,128)S(1)}, u32[]{:S(2)}, u32[]{:S(2)}) collective-permute-start(s32[4,8]{1,0:T(4,128)S(1)} %pad_add_fusion.own_ref), channel_id=1, source_target_pairs={{0,4},{4,0},{8,12},{12,8},{1,5},{5,1},{9,13},{13,9},{2,6},{6,2},{1... | collective-permute-start | bytes 392 | tf_op jit(solution)/shard_map/ppermute | solution.py:378
  9.0 7.7 %copy-start = (bf16[512,4096]{1,0:T(8,128)(2,1)S(1)}, bf16[512,4096]{1,0:T(8,128)(2,1)}, u32[]{:S(2)}) copy-start(bf16[512,4096]{1,0:T(8,128)(2,1)} %refs_2_.27) | copy-start | bytes 12582916
  11.1 15.5 %collective-permute-start.4 = (bf16[4,32,896]{2,1,0:T(8,128)(2,1)S(1)}, bf16[4,32,896]{2,1,0:T(8,128)(2,1)S(1)}, u32[]{:S(2)}, u32[]{:S(2)}) collective-permute-start(bf16[4,32,896]{2,1,0:T(8,128)(2,1)S(1)} %get-tuple-element.58), channel_id=1, source_target_pairs={{0,8},{4,12},{8,0},{12,4},{1,9},{5,13},{9,1},{13,5},{2,10},{6,14},... | collective-permute-start | bytes 688136 | tf_op jit(solution)/shard_map/ppermute | solution.py:386
  13.2 7.0 %collective-permute-start.5 = (bf16[2,32,896]{2,1,0:T(8,128)(2,1)S(1)}, bf16[2,32,896]{2,1,0:T(8,128)(2,1)S(1)}, u32[]{:S(2)}, u32[]{:S(2)}) collective-permute-start(bf16[2,32,896]{2,1,0:T(8,128)(2,1)S(1)} %get-tuple-element.61), channel_id=1, source_target_pairs={{0,4},{4,0},{8,12},{12,8},{1,5},{5,1},{9,13},{13,9},{2,6},{6,2},{1... | collective-permute-start | bytes 344072 | tf_op jit(solution)/shard_map/ppermute | solution.py:386
  14.3 9.3 %collective-permute-start.6 = (bf16[2,32,896]{2,1,0:T(8,128)(2,1)S(1)}, bf16[2,32,896]{2,1,0:T(8,128)(2,1)S(1)}, u32[]{:S(2)}, u32[]{:S(2)}) collective-permute-start(bf16[2,32,896]{2,1,0:T(8,128)(2,1)S(1)} %get-tuple-element.62), channel_id=1, source_target_pairs={{0,4},{4,0},{8,12},{12,8},{1,5},{5,1},{9,13},{13,9},{2,6},{6,2},{1... | collective-permute-start | bytes 344072 | tf_op jit(solution)/shard_map/ppermute | solution.py:386
  15.2 13.3 %collective-permute-start = (bf16[4,32,896]{2,1,0:T(8,128)(2,1)S(1)}, bf16[4,32,896]{2,1,0:T(8,128)(2,1)S(1)}, u32[]{:S(2)}, u32[]{:S(2)}) collective-permute-start(bf16[4,32,896]{2,1,0:T(8,128)(2,1)S(1)} %encode_local.1), channel_id=1, source_target_pairs={{0,2},{2,0},{1,3},{3,1},{4,6},{6,4},{5,7},{7,5},{8,10},{10,8},{9,1... | collective-permute-start | bytes 688136 | tf_op jit(solution)/shard_map/ppermute | solution.py:363
  16.7 31.3 %collective-permute-start.16 = (bf16[512,4096]{1,0:T(8,128)(2,1)S(1)}, bf16[512,4096]{1,0:T(8,128)(2,1)S(1)}, u32[]{:S(2)}, u32[]{:S(2)}) collective-permute-start(bf16[512,4096]{1,0:T(8,128)(2,1)S(1)} %copy-done), channel_id=1, source_target_pairs={{0,1},{1,0},{2,3},{3,2},{4,5},{5,4},{6,7},{7,6},{8,9},{9,8},{10,11... | collective-permute-start | bytes 12582920 | tf_op jit(solution)/shard_map/ppermute | solution.py:366
  25.1 7.6 %collective-permute-start.8 = (bf16[4,32,896]{2,1,0:T(8,128)(2,1)S(1)}, bf16[4,32,896]{2,1,0:T(8,128)(2,1)S(1)}, u32[]{:S(2)}, u32[]{:S(2)}) collective-permute-start(bf16[4,32,896]{2,1,0:T(8,128)(2,1)S(1)} %encode.3), channel_id=1, source_target_pairs={{0,2},{2,0},{1,3},{3,1},{4,6},{6,4},{5,7},{7,5},{8,10},{10,8},{9,1... | collective-permute-start | bytes 688136 | tf_op jit(solution)/shard_map/ppermute | solution.py:363
  26.6 7.9 %collective-permute-start.11 = (bf16[4,32,896]{2,1,0:T(8,128)(2,1)S(1)}, bf16[4,32,896]{2,1,0:T(8,128)(2,1)S(1)}, u32[]{:S(2)}, u32[]{:S(2)}) collective-permute-start(bf16[4,32,896]{2,1,0:T(8,128)(2,1)S(1)} %get-tuple-element.75), channel_id=1, source_target_pairs={{0,12},{4,8},{8,4},{12,0},{1,13},{5,9},{9,5},{13,1},{2,14},{6,10},... | collective-permute-start | bytes 688136 | tf_op jit(solution)/shard_map/ppermute | solution.py:386
  27.9 8.5 %collective-permute-start.10 = (bf16[4,32,896]{2,1,0:T(8,128)(2,1)S(1)}, bf16[4,32,896]{2,1,0:T(8,128)(2,1)S(1)}, u32[]{:S(2)}, u32[]{:S(2)}) collective-permute-start(bf16[4,32,896]{2,1,0:T(8,128)(2,1)S(1)} %encode.4), channel_id=1, source_target_pairs={{0,2},{2,0},{1,3},{3,1},{4,6},{6,4},{5,7},{7,5},{8,10},{10,8},{9,1... | collective-permute-start | bytes 688136 | tf_op jit(solution)/shard_map/ppermute | solution.py:363
  28.6 8.0 %collective-permute-start.7 = (bf16[2,4,32,896]{3,2,1,0:T(8,128)(2,1)S(1)}, bf16[2,4,32,896]{3,2,1,0:T(8,128)(2,1)S(1)}, u32[]{:S(2)}, u32[]{:S(2)}) collective-permute-start(bf16[2,4,32,896]{3,2,1,0:T(8,128)(2,1)S(1)} %pad_maximum_fusion.refs_0_), channel_id=1, source_target_pairs={{0,1},{1,0},{2,3},{3,2},{4,5},{5,4},{6,7},{7,6},{8,9},{9,8},{10,11... | collective-permute-start | bytes 1376264 | tf_op jit(solution)/shard_map/ppermute | solution.py:366
  32.7 3.8 %copy-start.2 = (bf16[896,512]{1,0:T(8,128)(2,1)S(1)}, bf16[896,512]{1,0:T(8,128)(2,1)}, u32[]{:S(2)}) copy-start(bf16[896,512]{1,0:T(8,128)(2,1)} %refs_5_.1) | copy-start | bytes 2752516
  32.7 3.8 %copy-start.3 = (bf16[896,512]{1,0:T(8,128)(2,1)S(1)}, bf16[896,512]{1,0:T(8,128)(2,1)}, u32[]{:S(2)}) copy-start(bf16[896,512]{1,0:T(8,128)(2,1)} %refs_6_.1) | copy-start | bytes 2752516
  32.7 5.1 %collective-permute-start.9 = (bf16[2,4,32,896]{3,2,1,0:T(8,128)(2,1)S(1)}, bf16[2,4,32,896]{3,2,1,0:T(8,128)(2,1)S(1)}, u32[]{:S(2)}, u32[]{:S(2)}) collective-permute-start(bf16[2,4,32,896]{3,2,1,0:T(8,128)(2,1)S(1)} %pad_maximum_fusion.1.refs_0_), channel_id=1, source_target_pairs={{0,1},{1,0},{2,3},{3,2},{4,5},{5,4},{6,7},{7,6},{8,9},{9,8},{10,11... | collective-permute-start | bytes 1376264 | tf_op jit(solution)/shard_map/ppermute | solution.py:366
  35.8 6.3 %collective-permute-start.13 = (bf16[4,32,896]{2,1,0:T(8,128)(2,1)S(1)}, bf16[4,32,896]{2,1,0:T(8,128)(2,1)S(1)}, u32[]{:S(2)}, u32[]{:S(2)}) collective-permute-start(bf16[4,32,896]{2,1,0:T(8,128)(2,1)S(1)} %encode.5), channel_id=1, source_target_pairs={{0,2},{2,0},{1,3},{3,1},{4,6},{6,4},{5,7},{7,5},{8,10},{10,8},{9,1... | collective-permute-start | bytes 688136 | tf_op jit(solution)/shard_map/ppermute | solution.py:363
  36.5 2.7 %collective-permute-start.12 = (bf16[2,4,32,896]{3,2,1,0:T(8,128)(2,1)S(1)}, bf16[2,4,32,896]{3,2,1,0:T(8,128)(2,1)S(1)}, u32[]{:S(2)}, u32[]{:S(2)}) collective-permute-start(bf16[2,4,32,896]{3,2,1,0:T(8,128)(2,1)S(1)} %pad_maximum_fusion.2.refs_0_), channel_id=1, source_target_pairs={{0,1},{1,0},{2,3},{3,2},{4,5},{5,4},{6,7},{7,6},{8,9},{9,8},{10,11... | collective-permute-start | bytes 1376264 | tf_op jit(solution)/shard_map/ppermute | solution.py:366
  42.2 1.9 %copy-start.1 = (bf16[512,512]{1,0:T(8,128)(2,1)S(1)}, bf16[512,512]{1,0:T(8,128)(2,1)}, u32[]{:S(2)}) copy-start(bf16[512,512]{1,0:T(8,128)(2,1)} %q_ref.5) | copy-start | bytes 1572868
  42.2 1.9 %collective-permute-start.14 = (bf16[2,4,32,896]{3,2,1,0:T(8,128)(2,1)S(1)}, bf16[2,4,32,896]{3,2,1,0:T(8,128)(2,1)S(1)}, u32[]{:S(2)}, u32[]{:S(2)}) collective-permute-start(bf16[2,4,32,896]{3,2,1,0:T(8,128)(2,1)S(1)} %pad_maximum_fusion.3.refs_0_), channel_id=1, source_target_pairs={{0,1},{1,0},{2,3},{3,2},{4,5},{5,4},{6,7},{7,6},{8,9},{9,8},{10,11... | collective-permute-start | bytes 1376264 | tf_op jit(solution)/shard_map/ppermute | solution.py:366
  46.3 1.7 %collective-permute-start.15 = (bf16[1,128,512]{2,1,0:T(8,128)(2,1)S(1)}, bf16[1,128,512]{2,1,0:T(8,128)(2,1)S(1)}, u32[]{:S(2)}, u32[]{:S(2)}) collective-permute-start(bf16[1,128,512]{2,1,0:T(8,128)(2,1)S(1)} %get-tuple-element.84), channel_id=1, source_target_pairs={{0,1},{1,0},{2,3},{3,2},{4,5},{5,4},{6,7},{7,6},{8,9},{9,8},{10,11... | collective-permute-start | bytes 393224 | tf_op jit(solution)/shard_map/ppermute | solution.py:420
  49.1 11.1 %collective-permute-start.22 = (bf16[128,1024]{1,0:T(8,128)(2,1)S(1)}, bf16[128,1024]{1,0:T(8,128)(2,1)S(1)}, u32[]{:S(2)}, u32[]{:S(2)}) collective-permute-start(bf16[128,1024]{1,0:T(8,128)(2,1)S(1)} %out_project.5), channel_id=1, source_target_pairs={{0,2},{2,0},{1,3},{3,1},{4,6},{6,4},{5,7},{7,5},{8,10},{10,8},{9,1... | collective-permute-start | bytes 786440 | tf_op jit(solution)/shard_map/ppermute | solution.py:437
  50.5 13.3 %collective-permute-start.21 = (bf16[128,1024]{1,0:T(8,128)(2,1)S(1)}, bf16[128,1024]{1,0:T(8,128)(2,1)S(1)}, u32[]{:S(2)}, u32[]{:S(2)}) collective-permute-start(bf16[128,1024]{1,0:T(8,128)(2,1)S(1)} %out_project.6), channel_id=1, source_target_pairs={{0,2},{2,0},{1,3},{3,1},{4,6},{6,4},{5,7},{7,5},{8,10},{10,8},{9,1... | collective-permute-start | bytes 786440 | tf_op jit(solution)/shard_map/ppermute | solution.py:437
  53.0 16.5 %collective-permute-start.20 = (bf16[128,1024]{1,0:T(8,128)(2,1)S(1)}, bf16[128,1024]{1,0:T(8,128)(2,1)S(1)}, u32[]{:S(2)}, u32[]{:S(2)}) collective-permute-start(bf16[128,1024]{1,0:T(8,128)(2,1)S(1)} %out_project.7), channel_id=1, source_target_pairs={{0,2},{2,0},{1,3},{3,1},{4,6},{6,4},{5,7},{7,5},{8,10},{10,8},{9,1... | collective-permute-start | bytes 786440 | tf_op jit(solution)/shard_map/ppermute | solution.py:437
  55.7 1.6 %collective-permute-start.17 = (bf16[1,128,512]{2,1,0:T(8,128)(2,1)S(1)}, bf16[1,128,512]{2,1,0:T(8,128)(2,1)S(1)}, u32[]{:S(2)}, u32[]{:S(2)}) collective-permute-start(bf16[1,128,512]{2,1,0:T(8,128)(2,1)S(1)} %attend.7), channel_id=1, source_target_pairs={{0,1},{1,0},{2,3},{3,2},{4,5},{5,4},{6,7},{7,6},{8,9},{9,8},{10,11... | collective-permute-start | bytes 393224 | tf_op jit(solution)/shard_map/ppermute | solution.py:420
  55.8 16.5 %collective-permute-start.19 = (bf16[128,512]{1,0:T(8,128)(2,1)S(1)}, bf16[128,512]{1,0:T(8,128)(2,1)S(1)}, u32[]{:S(2)}, u32[]{:S(2)}) collective-permute-start(bf16[128,512]{1,0:T(8,128)(2,1)S(1)} %out_project.8), channel_id=1, source_target_pairs={{0,2},{2,0},{1,3},{3,1},{4,6},{6,4},{5,7},{7,5},{8,10},{10,8},{9,1... | collective-permute-start | bytes 393224 | tf_op jit(solution)/shard_map/ppermute | solution.py:437
  57.3 17.2 %collective-permute-start.18 = (bf16[128,512]{1,0:T(8,128)(2,1)S(1)}, bf16[128,512]{1,0:T(8,128)(2,1)S(1)}, u32[]{:S(2)}, u32[]{:S(2)}) collective-permute-start(bf16[128,512]{1,0:T(8,128)(2,1)S(1)} %out_project.9), channel_id=1, source_target_pairs={{0,2},{2,0},{1,3},{3,1},{4,6},{6,4},{5,7},{7,5},{8,10},{10,8},{9,1... | collective-permute-start | bytes 393224 | tf_op jit(solution)/shard_map/ppermute | solution.py:437

commit v11 on v10

--- a/solution.py
+++ b/solution.py
@@ -11,9 +11,10 @@
 ENCODER_HEAD_DIM = 128
 F32 = jnp.float32
 BF16 = jnp.bfloat16
-LATER_GROUPS = 2
 COL_TILE = 512
-ENCODE_COST = (None, 0.1, 10, 10)
+ENCODE_COST = (None, 0.1, 0.1, 10, 10, 10)
+SEND_AFTER = (None, 1, 3)
+STACK_AFTER = {3: ((0,), (1, 2)), 4: ((3,),)}
 
 VMEM = pl.BlockSpec(memory_space=pltpu.VMEM)
 SMEM = pl.BlockSpec(memory_space=pltpu.SMEM)
@@ -368,11 +369,11 @@
     order = list(range(n_lanes))
     items = []
     for d in order[1:]:
-        cuts = (0, cap // 2, cap) if d == 1 else (0, cap)
+        cuts = (0, cap // 2, cap) if d in (1, n_lanes - 1) else (0, cap)
         items += [(d, low, high) for low, high in zip(cuts, cuts[1:])]
-    size = max(1, -(-(len(items) - 2) // LATER_GROUPS))
-    cuts = [0] + list(range(2, len(items), size)) + [len(items)]
-    parts = [range(low, high) for low, high in zip(cuts, cuts[1:])]
+    middle = range(2, max(2, len(items) - 2))
+    parts = [part for part in (range(0, 1), range(1, 2), middle, *(range(i, i + 1) for i in range(len(items))[-2:])) if part]
+    groups = ((1, 2), (3,), (4, 5))
 
     own = jnp.concatenate([owners.T, entry_ids.T], axis=0)
     asked = [lax.ppermute(own, "lanes", lane_pairs(n_lanes, d, False)) for d in range(1, n_lanes)]
@@ -387,27 +388,31 @@
             for block, i in zip(ready, part)
         ]
 
+    def stack(members, *earlier):
+        ready = after([crossed[i] for i in members], *earlier)
+        return jnp.stack([jnp.concatenate(piece, axis=0) for piece in zip(*ready)])
+
     crossed, pieces = [over_heads(encoded)], []
-    arrived = [None] + [send(part) for part in parts[:2]]
+    arrived = [None] + [send(part) for part in parts[:3]]
     last = blocks
     for i, part in enumerate(parts, 1):
-        if i + 2 <= len(parts):
-            arrived.append(send(parts[i + 1], arrived[i], last))
+        if i + 3 <= len(parts):
+            arrived.append(send(parts[i + 2], arrived[SEND_AFTER[i]], last))
         first = items[part[0]][0] * cap + items[part[0]][1]
         encoded = encode(
             req, span_states, after(arrived[i], last), first, fanout, span_len, ENCODE_COST[i]
         )
         crossed.append(over_heads(encoded))
         last = encoded
-        while i > 1 and len(pieces) < i:
-            last = jnp.stack(after(crossed[len(pieces)], last))
+        for members in STACK_AFTER.get(i, ()):
+            last = stack(members, last)
             pieces.append(over_rep(last))
     w_outs = over_rep(w_out)
     kvs, last = [], after(last, w_outs)
     while len(kvs) < len(pieces):
         last = project(after(pieces[len(kvs)], last), w_key, w_value)
         kvs.append(last)
-    pieces = over_rep(jnp.stack(after(crossed[-1], kvs)))
+    pieces = over_rep(stack(groups[-1], kvs))
     own_kv, rest = project(pieces[:1], w_key, w_value), pieces[1:]
 
     def mix(turns, q, rest):

time: 75.7 us -> 77.1 us (1.018)
  waiting for transfers between devices: 25.7 us -> 17.8 us
  starting transfers between devices: 20.3 us -> 27.9 us
  Pallas kernels: 28.3 us -> 29.8 us
    ppermute x4 -> x6, waiting for transfers between devices: 5.78 us -> 0.97 us  [over_heads(): lax.ppermute(array, 'heads', shift_pairs(n_heads, s))]
    ppermute x4 -> x5, starting transfers between devices: 4.12 us -> 8 us  [send(): lax.ppermute(block, 'lanes', lane_pairs(n_lanes, items[i][0], True))]
    ppermute x4 -> x6, starting transfers between devices: 4.25 us -> 7.58 us  [over_heads(): lax.ppermute(array, 'heads', shift_pairs(n_heads, s))]
    ppermute x4 -> x5, waiting for transfers between devices: 8.6 us -> 5.47 us  [send(): lax.ppermute(block, 'lanes', lane_pairs(n_lanes, items[i][0], True))]
    pallas_call x3 -> x5, Pallas kernels: 3.97 us -> 5.52 us  [encode(): pl.pallas_call(functools.partial(encode_kernel, first, fanout, span_len),...]
  transfers between devices with their start and end apart: 23 -> 26, of which waited for: 11 -> 9; matrix products, arithmetic and copies ran while one was open for 0% -> 0% of each run, Pallas kernels for 34% -> 35%
where the time goes in v11:
time: 77.1 us; the launch traced here: 77 us
  Pallas kernels  29.8 us (39%)
  starting transfers between devices  27.9 us (36%)
  waiting for transfers between devices  17.8 us (23%)
  other arithmetic  1.01 us (1%)
    pallas_call x10, Pallas kernels, out_project(): pl.pallas_call(functools.partial(out_kernel, n, len(received)), grid=((st...  9.81 us
    ppermute x5, waiting for transfers between devices, shards(): received[i].append(lax.ppermute(partial, 'heads', shift_pairs(n_heads, t)))  8.97 us
    ppermute x5, starting transfers between devices, send(): lax.ppermute(block, 'lanes', lane_pairs(n_lanes, items[i][0], True))  8 us
    ppermute x6, starting transfers between devices, over_heads(): lax.ppermute(array, 'heads', shift_pairs(n_heads, s))  7.58 us
    pallas_call x4, Pallas kernels, attend(): pl.pallas_call(functools.partial(attend_kernel, firsts, n_heads, n_rep, t...  6.7 us
    ppermute x3, starting transfers between devices, shards(): lax.ppermute(own, 'lanes', lane_pairs(n_lanes, d, False))  5.76 us
    ppermute x5, starting transfers between devices, shards(): received[i].append(lax.ppermute(partial, 'heads', shift_pairs(n_heads, t)))  5.59 us
    pallas_call x5, Pallas kernels, encode(): pl.pallas_call(functools.partial(encode_kernel, first, fanout, span_len),...  5.52 us
  transfers between devices with their start and end apart: 26, of which 9 were waited for; matrix products, arithmetic and copies ran while one was open for 0% of the time, Pallas kernels for 35%

profile of v11, /device:TPU:0, one launch (start us, length us, event | category | flops | bytes accessed | tf_op | source)
XLA Modules:
  0.0 77.0 jit_solution(16839646324403331242)
XLA Ops:
  0.7 5.1 %collective-permute-start.3 = (s32[4,8]{1,0:T(4,128)S(1)}, s32[4,8]{1,0:T(4,128)S(1)}, u32[]{:S(2)}, u32[]{:S(2)}) collective-permute-start(s32[4,8]{1,0:T(4,128)S(1)} %pad_add_fusion.own_ref), channel_id=1, source_target_pairs={{0,12},{4,8},{8,4},{12,0},{1,13},{5,9},{9,5},{13,1},{2,14},{6,10},... | collective-permute-start | bytes 392 | tf_op jit(solution)/shard_map/ppermute | solution.py:379
  6.5 1.3 %plan.1 = (s32[16]{0:T(128)S(1)}, s32[16]{0:T(128)S(1)}, s32[16]{0:T(128)S(1)}) custom-call(s32[4,8]{1,0:T(4,128)S(1)} %pad_add_fusion.own_ref), custom_call_target="tpu_custom_call" | custom-call | flops 10000000000 | bytes 1024 | tf_op jit(solution)/shard_map/plan/pallas_call | solution.py:77
  7.8 1.3 %encode_local.1 = bf16[4,32,896]{2,1,0:T(8,128)(2,1)S(1)} custom-call(s32[16]{0:T(128)S(1)} %get-tuple-element.58.req_ref, s32[16]{0:T(128)S(1)} %get-tuple-element.59.pick_ref, bf16[512,896]{1,0:T(8,128)(2,1)S(1)} %copy-done.2, bf16[16,32,896]{2,1,0:T(8,128)(2,1)S(1)} %copy-done.5), custom_call_target="tpu_custom_call" | custom-call | flops 10000000000 | bytes 1024 | tf_op jit(solution)/shard_map/encode_local/pallas_call | solution.py:206
  9.1 1.3 %collective-permute-done.2.refs_1_ = s32[4,8]{1,0:T(4,128)S(1)} collective-permute-done((s32[4,8]{1,0:T(4,128)S(1)}, s32[4,8]{1,0:T(4,128)S(1)}, u32[]{:S(2)}, u32[]{:S(2)}) %collective-permute-start.2) | collective-permute-done | bytes 160 | tf_op jit(solution)/shard_map/ppermute | solution.py:379
  10.3 0.8 %fetch.1 = (bf16[2,32,896]{2,1,0:T(8,128)(2,1)S(1)}, bf16[2,32,896]{2,1,0:T(8,128)(2,1)S(1)}, bf16[4,32,896]{2,1,0:T(8,128)(2,1)S(1)}, bf16[2,32,896]{2,1,0:T(8,128)(2,1)S(1)}, bf16[2,32,896]{2,1,0:T(8,128)(2,1)S(1)}) custom-call(s32[4,8]{1,0:T(4,128)S(1)} %collective-permute-done.1.refs_0_, s32[4,8]{1,0:T(4,128)S(1)} %collective-permute-done.2.refs_1_, ...), custom_call_target="tpu_custom_call" | custom-call | flops 10000000000 | bytes 1024 | tf_op jit(solution)/shard_map/fetch/pallas_call | solution.py:110
  11.1 2.1 %collective-permute-start.4 = (bf16[4,32,896]{2,1,0:T(8,128)(2,1)S(1)}, bf16[4,32,896]{2,1,0:T(8,128)(2,1)S(1)}, u32[]{:S(2)}, u32[]{:S(2)}) collective-permute-start(bf16[4,32,896]{2,1,0:T(8,128)(2,1)S(1)} %get-tuple-element.63), channel_id=1, source_target_pairs={{0,8},{4,12},{8,0},{12,4},{1,9},{5,13},{9,1},{13,5},{2,10},{6,14},... | collective-permute-start | bytes 688136 | tf_op jit(solution)/shard_map/ppermute | solution.py:387
  13.2 1.0 %collective-permute-start.6 = (bf16[2,32,896]{2,1,0:T(8,128)(2,1)S(1)}, bf16[2,32,896]{2,1,0:T(8,128)(2,1)S(1)}, u32[]{:S(2)}, u32[]{:S(2)}) collective-permute-start(bf16[2,32,896]{2,1,0:T(8,128)(2,1)S(1)} %get-tuple-element.65), channel_id=1, source_target_pairs={{0,4},{4,0},{8,12},{12,8},{1,5},{5,1},{9,13},{13,9},{2,6},{6,2},{1... | collective-permute-start | bytes 344072 | tf_op jit(solution)/shard_map/ppermute | solution.py:387
  14.3 1.0 %collective-permute-start.5 = (bf16[2,32,896]{2,1,0:T(8,128)(2,1)S(1)}, bf16[2,32,896]{2,1,0:T(8,128)(2,1)S(1)}, u32[]{:S(2)}, u32[]{:S(2)}) collective-permute-start(bf16[2,32,896]{2,1,0:T(8,128)(2,1)S(1)} %get-tuple-element.64), channel_id=1, source_target_pairs={{0,4},{4,0},{8,12},{12,8},{1,5},{5,1},{9,13},{13,9},{2,6},{6,2},{1... | collective-permute-start | bytes 344072 | tf_op jit(solution)/shard_map/ppermute | solution.py:387
  15.2 1.5 %collective-permute-start = (bf16[4,32,896]{2,1,0:T(8,128)(2,1)S(1)}, bf16[4,32,896]{2,1,0:T(8,128)(2,1)S(1)}, u32[]{:S(2)}, u32[]{:S(2)}) collective-permute-start(bf16[4,32,896]{2,1,0:T(8,128)(2,1)S(1)} %encode_local.1), channel_id=1, source_target_pairs={{0,2},{2,0},{1,3},{3,1},{4,6},{6,4},{5,7},{7,5},{8,10},{10,8},{9,1... | collective-permute-start | bytes 688136 | tf_op jit(solution)/shard_map/ppermute | solution.py:364
  16.7 3.5 %collective-permute-done.6.refs_0_ = bf16[2,32,896]{2,1,0:T(8,128)(2,1)S(1)} collective-permute-done((bf16[2,32,896]{2,1,0:T(8,128)(2,1)S(1)}, bf16[2,32,896]{2,1,0:T(8,128)(2,1)S(1)}, u32[]{:S(2)}, u32[]{:S(2)}) %collective-permute-start.6) | collective-permute-done | bytes 114720 | tf_op jit(solution)/shard_map/ppermute | solution.py:387
  20.3 1.1 %encode.5 = bf16[2,32,896]{2,1,0:T(8,128)(2,1)S(1)} custom-call(s32[16]{0:T(128)S(1)} %get-tuple-element.58.req_ref, bf16[512,896]{1,0:T(8,128)(2,1)S(1)} %copy-done.2, bf16[2,32,896]{2,1,0:T(8,128)(2,1)S(1)} %collective-permute-done.6.refs_0_), custom_call_target="tpu_custom_call" | custom-call | flops 100000000 | bytes 1024 | tf_op jit(solution)/shard_map/encode/pallas_call | solution.py:187
  21.3 1.6 %collective-permute-start.8 = (bf16[2,32,896]{2,1,0:T(8,128)(2,1)S(1)}, bf16[2,32,896]{2,1,0:T(8,128)(2,1)S(1)}, u32[]{:S(2)}, u32[]{:S(2)}) collective-permute-start(bf16[2,32,896]{2,1,0:T(8,128)(2,1)S(1)} %encode.5), channel_id=1, source_target_pairs={{0,2},{2,0},{1,3},{3,1},{4,6},{6,4},{5,7},{7,5},{8,10},{10,8},{9,1... | collective-permute-start | bytes 344072 | tf_op jit(solution)/shard_map/ppermute | solution.py:364
  22.9 1.9 %collective-permute-done.5.refs_0_ = bf16[2,32,896]{2,1,0:T(8,128)(2,1)S(1)} collective-permute-done((bf16[2,32,896]{2,1,0:T(8,128)(2,1)S(1)}, bf16[2,32,896]{2,1,0:T(8,128)(2,1)S(1)}, u32[]{:S(2)}, u32[]{:S(2)}) %collective-permute-start.5) | collective-permute-done | bytes 114720 | tf_op jit(solution)/shard_map/ppermute | solution.py:387
  24.8 1.1 %encode.6 = bf16[2,32,896]{2,1,0:T(8,128)(2,1)S(1)} custom-call(s32[16]{0:T(128)S(1)} %get-tuple-element.58.req_ref, bf16[512,896]{1,0:T(8,128)(2,1)S(1)} %copy-done.2, bf16[2,32,896]{2,1,0:T(8,128)(2,1)S(1)} %collective-permute-done.5.refs_0_), custom_call_target="tpu_custom_call" | custom-call | flops 100000000 | bytes 1024 | tf_op jit(solution)/shard_map/encode/pallas_call | solution.py:187
  25.9 1.6 %collective-permute-start.9 = (bf16[2,32,896]{2,1,0:T(8,128)(2,1)S(1)}, bf16[2,32,896]{2,1,0:T(8,128)(2,1)S(1)}, u32[]{:S(2)}, u32[]{:S(2)}) collective-permute-start(bf16[2,32,896]{2,1,0:T(8,128)(2,1)S(1)} %encode.6), channel_id=1, source_target_pairs={{0,2},{2,0},{1,3},{3,1},{4,6},{6,4},{5,7},{7,5},{8,10},{10,8},{9,1... | collective-permute-start | bytes 344072 | tf_op jit(solution)/shard_map/ppermute | solution.py:364
  27.5 1.3 %encode.7 = bf16[4,32,896]{2,1,0:T(8,128)(2,1)S(1)} custom-call(s32[16]{0:T(128)S(1)} %get-tuple-element.58.req_ref, bf16[512,896]{1,0:T(8,128)(2,1)S(1)} %copy-done.2, bf16[4,32,896]{2,1,0:T(8,128)(2,1)S(1)} %collective-permute-done.4.refs_0_), custom_call_target="tpu_custom_call" | custom-call | flops 10000000000 | bytes 1024 | tf_op jit(solution)/shard_map/encode/pallas_call | solution.py:187
  29.4 3.9 %collective-permute-start.15 = (bf16[2,32,896]{2,1,0:T(8,128)(2,1)S(1)}, bf16[2,32,896]{2,1,0:T(8,128)(2,1)S(1)}, u32[]{:S(2)}, u32[]{:S(2)}) collective-permute-start(bf16[2,32,896]{2,1,0:T(8,128)(2,1)S(1)} %get-tuple-element.87), channel_id=1, source_target_pairs={{0,12},{4,8},{8,4},{12,0},{1,13},{5,9},{9,5},{13,1},{2,14},{6,10},... | collective-permute-start | bytes 344072 | tf_op jit(solution)/shard_map/ppermute | solution.py:387
  34.0 1.1 %encode.8 = bf16[2,32,896]{2,1,0:T(8,128)(2,1)S(1)} custom-call(s32[16]{0:T(128)S(1)} %get-tuple-element.58.req_ref, bf16[512,896]{1,0:T(8,128)(2,1)S(1)} %copy-done.2, bf16[2,32,896]{2,1,0:T(8,128)(2,1)S(1)} %collective-permute-done.12.refs_0_), custom_call_target="tpu_custom_call" | custom-call | flops 10000000000 | bytes 1024 | tf_op jit(solution)/shard_map/encode/pallas_call | solution.py:187
  35.1 1.6 %collective-permute-start.14 = (bf16[2,32,896]{2,1,0:T(8,128)(2,1)S(1)}, bf16[2,32,896]{2,1,0:T(8,128)(2,1)S(1)}, u32[]{:S(2)}, u32[]{:S(2)}) collective-permute-start(bf16[2,32,896]{2,1,0:T(8,128)(2,1)S(1)} %encode.8), channel_id=1, source_target_pairs={{0,2},{2,0},{1,3},{3,1},{4,6},{6,4},{5,7},{7,5},{8,10},{10,8},{9,1... | collective-permute-start | bytes 344072 | tf_op jit(solution)/shard_map/ppermute | solution.py:364
  36.8 1.1 %encode.9 = bf16[2,32,896]{2,1,0:T(8,128)(2,1)S(1)} custom-call(s32[16]{0:T(128)S(1)} %get-tuple-element.58.req_ref, bf16[512,896]{1,0:T(8,128)(2,1)S(1)} %copy-done.2, bf16[2,32,896]{2,1,0:T(8,128)(2,1)S(1)} %collective-permute-done.15.refs_0_), custom_call_target="tpu_custom_call" | custom-call | flops 10000000000 | bytes 1024 | tf_op jit(solution)/shard_map/encode/pallas_call | solution.py:187
  37.9 0.8 %collective-permute-start.16 = (bf16[2,32,896]{2,1,0:T(8,128)(2,1)S(1)}, bf16[2,32,896]{2,1,0:T(8,128)(2,1)S(1)}, u32[]{:S(2)}, u32[]{:S(2)}) collective-permute-start(bf16[2,32,896]{2,1,0:T(8,128)(2,1)S(1)} %encode.9), channel_id=1, source_target_pairs={{0,2},{2,0},{1,3},{3,1},{4,6},{6,4},{5,7},{7,5},{8,10},{10,8},{9,1... | collective-permute-start | bytes 344072 | tf_op jit(solution)/shard_map/ppermute | solution.py:364
  38.7 1.3 %project.4.refs_0_ = bf16[4,4,32,1024]{3,2,1,0:T(8,128)(2,1)S(1)} custom-call(bf16[2,4,32,896]{3,2,1,0:T(8,128)(2,1)S(1)} %pad_maximum_fusion.refs_0_, bf16[2,4,32,896]{3,2,1,0:T(8,128)(2,1)S(1)} %collective-permute-done.7.refs_1_, bf16[896,512]{1,0:T(8,128)(2,1)S(1)} %copy-done.3, bf16[896,512]{1,0:T(8,128)(2,1)S(1)} %copy-done.4), custom_call_target="tpu_custom_call" | custom-call | flops 10000000000 | bytes 1024 | tf_op jit(solution)/shard_map/project/pallas_call | solution.py:239
  40.0 1.3 %project.5.refs_1_ = bf16[4,4,32,1024]{3,2,1,0:T(8,128)(2,1)S(1)} custom-call(bf16[2,4,32,896]{3,2,1,0:T(8,128)(2,1)S(1)} %pad_maximum_fusion.1.refs_0_, bf16[2,4,32,896]{3,2,1,0:T(8,128)(2,1)S(1)} %collective-permute-done.10.refs_1_, bf16[896,512]{1,0:T(8,128)(2,1)S(1)} %copy-done.3, bf16[896,512]{1,0:T(8,128)(2,1)S(1)} %copy-done.4), custom_call_target="tpu_custom_call" | custom-call | flops 10000000000 | bytes 1024 | tf_op jit(solution)/shard_map/project/pallas_call | solution.py:239
  41.3 1.3 %project.6.refs_2_ = bf16[4,4,32,1024]{3,2,1,0:T(8,128)(2,1)S(1)} custom-call(bf16[2,4,32,896]{3,2,1,0:T(8,128)(2,1)S(1)} %pad_maximum_fusion.2.refs_0_, bf16[2,4,32,896]{3,2,1,0:T(8,128)(2,1)S(1)} %collective-permute-done.13.refs_1_, bf16[896,512]{1,0:T(8,128)(2,1)S(1)} %copy-done.3, bf16[896,512]{1,0:T(8,128)(2,1)S(1)} %copy-done.4), custom_call_target="tpu_custom_call" | custom-call | flops 10000000000 | bytes 1024 | tf_op jit(solution)/shard_map/project/pallas_call | solution.py:239
  42.6 1.0 %collective-permute-done.16 = bf16[2,32,896]{2,1,0:T(8,128)(2,1)S(1)} collective-permute-done((bf16[2,32,896]{2,1,0:T(8,128)(2,1)S(1)}, bf16[2,32,896]{2,1,0:T(8,128)(2,1)S(1)}, u32[]{:S(2)}, u32[]{:S(2)}) %collective-permute-start.16) | collective-permute-done | bytes 114720 | tf_op jit(solution)/shard_map/ppermute | solution.py:364
  43.7 0.7 project.7.refs_3_
  44.4 1.1 %collective-permute-done.17.refs_4_ = bf16[2,4,32,896]{3,2,1,0:T(8,128)(2,1)S(1)} collective-permute-done((bf16[2,4,32,896]{3,2,1,0:T(8,128)(2,1)S(1)}, bf16[2,4,32,896]{3,2,1,0:T(8,128)(2,1)S(1)}, u32[]{:S(2)}, u32[]{:S(2)}) %collective-permute-start.17) | collective-permute-done | bytes 458784 | tf_op jit(solution)/shard_map/ppermute | solution.py:367
  45.5 2.2 %attend.4 = (bf16[1,128,512]{2,1,0:T(8,128)(2,1)S(1)}, bf16[4,2,32,1024]{3,2,1,0:T(8,128)(2,1)S(1)}) custom-call(s32[16]{0:T(128)S(1)} %get-tuple-element.57.slot_ref, bf16[512,512]{1,0:T(8,128)(2,1)S(1)} %copy-done.1, bf16[4,4,32,1024]{3,2,1,0:T(8,128)(2,1)S(1)} %project.4.refs_0_, bf16[4,4,32,1024]{3,2,1,0:T(8,128)(2,1)S(1)} %project.5.refs_1_, ...), custom_call_target="tpu_custom_call" | custom-call | flops 1000000 | bytes 1024 | tf_op jit(solution)/shard_map/attend/pallas_call | solution.py:309
  47.9 1.5 %attend.5.refs_0_ = bf16[1,128,512]{2,1,0:T(8,128)(2,1)S(1)} custom-call(s32[16]{0:T(128)S(1)} %get-tuple-element.57.slot_ref, bf16[512,512]{1,0:T(8,128)(2,1)S(1)} %copy-done.1, bf16[4,4,32,1024]{3,2,1,0:T(8,128)(2,1)S(1)} %project.4.refs_0_, bf16[4,4,32,1024]{3,2,1,0:T(8,128)(2,1)S(1)} %project.5.refs_1_, bf16[4,4,32,1024]{3,2,1,0:T(8,128)(2,1)S(1)} %project.6.refs_2_, ...), custom_call_target="tpu_custom_call" | custom-call | flops 1000000 | bytes 1024 | tf_op jit(solution)/shard_map/attend/pallas_call | solution.py:309
  49.4 1.0 %out_project.5 = bf16[128,1024]{1,0:T(8,128)(2,1)S(1)} custom-call(bf16[1,128,512]{2,1,0:T(8,128)(2,1)S(1)} %attend.5.refs_0_, bf16[1,128,512]{2,1,0:T(8,128)(2,1)S(1)} %collective-permute-done.18.refs_1_, bf16[512,4096]{1,0:T(8,128)(2,1)S(1)} %copy-done, bf16[512,4096]{1,0:T(8,128)(2,1)S(1)} %collective-permute-done.19.refs_3_), custom_call_target="tpu_custom_call" | custom-call | flops 1000000 | bytes 1024 | tf_op jit(solution)/shard_map/out_project/pallas_call | solution.py:336
  50.5 0.8 %collective-permute-start.25 = (bf16[128,1024]{1,0:T(8,128)(2,1)S(1)}, bf16[128,1024]{1,0:T(8,128)(2,1)S(1)}, u32[]{:S(2)}, u32[]{:S(2)}) collective-permute-start(bf16[128,1024]{1,0:T(8,128)(2,1)S(1)} %out_project.5), channel_id=1, source_target_pairs={{0,2},{2,0},{1,3},{3,1},{4,6},{6,4},{5,7},{7,5},{8,10},{10,8},{9,1... | collective-permute-start | bytes 786440 | tf_op jit(solution)/shard_map/ppermute | solution.py:442
  51.3 0.9 %out_project.6 = bf16[128,1024]{1,0:T(8,128)(2,1)S(1)} custom-call(bf16[1,128,512]{2,1,0:T(8,128)(2,1)S(1)} %attend.5.refs_0_, bf16[1,128,512]{2,1,0:T(8,128)(2,1)S(1)} %collective-permute-done.18.refs_1_, bf16[512,4096]{1,0:T(8,128)(2,1)S(1)} %copy-done, bf16[512,4096]{1,0:T(8,128)(2,1)S(1)} %collective-permute-done.19.refs_3_), custom_call_target="tpu_custom_call" | custom-call | flops 1000000 | bytes 1024 | tf_op jit(solution)/shard_map/out_project/pallas_call | solution.py:336
  52.2 1.3 %collective-permute-start.24 = (bf16[128,1024]{1,0:T(8,128)(2,1)S(1)}, bf16[128,1024]{1,0:T(8,128)(2,1)S(1)}, u32[]{:S(2)}, u32[]{:S(2)}) collective-permute-start(bf16[128,1024]{1,0:T(8,128)(2,1)S(1)} %out_project.6), channel_id=1, source_target_pairs={{0,2},{2,0},{1,3},{3,1},{4,6},{6,4},{5,7},{7,5},{8,10},{10,8},{9,1... | collective-permute-start | bytes 786440 | tf_op jit(solution)/shard_map/ppermute | solution.py:442
  53.5 0.9 %out_project.7 = bf16[128,1024]{1,0:T(8,128)(2,1)S(1)} custom-call(bf16[1,128,512]{2,1,0:T(8,128)(2,1)S(1)} %attend.5.refs_0_, bf16[1,128,512]{2,1,0:T(8,128)(2,1)S(1)} %collective-permute-done.18.refs_1_, bf16[512,4096]{1,0:T(8,128)(2,1)S(1)} %copy-done, bf16[512,4096]{1,0:T(8,128)(2,1)S(1)} %collective-permute-done.19.refs_3_), custom_call_target="tpu_custom_call" | custom-call | flops 1000000 | bytes 1024 | tf_op jit(solution)/shard_map/out_project/pallas_call | solution.py:336
  54.4 0.8 %collective-permute-start.23 = (bf16[128,1024]{1,0:T(8,128)(2,1)S(1)}, bf16[128,1024]{1,0:T(8,128)(2,1)S(1)}, u32[]{:S(2)}, u32[]{:S(2)}) collective-permute-start(bf16[128,1024]{1,0:T(8,128)(2,1)S(1)} %out_project.7), channel_id=1, source_target_pairs={{0,2},{2,0},{1,3},{3,1},{4,6},{6,4},{5,7},{7,5},{8,10},{10,8},{9,1... | collective-permute-start | bytes 786440 | tf_op jit(solution)/shard_map/ppermute | solution.py:442
  55.9 1.5 %attend.7 = bf16[1,128,512]{2,1,0:T(8,128)(2,1)S(1)} custom-call(s32[16]{0:T(128)S(1)} %get-tuple-element.57.slot_ref, bf16[512,512]{1,0:T(8,128)(2,1)S(1)} %copy-done.1, bf16[4,4,32,1024]{3,2,1,0:T(8,128)(2,1)S(1)} %project.4.refs_0_, bf16[4,4,32,1024]{3,2,1,0:T(8,128)(2,1)S(1)} %project.5.refs_1_, bf16[4,4,32,1024]{3,2,1,0:T(8,128)(2,1)S(1)} %project.6.refs_2_, ...), custom_call_target="tpu_custom_call" | custom-call | flops 1000000 | bytes 1024 | tf_op jit(solution)/shard_map/attend/pallas_call | solution.py:309
  57.4 1.3 %collective-permute-start.22 = (bf16[128,512]{1,0:T(8,128)(2,1)S(1)}, bf16[128,512]{1,0:T(8,128)(2,1)S(1)}, u32[]{:S(2)}, u32[]{:S(2)}) collective-permute-start(bf16[128,512]{1,0:T(8,128)(2,1)S(1)} %out_project.8), channel_id=1, source_target_pairs={{0,2},{2,0},{1,3},{3,1},{4,6},{6,4},{5,7},{7,5},{8,10},{10,8},{9,1... | collective-permute-start | bytes 393224 | tf_op jit(solution)/shard_map/ppermute | solution.py:442
  58.8 1.3 %collective-permute-start.21 = (bf16[128,512]{1,0:T(8,128)(2,1)S(1)}, bf16[128,512]{1,0:T(8,128)(2,1)S(1)}, u32[]{:S(2)}, u32[]{:S(2)}) collective-permute-start(bf16[128,512]{1,0:T(8,128)(2,1)S(1)} %out_project.9), channel_id=1, source_target_pairs={{0,2},{2,0},{1,3},{3,1},{4,6},{6,4},{5,7},{7,5},{8,10},{10,8},{9,1... | collective-permute-start | bytes 393224 | tf_op jit(solution)/shard_map/ppermute | solution.py:442
  60.0 1.5 %attend.6.refs_0_ = bf16[1,128,512]{2,1,0:T(8,128)(2,1)S(1)} custom-call(s32[16]{0:T(128)S(1)} %get-tuple-element.57.slot_ref, bf16[512,512]{1,0:T(8,128)(2,1)S(1)} %copy-done.1, bf16[4,4,32,1024]{3,2,1,0:T(8,128)(2,1)S(1)} %project.4.refs_0_, bf16[4,4,32,1024]{3,2,1,0:T(8,128)(2,1)S(1)} %project.5.refs_1_, bf16[4,4,32,1024]{3,2,1,0:T(8,128)(2,1)S(1)} %project.6.refs_2_, ...), custom_call_target="tpu_custom_call" | custom-call | flops 1000000 | bytes 1024 | tf_op jit(solution)/shard_map/attend/pallas_call | solution.py:309
  61.5 1.5 %out_final.5.refs_5_ = bf16[128,4096]{1,0:T(8,128)(2,1)} custom-call(bf16[1,128,512]{2,1,0:T(8,128)(2,1)S(1)} %attend.6.refs_0_, bf16[1,128,512]{2,1,0:T(8,128)(2,1)S(1)} %collective-permute-done.20.refs_1_, bf16[512,4096]{1,0:T(8,128)(2,1)S(1)} %copy-done, bf16[512,4096]{1,0:T(8,128)(2,1)S(1)} %collective-permute-done.19.refs_3_, ...), custom_call_target="tpu_custom_call" | custom-call | flops 200000000 | bytes 1024 | tf_op jit(solution)/shard_map/out_final/pallas_call | solution.py:336
  63.1 2.3 %collective-permute-done.24.refs_4_ = bf16[128,1024]{1,0:T(8,128)(2,1)S(1)} collective-permute-done((bf16[128,1024]{1,0:T(8,128)(2,1)S(1)}, bf16[128,1024]{1,0:T(8,128)(2,1)S(1)}, u32[]{:S(2)}, u32[]{:S(2)}) %collective-permute-start.24) | collective-permute-done | bytes 262176 | tf_op jit(solution)/shard_map/ppermute | solution.py:442
  65.3 1.5 %out_final.6.refs_5_ = bf16[128,4096]{1,0:T(8,128)(2,1)} custom-call(bf16[1,128,512]{2,1,0:T(8,128)(2,1)S(1)} %attend.6.refs_0_, bf16[1,128,512]{2,1,0:T(8,128)(2,1)S(1)} %collective-permute-done.20.refs_1_, bf16[512,4096]{1,0:T(8,128)(2,1)S(1)} %copy-done, bf16[512,4096]{1,0:T(8,128)(2,1)S(1)} %collective-permute-done.19.refs_3_, ...), custom_call_target="tpu_custom_call", output_to_operand_aliasing={{}: (5, {})} | custom-call | flops 200000000 | bytes 1024 | tf_op jit(solution)/shard_map/out_final/pallas_call | solution.py:336
  66.8 4.1 %collective-permute-done.23.refs_4_ = bf16[128,1024]{1,0:T(8,128)(2,1)S(1)} collective-permute-done((bf16[128,1024]{1,0:T(8,128)(2,1)S(1)}, bf16[128,1024]{1,0:T(8,128)(2,1)S(1)}, u32[]{:S(2)}, u32[]{:S(2)}) %collective-permute-start.23) | collective-permute-done | bytes 262176 | tf_op jit(solution)/shard_map/ppermute | solution.py:442
  70.9 1.5 %out_final.7.refs_5_ = bf16[128,4096]{1,0:T(8,128)(2,1)} custom-call(bf16[1,128,512]{2,1,0:T(8,128)(2,1)S(1)} %attend.6.refs_0_, bf16[1,128,512]{2,1,0:T(8,128)(2,1)S(1)} %collective-permute-done.20.refs_1_, bf16[512,4096]{1,0:T(8,128)(2,1)S(1)} %copy-done, bf16[512,4096]{1,0:T(8,128)(2,1)S(1)} %collective-permute-done.19.refs_3_, ...), custom_call_target="tpu_custom_call", output_to_operand_aliasing={{}: (5, {})} | custom-call | flops 200000000 | bytes 1024 | tf_op jit(solution)/shard_map/out_final/pallas_call | solution.py:336
  72.4 1.3 %collective-permute-done.22.refs_4_ = bf16[128,512]{1,0:T(8,128)(2,1)S(1)} collective-permute-done((bf16[128,512]{1,0:T(8,128)(2,1)S(1)}, bf16[128,512]{1,0:T(8,128)(2,1)S(1)}, u32[]{:S(2)}, u32[]{:S(2)}) %collective-permute-start.22) | collective-permute-done | bytes 131104 | tf_op jit(solution)/shard_map/ppermute | solution.py:442
  73.7 1.0 %out_final.8.refs_5_ = bf16[128,4096]{1,0:T(8,128)(2,1)} custom-call(bf16[1,128,512]{2,1,0:T(8,128)(2,1)S(1)} %attend.6.refs_0_, bf16[1,128,512]{2,1,0:T(8,128)(2,1)S(1)} %collective-permute-done.20.refs_1_, bf16[512,4096]{1,0:T(8,128)(2,1)S(1)} %copy-done, bf16[512,4096]{1,0:T(8,128)(2,1)S(1)} %collective-permute-done.19.refs_3_, ...), custom_call_target="tpu_custom_call", output_to_operand_aliasing={{}: (5, {})} | custom-call | flops 200000000 | bytes 1024 | tf_op jit(solution)/shard_map/out_final/pallas_call | solution.py:336
  74.7 1.3 %collective-permute-done.21.refs_4_ = bf16[128,512]{1,0:T(8,128)(2,1)S(1)} collective-permute-done((bf16[128,512]{1,0:T(8,128)(2,1)S(1)}, bf16[128,512]{1,0:T(8,128)(2,1)S(1)}, u32[]{:S(2)}, u32[]{:S(2)}) %collective-permute-start.21) | collective-permute-done | bytes 131104 | tf_op jit(solution)/shard_map/ppermute | solution.py:442
  76.0 1.0 %out_final.9 = bf16[128,4096]{1,0:T(8,128)(2,1)} custom-call(bf16[1,128,512]{2,1,0:T(8,128)(2,1)S(1)} %attend.6.refs_0_, bf16[1,128,512]{2,1,0:T(8,128)(2,1)S(1)} %collective-permute-done.20.refs_1_, bf16[512,4096]{1,0:T(8,128)(2,1)S(1)} %copy-done, bf16[512,4096]{1,0:T(8,128)(2,1)S(1)} %collective-permute-done.19.refs_3_, ...), custom_call_target="tpu_custom_call", output_to_operand_aliasing={{}: (5, {})} | custom-call | flops 200000000 | bytes 1024 | tf_op jit(solution)/shard_map/out_final/pallas_call | solution.py:336
  (50 shorter events, 4.0 us)
Async XLA Ops:
  0.7 7.0 %copy-start.2 = (bf16[512,896]{1,0:T(8,128)(2,1)S(1)}, bf16[512,896]{1,0:T(8,128)(2,1)}, u32[]{:S(2)}) copy-start(bf16[512,896]{1,0:T(8,128)(2,1)} %states_ref.11) | copy-start | bytes 2752516
  0.7 7.0 %copy-start.5 = (bf16[16,32,896]{2,1,0:T(8,128)(2,1)S(1)}, bf16[16,32,896]{2,1,0:T(8,128)(2,1)}, u32[]{:S(2)}) copy-start(bf16[16,32,896]{2,1,0:T(8,128)(2,1)} %refs_3_.4) | copy-start | bytes 2752516
  0.7 8.3 %collective-permute-start.3 = (s32[4,8]{1,0:T(4,128)S(1)}, s32[4,8]{1,0:T(4,128)S(1)}, u32[]{:S(2)}, u32[]{:S(2)}) collective-permute-start(s32[4,8]{1,0:T(4,128)S(1)} %pad_add_fusion.own_ref), channel_id=1, source_target_pairs={{0,12},{4,8},{8,4},{12,0},{1,13},{5,9},{9,5},{13,1},{2,14},{6,10},... | collective-permute-start | bytes 392 | tf_op jit(solution)/shard_map/ppermute | solution.py:379
  5.8 4.5 %collective-permute-start.2 = (s32[4,8]{1,0:T(4,128)S(1)}, s32[4,8]{1,0:T(4,128)S(1)}, u32[]{:S(2)}, u32[]{:S(2)}) collective-permute-start(s32[4,8]{1,0:T(4,128)S(1)} %pad_add_fusion.own_ref), channel_id=1, source_target_pairs={{0,8},{4,12},{8,0},{12,4},{1,9},{5,13},{9,1},{13,5},{2,10},{6,14},... | collective-permute-start | bytes 392 | tf_op jit(solution)/shard_map/ppermute | solution.py:379
  5.8 4.5 %collective-permute-start.1 = (s32[4,8]{1,0:T(4,128)S(1)}, s32[4,8]{1,0:T(4,128)S(1)}, u32[]{:S(2)}, u32[]{:S(2)}) collective-permute-start(s32[4,8]{1,0:T(4,128)S(1)} %pad_add_fusion.own_ref), channel_id=1, source_target_pairs={{0,4},{4,0},{8,12},{12,8},{1,5},{5,1},{9,13},{13,9},{2,6},{6,2},{1... | collective-permute-start | bytes 392 | tf_op jit(solution)/shard_map/ppermute | solution.py:379
  9.0 7.7 %copy-start = (bf16[512,4096]{1,0:T(8,128)(2,1)S(1)}, bf16[512,4096]{1,0:T(8,128)(2,1)}, u32[]{:S(2)}) copy-start(bf16[512,4096]{1,0:T(8,128)(2,1)} %refs_2_.27) | copy-start | bytes 12582916
  11.1 14.8 %collective-permute-start.4 = (bf16[4,32,896]{2,1,0:T(8,128)(2,1)S(1)}, bf16[4,32,896]{2,1,0:T(8,128)(2,1)S(1)}, u32[]{:S(2)}, u32[]{:S(2)}) collective-permute-start(bf16[4,32,896]{2,1,0:T(8,128)(2,1)S(1)} %get-tuple-element.63), channel_id=1, source_target_pairs={{0,8},{4,12},{8,0},{12,4},{1,9},{5,13},{9,1},{13,5},{2,10},{6,14},... | collective-permute-start | bytes 688136 | tf_op jit(solution)/shard_map/ppermute | solution.py:387
  13.2 7.0 %collective-permute-start.6 = (bf16[2,32,896]{2,1,0:T(8,128)(2,1)S(1)}, bf16[2,32,896]{2,1,0:T(8,128)(2,1)S(1)}, u32[]{:S(2)}, u32[]{:S(2)}) collective-permute-start(bf16[2,32,896]{2,1,0:T(8,128)(2,1)S(1)} %get-tuple-element.65), channel_id=1, source_target_pairs={{0,4},{4,0},{8,12},{12,8},{1,5},{5,1},{9,13},{13,9},{2,6},{6,2},{1... | collective-permute-start | bytes 344072 | tf_op jit(solution)/shard_map/ppermute | solution.py:387
  14.3 10.6 %collective-permute-start.5 = (bf16[2,32,896]{2,1,0:T(8,128)(2,1)S(1)}, bf16[2,32,896]{2,1,0:T(8,128)(2,1)S(1)}, u32[]{:S(2)}, u32[]{:S(2)}) collective-permute-start(bf16[2,32,896]{2,1,0:T(8,128)(2,1)S(1)} %get-tuple-element.64), channel_id=1, source_target_pairs={{0,4},{4,0},{8,12},{12,8},{1,5},{5,1},{9,13},{13,9},{2,6},{6,2},{1... | collective-permute-start | bytes 344072 | tf_op jit(solution)/shard_map/ppermute | solution.py:387
  15.2 13.5 %collective-permute-start = (bf16[4,32,896]{2,1,0:T(8,128)(2,1)S(1)}, bf16[4,32,896]{2,1,0:T(8,128)(2,1)S(1)}, u32[]{:S(2)}, u32[]{:S(2)}) collective-permute-start(bf16[4,32,896]{2,1,0:T(8,128)(2,1)S(1)} %encode_local.1), channel_id=1, source_target_pairs={{0,2},{2,0},{1,3},{3,1},{4,6},{6,4},{5,7},{7,5},{8,10},{10,8},{9,1... | collective-permute-start | bytes 688136 | tf_op jit(solution)/shard_map/ppermute | solution.py:364
  16.7 32.7 %collective-permute-start.19 = (bf16[512,4096]{1,0:T(8,128)(2,1)S(1)}, bf16[512,4096]{1,0:T(8,128)(2,1)S(1)}, u32[]{:S(2)}, u32[]{:S(2)}) collective-permute-start(bf16[512,4096]{1,0:T(8,128)(2,1)S(1)} %copy-done), channel_id=1, source_target_pairs={{0,1},{1,0},{2,3},{3,2},{4,5},{5,4},{6,7},{7,6},{8,9},{9,8},{10,11... | collective-permute-start | bytes 12582920 | tf_op jit(solution)/shard_map/ppermute | solution.py:367
  21.3 8.1 %collective-permute-start.8 = (bf16[2,32,896]{2,1,0:T(8,128)(2,1)S(1)}, bf16[2,32,896]{2,1,0:T(8,128)(2,1)S(1)}, u32[]{:S(2)}, u32[]{:S(2)}) collective-permute-start(bf16[2,32,896]{2,1,0:T(8,128)(2,1)S(1)} %encode.5), channel_id=1, source_target_pairs={{0,2},{2,0},{1,3},{3,1},{4,6},{6,4},{5,7},{7,5},{8,10},{10,8},{9,1... | collective-permute-start | bytes 344072 | tf_op jit(solution)/shard_map/ppermute | solution.py:364
  24.8 8.6 %collective-permute-start.12 = (bf16[2,32,896]{2,1,0:T(8,128)(2,1)S(1)}, bf16[2,32,896]{2,1,0:T(8,128)(2,1)S(1)}, u32[]{:S(2)}, u32[]{:S(2)}) collective-permute-start(bf16[2,32,896]{2,1,0:T(8,128)(2,1)S(1)} %get-tuple-element.81), channel_id=1, source_target_pairs={{0,12},{4,8},{8,4},{12,0},{1,13},{5,9},{9,5},{13,1},{2,14},{6,10},... | collective-permute-start | bytes 344072 | tf_op jit(solution)/shard_map/ppermute | solution.py:387
  25.9 7.4 %collective-permute-start.9 = (bf16[2,32,896]{2,1,0:T(8,128)(2,1)S(1)}, bf16[2,32,896]{2,1,0:T(8,128)(2,1)S(1)}, u32[]{:S(2)}, u32[]{:S(2)}) collective-permute-start(bf16[2,32,896]{2,1,0:T(8,128)(2,1)S(1)} %encode.6), channel_id=1, source_target_pairs={{0,2},{2,0},{1,3},{3,1},{4,6},{6,4},{5,7},{7,5},{8,10},{10,8},{9,1... | collective-permute-start | bytes 344072 | tf_op jit(solution)/shard_map/ppermute | solution.py:364
  28.8 6.3 %collective-permute-start.11 = (bf16[4,32,896]{2,1,0:T(8,128)(2,1)S(1)}, bf16[4,32,896]{2,1,0:T(8,128)(2,1)S(1)}, u32[]{:S(2)}, u32[]{:S(2)}) collective-permute-start(bf16[4,32,896]{2,1,0:T(8,128)(2,1)S(1)} %encode.7), channel_id=1, source_target_pairs={{0,2},{2,0},{1,3},{3,1},{4,6},{6,4},{5,7},{7,5},{8,10},{10,8},{9,1... | collective-permute-start | bytes 688136 | tf_op jit(solution)/shard_map/ppermute | solution.py:364
  29.4 7.3 %collective-permute-start.15 = (bf16[2,32,896]{2,1,0:T(8,128)(2,1)S(1)}, bf16[2,32,896]{2,1,0:T(8,128)(2,1)S(1)}, u32[]{:S(2)}, u32[]{:S(2)}) collective-permute-start(bf16[2,32,896]{2,1,0:T(8,128)(2,1)S(1)} %get-tuple-element.87), channel_id=1, source_target_pairs={{0,12},{4,8},{8,4},{12,0},{1,13},{5,9},{9,5},{13,1},{2,14},{6,10},... | collective-permute-start | bytes 344072 | tf_op jit(solution)/shard_map/ppermute | solution.py:387
  33.3 4.6 %collective-permute-start.7 = (bf16[2,4,32,896]{3,2,1,0:T(8,128)(2,1)S(1)}, bf16[2,4,32,896]{3,2,1,0:T(8,128)(2,1)S(1)}, u32[]{:S(2)}, u32[]{:S(2)}) collective-permute-start(bf16[2,4,32,896]{3,2,1,0:T(8,128)(2,1)S(1)} %pad_maximum_fusion.refs_0_), channel_id=1, source_target_pairs={{0,1},{1,0},{2,3},{3,2},{4,5},{5,4},{6,7},{7,6},{8,9},{9,8},{10,11... | collective-permute-start | bytes 1376264 | tf_op jit(solution)/shard_map/ppermute | solution.py:367
  33.4 6.6 %collective-permute-start.10 = (bf16[2,4,32,896]{3,2,1,0:T(8,128)(2,1)S(1)}, bf16[2,4,32,896]{3,2,1,0:T(8,128)(2,1)S(1)}, u32[]{:S(2)}, u32[]{:S(2)}) collective-permute-start(bf16[2,4,32,896]{3,2,1,0:T(8,128)(2,1)S(1)} %pad_maximum_fusion.1.refs_0_), channel_id=1, source_target_pairs={{0,1},{1,0},{2,3},{3,2},{4,5},{5,4},{6,7},{7,6},{8,9},{9,8},{10,11... | collective-permute-start | bytes 1376264 | tf_op jit(solution)/shard_map/ppermute | solution.py:367
  35.1 7.5 %collective-permute-start.14 = (bf16[2,32,896]{2,1,0:T(8,128)(2,1)S(1)}, bf16[2,32,896]{2,1,0:T(8,128)(2,1)S(1)}, u32[]{:S(2)}, u32[]{:S(2)}) collective-permute-start(bf16[2,32,896]{2,1,0:T(8,128)(2,1)S(1)} %encode.8), channel_id=1, source_target_pairs={{0,2},{2,0},{1,3},{3,1},{4,6},{6,4},{5,7},{7,5},{8,10},{10,8},{9,1... | collective-permute-start | bytes 344072 | tf_op jit(solution)/shard_map/ppermute | solution.py:364
  36.7 2.0 %copy-start.3 = (bf16[896,512]{1,0:T(8,128)(2,1)S(1)}, bf16[896,512]{1,0:T(8,128)(2,1)}, u32[]{:S(2)}) copy-start(bf16[896,512]{1,0:T(8,128)(2,1)} %refs_5_.1) | copy-start | bytes 2752516
  36.7 2.0 %copy-start.4 = (bf16[896,512]{1,0:T(8,128)(2,1)S(1)}, bf16[896,512]{1,0:T(8,128)(2,1)}, u32[]{:S(2)}) copy-start(bf16[896,512]{1,0:T(8,128)(2,1)} %refs_6_.1) | copy-start | bytes 2752516
  36.7 4.5 %collective-permute-start.13 = (bf16[2,4,32,896]{3,2,1,0:T(8,128)(2,1)S(1)}, bf16[2,4,32,896]{3,2,1,0:T(8,128)(2,1)S(1)}, u32[]{:S(2)}, u32[]{:S(2)}) collective-permute-start(bf16[2,4,32,896]{3,2,1,0:T(8,128)(2,1)S(1)} %pad_maximum_fusion.2.refs_0_), channel_id=1, source_target_pairs={{0,1},{1,0},{2,3},{3,2},{4,5},{5,4},{6,7},{7,6},{8,9},{9,8},{10,11... | collective-permute-start | bytes 1376264 | tf_op jit(solution)/shard_map/ppermute | solution.py:367
  37.9 5.6 %collective-permute-start.16 = (bf16[2,32,896]{2,1,0:T(8,128)(2,1)S(1)}, bf16[2,32,896]{2,1,0:T(8,128)(2,1)S(1)}, u32[]{:S(2)}, u32[]{:S(2)}) collective-permute-start(bf16[2,32,896]{2,1,0:T(8,128)(2,1)S(1)} %encode.9), channel_id=1, source_target_pairs={{0,2},{2,0},{1,3},{3,1},{4,6},{6,4},{5,7},{7,5},{8,10},{10,8},{9,1... | collective-permute-start | bytes 344072 | tf_op jit(solution)/shard_map/ppermute | solution.py:364
  43.6 1.9 %copy-start.1 = (bf16[512,512]{1,0:T(8,128)(2,1)S(1)}, bf16[512,512]{1,0:T(8,128)(2,1)}, u32[]{:S(2)}) copy-start(bf16[512,512]{1,0:T(8,128)(2,1)} %q_ref.5) | copy-start | bytes 1572868
  43.6 1.9 %collective-permute-start.17 = (bf16[2,4,32,896]{3,2,1,0:T(8,128)(2,1)S(1)}, bf16[2,4,32,896]{3,2,1,0:T(8,128)(2,1)S(1)}, u32[]{:S(2)}, u32[]{:S(2)}) collective-permute-start(bf16[2,4,32,896]{3,2,1,0:T(8,128)(2,1)S(1)} %pad_maximum_fusion.3.refs_0_), channel_id=1, source_target_pairs={{0,1},{1,0},{2,3},{3,2},{4,5},{5,4},{6,7},{7,6},{8,9},{9,8},{10,11... | collective-permute-start | bytes 1376264 | tf_op jit(solution)/shard_map/ppermute | solution.py:367
  47.7 1.7 %collective-permute-start.18 = (bf16[1,128,512]{2,1,0:T(8,128)(2,1)S(1)}, bf16[1,128,512]{2,1,0:T(8,128)(2,1)S(1)}, u32[]{:S(2)}, u32[]{:S(2)}) collective-permute-start(bf16[1,128,512]{2,1,0:T(8,128)(2,1)S(1)} %get-tuple-element.94), channel_id=1, source_target_pairs={{0,1},{1,0},{2,3},{3,2},{4,5},{5,4},{6,7},{7,6},{8,9},{9,8},{10,11... | collective-permute-start | bytes 393224 | tf_op jit(solution)/shard_map/ppermute | solution.py:425
  50.5 11.1 %collective-permute-start.25 = (bf16[128,1024]{1,0:T(8,128)(2,1)S(1)}, bf16[128,1024]{1,0:T(8,128)(2,1)S(1)}, u32[]{:S(2)}, u32[]{:S(2)}) collective-permute-start(bf16[128,1024]{1,0:T(8,128)(2,1)S(1)} %out_project.5), channel_id=1, source_target_pairs={{0,2},{2,0},{1,3},{3,1},{4,6},{6,4},{5,7},{7,5},{8,10},{10,8},{9,1... | collective-permute-start | bytes 786440 | tf_op jit(solution)/shard_map/ppermute | solution.py:442
  52.2 13.1 %collective-permute-start.24 = (bf16[128,1024]{1,0:T(8,128)(2,1)S(1)}, bf16[128,1024]{1,0:T(8,128)(2,1)S(1)}, u32[]{:S(2)}, u32[]{:S(2)}) collective-permute-start(bf16[128,1024]{1,0:T(8,128)(2,1)S(1)} %out_project.6), channel_id=1, source_target_pairs={{0,2},{2,0},{1,3},{3,1},{4,6},{6,4},{5,7},{7,5},{8,10},{10,8},{9,1... | collective-permute-start | bytes 786440 | tf_op jit(solution)/shard_map/ppermute | solution.py:442
  54.4 16.5 %collective-permute-start.23 = (bf16[128,1024]{1,0:T(8,128)(2,1)S(1)}, bf16[128,1024]{1,0:T(8,128)(2,1)S(1)}, u32[]{:S(2)}, u32[]{:S(2)}) collective-permute-start(bf16[128,1024]{1,0:T(8,128)(2,1)S(1)} %out_project.7), channel_id=1, source_target_pairs={{0,2},{2,0},{1,3},{3,1},{4,6},{6,4},{5,7},{7,5},{8,10},{10,8},{9,1... | collective-permute-start | bytes 786440 | tf_op jit(solution)/shard_map/ppermute | solution.py:442
  57.4 1.4 %collective-permute-start.20 = (bf16[1,128,512]{2,1,0:T(8,128)(2,1)S(1)}, bf16[1,128,512]{2,1,0:T(8,128)(2,1)S(1)}, u32[]{:S(2)}, u32[]{:S(2)}) collective-permute-start(bf16[1,128,512]{2,1,0:T(8,128)(2,1)S(1)} %attend.7), channel_id=1, source_target_pairs={{0,1},{1,0},{2,3},{3,2},{4,5},{5,4},{6,7},{7,6},{8,9},{9,8},{10,11... | collective-permute-start | bytes 393224 | tf_op jit(solution)/shard_map/ppermute | solution.py:425
  57.4 16.3 %collective-permute-start.22 = (bf16[128,512]{1,0:T(8,128)(2,1)S(1)}, bf16[128,512]{1,0:T(8,128)(2,1)S(1)}, u32[]{:S(2)}, u32[]{:S(2)}) collective-permute-start(bf16[128,512]{1,0:T(8,128)(2,1)S(1)} %out_project.8), channel_id=1, source_target_pairs={{0,2},{2,0},{1,3},{3,1},{4,6},{6,4},{5,7},{7,5},{8,10},{10,8},{9,1... | collective-permute-start | bytes 393224 | tf_op jit(solution)/shard_map/ppermute | solution.py:442
  58.8 17.2 %collective-permute-start.21 = (bf16[128,512]{1,0:T(8,128)(2,1)S(1)}, bf16[128,512]{1,0:T(8,128)(2,1)S(1)}, u32[]{:S(2)}, u32[]{:S(2)}) collective-permute-start(bf16[128,512]{1,0:T(8,128)(2,1)S(1)} %out_project.9), channel_id=1, source_target_pairs={{0,2},{2,0},{1,3},{3,1},{4,6},{6,4},{5,7},{7,5},{8,10},{10,8},{9,1... | collective-permute-start | bytes 393224 | tf_op jit(solution)/shard_map/ppermute | solution.py:442

commit v12 on v10

--- a/solution.py
+++ b/solution.py
@@ -246,8 +246,9 @@
     )(*pieces, w_key, w_value)
 
 
-def attend_kernel(firsts, n_heads, n_rep, targets, fanout, spans, n_rest, slot_ref, q_ref, *refs):
-    ready, (own_ref, *refs) = refs[: len(firsts) - 1], refs[len(firsts) - 1 :]
+def attend_kernel(firsts, n_own, n_heads, n_rep, targets, fanout, spans, n_rest, slot_ref, q_ref, *refs):
+    ready, refs = refs[: len(firsts) - 1], refs[len(firsts) - 1 :]
+    own, refs = refs[:n_own], refs[n_own:]
     if n_rest:
         pieces, (wk_ref, wv_ref, out_ref, rest_ref) = refs[:n_rest], refs[n_rest:]
         project_into(rest_ref, 0, pieces, wk_ref, wv_ref)
@@ -262,8 +263,8 @@
         return jnp.clip(slot - first, 0, count - 1)
 
     def held(slot, lanes):
-        at = place(slot, firsts[-1], own_ref.shape[0])
-        value = jnp.concatenate([own_ref[at, :, :, lanes], rest_ref[at, :, :, lanes]], axis=0)
+        at = place(slot, firsts[-1], rest_ref.shape[0])
+        value = jnp.concatenate([ref[at, :, :, lanes] for ref in (*own, rest_ref)], axis=0)
         for ref, first in reversed(list(zip(ready, firsts))):
             there = slot < first + ref.shape[0]
             value = jnp.where(there, ref[place(slot, first, ref.shape[0]), :, :, lanes], value)
@@ -299,7 +300,7 @@
     cols = queries.shape[1]
     rows = queries.shape[0] // (n_heads * n_rep)
     todo = isinstance(rest, list)
-    slots, _, tokens, width = own.shape
+    slots, _, tokens, width = own[0].shape
     out_shape = [jax.ShapeDtypeStruct((len(targets), rows, cols), BF16)]
     if todo:
         others = sum(piece.shape[0] for piece in rest)
@@ -307,37 +308,35 @@
     operands = [*rest, *weights] if todo else [rest]
     return pl.pallas_call(
         functools.partial(
-            attend_kernel, firsts, n_heads, n_rep, targets, fanout, spans, len(rest) if todo else 0
+            attend_kernel, firsts, len(own), n_heads, n_rep, targets, fanout, spans, len(rest) if todo else 0
         ),
         out_shape=out_shape,
-        in_specs=[SMEM] + [VMEM] * (len(ready) + 2 + len(operands)),
+        in_specs=[SMEM] + [VMEM] * (len(ready) + 1 + len(own) + len(operands)),
         out_specs=[VMEM] * len(out_shape),
         compiler_params=params(32),
         cost_estimate=cost(0.001),
         name="attend",
-    )(slot, queries, *ready, own, *operands)
+    )(slot, queries, *ready, *own, *operands)
 
 
 def out_kernel(n_rep, n_received, *refs):
     mixed, weights, received = refs[:n_rep], refs[n_rep : 2 * n_rep], refs[2 * n_rep : 2 * n_rep + n_received]
-    total = sum(dot(a[0], w[...]) for a, w in zip(mixed, weights))
-    for part in received:
-        total = total + part[...].astype(F32)
-    refs[-1][...] = total.astype(BF16)
+    parts = [dot(a[0], w[...]) for a, w in zip(mixed, weights)] + [part[...].astype(F32) for part in received]
+    refs[-1][...] = sum(parts).astype(BF16)
 
 
 def out_project(mixed, weights, t, start, stop, tile, gflops, received=(), out=None, final=False):
-    _, rows, depth = mixed[0].shape
-    width = weights[0].shape[1]
+    rows = (mixed[0].shape[1:] if mixed else received[0].shape)[0]
     base = start // tile
     n = len(mixed)
     operands = [*mixed, *weights, *received] + ([] if out is None else [out])
+    width = (weights[0] if mixed else out).shape[1]
     return pl.pallas_call(
         functools.partial(out_kernel, n, len(received)),
         grid=((stop - start) // tile,),
         out_shape=jax.ShapeDtypeStruct((rows, width if final else stop - start), BF16),
-        in_specs=[pl.BlockSpec((1, rows, depth), lambda j: (t, 0, 0))] * n
-        + [pl.BlockSpec((depth, tile), lambda j: (0, base + j))] * n
+        in_specs=[pl.BlockSpec((1, *a.shape[1:]), lambda j: (t, 0, 0)) for a in mixed]
+        + [pl.BlockSpec((w.shape[0], tile), lambda j: (0, base + j)) for w in weights]
         + [pl.BlockSpec((rows, tile), lambda j: (0, j))] * len(received)
         + [ANY] * (out is not None),
         out_specs=pl.BlockSpec((rows, tile), lambda j: (0, (base if final else 0) + j)),
@@ -407,8 +406,13 @@
     while len(kvs) < len(pieces):
         last = project(after(pieces[len(kvs)], last), w_key, w_value)
         kvs.append(last)
-    pieces = over_rep(jnp.stack(after(crossed[-1], kvs)))
-    own_kv, rest = project(pieces[:1], w_key, w_value), pieces[1:]
+    local, *remote = crossed[-1]
+    early = [piece[None] for piece in over_rep(after(local, kvs[0]))]
+    last = project(after(early, last), w_key, w_value)
+    own_kv = [last]
+    remote = jnp.stack(after(remote, kvs, last))
+    _, *rest = over_rep(remote)
+    own_kv.append(project([remote], w_key, w_value))
 
     def mix(turns, q, rest):
         mixed = []
@@ -436,9 +440,12 @@
             partials.append(partial)
             received[i].append(lax.ppermute(partial, "heads", shift_pairs(n_heads, t)))
     mixed, rest = mix([0], after(queries, partials), rest)
-    out = None
-    for (start, stop), parts in zip(blocks, received):
-        out = out_project(mixed, w_outs, 0, start, stop, tile, 0.2, parts, out, True)
+    out, ahead = None, out_project(mixed, w_outs, 0, *blocks[-1], tile, 0.001)
+    for i, ((start, stop), parts) in enumerate(zip(blocks, received)):
+        if i + 1 < len(blocks):
+            out = out_project(mixed, w_outs, 0, start, stop, tile, 0.2, parts, out, True)
+        else:
+            out = out_project([], [], 0, start, stop, tile, 0.2, [ahead, *parts], out, True)
     return out
 
 

time: 75.7 us -> 74.7 us (0.987)
  waiting for transfers between devices: 25.7 us -> 24.4 us
    ppermute x4, waiting for transfers between devices: 5.78 us -> 4.52 us  [over_heads(): lax.ppermute(array, 'heads', shift_pairs(n_heads, s))]
    pallas_call x4 -> x5, Pallas kernels: 4.49 us -> 4.94 us  [project(): pl.pallas_call(functools.partial(project_kernel, len(pieces)), out_shape=...]
    pallas_call x10 -> x11, Pallas kernels: 9.81 us -> 9.84 us  [out_project(): pl.pallas_call(functools.partial(out_kernel, n, len(received)), grid=((st...]
  transfers between devices with their start and end apart: 23 -> 24, of which waited for: 11 -> 12; matrix products, arithmetic and copies ran while one was open for 0% -> 0% of each run, Pallas kernels for 34% -> 35%
where the time goes in v12:
time: 74.7 us; the launch traced here: 74.5 us
  Pallas kernels  28.5 us (38%)
  waiting for transfers between devices  24.4 us (33%)
  starting transfers between devices  20.4 us (27%)
  other arithmetic  0.85 us (1%)
    pallas_call x11, Pallas kernels, out_project(): pl.pallas_call(functools.partial(out_kernel, n, len(received)), grid=((st...  9.84 us
    ppermute x5, waiting for transfers between devices, shards(): received[i].append(lax.ppermute(partial, 'heads', shift_pairs(n_heads, t)))  8.63 us
    ppermute x4, waiting for transfers between devices, send(): lax.ppermute(block, 'lanes', lane_pairs(n_lanes, items[i][0], True))  8.6 us
    pallas_call x4, Pallas kernels, attend(): pl.pallas_call(functools.partial(attend_kernel, firsts, len(own), n_heads...  6.43 us
    ppermute x3, starting transfers between devices, shards(): lax.ppermute(own, 'lanes', lane_pairs(n_lanes, d, False))  5.76 us
    ppermute x5, starting transfers between devices, shards(): received[i].append(lax.ppermute(partial, 'heads', shift_pairs(n_heads, t)))  5.24 us
    pallas_call x5, Pallas kernels, project(): pl.pallas_call(functools.partial(project_kernel, len(pieces)), out_shape=...  4.94 us
    ppermute x4, waiting for transfers between devices, over_heads(): lax.ppermute(array, 'heads', shift_pairs(n_heads, s))  4.52 us
  transfers between devices with their start and end apart: 24, of which 12 were waited for; matrix products, arithmetic and copies ran while one was open for 0% of the time, Pallas kernels for 35%

profile of v12, /device:TPU:0, one launch (start us, length us, event | category | flops | bytes accessed | tf_op | source)
XLA Modules:
  0.0 74.5 jit_solution(6644594754880167496)
XLA Ops:
  0.0 0.7 pad_add_fusion.own_ref
  0.7 5.1 %collective-permute-start.3 = (s32[4,8]{1,0:T(4,128)S(1)}, s32[4,8]{1,0:T(4,128)S(1)}, u32[]{:S(2)}, u32[]{:S(2)}) collective-permute-start(s32[4,8]{1,0:T(4,128)S(1)} %pad_add_fusion.own_ref), channel_id=1, source_target_pairs={{0,12},{4,8},{8,4},{12,0},{1,13},{5,9},{9,5},{13,1},{2,14},{6,10},... | collective-permute-start | bytes 392 | tf_op jit(solution)/shard_map/ppermute | solution.py:377
  5.8 0.6 collective-permute-start.1
  6.5 1.3 %plan.1 = (s32[16]{0:T(128)S(1)}, s32[16]{0:T(128)S(1)}, s32[16]{0:T(128)S(1)}) custom-call(s32[4,8]{1,0:T(4,128)S(1)} %pad_add_fusion.own_ref), custom_call_target="tpu_custom_call" | custom-call | flops 10000000000 | bytes 1024 | tf_op jit(solution)/shard_map/plan/pallas_call | solution.py:76
  7.8 1.3 %encode_local.1 = bf16[4,32,896]{2,1,0:T(8,128)(2,1)S(1)} custom-call(s32[16]{0:T(128)S(1)} %get-tuple-element.55.req_ref, s32[16]{0:T(128)S(1)} %get-tuple-element.56.pick_ref, bf16[512,896]{1,0:T(8,128)(2,1)S(1)} %copy-done.4, bf16[16,32,896]{2,1,0:T(8,128)(2,1)S(1)} %copy-done.5), custom_call_target="tpu_custom_call" | custom-call | flops 10000000000 | bytes 1024 | tf_op jit(solution)/shard_map/encode_local/pallas_call | solution.py:205
  9.1 1.3 %collective-permute-done.2.refs_1_ = s32[4,8]{1,0:T(4,128)S(1)} collective-permute-done((s32[4,8]{1,0:T(4,128)S(1)}, s32[4,8]{1,0:T(4,128)S(1)}, u32[]{:S(2)}, u32[]{:S(2)}) %collective-permute-start.2) | collective-permute-done | bytes 160 | tf_op jit(solution)/shard_map/ppermute | solution.py:377
  10.3 0.8 %fetch.1 = (bf16[2,32,896]{2,1,0:T(8,128)(2,1)S(1)}, bf16[2,32,896]{2,1,0:T(8,128)(2,1)S(1)}, bf16[4,32,896]{2,1,0:T(8,128)(2,1)S(1)}, bf16[4,32,896]{2,1,0:T(8,128)(2,1)S(1)}) custom-call(s32[4,8]{1,0:T(4,128)S(1)} %collective-permute-done.1.refs_0_, s32[4,8]{1,0:T(4,128)S(1)} %collective-permute-done.2.refs_1_, s32[4,8]{1,0:T(4,128)S(1)} %collective-permute-done.3.refs_2_, ...), custom_call_target="tpu_custom_call" | custom-call | flops 10000000000 | bytes 1024 | tf_op jit(solution)/shard_map/fetch/pallas_call | solution.py:109
  11.1 2.1 %collective-permute-start.4 = (bf16[4,32,896]{2,1,0:T(8,128)(2,1)S(1)}, bf16[4,32,896]{2,1,0:T(8,128)(2,1)S(1)}, u32[]{:S(2)}, u32[]{:S(2)}) collective-permute-start(bf16[4,32,896]{2,1,0:T(8,128)(2,1)S(1)} %get-tuple-element.60), channel_id=1, source_target_pairs={{0,8},{4,12},{8,0},{12,4},{1,9},{5,13},{9,1},{13,5},{2,10},{6,14},... | collective-permute-start | bytes 688136 | tf_op jit(solution)/shard_map/ppermute | solution.py:385
  13.2 1.0 %collective-permute-start.5 = (bf16[2,32,896]{2,1,0:T(8,128)(2,1)S(1)}, bf16[2,32,896]{2,1,0:T(8,128)(2,1)S(1)}, u32[]{:S(2)}, u32[]{:S(2)}) collective-permute-start(bf16[2,32,896]{2,1,0:T(8,128)(2,1)S(1)} %get-tuple-element.63), channel_id=1, source_target_pairs={{0,4},{4,0},{8,12},{12,8},{1,5},{5,1},{9,13},{13,9},{2,6},{6,2},{1... | collective-permute-start | bytes 344072 | tf_op jit(solution)/shard_map/ppermute | solution.py:385
  14.3 1.0 %collective-permute-start.6 = (bf16[2,32,896]{2,1,0:T(8,128)(2,1)S(1)}, bf16[2,32,896]{2,1,0:T(8,128)(2,1)S(1)}, u32[]{:S(2)}, u32[]{:S(2)}) collective-permute-start(bf16[2,32,896]{2,1,0:T(8,128)(2,1)S(1)} %get-tuple-element.64), channel_id=1, source_target_pairs={{0,4},{4,0},{8,12},{12,8},{1,5},{5,1},{9,13},{13,9},{2,6},{6,2},{1... | collective-permute-start | bytes 344072 | tf_op jit(solution)/shard_map/ppermute | solution.py:385
  15.2 1.5 %collective-permute-start = (bf16[4,32,896]{2,1,0:T(8,128)(2,1)S(1)}, bf16[4,32,896]{2,1,0:T(8,128)(2,1)S(1)}, u32[]{:S(2)}, u32[]{:S(2)}) collective-permute-start(bf16[4,32,896]{2,1,0:T(8,128)(2,1)S(1)} %encode_local.1), channel_id=1, source_target_pairs={{0,2},{2,0},{1,3},{3,1},{4,6},{6,4},{5,7},{7,5},{8,10},{10,8},{9,1... | collective-permute-start | bytes 688136 | tf_op jit(solution)/shard_map/ppermute | solution.py:362
  16.7 3.5 %collective-permute-done.5.refs_0_ = bf16[2,32,896]{2,1,0:T(8,128)(2,1)S(1)} collective-permute-done((bf16[2,32,896]{2,1,0:T(8,128)(2,1)S(1)}, bf16[2,32,896]{2,1,0:T(8,128)(2,1)S(1)}, u32[]{:S(2)}, u32[]{:S(2)}) %collective-permute-start.5) | collective-permute-done | bytes 114720 | tf_op jit(solution)/shard_map/ppermute | solution.py:385
  20.3 3.3 %collective-permute-done.6.refs_1_ = bf16[2,32,896]{2,1,0:T(8,128)(2,1)S(1)} collective-permute-done((bf16[2,32,896]{2,1,0:T(8,128)(2,1)S(1)}, bf16[2,32,896]{2,1,0:T(8,128)(2,1)S(1)}, u32[]{:S(2)}, u32[]{:S(2)}) %collective-permute-start.6) | collective-permute-done | bytes 114720 | tf_op jit(solution)/shard_map/ppermute | solution.py:385
  23.6 1.5 %encode.3 = bf16[4,32,896]{2,1,0:T(8,128)(2,1)S(1)} custom-call(s32[16]{0:T(128)S(1)} %get-tuple-element.55.req_ref, bf16[512,896]{1,0:T(8,128)(2,1)S(1)} %copy-done.4, bf16[2,32,896]{2,1,0:T(8,128)(2,1)S(1)} %collective-permute-done.5.refs_0_, bf16[2,32,896]{2,1,0:T(8,128)(2,1)S(1)} %collective-permute-done.6.refs_1_), custom_call_target="tpu_custom_call" | custom-call | flops 100000000 | bytes 1024 | tf_op jit(solution)/shard_map/encode/pallas_call | solution.py:186
  25.1 1.6 %collective-permute-start.8 = (bf16[4,32,896]{2,1,0:T(8,128)(2,1)S(1)}, bf16[4,32,896]{2,1,0:T(8,128)(2,1)S(1)}, u32[]{:S(2)}, u32[]{:S(2)}) collective-permute-start(bf16[4,32,896]{2,1,0:T(8,128)(2,1)S(1)} %encode.3), channel_id=1, source_target_pairs={{0,2},{2,0},{1,3},{3,1},{4,6},{6,4},{5,7},{7,5},{8,10},{10,8},{9,1... | collective-permute-start | bytes 688136 | tf_op jit(solution)/shard_map/ppermute | solution.py:362
  26.6 1.3 %encode.4 = bf16[4,32,896]{2,1,0:T(8,128)(2,1)S(1)} custom-call(s32[16]{0:T(128)S(1)} %get-tuple-element.55.req_ref, bf16[512,896]{1,0:T(8,128)(2,1)S(1)} %copy-done.4, bf16[4,32,896]{2,1,0:T(8,128)(2,1)S(1)} %collective-permute-done.4.refs_0_), custom_call_target="tpu_custom_call" | custom-call | flops 10000000000 | bytes 1024 | tf_op jit(solution)/shard_map/encode/pallas_call | solution.py:186
  27.9 0.6 collective-permute-start.10
  28.6 4.0 %collective-permute-done.8 = bf16[4,32,896]{2,1,0:T(8,128)(2,1)S(1)} collective-permute-done((bf16[4,32,896]{2,1,0:T(8,128)(2,1)S(1)}, bf16[4,32,896]{2,1,0:T(8,128)(2,1)S(1)}, u32[]{:S(2)}, u32[]{:S(2)}) %collective-permute-start.8) | collective-permute-done | bytes 229408 | tf_op jit(solution)/shard_map/ppermute | solution.py:362
  32.8 1.7 %collective-permute-done.11.refs_0_ = bf16[4,32,896]{2,1,0:T(8,128)(2,1)S(1)} collective-permute-done((bf16[4,32,896]{2,1,0:T(8,128)(2,1)S(1)}, bf16[4,32,896]{2,1,0:T(8,128)(2,1)S(1)}, u32[]{:S(2)}, u32[]{:S(2)}) %collective-permute-start.11) | collective-permute-done | bytes 229408 | tf_op jit(solution)/shard_map/ppermute | solution.py:385
  34.6 1.3 %encode.5 = bf16[4,32,896]{2,1,0:T(8,128)(2,1)S(1)} custom-call(s32[16]{0:T(128)S(1)} %get-tuple-element.55.req_ref, bf16[512,896]{1,0:T(8,128)(2,1)S(1)} %copy-done.4, bf16[4,32,896]{2,1,0:T(8,128)(2,1)S(1)} %collective-permute-done.11.refs_0_), custom_call_target="tpu_custom_call" | custom-call | flops 10000000000 | bytes 1024 | tf_op jit(solution)/shard_map/encode/pallas_call | solution.py:186
  35.8 0.6 collective-permute-start.14
  36.6 1.3 %project.5.refs_0_ = bf16[4,4,32,1024]{3,2,1,0:T(8,128)(2,1)S(1)} custom-call(bf16[2,4,32,896]{3,2,1,0:T(8,128)(2,1)S(1)} %pad_maximum_fusion.refs_0_, bf16[2,4,32,896]{3,2,1,0:T(8,128)(2,1)S(1)} %collective-permute-done.7.refs_1_, bf16[896,512]{1,0:T(8,128)(2,1)S(1)} %copy-done.2, bf16[896,512]{1,0:T(8,128)(2,1)S(1)} %copy-done.3), custom_call_target="tpu_custom_call" | custom-call | flops 10000000000 | bytes 1024 | tf_op jit(solution)/shard_map/project/pallas_call | solution.py:238
  37.9 0.5 collective-permute-start.13
  38.4 1.3 %project.6.refs_1_ = bf16[4,4,32,1024]{3,2,1,0:T(8,128)(2,1)S(1)} custom-call(bf16[2,4,32,896]{3,2,1,0:T(8,128)(2,1)S(1)} %pad_maximum_fusion.1.refs_0_, bf16[2,4,32,896]{3,2,1,0:T(8,128)(2,1)S(1)} %collective-permute-done.9.refs_1_, bf16[896,512]{1,0:T(8,128)(2,1)S(1)} %copy-done.2, bf16[896,512]{1,0:T(8,128)(2,1)S(1)} %copy-done.3), custom_call_target="tpu_custom_call" | custom-call | flops 10000000000 | bytes 1024 | tf_op jit(solution)/shard_map/project/pallas_call | solution.py:238
  39.7 1.3 %project.7.refs_2_ = bf16[4,4,32,1024]{3,2,1,0:T(8,128)(2,1)S(1)} custom-call(bf16[2,4,32,896]{3,2,1,0:T(8,128)(2,1)S(1)} %pad_maximum_fusion.2.refs_0_, bf16[2,4,32,896]{3,2,1,0:T(8,128)(2,1)S(1)} %collective-permute-done.12.refs_1_, bf16[896,512]{1,0:T(8,128)(2,1)S(1)} %copy-done.2, bf16[896,512]{1,0:T(8,128)(2,1)S(1)} %copy-done.3), custom_call_target="tpu_custom_call" | custom-call | flops 10000000000 | bytes 1024 | tf_op jit(solution)/shard_map/project/pallas_call | solution.py:238
  41.0 0.7 project.8.refs_3_
  42.6 1.0 %collective-permute-done.15.refs_5_ = bf16[1,4,32,896]{3,2,1,0:T(8,128)(2,1)S(1)} collective-permute-done((bf16[1,4,32,896]{3,2,1,0:T(8,128)(2,1)S(1)}, bf16[1,4,32,896]{3,2,1,0:T(8,128)(2,1)S(1)}, u32[]{:S(2)}, u32[]{:S(2)}) %collective-permute-start.15) | collective-permute-done | bytes 229408 | tf_op jit(solution)/shard_map/ppermute | solution.py:365
  43.7 1.9 %attend.4 = (bf16[1,128,512]{2,1,0:T(8,128)(2,1)S(1)}, bf16[4,1,32,1024]{3,2,1,0:T(8,128)(2,1)S(1)}) custom-call(s32[16]{0:T(128)S(1)} %get-tuple-element.54.slot_ref, bf16[512,512]{1,0:T(8,128)(2,1)S(1)} %copy-done.1, bf16[4,4,32,1024]{3,2,1,0:T(8,128)(2,1)S(1)} %project.5.refs_0_, bf16[4,4,32,1024]{3,2,1,0:T(8,128)(2,1)S(1)} %project.6.refs_1_, ...), custom_call_target="tpu_custom_call" | custom-call | flops 1000000 | bytes 1024 | tf_op jit(solution)/shard_map/attend/pallas_call | solution.py:309
  45.7 1.5 %attend.5.refs_0_ = bf16[1,128,512]{2,1,0:T(8,128)(2,1)S(1)} custom-call(s32[16]{0:T(128)S(1)} %get-tuple-element.54.slot_ref, bf16[512,512]{1,0:T(8,128)(2,1)S(1)} %copy-done.1, bf16[4,4,32,1024]{3,2,1,0:T(8,128)(2,1)S(1)} %project.5.refs_0_, bf16[4,4,32,1024]{3,2,1,0:T(8,128)(2,1)S(1)} %project.6.refs_1_, bf16[4,4,32,1024]{3,2,1,0:T(8,128)(2,1)S(1)} %project.7.refs_2_, ...), custom_call_target="tpu_custom_call" | custom-call | flops 1000000 | bytes 1024 | tf_op jit(solution)/shard_map/attend/pallas_call | solution.py:309
  47.3 1.0 %out_project.6 = bf16[128,1024]{1,0:T(8,128)(2,1)S(1)} custom-call(bf16[1,128,512]{2,1,0:T(8,128)(2,1)S(1)} %attend.5.refs_0_, bf16[1,128,512]{2,1,0:T(8,128)(2,1)S(1)} %collective-permute-done.16.refs_1_, bf16[512,4096]{1,0:T(8,128)(2,1)S(1)} %copy-done, bf16[512,4096]{1,0:T(8,128)(2,1)S(1)} %collective-permute-done.17.refs_3_), custom_call_target="tpu_custom_call" | custom-call | flops 1000000 | bytes 1024 | tf_op jit(solution)/shard_map/out_project/pallas_call | solution.py:334
  48.3 1.2 %collective-permute-start.23 = (bf16[128,1024]{1,0:T(8,128)(2,1)S(1)}, bf16[128,1024]{1,0:T(8,128)(2,1)S(1)}, u32[]{:S(2)}, u32[]{:S(2)}) collective-permute-start(bf16[128,1024]{1,0:T(8,128)(2,1)S(1)} %out_project.6), channel_id=1, source_target_pairs={{0,2},{2,0},{1,3},{3,1},{4,6},{6,4},{5,7},{7,5},{8,10},{10,8},{9,1... | collective-permute-start | bytes 786440 | tf_op jit(solution)/shard_map/ppermute | solution.py:441
  49.5 0.9 %out_project.7 = bf16[128,1024]{1,0:T(8,128)(2,1)S(1)} custom-call(bf16[1,128,512]{2,1,0:T(8,128)(2,1)S(1)} %attend.5.refs_0_, bf16[1,128,512]{2,1,0:T(8,128)(2,1)S(1)} %collective-permute-done.16.refs_1_, bf16[512,4096]{1,0:T(8,128)(2,1)S(1)} %copy-done, bf16[512,4096]{1,0:T(8,128)(2,1)S(1)} %collective-permute-done.17.refs_3_), custom_call_target="tpu_custom_call" | custom-call | flops 1000000 | bytes 1024 | tf_op jit(solution)/shard_map/out_project/pallas_call | solution.py:334
  50.4 1.0 %collective-permute-start.22 = (bf16[128,1024]{1,0:T(8,128)(2,1)S(1)}, bf16[128,1024]{1,0:T(8,128)(2,1)S(1)}, u32[]{:S(2)}, u32[]{:S(2)}) collective-permute-start(bf16[128,1024]{1,0:T(8,128)(2,1)S(1)} %out_project.7), channel_id=1, source_target_pairs={{0,2},{2,0},{1,3},{3,1},{4,6},{6,4},{5,7},{7,5},{8,10},{10,8},{9,1... | collective-permute-start | bytes 786440 | tf_op jit(solution)/shard_map/ppermute | solution.py:441
  51.3 0.9 %out_project.8 = bf16[128,1024]{1,0:T(8,128)(2,1)S(1)} custom-call(bf16[1,128,512]{2,1,0:T(8,128)(2,1)S(1)} %attend.5.refs_0_, bf16[1,128,512]{2,1,0:T(8,128)(2,1)S(1)} %collective-permute-done.16.refs_1_, bf16[512,4096]{1,0:T(8,128)(2,1)S(1)} %copy-done, bf16[512,4096]{1,0:T(8,128)(2,1)S(1)} %collective-permute-done.17.refs_3_), custom_call_target="tpu_custom_call" | custom-call | flops 1000000 | bytes 1024 | tf_op jit(solution)/shard_map/out_project/pallas_call | solution.py:334
  52.2 1.2 %collective-permute-start.21 = (bf16[128,1024]{1,0:T(8,128)(2,1)S(1)}, bf16[128,1024]{1,0:T(8,128)(2,1)S(1)}, u32[]{:S(2)}, u32[]{:S(2)}) collective-permute-start(bf16[128,1024]{1,0:T(8,128)(2,1)S(1)} %out_project.8), channel_id=1, source_target_pairs={{0,2},{2,0},{1,3},{3,1},{4,6},{6,4},{5,7},{7,5},{8,10},{10,8},{9,1... | collective-permute-start | bytes 786440 | tf_op jit(solution)/shard_map/ppermute | solution.py:441
  54.0 1.5 %attend.7 = bf16[1,128,512]{2,1,0:T(8,128)(2,1)S(1)} custom-call(s32[16]{0:T(128)S(1)} %get-tuple-element.54.slot_ref, bf16[512,512]{1,0:T(8,128)(2,1)S(1)} %copy-done.1, bf16[4,4,32,1024]{3,2,1,0:T(8,128)(2,1)S(1)} %project.5.refs_0_, bf16[4,4,32,1024]{3,2,1,0:T(8,128)(2,1)S(1)} %project.6.refs_1_, bf16[4,4,32,1024]{3,2,1,0:T(8,128)(2,1)S(1)} %project.7.refs_2_, ...), custom_call_target="tpu_custom_call" | custom-call | flops 1000000 | bytes 1024 | tf_op jit(solution)/shard_map/attend/pallas_call | solution.py:309
  55.6 1.0 %collective-permute-start.20 = (bf16[128,512]{1,0:T(8,128)(2,1)S(1)}, bf16[128,512]{1,0:T(8,128)(2,1)S(1)}, u32[]{:S(2)}, u32[]{:S(2)}) collective-permute-start(bf16[128,512]{1,0:T(8,128)(2,1)S(1)} %out_project.9), channel_id=1, source_target_pairs={{0,2},{2,0},{1,3},{3,1},{4,6},{6,4},{5,7},{7,5},{8,10},{10,8},{9,1... | collective-permute-start | bytes 393224 | tf_op jit(solution)/shard_map/ppermute | solution.py:441
  56.9 0.9 %collective-permute-start.19 = (bf16[128,512]{1,0:T(8,128)(2,1)S(1)}, bf16[128,512]{1,0:T(8,128)(2,1)S(1)}, u32[]{:S(2)}, u32[]{:S(2)}) collective-permute-start(bf16[128,512]{1,0:T(8,128)(2,1)S(1)} %out_project.10), channel_id=1, source_target_pairs={{0,2},{2,0},{1,3},{3,1},{4,6},{6,4},{5,7},{7,5},{8,10},{10,8},{9,1... | collective-permute-start | bytes 393224 | tf_op jit(solution)/shard_map/ppermute | solution.py:441
  57.9 1.5 %attend.6.refs_0_ = bf16[1,128,512]{2,1,0:T(8,128)(2,1)S(1)} custom-call(s32[16]{0:T(128)S(1)} %get-tuple-element.54.slot_ref, bf16[512,512]{1,0:T(8,128)(2,1)S(1)} %copy-done.1, bf16[4,4,32,1024]{3,2,1,0:T(8,128)(2,1)S(1)} %project.5.refs_0_, bf16[4,4,32,1024]{3,2,1,0:T(8,128)(2,1)S(1)} %project.6.refs_1_, bf16[4,4,32,1024]{3,2,1,0:T(8,128)(2,1)S(1)} %project.7.refs_2_, ...), custom_call_target="tpu_custom_call" | custom-call | flops 1000000 | bytes 1024 | tf_op jit(solution)/shard_map/attend/pallas_call | solution.py:309
  59.7 1.5 %out_final.5.refs_5_ = bf16[128,4096]{1,0:T(8,128)(2,1)} custom-call(bf16[1,128,512]{2,1,0:T(8,128)(2,1)S(1)} %attend.6.refs_0_, bf16[1,128,512]{2,1,0:T(8,128)(2,1)S(1)} %collective-permute-done.18.refs_1_, bf16[512,4096]{1,0:T(8,128)(2,1)S(1)} %copy-done, bf16[512,4096]{1,0:T(8,128)(2,1)S(1)} %collective-permute-done.17.refs_3_, ...), custom_call_target="tpu_custom_call" | custom-call | flops 200000000 | bytes 1024 | tf_op jit(solution)/shard_map/out_final/pallas_call | solution.py:334
  61.2 1.9 %collective-permute-done.22.refs_4_ = bf16[128,1024]{1,0:T(8,128)(2,1)S(1)} collective-permute-done((bf16[128,1024]{1,0:T(8,128)(2,1)S(1)}, bf16[128,1024]{1,0:T(8,128)(2,1)S(1)}, u32[]{:S(2)}, u32[]{:S(2)}) %collective-permute-start.22) | collective-permute-done | bytes 262176 | tf_op jit(solution)/shard_map/ppermute | solution.py:441
  63.1 1.5 %out_final.6.refs_5_ = bf16[128,4096]{1,0:T(8,128)(2,1)} custom-call(bf16[1,128,512]{2,1,0:T(8,128)(2,1)S(1)} %attend.6.refs_0_, bf16[1,128,512]{2,1,0:T(8,128)(2,1)S(1)} %collective-permute-done.18.refs_1_, bf16[512,4096]{1,0:T(8,128)(2,1)S(1)} %copy-done, bf16[512,4096]{1,0:T(8,128)(2,1)S(1)} %collective-permute-done.17.refs_3_, ...), custom_call_target="tpu_custom_call", output_to_operand_aliasing={{}: (5, {})} | custom-call | flops 200000000 | bytes 1024 | tf_op jit(solution)/shard_map/out_final/pallas_call | solution.py:334
  64.6 4.1 %collective-permute-done.21.refs_4_ = bf16[128,1024]{1,0:T(8,128)(2,1)S(1)} collective-permute-done((bf16[128,1024]{1,0:T(8,128)(2,1)S(1)}, bf16[128,1024]{1,0:T(8,128)(2,1)S(1)}, u32[]{:S(2)}, u32[]{:S(2)}) %collective-permute-start.21) | collective-permute-done | bytes 262176 | tf_op jit(solution)/shard_map/ppermute | solution.py:441
  68.8 1.5 %out_final.7.refs_5_ = bf16[128,4096]{1,0:T(8,128)(2,1)} custom-call(bf16[1,128,512]{2,1,0:T(8,128)(2,1)S(1)} %attend.6.refs_0_, bf16[1,128,512]{2,1,0:T(8,128)(2,1)S(1)} %collective-permute-done.18.refs_1_, bf16[512,4096]{1,0:T(8,128)(2,1)S(1)} %copy-done, bf16[512,4096]{1,0:T(8,128)(2,1)S(1)} %collective-permute-done.17.refs_3_, ...), custom_call_target="tpu_custom_call", output_to_operand_aliasing={{}: (5, {})} | custom-call | flops 200000000 | bytes 1024 | tf_op jit(solution)/shard_map/out_final/pallas_call | solution.py:334
  70.3 1.3 %collective-permute-done.20.refs_4_ = bf16[128,512]{1,0:T(8,128)(2,1)S(1)} collective-permute-done((bf16[128,512]{1,0:T(8,128)(2,1)S(1)}, bf16[128,512]{1,0:T(8,128)(2,1)S(1)}, u32[]{:S(2)}, u32[]{:S(2)}) %collective-permute-start.20) | collective-permute-done | bytes 131104 | tf_op jit(solution)/shard_map/ppermute | solution.py:441
  71.6 1.0 %out_final.8.refs_2_ = bf16[128,4096]{1,0:T(8,128)(2,1)} custom-call(bf16[1,128,512]{2,1,0:T(8,128)(2,1)S(1)} %attend.6.refs_0_, bf16[1,128,512]{2,1,0:T(8,128)(2,1)S(1)} %collective-permute-done.18.refs_1_, bf16[512,4096]{1,0:T(8,128)(2,1)S(1)} %copy-done, bf16[512,4096]{1,0:T(8,128)(2,1)S(1)} %collective-permute-done.17.refs_3_, ...), custom_call_target="tpu_custom_call", output_to_operand_aliasing={{}: (5, {})} | custom-call | flops 200000000 | bytes 1024 | tf_op jit(solution)/shard_map/out_final/pallas_call | solution.py:334
  72.5 1.3 %collective-permute-done.19.refs_1_ = bf16[128,512]{1,0:T(8,128)(2,1)S(1)} collective-permute-done((bf16[128,512]{1,0:T(8,128)(2,1)S(1)}, bf16[128,512]{1,0:T(8,128)(2,1)S(1)}, u32[]{:S(2)}, u32[]{:S(2)}) %collective-permute-start.19) | collective-permute-done | bytes 131104 | tf_op jit(solution)/shard_map/ppermute | solution.py:441
  73.8 0.7 out_final.9
  (42 shorter events, 2.9 us)
Async XLA Ops:
  0.7 7.0 %copy-start.4 = (bf16[512,896]{1,0:T(8,128)(2,1)S(1)}, bf16[512,896]{1,0:T(8,128)(2,1)}, u32[]{:S(2)}) copy-start(bf16[512,896]{1,0:T(8,128)(2,1)} %states_ref.7) | copy-start | bytes 2752516
  0.7 7.0 %copy-start.5 = (bf16[16,32,896]{2,1,0:T(8,128)(2,1)S(1)}, bf16[16,32,896]{2,1,0:T(8,128)(2,1)}, u32[]{:S(2)}) copy-start(bf16[16,32,896]{2,1,0:T(8,128)(2,1)} %refs_3_.5) | copy-start | bytes 2752516
  0.7 8.3 %collective-permute-start.3 = (s32[4,8]{1,0:T(4,128)S(1)}, s32[4,8]{1,0:T(4,128)S(1)}, u32[]{:S(2)}, u32[]{:S(2)}) collective-permute-start(s32[4,8]{1,0:T(4,128)S(1)} %pad_add_fusion.own_ref), channel_id=1, source_target_pairs={{0,12},{4,8},{8,4},{12,0},{1,13},{5,9},{9,5},{13,1},{2,14},{6,10},... | collective-permute-start | bytes 392 | tf_op jit(solution)/shard_map/ppermute | solution.py:377
  5.8 4.5 %collective-permute-start.2 = (s32[4,8]{1,0:T(4,128)S(1)}, s32[4,8]{1,0:T(4,128)S(1)}, u32[]{:S(2)}, u32[]{:S(2)}) collective-permute-start(s32[4,8]{1,0:T(4,128)S(1)} %pad_add_fusion.own_ref), channel_id=1, source_target_pairs={{0,8},{4,12},{8,0},{12,4},{1,9},{5,13},{9,1},{13,5},{2,10},{6,14},... | collective-permute-start | bytes 392 | tf_op jit(solution)/shard_map/ppermute | solution.py:377
  5.8 4.5 %collective-permute-start.1 = (s32[4,8]{1,0:T(4,128)S(1)}, s32[4,8]{1,0:T(4,128)S(1)}, u32[]{:S(2)}, u32[]{:S(2)}) collective-permute-start(s32[4,8]{1,0:T(4,128)S(1)} %pad_add_fusion.own_ref), channel_id=1, source_target_pairs={{0,4},{4,0},{8,12},{12,8},{1,5},{5,1},{9,13},{13,9},{2,6},{6,2},{1... | collective-permute-start | bytes 392 | tf_op jit(solution)/shard_map/ppermute | solution.py:377
  9.0 7.7 %copy-start = (bf16[512,4096]{1,0:T(8,128)(2,1)S(1)}, bf16[512,4096]{1,0:T(8,128)(2,1)}, u32[]{:S(2)}) copy-start(bf16[512,4096]{1,0:T(8,128)(2,1)} %refs_2_.29) | copy-start | bytes 12582916
  11.1 15.5 %collective-permute-start.4 = (bf16[4,32,896]{2,1,0:T(8,128)(2,1)S(1)}, bf16[4,32,896]{2,1,0:T(8,128)(2,1)S(1)}, u32[]{:S(2)}, u32[]{:S(2)}) collective-permute-start(bf16[4,32,896]{2,1,0:T(8,128)(2,1)S(1)} %get-tuple-element.60), channel_id=1, source_target_pairs={{0,8},{4,12},{8,0},{12,4},{1,9},{5,13},{9,1},{13,5},{2,10},{6,14},... | collective-permute-start | bytes 688136 | tf_op jit(solution)/shard_map/ppermute | solution.py:385
  13.2 7.0 %collective-permute-start.5 = (bf16[2,32,896]{2,1,0:T(8,128)(2,1)S(1)}, bf16[2,32,896]{2,1,0:T(8,128)(2,1)S(1)}, u32[]{:S(2)}, u32[]{:S(2)}) collective-permute-start(bf16[2,32,896]{2,1,0:T(8,128)(2,1)S(1)} %get-tuple-element.63), channel_id=1, source_target_pairs={{0,4},{4,0},{8,12},{12,8},{1,5},{5,1},{9,13},{13,9},{2,6},{6,2},{1... | collective-permute-start | bytes 344072 | tf_op jit(solution)/shard_map/ppermute | solution.py:385
  14.3 9.3 %collective-permute-start.6 = (bf16[2,32,896]{2,1,0:T(8,128)(2,1)S(1)}, bf16[2,32,896]{2,1,0:T(8,128)(2,1)S(1)}, u32[]{:S(2)}, u32[]{:S(2)}) collective-permute-start(bf16[2,32,896]{2,1,0:T(8,128)(2,1)S(1)} %get-tuple-element.64), channel_id=1, source_target_pairs={{0,4},{4,0},{8,12},{12,8},{1,5},{5,1},{9,13},{13,9},{2,6},{6,2},{1... | collective-permute-start | bytes 344072 | tf_op jit(solution)/shard_map/ppermute | solution.py:385
  15.2 13.3 %collective-permute-start = (bf16[4,32,896]{2,1,0:T(8,128)(2,1)S(1)}, bf16[4,32,896]{2,1,0:T(8,128)(2,1)S(1)}, u32[]{:S(2)}, u32[]{:S(2)}) collective-permute-start(bf16[4,32,896]{2,1,0:T(8,128)(2,1)S(1)} %encode_local.1), channel_id=1, source_target_pairs={{0,2},{2,0},{1,3},{3,1},{4,6},{6,4},{5,7},{7,5},{8,10},{10,8},{9,1... | collective-permute-start | bytes 688136 | tf_op jit(solution)/shard_map/ppermute | solution.py:362
  16.7 30.5 %collective-permute-start.17 = (bf16[512,4096]{1,0:T(8,128)(2,1)S(1)}, bf16[512,4096]{1,0:T(8,128)(2,1)S(1)}, u32[]{:S(2)}, u32[]{:S(2)}) collective-permute-start(bf16[512,4096]{1,0:T(8,128)(2,1)S(1)} %copy-done), channel_id=1, source_target_pairs={{0,1},{1,0},{2,3},{3,2},{4,5},{5,4},{6,7},{7,6},{8,9},{9,8},{10,11... | collective-permute-start | bytes 12582920 | tf_op jit(solution)/shard_map/ppermute | solution.py:365
  25.1 7.6 %collective-permute-start.8 = (bf16[4,32,896]{2,1,0:T(8,128)(2,1)S(1)}, bf16[4,32,896]{2,1,0:T(8,128)(2,1)S(1)}, u32[]{:S(2)}, u32[]{:S(2)}) collective-permute-start(bf16[4,32,896]{2,1,0:T(8,128)(2,1)S(1)} %encode.3), channel_id=1, source_target_pairs={{0,2},{2,0},{1,3},{3,1},{4,6},{6,4},{5,7},{7,5},{8,10},{10,8},{9,1... | collective-permute-start | bytes 688136 | tf_op jit(solution)/shard_map/ppermute | solution.py:362
  26.6 7.9 %collective-permute-start.11 = (bf16[4,32,896]{2,1,0:T(8,128)(2,1)S(1)}, bf16[4,32,896]{2,1,0:T(8,128)(2,1)S(1)}, u32[]{:S(2)}, u32[]{:S(2)}) collective-permute-start(bf16[4,32,896]{2,1,0:T(8,128)(2,1)S(1)} %get-tuple-element.77), channel_id=1, source_target_pairs={{0,12},{4,8},{8,4},{12,0},{1,13},{5,9},{9,5},{13,1},{2,14},{6,10},... | collective-permute-start | bytes 688136 | tf_op jit(solution)/shard_map/ppermute | solution.py:385
  27.9 8.5 %collective-permute-start.10 = (bf16[4,32,896]{2,1,0:T(8,128)(2,1)S(1)}, bf16[4,32,896]{2,1,0:T(8,128)(2,1)S(1)}, u32[]{:S(2)}, u32[]{:S(2)}) collective-permute-start(bf16[4,32,896]{2,1,0:T(8,128)(2,1)S(1)} %encode.4), channel_id=1, source_target_pairs={{0,2},{2,0},{1,3},{3,1},{4,6},{6,4},{5,7},{7,5},{8,10},{10,8},{9,1... | collective-permute-start | bytes 688136 | tf_op jit(solution)/shard_map/ppermute | solution.py:362
  28.6 8.0 %collective-permute-start.7 = (bf16[2,4,32,896]{3,2,1,0:T(8,128)(2,1)S(1)}, bf16[2,4,32,896]{3,2,1,0:T(8,128)(2,1)S(1)}, u32[]{:S(2)}, u32[]{:S(2)}) collective-permute-start(bf16[2,4,32,896]{3,2,1,0:T(8,128)(2,1)S(1)} %pad_maximum_fusion.refs_0_), channel_id=1, source_target_pairs={{0,1},{1,0},{2,3},{3,2},{4,5},{5,4},{6,7},{7,6},{8,9},{9,8},{10,11... | collective-permute-start | bytes 1376264 | tf_op jit(solution)/shard_map/ppermute | solution.py:365
  32.7 3.8 %copy-start.2 = (bf16[896,512]{1,0:T(8,128)(2,1)S(1)}, bf16[896,512]{1,0:T(8,128)(2,1)}, u32[]{:S(2)}) copy-start(bf16[896,512]{1,0:T(8,128)(2,1)} %refs_6_.1) | copy-start | bytes 2752516
  32.7 3.8 %copy-start.3 = (bf16[896,512]{1,0:T(8,128)(2,1)S(1)}, bf16[896,512]{1,0:T(8,128)(2,1)}, u32[]{:S(2)}) copy-start(bf16[896,512]{1,0:T(8,128)(2,1)} %refs_7_.1) | copy-start | bytes 2752516
  32.7 5.7 %collective-permute-start.9 = (bf16[2,4,32,896]{3,2,1,0:T(8,128)(2,1)S(1)}, bf16[2,4,32,896]{3,2,1,0:T(8,128)(2,1)S(1)}, u32[]{:S(2)}, u32[]{:S(2)}) collective-permute-start(bf16[2,4,32,896]{3,2,1,0:T(8,128)(2,1)S(1)} %pad_maximum_fusion.1.refs_0_), channel_id=1, source_target_pairs={{0,1},{1,0},{2,3},{3,2},{4,5},{5,4},{6,7},{7,6},{8,9},{9,8},{10,11... | collective-permute-start | bytes 1376264 | tf_op jit(solution)/shard_map/ppermute | solution.py:365
  35.8 6.3 %collective-permute-start.14 = (bf16[4,32,896]{2,1,0:T(8,128)(2,1)S(1)}, bf16[4,32,896]{2,1,0:T(8,128)(2,1)S(1)}, u32[]{:S(2)}, u32[]{:S(2)}) collective-permute-start(bf16[4,32,896]{2,1,0:T(8,128)(2,1)S(1)} %encode.5), channel_id=1, source_target_pairs={{0,2},{2,0},{1,3},{3,1},{4,6},{6,4},{5,7},{7,5},{8,10},{10,8},{9,1... | collective-permute-start | bytes 688136 | tf_op jit(solution)/shard_map/ppermute | solution.py:362
  36.5 3.2 %collective-permute-start.12 = (bf16[2,4,32,896]{3,2,1,0:T(8,128)(2,1)S(1)}, bf16[2,4,32,896]{3,2,1,0:T(8,128)(2,1)S(1)}, u32[]{:S(2)}, u32[]{:S(2)}) collective-permute-start(bf16[2,4,32,896]{3,2,1,0:T(8,128)(2,1)S(1)} %pad_maximum_fusion.2.refs_0_), channel_id=1, source_target_pairs={{0,1},{1,0},{2,3},{3,2},{4,5},{5,4},{6,7},{7,6},{8,9},{9,8},{10,11... | collective-permute-start | bytes 1376264 | tf_op jit(solution)/shard_map/ppermute | solution.py:365
  37.9 3.1 %collective-permute-start.13 = (bf16[4,32,896]{2,1,0:T(8,128)(2,1)S(1)}, bf16[4,32,896]{2,1,0:T(8,128)(2,1)S(1)}, u32[]{:S(2)}, u32[]{:S(2)}) collective-permute-start(bf16[4,32,896]{2,1,0:T(8,128)(2,1)S(1)} %encode.5), channel_id=1, source_target_pairs={{0,1},{1,0},{2,3},{3,2},{4,5},{5,4},{6,7},{7,6},{8,9},{9,8},{10,11... | collective-permute-start | bytes 688136 | tf_op jit(solution)/shard_map/ppermute | solution.py:365
  42.2 1.5 %copy-start.1 = (bf16[512,512]{1,0:T(8,128)(2,1)S(1)}, bf16[512,512]{1,0:T(8,128)(2,1)}, u32[]{:S(2)}) copy-start(bf16[512,512]{1,0:T(8,128)(2,1)} %q_ref.5) | copy-start | bytes 1572868
  42.2 1.5 %collective-permute-start.15 = (bf16[1,4,32,896]{3,2,1,0:T(8,128)(2,1)S(1)}, bf16[1,4,32,896]{3,2,1,0:T(8,128)(2,1)S(1)}, u32[]{:S(2)}, u32[]{:S(2)}) collective-permute-start(bf16[1,4,32,896]{3,2,1,0:T(8,128)(2,1)S(1)} %bitcast.14), channel_id=1, source_target_pairs={{0,1},{1,0},{2,3},{3,2},{4,5},{5,4},{6,7},{7,6},{8,9},{9,8},{10,11... | collective-permute-start | bytes 688136 | tf_op jit(solution)/shard_map/ppermute | solution.py:365
  45.5 1.7 %collective-permute-start.16 = (bf16[1,128,512]{2,1,0:T(8,128)(2,1)S(1)}, bf16[1,128,512]{2,1,0:T(8,128)(2,1)S(1)}, u32[]{:S(2)}, u32[]{:S(2)}) collective-permute-start(bf16[1,128,512]{2,1,0:T(8,128)(2,1)S(1)} %get-tuple-element.88), channel_id=1, source_target_pairs={{0,1},{1,0},{2,3},{3,2},{4,5},{5,4},{6,7},{7,6},{8,9},{9,8},{10,11... | collective-permute-start | bytes 393224 | tf_op jit(solution)/shard_map/ppermute | solution.py:424
  48.3 11.4 %collective-permute-start.23 = (bf16[128,1024]{1,0:T(8,128)(2,1)S(1)}, bf16[128,1024]{1,0:T(8,128)(2,1)S(1)}, u32[]{:S(2)}, u32[]{:S(2)}) collective-permute-start(bf16[128,1024]{1,0:T(8,128)(2,1)S(1)} %out_project.6), channel_id=1, source_target_pairs={{0,2},{2,0},{1,3},{3,1},{4,6},{6,4},{5,7},{7,5},{8,10},{10,8},{9,1... | collective-permute-start | bytes 786440 | tf_op jit(solution)/shard_map/ppermute | solution.py:441
  50.4 12.8 %collective-permute-start.22 = (bf16[128,1024]{1,0:T(8,128)(2,1)S(1)}, bf16[128,1024]{1,0:T(8,128)(2,1)S(1)}, u32[]{:S(2)}, u32[]{:S(2)}) collective-permute-start(bf16[128,1024]{1,0:T(8,128)(2,1)S(1)} %out_project.7), channel_id=1, source_target_pairs={{0,2},{2,0},{1,3},{3,1},{4,6},{6,4},{5,7},{7,5},{8,10},{10,8},{9,1... | collective-permute-start | bytes 786440 | tf_op jit(solution)/shard_map/ppermute | solution.py:441
  52.2 16.6 %collective-permute-start.21 = (bf16[128,1024]{1,0:T(8,128)(2,1)S(1)}, bf16[128,1024]{1,0:T(8,128)(2,1)S(1)}, u32[]{:S(2)}, u32[]{:S(2)}) collective-permute-start(bf16[128,1024]{1,0:T(8,128)(2,1)S(1)} %out_project.8), channel_id=1, source_target_pairs={{0,2},{2,0},{1,3},{3,1},{4,6},{6,4},{5,7},{7,5},{8,10},{10,8},{9,1... | collective-permute-start | bytes 786440 | tf_op jit(solution)/shard_map/ppermute | solution.py:441
  55.5 1.4 %collective-permute-start.18 = (bf16[1,128,512]{2,1,0:T(8,128)(2,1)S(1)}, bf16[1,128,512]{2,1,0:T(8,128)(2,1)S(1)}, u32[]{:S(2)}, u32[]{:S(2)}) collective-permute-start(bf16[1,128,512]{2,1,0:T(8,128)(2,1)S(1)} %attend.7), channel_id=1, source_target_pairs={{0,1},{1,0},{2,3},{3,2},{4,5},{5,4},{6,7},{7,6},{8,9},{9,8},{10,11... | collective-permute-start | bytes 393224 | tf_op jit(solution)/shard_map/ppermute | solution.py:424
  55.6 16.0 %collective-permute-start.20 = (bf16[128,512]{1,0:T(8,128)(2,1)S(1)}, bf16[128,512]{1,0:T(8,128)(2,1)S(1)}, u32[]{:S(2)}, u32[]{:S(2)}) collective-permute-start(bf16[128,512]{1,0:T(8,128)(2,1)S(1)} %out_project.9), channel_id=1, source_target_pairs={{0,2},{2,0},{1,3},{3,1},{4,6},{6,4},{5,7},{7,5},{8,10},{10,8},{9,1... | collective-permute-start | bytes 393224 | tf_op jit(solution)/shard_map/ppermute | solution.py:441
  56.9 16.9 %collective-permute-start.19 = (bf16[128,512]{1,0:T(8,128)(2,1)S(1)}, bf16[128,512]{1,0:T(8,128)(2,1)S(1)}, u32[]{:S(2)}, u32[]{:S(2)}) collective-permute-start(bf16[128,512]{1,0:T(8,128)(2,1)S(1)} %out_project.10), channel_id=1, source_target_pairs={{0,2},{2,0},{1,3},{3,1},{4,6},{6,4},{5,7},{7,5},{8,10},{10,8},{9,1... | collective-permute-start | bytes 393224 | tf_op jit(solution)/shard_map/ppermute | solution.py:441

commit v13 on v12

--- a/solution.py
+++ b/solution.py
@@ -38,6 +38,18 @@
     if n & (n - 1) == 0:
         return [(i, i ^ d) for i in range(n)]
     return [(i, (i - d if reply else i + d) % n) for i in range(n)]
+
+
+def tables_of_lanes(own, n, meanwhile):
+    if n & (n - 1):
+        others = [lax.ppermute(own, "lanes", lane_pairs(n, d, False)) for d in range(1, n)]
+        return jnp.concatenate([own] + others, axis=0)
+    step, held = 1, own
+    while step < n:
+        other = lax.ppermute(held, "lanes", lane_pairs(n, step, False))
+        held = jnp.concatenate(after([held, other], meanwhile if step == 1 else ()), axis=0)
+        step *= 2
+    return held
 
 
 def shift_pairs(n, s):
@@ -85,39 +97,38 @@
     )(own)
 
 
-def fetch_kernel(items, cap, *refs):
-    others = max(d for d, _, _ in items)
-    asked, store_ref, refs = refs[:others], refs[others], refs[others + 1 :]
+def fetch_kernel(items, cap, fanout, tables_ref, store_ref, *refs):
     blocks, pick_ref = refs[:-1], refs[-1]
     lane = lax.axis_index("lanes")
-    fanout, spans = asked[0].shape[0] // 2, asked[0].shape[1]
+    spans = tables_ref.shape[1]
+    others = tables_ref.shape[0] // (2 * fanout) - 1
     for i in range(others * cap):
         pick_ref[i] = 0
     for d in range(others):
-        place = d * cap
+        place, row = d * cap, (d + 1) * 2 * fanout
         for span in range(spans):
             for k in range(fanout):
-                pick_ref[place] = asked[d][fanout + k, span]
-                place = place + (asked[d][k, span] == lane).astype(jnp.int32)
+                pick_ref[place] = tables_ref[row + fanout + k, span]
+                place = place + (tables_ref[row + k, span] == lane).astype(jnp.int32)
     for block, (d, low, high) in zip(blocks, items):
         for s in range(low, high):
             block[s - low] = store_ref[pick_ref[(d - 1) * cap + s]]
 
 
-def fetch(asked, store, items, cap):
-    others = len(asked)
-    return pl.pallas_call(
-        functools.partial(fetch_kernel, items, cap),
+def fetch(tables, store, items, cap, fanout):
+    others = tables.shape[0] // (2 * fanout) - 1
+    return pl.pallas_call(
+        functools.partial(fetch_kernel, items, cap, fanout),
         out_shape=[
             jax.ShapeDtypeStruct((high - low,) + store.shape[1:], store.dtype) for _, low, high in items
         ],
-        in_specs=[SMEM] * others + [VMEM],
+        in_specs=[SMEM, VMEM],
         out_specs=[VMEM] * len(items),
         scratch_shapes=[pltpu.SMEM((others * cap + 1,), jnp.int32)],
         compiler_params=params(16),
         cost_estimate=cost(10),
         name="fetch",
-    )(*asked, store)
+    )(tables, store)
 
 
 def encode_pairs(width):
@@ -374,10 +385,10 @@
     parts = [range(low, high) for low, high in zip(cuts, cuts[1:])]
 
     own = jnp.concatenate([owners.T, entry_ids.T], axis=0)
-    asked = [lax.ppermute(own, "lanes", lane_pairs(n_lanes, d, False)) for d in range(1, n_lanes)]
     req, slot, pick = plan(own, order, cap)
+    tables = tables_of_lanes(own, n_lanes, req)
     encoded = encode_local(req, pick, span_states, store, cap, fanout, span_len)
-    blocks = fetch(after(asked, encoded), store, items, cap)
+    blocks = fetch(after(tables, encoded), store, items, cap, fanout)
 
     def send(part, *earlier):
         ready = after([blocks[i] for i in part], *earlier)

time: 74.7 us -> 73.7 us (0.987)
  waiting for transfers between devices: 24.4 us -> 21.6 us
  starting transfers between devices: 20.4 us -> 22.2 us
    ppermute x4, waiting for transfers between devices: 4.52 us -> 2.96 us  [over_heads(): lax.ppermute(array, 'heads', shift_pairs(n_heads, s))]
    ppermute x4, starting transfers between devices: 4.12 us -> 5.63 us  [send(): lax.ppermute(block, 'lanes', lane_pairs(n_lanes, items[i][0], True))]
    ppermute x3 -> x2, starting transfers between devices: 5.76 us -> 6.18 us  [tables_of_lanes(): other = lax.ppermute(held, 'lanes', lane_pairs(n, step, False))]
  transfers between devices with their start and end apart: 24 -> 23, of which waited for: 12 -> 13; matrix products, arithmetic and copies ran while one was open for 0% -> 0% of each run, Pallas kernels for 35% -> 35%
where the time goes in v13:
time: 73.7 us; the launch traced here: 73.5 us
  Pallas kernels  28.5 us (39%)
  starting transfers between devices  22.2 us (30%)
  waiting for transfers between devices  21.6 us (29%)
  other arithmetic  0.86 us (1%)
    pallas_call x11, Pallas kernels, out_project(): pl.pallas_call(functools.partial(out_kernel, n, len(received)), grid=((st...  9.83 us
    ppermute x5, waiting for transfers between devices, shards(): received[i].append(lax.ppermute(partial, 'heads', shift_pairs(n_heads, t)))  8.55 us
    ppermute x4, waiting for transfers between devices, send(): lax.ppermute(block, 'lanes', lane_pairs(n_lanes, items[i][0], True))  7.87 us
    pallas_call x4, Pallas kernels, attend(): pl.pallas_call(functools.partial(attend_kernel, firsts, len(own), n_heads...  6.43 us
    ppermute x2, starting transfers between devices, tables_of_lanes(): other = lax.ppermute(held, 'lanes', lane_pairs(n, step, False))  6.18 us
    ppermute x4, starting transfers between devices, send(): lax.ppermute(block, 'lanes', lane_pairs(n_lanes, items[i][0], True))  5.63 us
    ppermute x5, starting transfers between devices, shards(): received[i].append(lax.ppermute(partial, 'heads', shift_pairs(n_heads, t)))  5.08 us
    pallas_call x5, Pallas kernels, project(): pl.pallas_call(functools.partial(project_kernel, len(pieces)), out_shape=...  4.94 us
  transfers between devices with their start and end apart: 23, of which 13 were waited for; matrix products, arithmetic and copies ran while one was open for 0% of the time, Pallas kernels for 35%

profile of v13, /device:TPU:0, one launch (start us, length us, event | category | flops | bytes accessed | tf_op | source)
XLA Modules:
  0.0 73.5 jit_solution(835837747332739171)
XLA Ops:
  0.0 0.7 pad_add_fusion.2.own_ref
  0.7 3.1 %collective-permute-start.1 = (s32[4,8]{1,0:T(4,128)S(1)}, s32[4,8]{1,0:T(4,128)S(1)}, u32[]{:S(2)}, u32[]{:S(2)}) collective-permute-start(s32[4,8]{1,0:T(4,128)S(1)} %pad_add_fusion.2.own_ref), channel_id=1, source_target_pairs={{0,4},{4,0},{8,12},{12,8},{1,5},{5,1},{9,13},{13,9},{2,6},{6,2},{1... | collective-permute-start | bytes 392 | tf_op jit(solution)/shard_map/ppermute | solution.py:49
  3.8 1.3 %plan.1 = (s32[16]{0:T(128)S(1)}, s32[16]{0:T(128)S(1)}, s32[16]{0:T(128)S(1)}) custom-call(s32[4,8]{1,0:T(4,128)S(1)} %pad_add_fusion.2.own_ref), custom_call_target="tpu_custom_call" | custom-call | flops 10000000000 | bytes 1024 | tf_op jit(solution)/shard_map/plan/pallas_call | solution.py:88
  5.4 3.1 %collective-permute-start.2 = (s32[8,8]{1,0:T(8,128)S(1)}, s32[8,8]{1,0:T(8,128)S(1)}, u32[]{:S(2)}, u32[]{:S(2)}) collective-permute-start(s32[8,8]{1,0:T(8,128)S(1)} %pad_add_fusion.1), channel_id=1, source_target_pairs={{0,8},{4,12},{8,0},{12,4},{1,9},{5,13},{9,1},{13,5},{2,10},{6,14},... | collective-permute-start | bytes 776 | tf_op jit(solution)/shard_map/ppermute | solution.py:49
  8.5 1.3 %encode_local.1 = bf16[4,32,896]{2,1,0:T(8,128)(2,1)S(1)} custom-call(s32[16]{0:T(128)S(1)} %get-tuple-element.57.req_ref, s32[16]{0:T(128)S(1)} %get-tuple-element.58.pick_ref, bf16[512,896]{1,0:T(8,128)(2,1)S(1)} %copy-done.4, bf16[16,32,896]{2,1,0:T(8,128)(2,1)S(1)} %copy-done.5), custom_call_target="tpu_custom_call" | custom-call | flops 10000000000 | bytes 1024 | tf_op jit(solution)/shard_map/encode_local/pallas_call | solution.py:216
  10.1 0.8 %fetch.1 = (bf16[2,32,896]{2,1,0:T(8,128)(2,1)S(1)}, bf16[2,32,896]{2,1,0:T(8,128)(2,1)S(1)}, bf16[4,32,896]{2,1,0:T(8,128)(2,1)S(1)}, bf16[4,32,896]{2,1,0:T(8,128)(2,1)S(1)}) custom-call(s32[16,8]{1,0:T(8,128)S(1)} %pad_add_fusion.tables_ref, bf16[16,32,896]{2,1,0:T(8,128)(2,1)S(1)} %copy-done.5), custom_call_target="tpu_custom_call" | custom-call | flops 10000000000 | bytes 1024 | tf_op jit(solution)/shard_map/fetch/pallas_call | solution.py:120
  10.9 3.0 %collective-permute-start.3 = (bf16[4,32,896]{2,1,0:T(8,128)(2,1)S(1)}, bf16[4,32,896]{2,1,0:T(8,128)(2,1)S(1)}, u32[]{:S(2)}, u32[]{:S(2)}) collective-permute-start(bf16[4,32,896]{2,1,0:T(8,128)(2,1)S(1)} %get-tuple-element.64), channel_id=1, source_target_pairs={{0,8},{4,12},{8,0},{12,4},{1,9},{5,13},{9,1},{13,5},{2,10},{6,14},... | collective-permute-start | bytes 688136 | tf_op jit(solution)/shard_map/ppermute | solution.py:396
  13.9 1.6 %collective-permute-start.4 = (bf16[2,32,896]{2,1,0:T(8,128)(2,1)S(1)}, bf16[2,32,896]{2,1,0:T(8,128)(2,1)S(1)}, u32[]{:S(2)}, u32[]{:S(2)}) collective-permute-start(bf16[2,32,896]{2,1,0:T(8,128)(2,1)S(1)} %get-tuple-element.67), channel_id=1, source_target_pairs={{0,4},{4,0},{8,12},{12,8},{1,5},{5,1},{9,13},{13,9},{2,6},{6,2},{1... | collective-permute-start | bytes 344072 | tf_op jit(solution)/shard_map/ppermute | solution.py:396
  15.9 1.5 %collective-permute-start = (bf16[4,32,896]{2,1,0:T(8,128)(2,1)S(1)}, bf16[4,32,896]{2,1,0:T(8,128)(2,1)S(1)}, u32[]{:S(2)}, u32[]{:S(2)}) collective-permute-start(bf16[4,32,896]{2,1,0:T(8,128)(2,1)S(1)} %encode_local.1), channel_id=1, source_target_pairs={{0,2},{2,0},{1,3},{3,1},{4,6},{6,4},{5,7},{7,5},{8,10},{10,8},{9,1... | collective-permute-start | bytes 688136 | tf_op jit(solution)/shard_map/ppermute | solution.py:373
  17.4 2.9 %collective-permute-done.4.refs_0_ = bf16[2,32,896]{2,1,0:T(8,128)(2,1)S(1)} collective-permute-done((bf16[2,32,896]{2,1,0:T(8,128)(2,1)S(1)}, bf16[2,32,896]{2,1,0:T(8,128)(2,1)S(1)}, u32[]{:S(2)}, u32[]{:S(2)}) %collective-permute-start.4) | collective-permute-done | bytes 114720 | tf_op jit(solution)/shard_map/ppermute | solution.py:396
  20.4 2.5 %collective-permute-done.5.refs_1_ = bf16[2,32,896]{2,1,0:T(8,128)(2,1)S(1)} collective-permute-done((bf16[2,32,896]{2,1,0:T(8,128)(2,1)S(1)}, bf16[2,32,896]{2,1,0:T(8,128)(2,1)S(1)}, u32[]{:S(2)}, u32[]{:S(2)}) %collective-permute-start.5) | collective-permute-done | bytes 114720 | tf_op jit(solution)/shard_map/ppermute | solution.py:396
  22.9 1.5 %encode.3 = bf16[4,32,896]{2,1,0:T(8,128)(2,1)S(1)} custom-call(s32[16]{0:T(128)S(1)} %get-tuple-element.57.req_ref, bf16[512,896]{1,0:T(8,128)(2,1)S(1)} %copy-done.4, bf16[2,32,896]{2,1,0:T(8,128)(2,1)S(1)} %collective-permute-done.4.refs_0_, bf16[2,32,896]{2,1,0:T(8,128)(2,1)S(1)} %collective-permute-done.5.refs_1_), custom_call_target="tpu_custom_call" | custom-call | flops 100000000 | bytes 1024 | tf_op jit(solution)/shard_map/encode/pallas_call | solution.py:197
  24.3 1.6 %collective-permute-start.7 = (bf16[4,32,896]{2,1,0:T(8,128)(2,1)S(1)}, bf16[4,32,896]{2,1,0:T(8,128)(2,1)S(1)}, u32[]{:S(2)}, u32[]{:S(2)}) collective-permute-start(bf16[4,32,896]{2,1,0:T(8,128)(2,1)S(1)} %encode.3), channel_id=1, source_target_pairs={{0,2},{2,0},{1,3},{3,1},{4,6},{6,4},{5,7},{7,5},{8,10},{10,8},{9,1... | collective-permute-start | bytes 688136 | tf_op jit(solution)/shard_map/ppermute | solution.py:373
  25.9 0.6 collective-permute-start.10
  26.5 1.3 %encode.4 = bf16[4,32,896]{2,1,0:T(8,128)(2,1)S(1)} custom-call(s32[16]{0:T(128)S(1)} %get-tuple-element.57.req_ref, bf16[512,896]{1,0:T(8,128)(2,1)S(1)} %copy-done.4, bf16[4,32,896]{2,1,0:T(8,128)(2,1)S(1)} %collective-permute-done.3.refs_0_), custom_call_target="tpu_custom_call" | custom-call | flops 10000000000 | bytes 1024 | tf_op jit(solution)/shard_map/encode/pallas_call | solution.py:197
  27.8 0.6 collective-permute-start.9
  28.5 2.7 %collective-permute-done.7 = bf16[4,32,896]{2,1,0:T(8,128)(2,1)S(1)} collective-permute-done((bf16[4,32,896]{2,1,0:T(8,128)(2,1)S(1)}, bf16[4,32,896]{2,1,0:T(8,128)(2,1)S(1)}, u32[]{:S(2)}, u32[]{:S(2)}) %collective-permute-start.7) | collective-permute-done | bytes 229408 | tf_op jit(solution)/shard_map/ppermute | solution.py:373
  31.4 2.4 %collective-permute-done.10.refs_0_ = bf16[4,32,896]{2,1,0:T(8,128)(2,1)S(1)} collective-permute-done((bf16[4,32,896]{2,1,0:T(8,128)(2,1)S(1)}, bf16[4,32,896]{2,1,0:T(8,128)(2,1)S(1)}, u32[]{:S(2)}, u32[]{:S(2)}) %collective-permute-start.10) | collective-permute-done | bytes 229408 | tf_op jit(solution)/shard_map/ppermute | solution.py:396
  33.8 1.3 %encode.5 = bf16[4,32,896]{2,1,0:T(8,128)(2,1)S(1)} custom-call(s32[16]{0:T(128)S(1)} %get-tuple-element.57.req_ref, bf16[512,896]{1,0:T(8,128)(2,1)S(1)} %copy-done.4, bf16[4,32,896]{2,1,0:T(8,128)(2,1)S(1)} %collective-permute-done.10.refs_0_), custom_call_target="tpu_custom_call" | custom-call | flops 10000000000 | bytes 1024 | tf_op jit(solution)/shard_map/encode/pallas_call | solution.py:197
  35.1 0.6 collective-permute-start.13
  35.9 1.3 %project.5.refs_0_ = bf16[4,4,32,1024]{3,2,1,0:T(8,128)(2,1)S(1)} custom-call(bf16[2,4,32,896]{3,2,1,0:T(8,128)(2,1)S(1)} %pad_maximum_fusion.refs_0_, bf16[2,4,32,896]{3,2,1,0:T(8,128)(2,1)S(1)} %collective-permute-done.6.refs_1_, bf16[896,512]{1,0:T(8,128)(2,1)S(1)} %copy-done.2, bf16[896,512]{1,0:T(8,128)(2,1)S(1)} %copy-done.3), custom_call_target="tpu_custom_call" | custom-call | flops 10000000000 | bytes 1024 | tf_op jit(solution)/shard_map/project/pallas_call | solution.py:249
  37.1 0.5 collective-permute-start.12
  37.7 1.3 %project.6.refs_1_ = bf16[4,4,32,1024]{3,2,1,0:T(8,128)(2,1)S(1)} custom-call(bf16[2,4,32,896]{3,2,1,0:T(8,128)(2,1)S(1)} %pad_maximum_fusion.1.refs_0_, bf16[2,4,32,896]{3,2,1,0:T(8,128)(2,1)S(1)} %collective-permute-done.8.refs_1_, bf16[896,512]{1,0:T(8,128)(2,1)S(1)} %copy-done.2, bf16[896,512]{1,0:T(8,128)(2,1)S(1)} %copy-done.3), custom_call_target="tpu_custom_call" | custom-call | flops 10000000000 | bytes 1024 | tf_op jit(solution)/shard_map/project/pallas_call | solution.py:249
  38.9 1.3 %project.7.refs_2_ = bf16[4,4,32,1024]{3,2,1,0:T(8,128)(2,1)S(1)} custom-call(bf16[2,4,32,896]{3,2,1,0:T(8,128)(2,1)S(1)} %pad_maximum_fusion.2.refs_0_, bf16[2,4,32,896]{3,2,1,0:T(8,128)(2,1)S(1)} %collective-permute-done.11.refs_1_, bf16[896,512]{1,0:T(8,128)(2,1)S(1)} %copy-done.2, bf16[896,512]{1,0:T(8,128)(2,1)S(1)} %copy-done.3), custom_call_target="tpu_custom_call" | custom-call | flops 10000000000 | bytes 1024 | tf_op jit(solution)/shard_map/project/pallas_call | solution.py:249
  40.2 0.7 project.8.refs_3_
  41.6 1.0 %collective-permute-done.14.refs_5_ = bf16[1,4,32,896]{3,2,1,0:T(8,128)(2,1)S(1)} collective-permute-done((bf16[1,4,32,896]{3,2,1,0:T(8,128)(2,1)S(1)}, bf16[1,4,32,896]{3,2,1,0:T(8,128)(2,1)S(1)}, u32[]{:S(2)}, u32[]{:S(2)}) %collective-permute-start.14) | collective-permute-done | bytes 229408 | tf_op jit(solution)/shard_map/ppermute | solution.py:376
  42.7 1.9 %attend.4 = (bf16[1,128,512]{2,1,0:T(8,128)(2,1)S(1)}, bf16[4,1,32,1024]{3,2,1,0:T(8,128)(2,1)S(1)}) custom-call(s32[16]{0:T(128)S(1)} %get-tuple-element.56.slot_ref, bf16[512,512]{1,0:T(8,128)(2,1)S(1)} %copy-done.1, bf16[4,4,32,1024]{3,2,1,0:T(8,128)(2,1)S(1)} %project.5.refs_0_, bf16[4,4,32,1024]{3,2,1,0:T(8,128)(2,1)S(1)} %project.6.refs_1_, ...), custom_call_target="tpu_custom_call" | custom-call | flops 1000000 | bytes 1024 | tf_op jit(solution)/shard_map/attend/pallas_call | solution.py:320
  44.8 1.5 %attend.5.refs_0_ = bf16[1,128,512]{2,1,0:T(8,128)(2,1)S(1)} custom-call(s32[16]{0:T(128)S(1)} %get-tuple-element.56.slot_ref, bf16[512,512]{1,0:T(8,128)(2,1)S(1)} %copy-done.1, bf16[4,4,32,1024]{3,2,1,0:T(8,128)(2,1)S(1)} %project.5.refs_0_, bf16[4,4,32,1024]{3,2,1,0:T(8,128)(2,1)S(1)} %project.6.refs_1_, bf16[4,4,32,1024]{3,2,1,0:T(8,128)(2,1)S(1)} %project.7.refs_2_, ...), custom_call_target="tpu_custom_call" | custom-call | flops 1000000 | bytes 1024 | tf_op jit(solution)/shard_map/attend/pallas_call | solution.py:320
  46.3 1.0 %out_project.6 = bf16[128,1024]{1,0:T(8,128)(2,1)S(1)} custom-call(bf16[1,128,512]{2,1,0:T(8,128)(2,1)S(1)} %attend.5.refs_0_, bf16[1,128,512]{2,1,0:T(8,128)(2,1)S(1)} %collective-permute-done.15.refs_1_, bf16[512,4096]{1,0:T(8,128)(2,1)S(1)} %copy-done, bf16[512,4096]{1,0:T(8,128)(2,1)S(1)} %collective-permute-done.16.refs_3_), custom_call_target="tpu_custom_call" | custom-call | flops 1000000 | bytes 1024 | tf_op jit(solution)/shard_map/out_project/pallas_call | solution.py:345
  47.3 1.4 %collective-permute-start.22 = (bf16[128,1024]{1,0:T(8,128)(2,1)S(1)}, bf16[128,1024]{1,0:T(8,128)(2,1)S(1)}, u32[]{:S(2)}, u32[]{:S(2)}) collective-permute-start(bf16[128,1024]{1,0:T(8,128)(2,1)S(1)} %out_project.6), channel_id=1, source_target_pairs={{0,2},{2,0},{1,3},{3,1},{4,6},{6,4},{5,7},{7,5},{8,10},{10,8},{9,1... | collective-permute-start | bytes 786440 | tf_op jit(solution)/shard_map/ppermute | solution.py:452
  48.8 0.9 %out_project.7 = bf16[128,1024]{1,0:T(8,128)(2,1)S(1)} custom-call(bf16[1,128,512]{2,1,0:T(8,128)(2,1)S(1)} %attend.5.refs_0_, bf16[1,128,512]{2,1,0:T(8,128)(2,1)S(1)} %collective-permute-done.15.refs_1_, bf16[512,4096]{1,0:T(8,128)(2,1)S(1)} %copy-done, bf16[512,4096]{1,0:T(8,128)(2,1)S(1)} %collective-permute-done.16.refs_3_), custom_call_target="tpu_custom_call" | custom-call | flops 1000000 | bytes 1024 | tf_op jit(solution)/shard_map/out_project/pallas_call | solution.py:345
  49.6 0.7 collective-permute-start.21
  50.4 0.9 %out_project.8 = bf16[128,1024]{1,0:T(8,128)(2,1)S(1)} custom-call(bf16[1,128,512]{2,1,0:T(8,128)(2,1)S(1)} %attend.5.refs_0_, bf16[1,128,512]{2,1,0:T(8,128)(2,1)S(1)} %collective-permute-done.15.refs_1_, bf16[512,4096]{1,0:T(8,128)(2,1)S(1)} %copy-done, bf16[512,4096]{1,0:T(8,128)(2,1)S(1)} %collective-permute-done.16.refs_3_), custom_call_target="tpu_custom_call" | custom-call | flops 1000000 | bytes 1024 | tf_op jit(solution)/shard_map/out_project/pallas_call | solution.py:345
  51.2 1.4 %collective-permute-start.20 = (bf16[128,1024]{1,0:T(8,128)(2,1)S(1)}, bf16[128,1024]{1,0:T(8,128)(2,1)S(1)}, u32[]{:S(2)}, u32[]{:S(2)}) collective-permute-start(bf16[128,1024]{1,0:T(8,128)(2,1)S(1)} %out_project.8), channel_id=1, source_target_pairs={{0,2},{2,0},{1,3},{3,1},{4,6},{6,4},{5,7},{7,5},{8,10},{10,8},{9,1... | collective-permute-start | bytes 786440 | tf_op jit(solution)/shard_map/ppermute | solution.py:452
  53.3 1.5 %attend.7 = bf16[1,128,512]{2,1,0:T(8,128)(2,1)S(1)} custom-call(s32[16]{0:T(128)S(1)} %get-tuple-element.56.slot_ref, bf16[512,512]{1,0:T(8,128)(2,1)S(1)} %copy-done.1, bf16[4,4,32,1024]{3,2,1,0:T(8,128)(2,1)S(1)} %project.5.refs_0_, bf16[4,4,32,1024]{3,2,1,0:T(8,128)(2,1)S(1)} %project.6.refs_1_, bf16[4,4,32,1024]{3,2,1,0:T(8,128)(2,1)S(1)} %project.7.refs_2_, ...), custom_call_target="tpu_custom_call" | custom-call | flops 1000000 | bytes 1024 | tf_op jit(solution)/shard_map/attend/pallas_call | solution.py:320
  54.9 0.7 collective-permute-start.19
  55.6 0.6 collective-permute-done.17.refs_1_
  56.2 0.8 %collective-permute-start.18 = (bf16[128,512]{1,0:T(8,128)(2,1)S(1)}, bf16[128,512]{1,0:T(8,128)(2,1)S(1)}, u32[]{:S(2)}, u32[]{:S(2)}) collective-permute-start(bf16[128,512]{1,0:T(8,128)(2,1)S(1)} %out_project.10), channel_id=1, source_target_pairs={{0,2},{2,0},{1,3},{3,1},{4,6},{6,4},{5,7},{7,5},{8,10},{10,8},{9,1... | collective-permute-start | bytes 393224 | tf_op jit(solution)/shard_map/ppermute | solution.py:452
  57.0 1.5 %attend.6.refs_0_ = bf16[1,128,512]{2,1,0:T(8,128)(2,1)S(1)} custom-call(s32[16]{0:T(128)S(1)} %get-tuple-element.56.slot_ref, bf16[512,512]{1,0:T(8,128)(2,1)S(1)} %copy-done.1, bf16[4,4,32,1024]{3,2,1,0:T(8,128)(2,1)S(1)} %project.5.refs_0_, bf16[4,4,32,1024]{3,2,1,0:T(8,128)(2,1)S(1)} %project.6.refs_1_, bf16[4,4,32,1024]{3,2,1,0:T(8,128)(2,1)S(1)} %project.7.refs_2_, ...), custom_call_target="tpu_custom_call" | custom-call | flops 1000000 | bytes 1024 | tf_op jit(solution)/shard_map/attend/pallas_call | solution.py:320
  58.8 1.5 %out_final.5.refs_5_ = bf16[128,4096]{1,0:T(8,128)(2,1)} custom-call(bf16[1,128,512]{2,1,0:T(8,128)(2,1)S(1)} %attend.6.refs_0_, bf16[1,128,512]{2,1,0:T(8,128)(2,1)S(1)} %collective-permute-done.17.refs_1_, bf16[512,4096]{1,0:T(8,128)(2,1)S(1)} %copy-done, bf16[512,4096]{1,0:T(8,128)(2,1)S(1)} %collective-permute-done.16.refs_3_, ...), custom_call_target="tpu_custom_call" | custom-call | flops 200000000 | bytes 1024 | tf_op jit(solution)/shard_map/out_final/pallas_call | solution.py:345
  60.3 1.8 %collective-permute-done.21.refs_4_ = bf16[128,1024]{1,0:T(8,128)(2,1)S(1)} collective-permute-done((bf16[128,1024]{1,0:T(8,128)(2,1)S(1)}, bf16[128,1024]{1,0:T(8,128)(2,1)S(1)}, u32[]{:S(2)}, u32[]{:S(2)}) %collective-permute-start.21) | collective-permute-done | bytes 262176 | tf_op jit(solution)/shard_map/ppermute | solution.py:452
  62.2 1.5 %out_final.6.refs_5_ = bf16[128,4096]{1,0:T(8,128)(2,1)} custom-call(bf16[1,128,512]{2,1,0:T(8,128)(2,1)S(1)} %attend.6.refs_0_, bf16[1,128,512]{2,1,0:T(8,128)(2,1)S(1)} %collective-permute-done.17.refs_1_, bf16[512,4096]{1,0:T(8,128)(2,1)S(1)} %copy-done, bf16[512,4096]{1,0:T(8,128)(2,1)S(1)} %collective-permute-done.16.refs_3_, ...), custom_call_target="tpu_custom_call", output_to_operand_aliasing={{}: (5, {})} | custom-call | flops 200000000 | bytes 1024 | tf_op jit(solution)/shard_map/out_final/pallas_call | solution.py:345
  63.6 4.1 %collective-permute-done.20.refs_4_ = bf16[128,1024]{1,0:T(8,128)(2,1)S(1)} collective-permute-done((bf16[128,1024]{1,0:T(8,128)(2,1)S(1)}, bf16[128,1024]{1,0:T(8,128)(2,1)S(1)}, u32[]{:S(2)}, u32[]{:S(2)}) %collective-permute-start.20) | collective-permute-done | bytes 262176 | tf_op jit(solution)/shard_map/ppermute | solution.py:452
  67.8 1.5 %out_final.7.refs_5_ = bf16[128,4096]{1,0:T(8,128)(2,1)} custom-call(bf16[1,128,512]{2,1,0:T(8,128)(2,1)S(1)} %attend.6.refs_0_, bf16[1,128,512]{2,1,0:T(8,128)(2,1)S(1)} %collective-permute-done.17.refs_1_, bf16[512,4096]{1,0:T(8,128)(2,1)S(1)} %copy-done, bf16[512,4096]{1,0:T(8,128)(2,1)S(1)} %collective-permute-done.16.refs_3_, ...), custom_call_target="tpu_custom_call", output_to_operand_aliasing={{}: (5, {})} | custom-call | flops 200000000 | bytes 1024 | tf_op jit(solution)/shard_map/out_final/pallas_call | solution.py:345
  69.3 1.3 %collective-permute-done.19.refs_4_ = bf16[128,512]{1,0:T(8,128)(2,1)S(1)} collective-permute-done((bf16[128,512]{1,0:T(8,128)(2,1)S(1)}, bf16[128,512]{1,0:T(8,128)(2,1)S(1)}, u32[]{:S(2)}, u32[]{:S(2)}) %collective-permute-start.19) | collective-permute-done | bytes 131104 | tf_op jit(solution)/shard_map/ppermute | solution.py:452
  70.6 1.0 %out_final.8.refs_2_ = bf16[128,4096]{1,0:T(8,128)(2,1)} custom-call(bf16[1,128,512]{2,1,0:T(8,128)(2,1)S(1)} %attend.6.refs_0_, bf16[1,128,512]{2,1,0:T(8,128)(2,1)S(1)} %collective-permute-done.17.refs_1_, bf16[512,4096]{1,0:T(8,128)(2,1)S(1)} %copy-done, bf16[512,4096]{1,0:T(8,128)(2,1)S(1)} %collective-permute-done.16.refs_3_, ...), custom_call_target="tpu_custom_call", output_to_operand_aliasing={{}: (5, {})} | custom-call | flops 200000000 | bytes 1024 | tf_op jit(solution)/shard_map/out_final/pallas_call | solution.py:345
  71.6 1.3 %collective-permute-done.18.refs_1_ = bf16[128,512]{1,0:T(8,128)(2,1)S(1)} collective-permute-done((bf16[128,512]{1,0:T(8,128)(2,1)S(1)}, bf16[128,512]{1,0:T(8,128)(2,1)S(1)}, u32[]{:S(2)}, u32[]{:S(2)}) %collective-permute-start.18) | collective-permute-done | bytes 131104 | tf_op jit(solution)/shard_map/ppermute | solution.py:452
  72.8 0.7 out_final.9
  (42 shorter events, 3.4 us)
Async XLA Ops:
  0.7 7.8 %copy-start.4 = (bf16[512,896]{1,0:T(8,128)(2,1)S(1)}, bf16[512,896]{1,0:T(8,128)(2,1)}, u32[]{:S(2)}) copy-start(bf16[512,896]{1,0:T(8,128)(2,1)} %states_ref.7) | copy-start | bytes 2752516
  0.7 7.8 %copy-start.5 = (bf16[16,32,896]{2,1,0:T(8,128)(2,1)S(1)}, bf16[16,32,896]{2,1,0:T(8,128)(2,1)}, u32[]{:S(2)}) copy-start(bf16[16,32,896]{2,1,0:T(8,128)(2,1)} %store_ref.3) | copy-start | bytes 2752516
  0.7 4.7 %collective-permute-start.1 = (s32[4,8]{1,0:T(4,128)S(1)}, s32[4,8]{1,0:T(4,128)S(1)}, u32[]{:S(2)}, u32[]{:S(2)}) collective-permute-start(s32[4,8]{1,0:T(4,128)S(1)} %pad_add_fusion.2.own_ref), channel_id=1, source_target_pairs={{0,4},{4,0},{8,12},{12,8},{1,5},{5,1},{9,13},{13,9},{2,6},{6,2},{1... | collective-permute-start | bytes 392 | tf_op jit(solution)/shard_map/ppermute | solution.py:49
  5.4 4.7 %collective-permute-start.2 = (s32[8,8]{1,0:T(8,128)S(1)}, s32[8,8]{1,0:T(8,128)S(1)}, u32[]{:S(2)}, u32[]{:S(2)}) collective-permute-start(s32[8,8]{1,0:T(8,128)S(1)} %pad_add_fusion.1), channel_id=1, source_target_pairs={{0,8},{4,12},{8,0},{12,4},{1,9},{5,13},{9,1},{13,5},{2,10},{6,14},... | collective-permute-start | bytes 776 | tf_op jit(solution)/shard_map/ppermute | solution.py:49
  10.1 7.4 %copy-start = (bf16[512,4096]{1,0:T(8,128)(2,1)S(1)}, bf16[512,4096]{1,0:T(8,128)(2,1)}, u32[]{:S(2)}) copy-start(bf16[512,4096]{1,0:T(8,128)(2,1)} %refs_2_.29) | copy-start | bytes 12582916
  10.9 15.6 %collective-permute-start.3 = (bf16[4,32,896]{2,1,0:T(8,128)(2,1)S(1)}, bf16[4,32,896]{2,1,0:T(8,128)(2,1)S(1)}, u32[]{:S(2)}, u32[]{:S(2)}) collective-permute-start(bf16[4,32,896]{2,1,0:T(8,128)(2,1)S(1)} %get-tuple-element.64), channel_id=1, source_target_pairs={{0,8},{4,12},{8,0},{12,4},{1,9},{5,13},{9,1},{13,5},{2,10},{6,14},... | collective-permute-start | bytes 688136 | tf_op jit(solution)/shard_map/ppermute | solution.py:396
  13.9 6.5 %collective-permute-start.4 = (bf16[2,32,896]{2,1,0:T(8,128)(2,1)S(1)}, bf16[2,32,896]{2,1,0:T(8,128)(2,1)S(1)}, u32[]{:S(2)}, u32[]{:S(2)}) collective-permute-start(bf16[2,32,896]{2,1,0:T(8,128)(2,1)S(1)} %get-tuple-element.67), channel_id=1, source_target_pairs={{0,4},{4,0},{8,12},{12,8},{1,5},{5,1},{9,13},{13,9},{2,6},{6,2},{1... | collective-permute-start | bytes 344072 | tf_op jit(solution)/shard_map/ppermute | solution.py:396
  15.5 7.4 %collective-permute-start.5 = (bf16[2,32,896]{2,1,0:T(8,128)(2,1)S(1)}, bf16[2,32,896]{2,1,0:T(8,128)(2,1)S(1)}, u32[]{:S(2)}, u32[]{:S(2)}) collective-permute-start(bf16[2,32,896]{2,1,0:T(8,128)(2,1)S(1)} %get-tuple-element.68), channel_id=1, source_target_pairs={{0,4},{4,0},{8,12},{12,8},{1,5},{5,1},{9,13},{13,9},{2,6},{6,2},{1... | collective-permute-start | bytes 344072 | tf_op jit(solution)/shard_map/ppermute | solution.py:396
  15.9 12.5 %collective-permute-start = (bf16[4,32,896]{2,1,0:T(8,128)(2,1)S(1)}, bf16[4,32,896]{2,1,0:T(8,128)(2,1)S(1)}, u32[]{:S(2)}, u32[]{:S(2)}) collective-permute-start(bf16[4,32,896]{2,1,0:T(8,128)(2,1)S(1)} %encode_local.1), channel_id=1, source_target_pairs={{0,2},{2,0},{1,3},{3,1},{4,6},{6,4},{5,7},{7,5},{8,10},{10,8},{9,1... | collective-permute-start | bytes 688136 | tf_op jit(solution)/shard_map/ppermute | solution.py:373
  17.4 28.9 %collective-permute-start.16 = (bf16[512,4096]{1,0:T(8,128)(2,1)S(1)}, bf16[512,4096]{1,0:T(8,128)(2,1)S(1)}, u32[]{:S(2)}, u32[]{:S(2)}) collective-permute-start(bf16[512,4096]{1,0:T(8,128)(2,1)S(1)} %copy-done), channel_id=1, source_target_pairs={{0,1},{1,0},{2,3},{3,2},{4,5},{5,4},{6,7},{7,6},{8,9},{9,8},{10,11... | collective-permute-start | bytes 12582920 | tf_op jit(solution)/shard_map/ppermute | solution.py:376
  24.3 6.9 %collective-permute-start.7 = (bf16[4,32,896]{2,1,0:T(8,128)(2,1)S(1)}, bf16[4,32,896]{2,1,0:T(8,128)(2,1)S(1)}, u32[]{:S(2)}, u32[]{:S(2)}) collective-permute-start(bf16[4,32,896]{2,1,0:T(8,128)(2,1)S(1)} %encode.3), channel_id=1, source_target_pairs={{0,2},{2,0},{1,3},{3,1},{4,6},{6,4},{5,7},{7,5},{8,10},{10,8},{9,1... | collective-permute-start | bytes 688136 | tf_op jit(solution)/shard_map/ppermute | solution.py:373
  25.9 7.9 %collective-permute-start.10 = (bf16[4,32,896]{2,1,0:T(8,128)(2,1)S(1)}, bf16[4,32,896]{2,1,0:T(8,128)(2,1)S(1)}, u32[]{:S(2)}, u32[]{:S(2)}) collective-permute-start(bf16[4,32,896]{2,1,0:T(8,128)(2,1)S(1)} %get-tuple-element.81), channel_id=1, source_target_pairs={{0,12},{4,8},{8,4},{12,0},{1,13},{5,9},{9,5},{13,1},{2,14},{6,10},... | collective-permute-start | bytes 688136 | tf_op jit(solution)/shard_map/ppermute | solution.py:396
  27.8 7.9 %collective-permute-start.9 = (bf16[4,32,896]{2,1,0:T(8,128)(2,1)S(1)}, bf16[4,32,896]{2,1,0:T(8,128)(2,1)S(1)}, u32[]{:S(2)}, u32[]{:S(2)}) collective-permute-start(bf16[4,32,896]{2,1,0:T(8,128)(2,1)S(1)} %encode.4), channel_id=1, source_target_pairs={{0,2},{2,0},{1,3},{3,1},{4,6},{6,4},{5,7},{7,5},{8,10},{10,8},{9,1... | collective-permute-start | bytes 688136 | tf_op jit(solution)/shard_map/ppermute | solution.py:373
  28.4 7.4 %collective-permute-start.6 = (bf16[2,4,32,896]{3,2,1,0:T(8,128)(2,1)S(1)}, bf16[2,4,32,896]{3,2,1,0:T(8,128)(2,1)S(1)}, u32[]{:S(2)}, u32[]{:S(2)}) collective-permute-start(bf16[2,4,32,896]{3,2,1,0:T(8,128)(2,1)S(1)} %pad_maximum_fusion.refs_0_), channel_id=1, source_target_pairs={{0,1},{1,0},{2,3},{3,2},{4,5},{5,4},{6,7},{7,6},{8,9},{9,8},{10,11... | collective-permute-start | bytes 1376264 | tf_op jit(solution)/shard_map/ppermute | solution.py:376
  31.3 4.5 %copy-start.2 = (bf16[896,512]{1,0:T(8,128)(2,1)S(1)}, bf16[896,512]{1,0:T(8,128)(2,1)}, u32[]{:S(2)}) copy-start(bf16[896,512]{1,0:T(8,128)(2,1)} %refs_6_.1) | copy-start | bytes 2752516
  31.3 4.5 %copy-start.3 = (bf16[896,512]{1,0:T(8,128)(2,1)S(1)}, bf16[896,512]{1,0:T(8,128)(2,1)}, u32[]{:S(2)}) copy-start(bf16[896,512]{1,0:T(8,128)(2,1)} %refs_7_.1) | copy-start | bytes 2752516
  31.3 6.3 %collective-permute-start.8 = (bf16[2,4,32,896]{3,2,1,0:T(8,128)(2,1)S(1)}, bf16[2,4,32,896]{3,2,1,0:T(8,128)(2,1)S(1)}, u32[]{:S(2)}, u32[]{:S(2)}) collective-permute-start(bf16[2,4,32,896]{3,2,1,0:T(8,128)(2,1)S(1)} %pad_maximum_fusion.1.refs_0_), channel_id=1, source_target_pairs={{0,1},{1,0},{2,3},{3,2},{4,5},{5,4},{6,7},{7,6},{8,9},{9,8},{10,11... | collective-permute-start | bytes 1376264 | tf_op jit(solution)/shard_map/ppermute | solution.py:376
  35.1 6.1 %collective-permute-start.13 = (bf16[4,32,896]{2,1,0:T(8,128)(2,1)S(1)}, bf16[4,32,896]{2,1,0:T(8,128)(2,1)S(1)}, u32[]{:S(2)}, u32[]{:S(2)}) collective-permute-start(bf16[4,32,896]{2,1,0:T(8,128)(2,1)S(1)} %encode.5), channel_id=1, source_target_pairs={{0,2},{2,0},{1,3},{3,1},{4,6},{6,4},{5,7},{7,5},{8,10},{10,8},{9,1... | collective-permute-start | bytes 688136 | tf_op jit(solution)/shard_map/ppermute | solution.py:373
  35.7 3.2 %collective-permute-start.11 = (bf16[2,4,32,896]{3,2,1,0:T(8,128)(2,1)S(1)}, bf16[2,4,32,896]{3,2,1,0:T(8,128)(2,1)S(1)}, u32[]{:S(2)}, u32[]{:S(2)}) collective-permute-start(bf16[2,4,32,896]{3,2,1,0:T(8,128)(2,1)S(1)} %pad_maximum_fusion.2.refs_0_), channel_id=1, source_target_pairs={{0,1},{1,0},{2,3},{3,2},{4,5},{5,4},{6,7},{7,6},{8,9},{9,8},{10,11... | collective-permute-start | bytes 1376264 | tf_op jit(solution)/shard_map/ppermute | solution.py:376
  37.1 3.1 %collective-permute-start.12 = (bf16[4,32,896]{2,1,0:T(8,128)(2,1)S(1)}, bf16[4,32,896]{2,1,0:T(8,128)(2,1)S(1)}, u32[]{:S(2)}, u32[]{:S(2)}) collective-permute-start(bf16[4,32,896]{2,1,0:T(8,128)(2,1)S(1)} %encode.5), channel_id=1, source_target_pairs={{0,1},{1,0},{2,3},{3,2},{4,5},{5,4},{6,7},{7,6},{8,9},{9,8},{10,11... | collective-permute-start | bytes 688136 | tf_op jit(solution)/shard_map/ppermute | solution.py:376
  41.2 1.5 %copy-start.1 = (bf16[512,512]{1,0:T(8,128)(2,1)S(1)}, bf16[512,512]{1,0:T(8,128)(2,1)}, u32[]{:S(2)}) copy-start(bf16[512,512]{1,0:T(8,128)(2,1)} %q_ref.5) | copy-start | bytes 1572868
  41.2 1.5 %collective-permute-start.14 = (bf16[1,4,32,896]{3,2,1,0:T(8,128)(2,1)S(1)}, bf16[1,4,32,896]{3,2,1,0:T(8,128)(2,1)S(1)}, u32[]{:S(2)}, u32[]{:S(2)}) collective-permute-start(bf16[1,4,32,896]{3,2,1,0:T(8,128)(2,1)S(1)} %bitcast.14), channel_id=1, source_target_pairs={{0,1},{1,0},{2,3},{3,2},{4,5},{5,4},{6,7},{7,6},{8,9},{9,8},{10,11... | collective-permute-start | bytes 688136 | tf_op jit(solution)/shard_map/ppermute | solution.py:376
  44.6 1.7 %collective-permute-start.15 = (bf16[1,128,512]{2,1,0:T(8,128)(2,1)S(1)}, bf16[1,128,512]{2,1,0:T(8,128)(2,1)S(1)}, u32[]{:S(2)}, u32[]{:S(2)}) collective-permute-start(bf16[1,128,512]{2,1,0:T(8,128)(2,1)S(1)} %get-tuple-element.92), channel_id=1, source_target_pairs={{0,1},{1,0},{2,3},{3,2},{4,5},{5,4},{6,7},{7,6},{8,9},{9,8},{10,11... | collective-permute-start | bytes 393224 | tf_op jit(solution)/shard_map/ppermute | solution.py:435
  47.3 11.5 %collective-permute-start.22 = (bf16[128,1024]{1,0:T(8,128)(2,1)S(1)}, bf16[128,1024]{1,0:T(8,128)(2,1)S(1)}, u32[]{:S(2)}, u32[]{:S(2)}) collective-permute-start(bf16[128,1024]{1,0:T(8,128)(2,1)S(1)} %out_project.6), channel_id=1, source_target_pairs={{0,2},{2,0},{1,3},{3,1},{4,6},{6,4},{5,7},{7,5},{8,10},{10,8},{9,1... | collective-permute-start | bytes 786440 | tf_op jit(solution)/shard_map/ppermute | solution.py:452
  49.6 12.5 %collective-permute-start.21 = (bf16[128,1024]{1,0:T(8,128)(2,1)S(1)}, bf16[128,1024]{1,0:T(8,128)(2,1)S(1)}, u32[]{:S(2)}, u32[]{:S(2)}) collective-permute-start(bf16[128,1024]{1,0:T(8,128)(2,1)S(1)} %out_project.7), channel_id=1, source_target_pairs={{0,2},{2,0},{1,3},{3,1},{4,6},{6,4},{5,7},{7,5},{8,10},{10,8},{9,1... | collective-permute-start | bytes 786440 | tf_op jit(solution)/shard_map/ppermute | solution.py:452
  51.2 16.5 %collective-permute-start.20 = (bf16[128,1024]{1,0:T(8,128)(2,1)S(1)}, bf16[128,1024]{1,0:T(8,128)(2,1)S(1)}, u32[]{:S(2)}, u32[]{:S(2)}) collective-permute-start(bf16[128,1024]{1,0:T(8,128)(2,1)S(1)} %out_project.8), channel_id=1, source_target_pairs={{0,2},{2,0},{1,3},{3,1},{4,6},{6,4},{5,7},{7,5},{8,10},{10,8},{9,1... | collective-permute-start | bytes 786440 | tf_op jit(solution)/shard_map/ppermute | solution.py:452
  54.8 1.4 %collective-permute-start.17 = (bf16[1,128,512]{2,1,0:T(8,128)(2,1)S(1)}, bf16[1,128,512]{2,1,0:T(8,128)(2,1)S(1)}, u32[]{:S(2)}, u32[]{:S(2)}) collective-permute-start(bf16[1,128,512]{2,1,0:T(8,128)(2,1)S(1)} %attend.7), channel_id=1, source_target_pairs={{0,1},{1,0},{2,3},{3,2},{4,5},{5,4},{6,7},{7,6},{8,9},{9,8},{10,11... | collective-permute-start | bytes 393224 | tf_op jit(solution)/shard_map/ppermute | solution.py:435
  54.9 15.7 %collective-permute-start.19 = (bf16[128,512]{1,0:T(8,128)(2,1)S(1)}, bf16[128,512]{1,0:T(8,128)(2,1)S(1)}, u32[]{:S(2)}, u32[]{:S(2)}) collective-permute-start(bf16[128,512]{1,0:T(8,128)(2,1)S(1)} %out_project.9), channel_id=1, source_target_pairs={{0,2},{2,0},{1,3},{3,1},{4,6},{6,4},{5,7},{7,5},{8,10},{10,8},{9,1... | collective-permute-start | bytes 393224 | tf_op jit(solution)/shard_map/ppermute | solution.py:452
  56.2 16.6 %collective-permute-start.18 = (bf16[128,512]{1,0:T(8,128)(2,1)S(1)}, bf16[128,512]{1,0:T(8,128)(2,1)S(1)}, u32[]{:S(2)}, u32[]{:S(2)}) collective-permute-start(bf16[128,512]{1,0:T(8,128)(2,1)S(1)} %out_project.10), channel_id=1, source_target_pairs={{0,2},{2,0},{1,3},{3,1},{4,6},{6,4},{5,7},{7,5},{8,10},{10,8},{9,1... | collective-permute-start | bytes 393224 | tf_op jit(solution)/shard_map/ppermute | solution.py:452

commit v14 on v13

--- a/solution.py
+++ b/solution.py
@@ -239,15 +239,20 @@
 
 
 def project_kernel(n_pieces, *refs):
-    pieces, (wk_ref, wv_ref, kv_ref) = refs[:n_pieces], refs[n_pieces:]
-    project_into(kv_ref, 0, pieces, wk_ref, wv_ref)
-
-
-def project(pieces, w_key, w_value):
-    n, slots, tokens, _ = pieces[0].shape
-    shape = (slots, n * len(pieces), tokens, 2 * w_key.shape[1])
-    return pl.pallas_call(
-        functools.partial(project_kernel, len(pieces)),
+    pieces, (wk_ref, wv_ref, kv_ref) = refs[:-3], refs[-3:]
+    first = 0
+    for at in range(0, len(pieces), n_pieces):
+        project_into(kv_ref, first, pieces[at : at + n_pieces], wk_ref, wv_ref)
+        first += pieces[at].shape[1]
+
+
+def project(pieces, w_key, w_value, n_groups=1):
+    n_pieces = len(pieces) // n_groups
+    n, _, tokens, _ = pieces[0].shape
+    slots = sum(piece.shape[1] for piece in pieces[::n_pieces])
+    shape = (slots, n * n_pieces, tokens, 2 * w_key.shape[1])
+    return pl.pallas_call(
+        functools.partial(project_kernel, n_pieces),
         out_shape=jax.ShapeDtypeStruct(shape, BF16),
         in_specs=[VMEM] * (len(pieces) + 2),
         out_specs=VMEM,
@@ -414,9 +419,10 @@
             pieces.append(over_rep(last))
     w_outs = over_rep(w_out)
     kvs, last = [], after(last, w_outs)
-    while len(kvs) < len(pieces):
-        last = project(after(pieces[len(kvs)], last), w_key, w_value)
-        kvs.append(last)
+    for some in (pieces[:2], pieces[2:]):
+        if some:
+            last = project(after(sum(some, []), last), w_key, w_value, len(some))
+            kvs.append(last)
     local, *remote = crossed[-1]
     early = [piece[None] for piece in over_rep(after(local, kvs[0]))]
     last = project(after(early, last), w_key, w_value)

time: 73.7 us -> 73.5 us (level)
    pallas_call x5 -> x4, Pallas kernels: 4.94 us -> 4.76 us  [project(): pl.pallas_call(functools.partial(project_kernel, n_pieces), out_shape=jax...]
where the time goes in v14:
time: 73.5 us; the launch traced here: 73.4 us
  Pallas kernels  27.9 us (38%)
  starting transfers between devices  22.2 us (30%)
  waiting for transfers between devices  22 us (30%)
  other arithmetic  0.86 us (1%)
    pallas_call x11, Pallas kernels, out_project(): pl.pallas_call(functools.partial(out_kernel, n, len(received)), grid=((st...  9.84 us
    ppermute x5, waiting for transfers between devices, shards(): received[i].append(lax.ppermute(partial, 'heads', shift_pairs(n_heads, t)))  8.86 us
    ppermute x4, waiting for transfers between devices, send(): lax.ppermute(block, 'lanes', lane_pairs(n_lanes, items[i][0], True))  7.88 us
    ppermute x2, starting transfers between devices, tables_of_lanes(): other = lax.ppermute(held, 'lanes', lane_pairs(n, step, False))  6.18 us
    pallas_call x4, Pallas kernels, attend(): pl.pallas_call(functools.partial(attend_kernel, firsts, len(own), n_heads...  5.99 us
    ppermute x4, starting transfers between devices, send(): lax.ppermute(block, 'lanes', lane_pairs(n_lanes, items[i][0], True))  5.63 us
    ppermute x5, starting transfers between devices, shards(): received[i].append(lax.ppermute(partial, 'heads', shift_pairs(n_heads, t)))  5.14 us
    pallas_call x4, Pallas kernels, project(): pl.pallas_call(functools.partial(project_kernel, n_pieces), out_shape=jax...  4.76 us
  transfers between devices with their start and end apart: 23, of which 13 were waited for; matrix products, arithmetic and copies ran while one was open for 0% of the time, Pallas kernels for 35%

profile of v14, /device:TPU:0, one launch (start us, length us, event | category | flops | bytes accessed | tf_op | source)
XLA Modules:
  0.0 73.4 jit_solution(18284425687371928348)
XLA Ops:
  0.0 0.7 pad_add_fusion.2.own_ref
  0.7 3.1 %collective-permute-start.1 = (s32[4,8]{1,0:T(4,128)S(1)}, s32[4,8]{1,0:T(4,128)S(1)}, u32[]{:S(2)}, u32[]{:S(2)}) collective-permute-start(s32[4,8]{1,0:T(4,128)S(1)} %pad_add_fusion.2.own_ref), channel_id=1, source_target_pairs={{0,4},{4,0},{8,12},{12,8},{1,5},{5,1},{9,13},{13,9},{2,6},{6,2},{1... | collective-permute-start | bytes 392 | tf_op jit(solution)/shard_map/ppermute | solution.py:49
  3.8 1.3 %plan.1 = (s32[16]{0:T(128)S(1)}, s32[16]{0:T(128)S(1)}, s32[16]{0:T(128)S(1)}) custom-call(s32[4,8]{1,0:T(4,128)S(1)} %pad_add_fusion.2.own_ref), custom_call_target="tpu_custom_call" | custom-call | flops 10000000000 | bytes 1024 | tf_op jit(solution)/shard_map/plan/pallas_call | solution.py:88
  5.4 3.1 %collective-permute-start.2 = (s32[8,8]{1,0:T(8,128)S(1)}, s32[8,8]{1,0:T(8,128)S(1)}, u32[]{:S(2)}, u32[]{:S(2)}) collective-permute-start(s32[8,8]{1,0:T(8,128)S(1)} %pad_add_fusion.1), channel_id=1, source_target_pairs={{0,8},{4,12},{8,0},{12,4},{1,9},{5,13},{9,1},{13,5},{2,10},{6,14},... | collective-permute-start | bytes 776 | tf_op jit(solution)/shard_map/ppermute | solution.py:49
  8.5 1.3 %encode_local.1 = bf16[4,32,896]{2,1,0:T(8,128)(2,1)S(1)} custom-call(s32[16]{0:T(128)S(1)} %get-tuple-element.57.req_ref, s32[16]{0:T(128)S(1)} %get-tuple-element.58.pick_ref, bf16[512,896]{1,0:T(8,128)(2,1)S(1)} %copy-done.4, bf16[16,32,896]{2,1,0:T(8,128)(2,1)S(1)} %copy-done.5), custom_call_target="tpu_custom_call" | custom-call | flops 10000000000 | bytes 1024 | tf_op jit(solution)/shard_map/encode_local/pallas_call | solution.py:216
  10.1 0.8 %fetch.1 = (bf16[2,32,896]{2,1,0:T(8,128)(2,1)S(1)}, bf16[2,32,896]{2,1,0:T(8,128)(2,1)S(1)}, bf16[4,32,896]{2,1,0:T(8,128)(2,1)S(1)}, bf16[4,32,896]{2,1,0:T(8,128)(2,1)S(1)}) custom-call(s32[16,8]{1,0:T(8,128)S(1)} %pad_add_fusion.tables_ref, bf16[16,32,896]{2,1,0:T(8,128)(2,1)S(1)} %copy-done.5), custom_call_target="tpu_custom_call" | custom-call | flops 10000000000 | bytes 1024 | tf_op jit(solution)/shard_map/fetch/pallas_call | solution.py:120
  10.9 3.0 %collective-permute-start.3 = (bf16[4,32,896]{2,1,0:T(8,128)(2,1)S(1)}, bf16[4,32,896]{2,1,0:T(8,128)(2,1)S(1)}, u32[]{:S(2)}, u32[]{:S(2)}) collective-permute-start(bf16[4,32,896]{2,1,0:T(8,128)(2,1)S(1)} %get-tuple-element.64), channel_id=1, source_target_pairs={{0,8},{4,12},{8,0},{12,4},{1,9},{5,13},{9,1},{13,5},{2,10},{6,14},... | collective-permute-start | bytes 688136 | tf_op jit(solution)/shard_map/ppermute | solution.py:401
  13.9 1.6 %collective-permute-start.4 = (bf16[2,32,896]{2,1,0:T(8,128)(2,1)S(1)}, bf16[2,32,896]{2,1,0:T(8,128)(2,1)S(1)}, u32[]{:S(2)}, u32[]{:S(2)}) collective-permute-start(bf16[2,32,896]{2,1,0:T(8,128)(2,1)S(1)} %get-tuple-element.67), channel_id=1, source_target_pairs={{0,4},{4,0},{8,12},{12,8},{1,5},{5,1},{9,13},{13,9},{2,6},{6,2},{1... | collective-permute-start | bytes 344072 | tf_op jit(solution)/shard_map/ppermute | solution.py:401
  15.9 1.5 %collective-permute-start = (bf16[4,32,896]{2,1,0:T(8,128)(2,1)S(1)}, bf16[4,32,896]{2,1,0:T(8,128)(2,1)S(1)}, u32[]{:S(2)}, u32[]{:S(2)}) collective-permute-start(bf16[4,32,896]{2,1,0:T(8,128)(2,1)S(1)} %encode_local.1), channel_id=1, source_target_pairs={{0,2},{2,0},{1,3},{3,1},{4,6},{6,4},{5,7},{7,5},{8,10},{10,8},{9,1... | collective-permute-start | bytes 688136 | tf_op jit(solution)/shard_map/ppermute | solution.py:378
  17.4 2.9 %collective-permute-done.4.refs_0_ = bf16[2,32,896]{2,1,0:T(8,128)(2,1)S(1)} collective-permute-done((bf16[2,32,896]{2,1,0:T(8,128)(2,1)S(1)}, bf16[2,32,896]{2,1,0:T(8,128)(2,1)S(1)}, u32[]{:S(2)}, u32[]{:S(2)}) %collective-permute-start.4) | collective-permute-done | bytes 114720 | tf_op jit(solution)/shard_map/ppermute | solution.py:401
  20.4 2.5 %collective-permute-done.5.refs_1_ = bf16[2,32,896]{2,1,0:T(8,128)(2,1)S(1)} collective-permute-done((bf16[2,32,896]{2,1,0:T(8,128)(2,1)S(1)}, bf16[2,32,896]{2,1,0:T(8,128)(2,1)S(1)}, u32[]{:S(2)}, u32[]{:S(2)}) %collective-permute-start.5) | collective-permute-done | bytes 114720 | tf_op jit(solution)/shard_map/ppermute | solution.py:401
  22.9 1.5 %encode.3 = bf16[4,32,896]{2,1,0:T(8,128)(2,1)S(1)} custom-call(s32[16]{0:T(128)S(1)} %get-tuple-element.57.req_ref, bf16[512,896]{1,0:T(8,128)(2,1)S(1)} %copy-done.4, bf16[2,32,896]{2,1,0:T(8,128)(2,1)S(1)} %collective-permute-done.4.refs_0_, bf16[2,32,896]{2,1,0:T(8,128)(2,1)S(1)} %collective-permute-done.5.refs_1_), custom_call_target="tpu_custom_call" | custom-call | flops 100000000 | bytes 1024 | tf_op jit(solution)/shard_map/encode/pallas_call | solution.py:197
  24.3 1.6 %collective-permute-start.7 = (bf16[4,32,896]{2,1,0:T(8,128)(2,1)S(1)}, bf16[4,32,896]{2,1,0:T(8,128)(2,1)S(1)}, u32[]{:S(2)}, u32[]{:S(2)}) collective-permute-start(bf16[4,32,896]{2,1,0:T(8,128)(2,1)S(1)} %encode.3), channel_id=1, source_target_pairs={{0,2},{2,0},{1,3},{3,1},{4,6},{6,4},{5,7},{7,5},{8,10},{10,8},{9,1... | collective-permute-start | bytes 688136 | tf_op jit(solution)/shard_map/ppermute | solution.py:378
  25.9 0.6 collective-permute-start.10
  26.5 1.3 %encode.4 = bf16[4,32,896]{2,1,0:T(8,128)(2,1)S(1)} custom-call(s32[16]{0:T(128)S(1)} %get-tuple-element.57.req_ref, bf16[512,896]{1,0:T(8,128)(2,1)S(1)} %copy-done.4, bf16[4,32,896]{2,1,0:T(8,128)(2,1)S(1)} %collective-permute-done.3.refs_0_), custom_call_target="tpu_custom_call" | custom-call | flops 10000000000 | bytes 1024 | tf_op jit(solution)/shard_map/encode/pallas_call | solution.py:197
  27.8 0.6 collective-permute-start.9
  28.5 2.7 %collective-permute-done.7 = bf16[4,32,896]{2,1,0:T(8,128)(2,1)S(1)} collective-permute-done((bf16[4,32,896]{2,1,0:T(8,128)(2,1)S(1)}, bf16[4,32,896]{2,1,0:T(8,128)(2,1)S(1)}, u32[]{:S(2)}, u32[]{:S(2)}) %collective-permute-start.7) | collective-permute-done | bytes 229408 | tf_op jit(solution)/shard_map/ppermute | solution.py:378
  31.4 2.4 %collective-permute-done.10.refs_0_ = bf16[4,32,896]{2,1,0:T(8,128)(2,1)S(1)} collective-permute-done((bf16[4,32,896]{2,1,0:T(8,128)(2,1)S(1)}, bf16[4,32,896]{2,1,0:T(8,128)(2,1)S(1)}, u32[]{:S(2)}, u32[]{:S(2)}) %collective-permute-start.10) | collective-permute-done | bytes 229408 | tf_op jit(solution)/shard_map/ppermute | solution.py:401
  33.8 1.3 %encode.5 = bf16[4,32,896]{2,1,0:T(8,128)(2,1)S(1)} custom-call(s32[16]{0:T(128)S(1)} %get-tuple-element.57.req_ref, bf16[512,896]{1,0:T(8,128)(2,1)S(1)} %copy-done.4, bf16[4,32,896]{2,1,0:T(8,128)(2,1)S(1)} %collective-permute-done.10.refs_0_), custom_call_target="tpu_custom_call" | custom-call | flops 10000000000 | bytes 1024 | tf_op jit(solution)/shard_map/encode/pallas_call | solution.py:197
  35.1 0.6 collective-permute-start.13
  35.9 2.3 %project.4.refs_0_ = bf16[8,4,32,1024]{3,2,1,0:T(8,128)(2,1)S(1)} custom-call(bf16[2,4,32,896]{3,2,1,0:T(8,128)(2,1)S(1)} %pad_maximum_fusion.refs_0_, bf16[2,4,32,896]{3,2,1,0:T(8,128)(2,1)S(1)} %collective-permute-done.6.refs_1_, bf16[2,4,32,896]{3,2,1,0:T(8,128)(2,1)S(1)} %pad_maximum_fusion.1.refs_2_, ...), custom_call_target="tpu_custom_call" | custom-call | flops 10000000000 | bytes 1024 | tf_op jit(solution)/shard_map/project/pallas_call | solution.py:254
  38.2 0.5 collective-permute-start.12
  38.8 1.2 %project.5.refs_1_ = bf16[4,4,32,1024]{3,2,1,0:T(8,128)(2,1)S(1)} custom-call(bf16[2,4,32,896]{3,2,1,0:T(8,128)(2,1)S(1)} %pad_maximum_fusion.2.refs_0_, bf16[2,4,32,896]{3,2,1,0:T(8,128)(2,1)S(1)} %collective-permute-done.11.refs_1_, bf16[896,512]{1,0:T(8,128)(2,1)S(1)} %copy-done.2, bf16[896,512]{1,0:T(8,128)(2,1)S(1)} %copy-done.3), custom_call_target="tpu_custom_call" | custom-call | flops 10000000000 | bytes 1024 | tf_op jit(solution)/shard_map/project/pallas_call | solution.py:254
  40.0 0.7 project.6.refs_2_
  41.2 0.5 project.7.refs_3_
  41.6 1.0 %collective-permute-done.14.refs_4_ = bf16[1,4,32,896]{3,2,1,0:T(8,128)(2,1)S(1)} collective-permute-done((bf16[1,4,32,896]{3,2,1,0:T(8,128)(2,1)S(1)}, bf16[1,4,32,896]{3,2,1,0:T(8,128)(2,1)S(1)}, u32[]{:S(2)}, u32[]{:S(2)}) %collective-permute-start.14) | collective-permute-done | bytes 229408 | tf_op jit(solution)/shard_map/ppermute | solution.py:381
  42.7 1.8 %attend.4 = (bf16[1,128,512]{2,1,0:T(8,128)(2,1)S(1)}, bf16[4,1,32,1024]{3,2,1,0:T(8,128)(2,1)S(1)}) custom-call(s32[16]{0:T(128)S(1)} %get-tuple-element.56.slot_ref, bf16[512,512]{1,0:T(8,128)(2,1)S(1)} %copy-done.1, bf16[8,4,32,1024]{3,2,1,0:T(8,128)(2,1)S(1)} %project.4.refs_0_, bf16[4,4,32,1024]{3,2,1,0:T(8,128)(2,1)S(1)} %project.5.refs_1_, ...), custom_call_target="tpu_custom_call" | custom-call | flops 1000000 | bytes 1024 | tf_op jit(solution)/shard_map/attend/pallas_call | solution.py:325
  44.7 1.4 %attend.5.refs_0_ = bf16[1,128,512]{2,1,0:T(8,128)(2,1)S(1)} custom-call(s32[16]{0:T(128)S(1)} %get-tuple-element.56.slot_ref, bf16[512,512]{1,0:T(8,128)(2,1)S(1)} %copy-done.1, bf16[8,4,32,1024]{3,2,1,0:T(8,128)(2,1)S(1)} %project.4.refs_0_, bf16[4,4,32,1024]{3,2,1,0:T(8,128)(2,1)S(1)} %project.5.refs_1_, bf16[4,2,32,1024]{3,2,1,0:T(8,128)(2,1)S(1)} %project.6.refs_2_, ...), custom_call_target="tpu_custom_call" | custom-call | flops 1000000 | bytes 1024 | tf_op jit(solution)/shard_map/attend/pallas_call | solution.py:325
  46.1 1.0 %out_project.6 = bf16[128,1024]{1,0:T(8,128)(2,1)S(1)} custom-call(bf16[1,128,512]{2,1,0:T(8,128)(2,1)S(1)} %attend.5.refs_0_, bf16[1,128,512]{2,1,0:T(8,128)(2,1)S(1)} %collective-permute-done.15.refs_1_, bf16[512,4096]{1,0:T(8,128)(2,1)S(1)} %copy-done, bf16[512,4096]{1,0:T(8,128)(2,1)S(1)} %collective-permute-done.16.refs_3_), custom_call_target="tpu_custom_call" | custom-call | flops 1000000 | bytes 1024 | tf_op jit(solution)/shard_map/out_project/pallas_call | solution.py:350
  47.2 1.3 %collective-permute-start.22 = (bf16[128,1024]{1,0:T(8,128)(2,1)S(1)}, bf16[128,1024]{1,0:T(8,128)(2,1)S(1)}, u32[]{:S(2)}, u32[]{:S(2)}) collective-permute-start(bf16[128,1024]{1,0:T(8,128)(2,1)S(1)} %out_project.6), channel_id=1, source_target_pairs={{0,2},{2,0},{1,3},{3,1},{4,6},{6,4},{5,7},{7,5},{8,10},{10,8},{9,1... | collective-permute-start | bytes 786440 | tf_op jit(solution)/shard_map/ppermute | solution.py:458
  48.5 0.8 %out_project.7 = bf16[128,1024]{1,0:T(8,128)(2,1)S(1)} custom-call(bf16[1,128,512]{2,1,0:T(8,128)(2,1)S(1)} %attend.5.refs_0_, bf16[1,128,512]{2,1,0:T(8,128)(2,1)S(1)} %collective-permute-done.15.refs_1_, bf16[512,4096]{1,0:T(8,128)(2,1)S(1)} %copy-done, bf16[512,4096]{1,0:T(8,128)(2,1)S(1)} %collective-permute-done.16.refs_3_), custom_call_target="tpu_custom_call" | custom-call | flops 1000000 | bytes 1024 | tf_op jit(solution)/shard_map/out_project/pallas_call | solution.py:350
  49.3 0.9 %collective-permute-start.21 = (bf16[128,1024]{1,0:T(8,128)(2,1)S(1)}, bf16[128,1024]{1,0:T(8,128)(2,1)S(1)}, u32[]{:S(2)}, u32[]{:S(2)}) collective-permute-start(bf16[128,1024]{1,0:T(8,128)(2,1)S(1)} %out_project.7), channel_id=1, source_target_pairs={{0,2},{2,0},{1,3},{3,1},{4,6},{6,4},{5,7},{7,5},{8,10},{10,8},{9,1... | collective-permute-start | bytes 786440 | tf_op jit(solution)/shard_map/ppermute | solution.py:458
  50.2 0.9 %out_project.8 = bf16[128,1024]{1,0:T(8,128)(2,1)S(1)} custom-call(bf16[1,128,512]{2,1,0:T(8,128)(2,1)S(1)} %attend.5.refs_0_, bf16[1,128,512]{2,1,0:T(8,128)(2,1)S(1)} %collective-permute-done.15.refs_1_, bf16[512,4096]{1,0:T(8,128)(2,1)S(1)} %copy-done, bf16[512,4096]{1,0:T(8,128)(2,1)S(1)} %collective-permute-done.16.refs_3_), custom_call_target="tpu_custom_call" | custom-call | flops 1000000 | bytes 1024 | tf_op jit(solution)/shard_map/out_project/pallas_call | solution.py:350
  51.1 1.3 %collective-permute-start.20 = (bf16[128,1024]{1,0:T(8,128)(2,1)S(1)}, bf16[128,1024]{1,0:T(8,128)(2,1)S(1)}, u32[]{:S(2)}, u32[]{:S(2)}) collective-permute-start(bf16[128,1024]{1,0:T(8,128)(2,1)S(1)} %out_project.8), channel_id=1, source_target_pairs={{0,2},{2,0},{1,3},{3,1},{4,6},{6,4},{5,7},{7,5},{8,10},{10,8},{9,1... | collective-permute-start | bytes 786440 | tf_op jit(solution)/shard_map/ppermute | solution.py:458
  53.0 1.4 %attend.7 = bf16[1,128,512]{2,1,0:T(8,128)(2,1)S(1)} custom-call(s32[16]{0:T(128)S(1)} %get-tuple-element.56.slot_ref, bf16[512,512]{1,0:T(8,128)(2,1)S(1)} %copy-done.1, bf16[8,4,32,1024]{3,2,1,0:T(8,128)(2,1)S(1)} %project.4.refs_0_, bf16[4,4,32,1024]{3,2,1,0:T(8,128)(2,1)S(1)} %project.5.refs_1_, bf16[4,2,32,1024]{3,2,1,0:T(8,128)(2,1)S(1)} %project.6.refs_2_, ...), custom_call_target="tpu_custom_call" | custom-call | flops 1000000 | bytes 1024 | tf_op jit(solution)/shard_map/attend/pallas_call | solution.py:325
  54.4 0.9 %collective-permute-start.19 = (bf16[128,512]{1,0:T(8,128)(2,1)S(1)}, bf16[128,512]{1,0:T(8,128)(2,1)S(1)}, u32[]{:S(2)}, u32[]{:S(2)}) collective-permute-start(bf16[128,512]{1,0:T(8,128)(2,1)S(1)} %out_project.9), channel_id=1, source_target_pairs={{0,2},{2,0},{1,3},{3,1},{4,6},{6,4},{5,7},{7,5},{8,10},{10,8},{9,1... | collective-permute-start | bytes 393224 | tf_op jit(solution)/shard_map/ppermute | solution.py:458
  55.3 0.5 collective-permute-done.17.refs_1_
  55.8 0.8 %collective-permute-start.18 = (bf16[128,512]{1,0:T(8,128)(2,1)S(1)}, bf16[128,512]{1,0:T(8,128)(2,1)S(1)}, u32[]{:S(2)}, u32[]{:S(2)}) collective-permute-start(bf16[128,512]{1,0:T(8,128)(2,1)S(1)} %out_project.10), channel_id=1, source_target_pairs={{0,2},{2,0},{1,3},{3,1},{4,6},{6,4},{5,7},{7,5},{8,10},{10,8},{9,1... | collective-permute-start | bytes 393224 | tf_op jit(solution)/shard_map/ppermute | solution.py:458
  56.6 1.4 %attend.6.refs_0_ = bf16[1,128,512]{2,1,0:T(8,128)(2,1)S(1)} custom-call(s32[16]{0:T(128)S(1)} %get-tuple-element.56.slot_ref, bf16[512,512]{1,0:T(8,128)(2,1)S(1)} %copy-done.1, bf16[8,4,32,1024]{3,2,1,0:T(8,128)(2,1)S(1)} %project.4.refs_0_, bf16[4,4,32,1024]{3,2,1,0:T(8,128)(2,1)S(1)} %project.5.refs_1_, bf16[4,2,32,1024]{3,2,1,0:T(8,128)(2,1)S(1)} %project.6.refs_2_, ...), custom_call_target="tpu_custom_call" | custom-call | flops 1000000 | bytes 1024 | tf_op jit(solution)/shard_map/attend/pallas_call | solution.py:325
  58.3 1.5 %out_final.5.refs_5_ = bf16[128,4096]{1,0:T(8,128)(2,1)} custom-call(bf16[1,128,512]{2,1,0:T(8,128)(2,1)S(1)} %attend.6.refs_0_, bf16[1,128,512]{2,1,0:T(8,128)(2,1)S(1)} %collective-permute-done.17.refs_1_, bf16[512,4096]{1,0:T(8,128)(2,1)S(1)} %copy-done, bf16[512,4096]{1,0:T(8,128)(2,1)S(1)} %collective-permute-done.16.refs_3_, ...), custom_call_target="tpu_custom_call" | custom-call | flops 200000000 | bytes 1024 | tf_op jit(solution)/shard_map/out_final/pallas_call | solution.py:350
  59.8 2.2 %collective-permute-done.21.refs_4_ = bf16[128,1024]{1,0:T(8,128)(2,1)S(1)} collective-permute-done((bf16[128,1024]{1,0:T(8,128)(2,1)S(1)}, bf16[128,1024]{1,0:T(8,128)(2,1)S(1)}, u32[]{:S(2)}, u32[]{:S(2)}) %collective-permute-start.21) | collective-permute-done | bytes 262176 | tf_op jit(solution)/shard_map/ppermute | solution.py:458
  62.0 1.5 %out_final.6.refs_5_ = bf16[128,4096]{1,0:T(8,128)(2,1)} custom-call(bf16[1,128,512]{2,1,0:T(8,128)(2,1)S(1)} %attend.6.refs_0_, bf16[1,128,512]{2,1,0:T(8,128)(2,1)S(1)} %collective-permute-done.17.refs_1_, bf16[512,4096]{1,0:T(8,128)(2,1)S(1)} %copy-done, bf16[512,4096]{1,0:T(8,128)(2,1)S(1)} %collective-permute-done.16.refs_3_, ...), custom_call_target="tpu_custom_call", output_to_operand_aliasing={{}: (5, {})} | custom-call | flops 200000000 | bytes 1024 | tf_op jit(solution)/shard_map/out_final/pallas_call | solution.py:350
  63.5 4.1 %collective-permute-done.20.refs_4_ = bf16[128,1024]{1,0:T(8,128)(2,1)S(1)} collective-permute-done((bf16[128,1024]{1,0:T(8,128)(2,1)S(1)}, bf16[128,1024]{1,0:T(8,128)(2,1)S(1)}, u32[]{:S(2)}, u32[]{:S(2)}) %collective-permute-start.20) | collective-permute-done | bytes 262176 | tf_op jit(solution)/shard_map/ppermute | solution.py:458
  67.6 1.5 %out_final.7.refs_5_ = bf16[128,4096]{1,0:T(8,128)(2,1)} custom-call(bf16[1,128,512]{2,1,0:T(8,128)(2,1)S(1)} %attend.6.refs_0_, bf16[1,128,512]{2,1,0:T(8,128)(2,1)S(1)} %collective-permute-done.17.refs_1_, bf16[512,4096]{1,0:T(8,128)(2,1)S(1)} %copy-done, bf16[512,4096]{1,0:T(8,128)(2,1)S(1)} %collective-permute-done.16.refs_3_, ...), custom_call_target="tpu_custom_call", output_to_operand_aliasing={{}: (5, {})} | custom-call | flops 200000000 | bytes 1024 | tf_op jit(solution)/shard_map/out_final/pallas_call | solution.py:350
  69.1 1.3 %collective-permute-done.19.refs_4_ = bf16[128,512]{1,0:T(8,128)(2,1)S(1)} collective-permute-done((bf16[128,512]{1,0:T(8,128)(2,1)S(1)}, bf16[128,512]{1,0:T(8,128)(2,1)S(1)}, u32[]{:S(2)}, u32[]{:S(2)}) %collective-permute-start.19) | collective-permute-done | bytes 131104 | tf_op jit(solution)/shard_map/ppermute | solution.py:458
  70.4 1.0 %out_final.8.refs_2_ = bf16[128,4096]{1,0:T(8,128)(2,1)} custom-call(bf16[1,128,512]{2,1,0:T(8,128)(2,1)S(1)} %attend.6.refs_0_, bf16[1,128,512]{2,1,0:T(8,128)(2,1)S(1)} %collective-permute-done.17.refs_1_, bf16[512,4096]{1,0:T(8,128)(2,1)S(1)} %copy-done, bf16[512,4096]{1,0:T(8,128)(2,1)S(1)} %collective-permute-done.16.refs_3_, ...), custom_call_target="tpu_custom_call", output_to_operand_aliasing={{}: (5, {})} | custom-call | flops 200000000 | bytes 1024 | tf_op jit(solution)/shard_map/out_final/pallas_call | solution.py:350
  71.4 1.3 %collective-permute-done.18.refs_1_ = bf16[128,512]{1,0:T(8,128)(2,1)S(1)} collective-permute-done((bf16[128,512]{1,0:T(8,128)(2,1)S(1)}, bf16[128,512]{1,0:T(8,128)(2,1)S(1)}, u32[]{:S(2)}, u32[]{:S(2)}) %collective-permute-start.18) | collective-permute-done | bytes 131104 | tf_op jit(solution)/shard_map/ppermute | solution.py:458
  72.7 0.7 out_final.9
  (41 shorter events, 3.1 us)
Async XLA Ops:
  0.7 7.8 %copy-start.4 = (bf16[512,896]{1,0:T(8,128)(2,1)S(1)}, bf16[512,896]{1,0:T(8,128)(2,1)}, u32[]{:S(2)}) copy-start(bf16[512,896]{1,0:T(8,128)(2,1)} %states_ref.7) | copy-start | bytes 2752516
  0.7 7.8 %copy-start.5 = (bf16[16,32,896]{2,1,0:T(8,128)(2,1)S(1)}, bf16[16,32,896]{2,1,0:T(8,128)(2,1)}, u32[]{:S(2)}) copy-start(bf16[16,32,896]{2,1,0:T(8,128)(2,1)} %store_ref.3) | copy-start | bytes 2752516
  0.7 4.7 %collective-permute-start.1 = (s32[4,8]{1,0:T(4,128)S(1)}, s32[4,8]{1,0:T(4,128)S(1)}, u32[]{:S(2)}, u32[]{:S(2)}) collective-permute-start(s32[4,8]{1,0:T(4,128)S(1)} %pad_add_fusion.2.own_ref), channel_id=1, source_target_pairs={{0,4},{4,0},{8,12},{12,8},{1,5},{5,1},{9,13},{13,9},{2,6},{6,2},{1... | collective-permute-start | bytes 392 | tf_op jit(solution)/shard_map/ppermute | solution.py:49
  5.4 4.7 %collective-permute-start.2 = (s32[8,8]{1,0:T(8,128)S(1)}, s32[8,8]{1,0:T(8,128)S(1)}, u32[]{:S(2)}, u32[]{:S(2)}) collective-permute-start(s32[8,8]{1,0:T(8,128)S(1)} %pad_add_fusion.1), channel_id=1, source_target_pairs={{0,8},{4,12},{8,0},{12,4},{1,9},{5,13},{9,1},{13,5},{2,10},{6,14},... | collective-permute-start | bytes 776 | tf_op jit(solution)/shard_map/ppermute | solution.py:49
  10.1 7.4 %copy-start = (bf16[512,4096]{1,0:T(8,128)(2,1)S(1)}, bf16[512,4096]{1,0:T(8,128)(2,1)}, u32[]{:S(2)}) copy-start(bf16[512,4096]{1,0:T(8,128)(2,1)} %refs_2_.25) | copy-start | bytes 12582916
  10.9 15.6 %collective-permute-start.3 = (bf16[4,32,896]{2,1,0:T(8,128)(2,1)S(1)}, bf16[4,32,896]{2,1,0:T(8,128)(2,1)S(1)}, u32[]{:S(2)}, u32[]{:S(2)}) collective-permute-start(bf16[4,32,896]{2,1,0:T(8,128)(2,1)S(1)} %get-tuple-element.64), channel_id=1, source_target_pairs={{0,8},{4,12},{8,0},{12,4},{1,9},{5,13},{9,1},{13,5},{2,10},{6,14},... | collective-permute-start | bytes 688136 | tf_op jit(solution)/shard_map/ppermute | solution.py:401
  13.9 6.5 %collective-permute-start.4 = (bf16[2,32,896]{2,1,0:T(8,128)(2,1)S(1)}, bf16[2,32,896]{2,1,0:T(8,128)(2,1)S(1)}, u32[]{:S(2)}, u32[]{:S(2)}) collective-permute-start(bf16[2,32,896]{2,1,0:T(8,128)(2,1)S(1)} %get-tuple-element.67), channel_id=1, source_target_pairs={{0,4},{4,0},{8,12},{12,8},{1,5},{5,1},{9,13},{13,9},{2,6},{6,2},{1... | collective-permute-start | bytes 344072 | tf_op jit(solution)/shard_map/ppermute | solution.py:401
  15.5 7.4 %collective-permute-start.5 = (bf16[2,32,896]{2,1,0:T(8,128)(2,1)S(1)}, bf16[2,32,896]{2,1,0:T(8,128)(2,1)S(1)}, u32[]{:S(2)}, u32[]{:S(2)}) collective-permute-start(bf16[2,32,896]{2,1,0:T(8,128)(2,1)S(1)} %get-tuple-element.68), channel_id=1, source_target_pairs={{0,4},{4,0},{8,12},{12,8},{1,5},{5,1},{9,13},{13,9},{2,6},{6,2},{1... | collective-permute-start | bytes 344072 | tf_op jit(solution)/shard_map/ppermute | solution.py:401
  15.9 12.5 %collective-permute-start = (bf16[4,32,896]{2,1,0:T(8,128)(2,1)S(1)}, bf16[4,32,896]{2,1,0:T(8,128)(2,1)S(1)}, u32[]{:S(2)}, u32[]{:S(2)}) collective-permute-start(bf16[4,32,896]{2,1,0:T(8,128)(2,1)S(1)} %encode_local.1), channel_id=1, source_target_pairs={{0,2},{2,0},{1,3},{3,1},{4,6},{6,4},{5,7},{7,5},{8,10},{10,8},{9,1... | collective-permute-start | bytes 688136 | tf_op jit(solution)/shard_map/ppermute | solution.py:378
  17.4 28.7 %collective-permute-start.16 = (bf16[512,4096]{1,0:T(8,128)(2,1)S(1)}, bf16[512,4096]{1,0:T(8,128)(2,1)S(1)}, u32[]{:S(2)}, u32[]{:S(2)}) collective-permute-start(bf16[512,4096]{1,0:T(8,128)(2,1)S(1)} %copy-done), channel_id=1, source_target_pairs={{0,1},{1,0},{2,3},{3,2},{4,5},{5,4},{6,7},{7,6},{8,9},{9,8},{10,11... | collective-permute-start | bytes 12582920 | tf_op jit(solution)/shard_map/ppermute | solution.py:381
  24.3 6.9 %collective-permute-start.7 = (bf16[4,32,896]{2,1,0:T(8,128)(2,1)S(1)}, bf16[4,32,896]{2,1,0:T(8,128)(2,1)S(1)}, u32[]{:S(2)}, u32[]{:S(2)}) collective-permute-start(bf16[4,32,896]{2,1,0:T(8,128)(2,1)S(1)} %encode.3), channel_id=1, source_target_pairs={{0,2},{2,0},{1,3},{3,1},{4,6},{6,4},{5,7},{7,5},{8,10},{10,8},{9,1... | collective-permute-start | bytes 688136 | tf_op jit(solution)/shard_map/ppermute | solution.py:378
  25.9 7.9 %collective-permute-start.10 = (bf16[4,32,896]{2,1,0:T(8,128)(2,1)S(1)}, bf16[4,32,896]{2,1,0:T(8,128)(2,1)S(1)}, u32[]{:S(2)}, u32[]{:S(2)}) collective-permute-start(bf16[4,32,896]{2,1,0:T(8,128)(2,1)S(1)} %get-tuple-element.81), channel_id=1, source_target_pairs={{0,12},{4,8},{8,4},{12,0},{1,13},{5,9},{9,5},{13,1},{2,14},{6,10},... | collective-permute-start | bytes 688136 | tf_op jit(solution)/shard_map/ppermute | solution.py:401
  27.8 7.9 %collective-permute-start.9 = (bf16[4,32,896]{2,1,0:T(8,128)(2,1)S(1)}, bf16[4,32,896]{2,1,0:T(8,128)(2,1)S(1)}, u32[]{:S(2)}, u32[]{:S(2)}) collective-permute-start(bf16[4,32,896]{2,1,0:T(8,128)(2,1)S(1)} %encode.4), channel_id=1, source_target_pairs={{0,2},{2,0},{1,3},{3,1},{4,6},{6,4},{5,7},{7,5},{8,10},{10,8},{9,1... | collective-permute-start | bytes 688136 | tf_op jit(solution)/shard_map/ppermute | solution.py:378
  28.4 7.4 %collective-permute-start.6 = (bf16[2,4,32,896]{3,2,1,0:T(8,128)(2,1)S(1)}, bf16[2,4,32,896]{3,2,1,0:T(8,128)(2,1)S(1)}, u32[]{:S(2)}, u32[]{:S(2)}) collective-permute-start(bf16[2,4,32,896]{3,2,1,0:T(8,128)(2,1)S(1)} %pad_maximum_fusion.refs_0_), channel_id=1, source_target_pairs={{0,1},{1,0},{2,3},{3,2},{4,5},{5,4},{6,7},{7,6},{8,9},{9,8},{10,11... | collective-permute-start | bytes 1376264 | tf_op jit(solution)/shard_map/ppermute | solution.py:381
  31.3 4.5 %copy-start.2 = (bf16[896,512]{1,0:T(8,128)(2,1)S(1)}, bf16[896,512]{1,0:T(8,128)(2,1)}, u32[]{:S(2)}) copy-start(bf16[896,512]{1,0:T(8,128)(2,1)} %refs_5_.3) | copy-start | bytes 2752516
  31.3 4.5 %copy-start.3 = (bf16[896,512]{1,0:T(8,128)(2,1)S(1)}, bf16[896,512]{1,0:T(8,128)(2,1)}, u32[]{:S(2)}) copy-start(bf16[896,512]{1,0:T(8,128)(2,1)} %refs_6_.1) | copy-start | bytes 2752516
  31.3 4.5 %collective-permute-start.8 = (bf16[2,4,32,896]{3,2,1,0:T(8,128)(2,1)S(1)}, bf16[2,4,32,896]{3,2,1,0:T(8,128)(2,1)S(1)}, u32[]{:S(2)}, u32[]{:S(2)}) collective-permute-start(bf16[2,4,32,896]{3,2,1,0:T(8,128)(2,1)S(1)} %pad_maximum_fusion.1.refs_2_), channel_id=1, source_target_pairs={{0,1},{1,0},{2,3},{3,2},{4,5},{5,4},{6,7},{7,6},{8,9},{9,8},{10,11... | collective-permute-start | bytes 1376264 | tf_op jit(solution)/shard_map/ppermute | solution.py:381
  35.1 6.1 %collective-permute-start.13 = (bf16[4,32,896]{2,1,0:T(8,128)(2,1)S(1)}, bf16[4,32,896]{2,1,0:T(8,128)(2,1)S(1)}, u32[]{:S(2)}, u32[]{:S(2)}) collective-permute-start(bf16[4,32,896]{2,1,0:T(8,128)(2,1)S(1)} %encode.5), channel_id=1, source_target_pairs={{0,2},{2,0},{1,3},{3,1},{4,6},{6,4},{5,7},{7,5},{8,10},{10,8},{9,1... | collective-permute-start | bytes 688136 | tf_op jit(solution)/shard_map/ppermute | solution.py:378
  35.7 3.0 %collective-permute-start.11 = (bf16[2,4,32,896]{3,2,1,0:T(8,128)(2,1)S(1)}, bf16[2,4,32,896]{3,2,1,0:T(8,128)(2,1)S(1)}, u32[]{:S(2)}, u32[]{:S(2)}) collective-permute-start(bf16[2,4,32,896]{3,2,1,0:T(8,128)(2,1)S(1)} %pad_maximum_fusion.2.refs_0_), channel_id=1, source_target_pairs={{0,1},{1,0},{2,3},{3,2},{4,5},{5,4},{6,7},{7,6},{8,9},{9,8},{10,11... | collective-permute-start | bytes 1376264 | tf_op jit(solution)/shard_map/ppermute | solution.py:381
  38.2 1.8 %collective-permute-start.12 = (bf16[4,32,896]{2,1,0:T(8,128)(2,1)S(1)}, bf16[4,32,896]{2,1,0:T(8,128)(2,1)S(1)}, u32[]{:S(2)}, u32[]{:S(2)}) collective-permute-start(bf16[4,32,896]{2,1,0:T(8,128)(2,1)S(1)} %encode.5), channel_id=1, source_target_pairs={{0,1},{1,0},{2,3},{3,2},{4,5},{5,4},{6,7},{7,6},{8,9},{9,8},{10,11... | collective-permute-start | bytes 688136 | tf_op jit(solution)/shard_map/ppermute | solution.py:381
  41.2 1.5 %copy-start.1 = (bf16[512,512]{1,0:T(8,128)(2,1)S(1)}, bf16[512,512]{1,0:T(8,128)(2,1)}, u32[]{:S(2)}) copy-start(bf16[512,512]{1,0:T(8,128)(2,1)} %q_ref.5) | copy-start | bytes 1572868
  41.2 1.5 %collective-permute-start.14 = (bf16[1,4,32,896]{3,2,1,0:T(8,128)(2,1)S(1)}, bf16[1,4,32,896]{3,2,1,0:T(8,128)(2,1)S(1)}, u32[]{:S(2)}, u32[]{:S(2)}) collective-permute-start(bf16[1,4,32,896]{3,2,1,0:T(8,128)(2,1)S(1)} %bitcast.14), channel_id=1, source_target_pairs={{0,1},{1,0},{2,3},{3,2},{4,5},{5,4},{6,7},{7,6},{8,9},{9,8},{10,11... | collective-permute-start | bytes 688136 | tf_op jit(solution)/shard_map/ppermute | solution.py:381
  44.5 1.6 %collective-permute-start.15 = (bf16[1,128,512]{2,1,0:T(8,128)(2,1)S(1)}, bf16[1,128,512]{2,1,0:T(8,128)(2,1)S(1)}, u32[]{:S(2)}, u32[]{:S(2)}) collective-permute-start(bf16[1,128,512]{2,1,0:T(8,128)(2,1)S(1)} %get-tuple-element.92), channel_id=1, source_target_pairs={{0,1},{1,0},{2,3},{3,2},{4,5},{5,4},{6,7},{7,6},{8,9},{9,8},{10,11... | collective-permute-start | bytes 393224 | tf_op jit(solution)/shard_map/ppermute | solution.py:441
  47.2 11.2 %collective-permute-start.22 = (bf16[128,1024]{1,0:T(8,128)(2,1)S(1)}, bf16[128,1024]{1,0:T(8,128)(2,1)S(1)}, u32[]{:S(2)}, u32[]{:S(2)}) collective-permute-start(bf16[128,1024]{1,0:T(8,128)(2,1)S(1)} %out_project.6), channel_id=1, source_target_pairs={{0,2},{2,0},{1,3},{3,1},{4,6},{6,4},{5,7},{7,5},{8,10},{10,8},{9,1... | collective-permute-start | bytes 786440 | tf_op jit(solution)/shard_map/ppermute | solution.py:458
  49.3 12.7 %collective-permute-start.21 = (bf16[128,1024]{1,0:T(8,128)(2,1)S(1)}, bf16[128,1024]{1,0:T(8,128)(2,1)S(1)}, u32[]{:S(2)}, u32[]{:S(2)}) collective-permute-start(bf16[128,1024]{1,0:T(8,128)(2,1)S(1)} %out_project.7), channel_id=1, source_target_pairs={{0,2},{2,0},{1,3},{3,1},{4,6},{6,4},{5,7},{7,5},{8,10},{10,8},{9,1... | collective-permute-start | bytes 786440 | tf_op jit(solution)/shard_map/ppermute | solution.py:458
  51.1 16.5 %collective-permute-start.20 = (bf16[128,1024]{1,0:T(8,128)(2,1)S(1)}, bf16[128,1024]{1,0:T(8,128)(2,1)S(1)}, u32[]{:S(2)}, u32[]{:S(2)}) collective-permute-start(bf16[128,1024]{1,0:T(8,128)(2,1)S(1)} %out_project.8), channel_id=1, source_target_pairs={{0,2},{2,0},{1,3},{3,1},{4,6},{6,4},{5,7},{7,5},{8,10},{10,8},{9,1... | collective-permute-start | bytes 786440 | tf_op jit(solution)/shard_map/ppermute | solution.py:458
  54.4 1.4 %collective-permute-start.17 = (bf16[1,128,512]{2,1,0:T(8,128)(2,1)S(1)}, bf16[1,128,512]{2,1,0:T(8,128)(2,1)S(1)}, u32[]{:S(2)}, u32[]{:S(2)}) collective-permute-start(bf16[1,128,512]{2,1,0:T(8,128)(2,1)S(1)} %attend.7), channel_id=1, source_target_pairs={{0,1},{1,0},{2,3},{3,2},{4,5},{5,4},{6,7},{7,6},{8,9},{9,8},{10,11... | collective-permute-start | bytes 393224 | tf_op jit(solution)/shard_map/ppermute | solution.py:441
  54.4 16.0 %collective-permute-start.19 = (bf16[128,512]{1,0:T(8,128)(2,1)S(1)}, bf16[128,512]{1,0:T(8,128)(2,1)S(1)}, u32[]{:S(2)}, u32[]{:S(2)}) collective-permute-start(bf16[128,512]{1,0:T(8,128)(2,1)S(1)} %out_project.9), channel_id=1, source_target_pairs={{0,2},{2,0},{1,3},{3,1},{4,6},{6,4},{5,7},{7,5},{8,10},{10,8},{9,1... | collective-permute-start | bytes 393224 | tf_op jit(solution)/shard_map/ppermute | solution.py:458
  55.8 16.9 %collective-permute-start.18 = (bf16[128,512]{1,0:T(8,128)(2,1)S(1)}, bf16[128,512]{1,0:T(8,128)(2,1)S(1)}, u32[]{:S(2)}, u32[]{:S(2)}) collective-permute-start(bf16[128,512]{1,0:T(8,128)(2,1)S(1)} %out_project.10), channel_id=1, source_target_pairs={{0,2},{2,0},{1,3},{3,1},{4,6},{6,4},{5,7},{7,5},{8,10},{10,8},{9,1... | collective-permute-start | bytes 393224 | tf_op jit(solution)/shard_map/ppermute | solution.py:458
